TPU v7x, 32 devices: a whole 2x2x4 slice. The times are simulated.
32 devices in a mesh: fsdp: 32 (over z, y, x, core).
Axes of the slice: x: 2, y: 2, z: 4, core: 2. Of those that a mesh axis runs over, the one named last changes fastest.
Arguments:
- hidden_in: bfloat16 [16384, 1536], P('fsdp'), may hold values from -12 to 12
- lengths: int32 [32, 4], P('fsdp'), may hold values from 1 to 384, 512 in all within a row
- routes: int32 [16384, 8], P('fsdp'), may hold values from 0 to 15, all different within a row; in each aligned block of 512 rows (0 to 511, 512 to 1023, ...) at most 320 rows name the same one
- norm_attn: bfloat16 [1536], P('fsdp'), may hold values from 0.5 to 1.5
- w_query: bfloat16 [1536, 1536], P('fsdp'), may hold values from -0.625 to 0.625
- w_key: bfloat16 [1536, 512], P('fsdp'), may hold values from -0.625 to 0.625
- w_value: bfloat16 [1536, 512], P('fsdp'), may hold values from -0.15625 to 0.15625
- w_out: bfloat16 [1536, 1536], P('fsdp'), may hold values from -2 to 2
- norm_moe: bfloat16 [1536], P('fsdp'), may hold values from 0.5 to 1.5
- w_router: bfloat16 [1536, 16], P('fsdp'), may hold values from -0.078125 to 0.078125
- w_gate: bfloat16 [16, 1536, 512], P(None, 'fsdp'), may hold values from -0.15625 to 0.15625
- w_up: bfloat16 [16, 1536, 512], P(None, 'fsdp'), may hold values from -0.15625 to 0.15625
- w_down: bfloat16 [16, 512, 1536], P(None, 'fsdp'), may hold values from -6 to 6
- cotangent: bfloat16 [16384, 1536], P('fsdp'), may hold values from -12 to 12
Outputs:
- mixed: bfloat16 [16384, 1536], P('fsdp')
- grad_input: float32 [16384, 1536], P('fsdp')
- grad_norm_attn: float32 [1536], P('fsdp')
- grad_query: float32 [1536, 1536], P('fsdp')
- grad_key: float32 [1536, 512], P('fsdp')
- grad_value: float32 [1536, 512], P('fsdp')
- grad_out: float32 [1536, 1536], P('fsdp')
- grad_norm_moe: float32 [1536], P('fsdp')
- grad_router: float32 [1536, 16], P('fsdp')
- grad_gate: float32 [16, 1536, 512], P(None, 'fsdp')
- grad_up: float32 [16, 1536, 512], P(None, 'fsdp')
- grad_down: float32 [16, 512, 1536], P(None, 'fsdp')
Inputs may be any that keep to these rules, and one draw needn't show every extreme that they name: Each device's 4 lengths sum to 512. `routes`: each row names 8 different experts; the rows of one device name no expert more than 320 times.
All inputs are finite; a program needn't handle non-finite values.
Results may differ from a plain program's by a relative error of at most 0.015.
The roundings to bfloat16 on the way count: a program that leaves them out, or rounds other values in their place, can miss the bound.
Values may be sent and summed in bfloat16 or wider, within the bound.
No kernel may reach another device: no remote copies, remote signals or barrier semaphores. Data moves between devices by JAX's collectives and lax.ppermute only.
A program may use at most 512 MiB of HBM per device.

v0:
```python
import math

import jax
import jax.numpy as jnp
from jax import lax
from jax.sharding import PartitionSpec as P

HQ = 24
HK = 8
HD = 64
TOPK = 8
E = 16
CAP = 320


norm_eps = 1e-06
resid_scale = 0.22
score_scale = 0.015625
rope_base = 10000.0
masked_score = -1e30


def matmul(left, right):
    return jnp.dot(left, right, preferred_element_type=jnp.float32)


def contract_rows(left, right):
    return lax.dot_general(
        left, right, (((0,), (0,)), ((), ())), preferred_element_type=jnp.float32
    )


def contract_last(left, right):
    return lax.dot_general(
        left, right, (((1,), (1,)), ((), ())), preferred_element_type=jnp.float32
    )


def norm_back(values, rinv, gain, grad):
    scaled = gain * grad
    return rinv * scaled - values * rinv * rinv * rinv * jnp.mean(
        scaled * values, axis=-1, keepdims=True
    )


def layout(seq_lengths, row_count):
    seq_ends = jnp.cumsum(seq_lengths)
    starts = seq_ends - seq_lengths
    places = jnp.arange(row_count, dtype=jnp.int32)
    member = (places[:, None] >= starts[None, :]) & (places[:, None] < seq_ends[None, :])
    labels = jnp.arange(seq_lengths.shape[0], dtype=jnp.int32)
    segment = jnp.sum(jnp.where(member, labels[None, :], 0), axis=1)
    offset = jnp.sum(jnp.where(member, starts[None, :], 0), axis=1)
    return (segment, places - offset)


def rotate(values, position, turn_sign):
    row_count = values.shape[0]
    head_count = values.shape[1] // HD
    half_dim = HD // 2
    split_heads = values.reshape(row_count, head_count, HD)
    inv_freq = jnp.exp(
        -(jnp.arange(half_dim, dtype=jnp.float32) * (2.0 / HD)) * math.log(rope_base)
    )
    angles = position.astype(jnp.float32)[:, None] * inv_freq[None, :]
    cosine = jnp.cos(angles)[:, None, :]
    sine_val = turn_sign * jnp.sin(angles)[:, None, :]
    lower_half = split_heads[..., :half_dim]
    upper_half = split_heads[..., half_dim:]
    turned = jnp.concatenate(
        [lower_half * cosine - upper_half * sine_val, upper_half * cosine + lower_half * sine_val],
        axis=-1,
    )
    return turned.reshape(row_count, head_count * HD)


def key_mask(segment, block_size):
    row_count = segment.shape[0]
    query_at = jnp.arange(block_size, dtype=jnp.int32)
    key_at = jnp.arange(row_count, dtype=jnp.int32)
    same_seq = segment[:, None] == segment[None, :]
    return same_seq & (key_at[None, :] <= query_at[:, None])


def group_forward(q_group, k_group, v_group, segment):
    row_count = q_group.shape[0]
    block_size = min(512, row_count)
    scores = (
        jnp.einsum("qgd,kd->gqk", q_group, k_group, preferred_element_type=jnp.float32)
        * score_scale
    )
    visible = key_mask(segment, block_size)
    scores = jnp.where(visible[None], scores, masked_score)
    peak_val = jnp.max(scores, axis=-1, keepdims=True)
    expo_val = jnp.exp(scores - peak_val)
    totals = jnp.sum(expo_val, axis=-1, keepdims=True)
    prob_low = (expo_val / totals).astype(jnp.bfloat16)
    pieces = [jnp.einsum("gqk,kd->qgd", prob_low, v_group, preferred_element_type=jnp.float32)]
    norms = [(peak_val + jnp.log(totals))[..., 0]]
    return (jnp.concatenate(pieces, axis=0), jnp.concatenate(norms, axis=1))


def group_backward(q_group, k_group, v_group, grad_group, norm_group, segment):
    row_count = q_group.shape[0]
    block_size = min(512, row_count)
    key_total = jnp.zeros((row_count, HD), jnp.float32)
    value_total = jnp.zeros((row_count, HD), jnp.float32)
    scores = (
        jnp.einsum("qgd,kd->gqk", q_group, k_group, preferred_element_type=jnp.float32)
        * score_scale
    )
    visible = key_mask(segment, block_size)
    scores = jnp.where(visible[None], scores, masked_score)
    prob_f32 = jnp.exp(scores - norm_group[:, 0:block_size, None])
    prob_low = prob_f32.astype(jnp.bfloat16)
    prob_grad = jnp.einsum("qgd,kd->gqk", grad_group, v_group, preferred_element_type=jnp.float32)
    centre = jnp.sum(prob_f32 * prob_grad, axis=-1, keepdims=True)
    score_grad = (prob_f32 * (prob_grad - centre)).astype(jnp.bfloat16)
    query_parts = [
        jnp.einsum("gqk,kd->qgd", score_grad, k_group, preferred_element_type=jnp.float32)
        * score_scale
    ]
    key_total = (
        key_total
        + jnp.einsum("gqk,qgd->kd", score_grad, q_group, preferred_element_type=jnp.float32)
        * score_scale
    )
    value_total = value_total + jnp.einsum(
        "gqk,qgd->kd", prob_low, grad_group, preferred_element_type=jnp.float32
    )
    return (jnp.concatenate(query_parts, axis=0), key_total, value_total)


def slot_tables(route_ids):
    flat_ids = route_ids.reshape(-1)
    row_total = flat_ids.shape[0]
    onehot = (flat_ids[:, None] == jnp.arange(E, dtype=jnp.int32)[None, :]).astype(jnp.int32)
    earlier = jnp.cumsum(onehot, axis=0) - onehot
    slot_at = jnp.sum(earlier * onehot, axis=1)
    places = flat_ids * CAP + slot_at
    source = jnp.zeros((E * CAP,), jnp.int32).at[places].set(jnp.arange(row_total, dtype=jnp.int32))
    filled = jnp.zeros((E * CAP,), jnp.float32).at[places].set(1.0)
    return (source.reshape(E, CAP), filled.reshape(E, CAP))


def route_gates(logits, route_ids):
    picked = route_ids[:, :, None] == jnp.arange(E, dtype=jnp.int32)[None, None, :]
    chosen = jnp.sum(jnp.where(picked, logits[:, None, :], 0.0), axis=-1)
    peak_val = jnp.max(chosen, axis=-1, keepdims=True)
    expo_val = jnp.exp(chosen - peak_val)
    return (expo_val / jnp.sum(expo_val, axis=-1, keepdims=True), picked)


def shards(
    hidden_in,
    lengths,
    routes,
    norm_attn,
    w_query,
    w_key,
    w_value,
    w_out,
    norm_moe,
    w_router,
    w_gate,
    w_up,
    w_down,
    cotangent,
):
    attn_set = (
        lax.all_gather(norm_attn, "fsdp", axis=0, tiled=True),
        lax.all_gather(w_query, "fsdp", axis=0, tiled=True),
        lax.all_gather(w_key, "fsdp", axis=0, tiled=True),
        lax.all_gather(w_value, "fsdp", axis=0, tiled=True),
        lax.all_gather(w_out, "fsdp", axis=0, tiled=True),
    )
    hidden_f32 = hidden_in.astype(jnp.float32)
    cot_f32 = cotangent.astype(jnp.float32)
    row_count = hidden_f32.shape[0]
    group_size = HQ // HK
    segment, position = layout(lengths[0], row_count)
    gain_one = attn_set[0].astype(jnp.float32)
    rinv_one = lax.rsqrt(jnp.mean(hidden_f32 * hidden_f32, axis=-1, keepdims=True) + norm_eps)
    normed = (hidden_f32 * rinv_one * gain_one).astype(jnp.bfloat16)
    queries = rotate(matmul(normed, attn_set[1]), position, 1.0).astype(jnp.bfloat16)
    keys_rot = rotate(matmul(normed, attn_set[2]), position, 1.0).astype(jnp.bfloat16)
    values_b = matmul(normed, attn_set[3]).astype(jnp.bfloat16)
    q_heads = queries.reshape(row_count, HK, group_size, HD).transpose(1, 0, 2, 3)
    k_heads = keys_rot.reshape(row_count, HK, HD).transpose(1, 0, 2)
    v_heads = values_b.reshape(row_count, HK, HD).transpose(1, 0, 2)
    attended, log_norm = lax.map(
        lambda packed: group_forward(packed[0], packed[1], packed[2], segment),
        (q_heads, k_heads, v_heads),
    )
    attn_out = attended.transpose(1, 0, 2, 3).reshape(row_count, HQ * HD).astype(jnp.bfloat16)
    middle = hidden_f32 + resid_scale * matmul(attn_out, attn_set[4])
    moe_set = (
        lax.all_gather(norm_moe, "fsdp", axis=0, tiled=True),
        lax.all_gather(w_router, "fsdp", axis=0, tiled=True),
        lax.all_gather(w_gate, "fsdp", axis=1, tiled=True),
        lax.all_gather(w_up, "fsdp", axis=1, tiled=True),
        lax.all_gather(w_down, "fsdp", axis=1, tiled=True),
    )
    gain_two = moe_set[0].astype(jnp.float32)
    rinv_two = lax.rsqrt(jnp.mean(middle * middle, axis=-1, keepdims=True) + norm_eps)
    inner_b = (middle * rinv_two * gain_two).astype(jnp.bfloat16)
    logits = matmul(inner_b, moe_set[1])
    gate_mix, picked = route_gates(logits, routes)
    source, filled = slot_tables(routes)
    token_ids = source // TOPK
    slot_gate = gate_mix.reshape(-1)[source] * filled

    def expert_forward(totals, packed):
        gate_weight, up_weight, down_weight, token_row, gate_row = packed
        rows_in = inner_b[token_row]
        gate_proj = matmul(rows_in, gate_weight)
        up_proj = matmul(rows_in, up_weight)
        mid_low = (gate_proj * jax.nn.sigmoid(gate_proj) * up_proj).astype(jnp.bfloat16)
        out_rows = matmul(mid_low, down_weight)
        mix_grad = resid_scale * jnp.sum(cot_f32[token_row] * out_rows, axis=-1)
        return (
            totals.at[token_row].add(gate_row[:, None] * out_rows),
            (gate_proj, up_proj, mix_grad),
        )

    totals, kept_rows = lax.scan(
        expert_forward,
        jnp.zeros_like(hidden_f32),
        (moe_set[2], moe_set[3], moe_set[4], token_ids, slot_gate),
    )
    gate_keep, up_keep, mix_grads = kept_rows
    mixed = (middle + resid_scale * totals).astype(jnp.bfloat16)
    moe_back = (
        lax.all_gather(norm_moe, "fsdp", axis=0, tiled=True),
        lax.all_gather(w_router, "fsdp", axis=0, tiled=True),
        lax.all_gather(w_gate, "fsdp", axis=1, tiled=True),
        lax.all_gather(w_up, "fsdp", axis=1, tiled=True),
        lax.all_gather(w_down, "fsdp", axis=1, tiled=True),
    )

    def expert_backward(totals, packed):
        gate_weight, up_weight, down_weight, token_row, gate_row, gate_proj, up_proj = packed
        rows_in = inner_b[token_row]
        sigmoid_g = jax.nn.sigmoid(gate_proj)
        active = gate_proj * sigmoid_g
        mid_low = (active * up_proj).astype(jnp.bfloat16)
        out_grad = (resid_scale * gate_row[:, None] * cot_f32[token_row]).astype(jnp.bfloat16)
        mid_grad = contract_last(out_grad, down_weight)
        gate_grad = (mid_grad * up_proj * sigmoid_g * (1.0 + gate_proj * (1.0 - sigmoid_g))).astype(
            jnp.bfloat16
        )
        up_grad = (mid_grad * active).astype(jnp.bfloat16)
        rows_grad = contract_last(gate_grad, gate_weight) + contract_last(up_grad, up_weight)
        weight_grads = (
            contract_rows(rows_in, gate_grad),
            contract_rows(rows_in, up_grad),
            contract_rows(mid_low, out_grad),
        )
        return (totals.at[token_row].add(rows_grad), weight_grads)

    inner_grad, expert_grads = lax.scan(
        expert_backward,
        jnp.zeros_like(hidden_f32),
        (moe_back[2], moe_back[3], moe_back[4], token_ids, slot_gate, gate_keep, up_keep),
    )
    gate_grad_flat = (
        jnp.zeros((row_count * TOPK,), jnp.float32)
        .at[source.reshape(-1)]
        .add((mix_grads * filled).reshape(-1))
    )
    gate_grad_rows = gate_grad_flat.reshape(row_count, TOPK)
    chosen_grad = gate_mix * (
        gate_grad_rows - jnp.sum(gate_mix * gate_grad_rows, axis=-1, keepdims=True)
    )
    logit_grad = jnp.sum(jnp.where(picked, chosen_grad[:, :, None], 0.0), axis=1).astype(
        jnp.bfloat16
    )
    grad_router = contract_rows(inner_b, logit_grad)
    inner_grad = inner_grad + contract_last(logit_grad, moe_back[1])
    grad_norm_moe = jnp.sum(inner_grad * middle * rinv_two, axis=0)
    middle_grad = cot_f32 + norm_back(middle, rinv_two, gain_two, inner_grad)
    moe_sums = (
        lax.psum_scatter(grad_norm_moe, "fsdp", scatter_dimension=0, tiled=True),
        lax.psum_scatter(grad_router, "fsdp", scatter_dimension=0, tiled=True),
        lax.psum_scatter(expert_grads[0], "fsdp", scatter_dimension=1, tiled=True),
        lax.psum_scatter(expert_grads[1], "fsdp", scatter_dimension=1, tiled=True),
        lax.psum_scatter(expert_grads[2], "fsdp", scatter_dimension=1, tiled=True),
    )
    attn_back = (
        lax.all_gather(norm_attn, "fsdp", axis=0, tiled=True),
        lax.all_gather(w_query, "fsdp", axis=0, tiled=True),
        lax.all_gather(w_key, "fsdp", axis=0, tiled=True),
        lax.all_gather(w_value, "fsdp", axis=0, tiled=True),
        lax.all_gather(w_out, "fsdp", axis=0, tiled=True),
    )
    proj_grad = (resid_scale * middle_grad).astype(jnp.bfloat16)
    grad_out = contract_rows(attn_out, proj_grad)
    attn_grad = contract_last(proj_grad, attn_back[4]).astype(jnp.bfloat16)
    grad_heads = attn_grad.reshape(row_count, HK, group_size, HD).transpose(1, 0, 2, 3)
    query_heads_grad, key_heads_grad, value_heads_grad = lax.map(
        lambda packed: group_backward(
            packed[0], packed[1], packed[2], packed[3], packed[4], segment
        ),
        (q_heads, k_heads, v_heads, grad_heads, log_norm),
    )
    query_grad = rotate(
        query_heads_grad.transpose(1, 0, 2, 3).reshape(row_count, HQ * HD), position, -1.0
    ).astype(jnp.bfloat16)
    key_grad = rotate(
        key_heads_grad.transpose(1, 0, 2).reshape(row_count, HK * HD), position, -1.0
    ).astype(jnp.bfloat16)
    value_grad = (
        value_heads_grad.transpose(1, 0, 2).reshape(row_count, HK * HD).astype(jnp.bfloat16)
    )
    grad_query = contract_rows(normed, query_grad)
    grad_key = contract_rows(normed, key_grad)
    grad_value = contract_rows(normed, value_grad)
    normed_grad = (
        contract_last(query_grad, attn_back[1])
        + contract_last(key_grad, attn_back[2])
        + contract_last(value_grad, attn_back[3])
    )
    grad_norm_attn = jnp.sum(normed_grad * hidden_f32 * rinv_one, axis=0)
    input_grad = middle_grad + norm_back(hidden_f32, rinv_one, gain_one, normed_grad)
    attn_sums = (
        lax.psum_scatter(grad_norm_attn, "fsdp", scatter_dimension=0, tiled=True),
        lax.psum_scatter(grad_query, "fsdp", scatter_dimension=0, tiled=True),
        lax.psum_scatter(grad_key, "fsdp", scatter_dimension=0, tiled=True),
        lax.psum_scatter(grad_value, "fsdp", scatter_dimension=0, tiled=True),
        lax.psum_scatter(grad_out, "fsdp", scatter_dimension=0, tiled=True),
    )
    return (
        mixed,
        input_grad,
        attn_sums[0],
        attn_sums[1],
        attn_sums[2],
        attn_sums[3],
        attn_sums[4],
        moe_sums[0],
        moe_sums[1],
        moe_sums[2],
        moe_sums[3],
        moe_sums[4],
    )


def solution(mesh):
    in_specs = (
        P("fsdp", None),
        P("fsdp", None),
        P("fsdp", None),
        P("fsdp"),
        P("fsdp", None),
        P("fsdp", None),
        P("fsdp", None),
        P("fsdp", None),
        P("fsdp"),
        P("fsdp", None),
        P(None, "fsdp", None),
        P(None, "fsdp", None),
        P(None, "fsdp", None),
        P("fsdp", None),
    )
    out_specs = (
        P("fsdp", None),
        P("fsdp", None),
        P("fsdp"),
        P("fsdp", None),
        P("fsdp", None),
        P("fsdp", None),
        P("fsdp", None),
        P("fsdp"),
        P("fsdp", None),
        P(None, "fsdp", None),
        P(None, "fsdp", None),
        P(None, "fsdp", None),
    )
    return jax.shard_map(shards, mesh=mesh, in_specs=in_specs, out_specs=out_specs, check_vma=False)
```

profile of v0, /device:TPU:0, one launch (start us, length us, event | category | flops | bytes accessed | tf_op | source)
XLA Modules:
  0.0 3835.8 jit_solution(14248037960528558340)
XLA Ops:
  19.2 15.5 scatter_custom_fusion.2
  35.6 42.5 %all-reduce.5 = (bf16[1536]{0:T(1024)(128)(2,1)S(1)}, bf16[1536]{0:T(1024)(128)(2,1)S(1)}) all-reduce(bf16[1536]{0:T(1024)(128)(2,1)S(1)} %dynamic-update-slice, bf16[1536]{0:T(1024)(128)(2,1)S(1)} %dynamic-update-slice.1), channel_id=1, replica_groups=mesh['fsdp'=32] {'fsdp'}, use_global_device_ids=true, to_apply=%add | all-reduce | flops 3072 | bytes 12288
  78.1 40.4 %all-gather = bf16[32,48,16]{1,2,0:T(8,128)(2,1)S(1)} all-gather(bf16[1,48,16]{1,2,0:T(8,128)(2,1)S(1)} %bitcast.438), channel_id=1, replica_groups=mesh['fsdp'=32] {'fsdp'}, dimensions={0}, use_global_device_ids=true | all-gather | bytes 50688 | tf_op jit(solution)/shard_map/all_gather | solution.py:199
  118.8 15.5 scatter_custom_fusion.3
  147.1 43.7 %all-gather.13.cloned.1.call-done = bf16[1536,1536]{1,0:T(8,128)(2,1)} async-done(((bf16[48,1536]{1,0:T(8,128)(2,1)}), bf16[1536,1536]{1,0:T(8,128)(2,1)}) %all-gather.13.cloned.1.call-update) | async-done | bytes 4718608 | tf_op jit(solution)/shard_map/all_gather | solution.py:172
  198.1 46.7 %while.62 = (s32[]{:T(128)}, bf16[8,512,3,64]{1,3,2,0:T(8,128)(2,1)}, f32[8,3,512]{2,1,0:T(4,128)}, bf16[8,512,64]{1,2,0:T(8,128)(2,1)}, s32[512]{0:T(512)S(1)},...) while((s32[]{:T(128)}, bf16[8,512,3,64]{1,3,2,0:T(8,128)(2,1)}, ...), condition=%wide.region_7.8_spmd.clone, body=%wide.region_4.7_spmd.sunk.clone | while | flops 211548672 | bytes 11262541 | solution.py:191
  244.8 11.3 all-gather.15.cloned.1.call-done
  265.6 28.7 gather_fusion.4
  294.4 117.9 %all-gather.17.cloned.1.call-done = bf16[16,1536,512]{2,1,0:T(8,128)(2,1)} async-done(((bf16[16,48,512]{2,1,0:T(8,128)(2,1)}), bf16[16,1536,512]{2,1,0:T(8,128)(2,1)}) %all-gather.17.cloned.1.call-update) | async-done | bytes 25165840 | tf_op jit(solution)/shard_map/all_gather | solution.py:200
  412.3 155.6 %all-gather.19.cloned.1.call-done = bf16[16,1536,512]{2,1,0:T(8,128)(2,1)} async-done(((bf16[16,48,512]{2,1,0:T(8,128)(2,1)}), bf16[16,1536,512]{2,1,0:T(8,128)(2,1)}) %all-gather.19.cloned.1.call-update) | async-done | bytes 25165840 | tf_op jit(solution)/shard_map/all_gather | solution.py:201
  567.8 155.7 %all-gather.21.cloned.1.call-done = bf16[16,512,1536]{2,1,0:T(8,128)(2,1)} async-done(((bf16[16,16,1536]{2,1,0:T(8,128)(2,1)}), bf16[16,512,1536]{2,1,0:T(8,128)(2,1)}) %all-gather.21.cloned.1.call-update) | async-done | bytes 25165840 | tf_op jit(solution)/shard_map/all_gather | solution.py:202
  725.6 449.3 %while.63 = (s32[]{:T(128)}, f32[512,1536]{1,0:T(8,128)}, f32[16,320,512]{2,1,0:T(8,128)}, f32[16,320,512]{2,1,0:T(8,128)}, f32[16,320]{1,0:T(8,128)S(1)}, /*ind...) while((s32[]{:T(128)}, f32[512,1536]{1,0:T(8,128)}, ...), condition=%wide.region_20.21_spmd.clone, body=%wide.region_17.20_spmd.sunk.clone | while | flops 1512900608 | bytes 29517980 | solution.py:226
  745.7 8.4 scatter_custom_fusion.16
  773.7 8.4 scatter_custom_fusion.16
  801.8 8.4 scatter_custom_fusion.16
  829.9 8.4 scatter_custom_fusion.16
  857.9 8.4 scatter_custom_fusion.16
  886.0 8.4 scatter_custom_fusion.16
  914.1 8.4 scatter_custom_fusion.16
  942.2 8.4 scatter_custom_fusion.16
  970.2 8.4 scatter_custom_fusion.16
  998.2 8.4 scatter_custom_fusion.16
  1026.3 8.4 scatter_custom_fusion.16
  1054.3 8.4 scatter_custom_fusion.16
  1082.3 8.4 scatter_custom_fusion.16
  1110.4 8.4 scatter_custom_fusion.16
  1138.5 8.4 scatter_custom_fusion.16
  1166.5 8.4 scatter_custom_fusion.16
  1175.7 35.6 scatter_custom_fusion.4
  1213.6 614.3 %while.64 = (s32[]{:T(128)}, f32[512,1536]{1,0:T(8,128)}, f32[16,1536,512]{2,1,0:T(8,128)}, f32[16,1536,512]{2,1,0:T(8,128)}, f32[16,512,1536]{2,1,0:T(8,128)}, ...) while((s32[]{:T(128)}, f32[512,1536]{1,0:T(8,128)}, ...), condition=%wide.region_23.24_spmd.clone, body=%wide.region_21.23_spmd.sunk.clone | while | flops 3025963264 | bytes 55464672 | solution.py:261
  1282.3 8.1 scatter_fusion
  1320.7 8.1 scatter_fusion
  1358.9 8.1 scatter_fusion
  1435.5 8.1 scatter_fusion
  1473.9 8.1 scatter_fusion
  1550.7 8.1 scatter_fusion
  1589.3 8.1 scatter_fusion
  1845.9 80.6 %while.65 = (s32[]{:T(128)}, f32[8,512,3,64]{1,3,2,0:T(8,128)}, f32[8,512,64]{1,2,0:T(8,128)}, bf16[8,512,64]{1,2,0:T(8,128)(2,1)S(1)}, bf16[8,512,64]{1,2,0:T(8...) while((s32[]{:T(128)}, f32[8,512,3,64]{1,3,2,0:T(8,128)}, ...), condition=%wide.region_30.31_spmd.clone, body=%wide.region_28.30_spmd.sunk.clone | while | flops 511310336 | bytes 25793640 | solution.py:300
  1943.7 8.6 fusion.116
  1964.2 38.8 %all-reduce.4 = (f32[1536]{0:T(1024)S(1)}, f32[1536]{0:T(1024)S(1)}) all-reduce(f32[1536]{0:T(1024)S(1)} %get-tuple-element.259, f32[1536]{0:T(1024)S(1)} %get-tuple-element.257), channel_id=2, replica_groups=mesh['fsdp'=32] {'fsdp'}, use_global_device_ids=true, to_apply=%region_33.34.clone | all-reduce | flops 3072 | bytes 24576
  2009.6 10.9 reduce-scatter.25.cloned.1.call-done
  2021.9 105.2 %reduce-scatter.13.cloned.1.call-done = f32[48,512]{1,0:T(8,128)} async-done(((f32[1536,512]{1,0:T(8,128)}), f32[48,512]{1,0:T(8,128)}) %reduce-scatter.13.cloned.1.call-update) | async-done | bytes 98320 | tf_op jit(solution)/shard_map/reduce_scatter | solution.py:328
  2127.1 106.4 %reduce-scatter.15.cloned.1.call-done = f32[48,512]{1,0:T(8,128)} async-done(((f32[1536,512]{1,0:T(8,128)}), f32[48,512]{1,0:T(8,128)}) %reduce-scatter.15.cloned.1.call-update) | async-done | bytes 98320 | tf_op jit(solution)/shard_map/reduce_scatter | solution.py:329
  2233.5 141.2 %reduce-scatter.11.cloned.1.call-done = f32[48,1536]{1,0:T(8,128)} async-done(((f32[1536,1536]{1,0:T(8,128)}), f32[48,1536]{1,0:T(8,128)}) %reduce-scatter.11.cloned.1.call-update) | async-done | bytes 294928 | tf_op jit(solution)/shard_map/reduce_scatter | solution.py:327
  2374.7 141.9 %reduce-scatter.17.cloned.1.call-done = f32[48,1536]{1,0:T(8,128)} async-done(((f32[1536,1536]{1,0:T(8,128)}), f32[48,1536]{1,0:T(8,128)}) %reduce-scatter.17.cloned.1.call-update) | async-done | bytes 294928 | tf_op jit(solution)/shard_map/reduce_scatter | solution.py:330
  2516.6 437.5 %reduce-scatter.19.cloned.1.call-done = f32[16,48,512]{2,1,0:T(8,128)} async-done(((f32[16,1536,512]{2,1,0:T(8,128)}), f32[16,48,512]{2,1,0:T(8,128)}) %reduce-scatter.19.cloned.1.call-update) | async-done | bytes 1572880 | tf_op jit(solution)/shard_map/reduce_scatter | solution.py:285
  2954.1 437.5 %reduce-scatter.21.cloned.1.call-done = f32[16,48,512]{2,1,0:T(8,128)} async-done(((f32[16,1536,512]{2,1,0:T(8,128)}), f32[16,48,512]{2,1,0:T(8,128)}) %reduce-scatter.21.cloned.1.call-update) | async-done | bytes 1572880 | tf_op jit(solution)/shard_map/reduce_scatter | solution.py:286
  3391.6 437.3 %reduce-scatter.23.cloned.1.call-done = f32[16,16,1536]{2,1,0:T(8,128)} async-done(((f32[16,512,1536]{2,1,0:T(8,128)}), f32[16,16,1536]{2,1,0:T(8,128)}) %reduce-scatter.23.cloned.1.call-update) | async-done | bytes 1572880 | tf_op jit(solution)/shard_map/reduce_scatter | solution.py:287
  (800 shorter events, 1100.1 us)
Async XLA Ops:
  7.2 11.3 copy-start.25
  7.2 27.7 copy-start.38
  7.2 132.1 %all-gather.11.cloned.1.call-start = ((), (), s32[]{:S(2)}) async-start(), calls=%async_computation.9 | async-start | bytes 1622016 | tf_op jit(solution)/shard_map/all_gather | solution.py:173
  7.9 27.2 copy-start.36
  7.9 27.4 copy-start.37
  8.0 135.4 %all-gather.9.cloned.1.call-start = ((), (), s32[]{:S(2)}) async-start(), calls=%async_computation.8 | async-start | bytes 1622016 | tf_op jit(solution)/shard_map/all_gather | solution.py:174
  8.7 69.4 %copy-start.35 = (bf16[48,16]{0,1:T(8,128)(2,1)S(1)}, bf16[48,16]{0,1:T(8,128)(2,1)}, u32[]{:S(2)}) copy-start(bf16[48,16]{0,1:T(8,128)(2,1)} %param.31) | copy-start | bytes 4612
  8.7 182.1 %all-gather.13.cloned.1.call-start = ((), (), s32[]{:S(2)}) async-start(), calls=%async_computation.10 | async-start | bytes 4866048 | tf_op jit(solution)/shard_map/all_gather | solution.py:172
  9.4 246.6 %all-gather.15.cloned.1.call-start = ((), (), s32[]{:S(2)}) async-start(), calls=%async_computation.11 | async-start | bytes 4866048 | tf_op jit(solution)/shard_map/all_gather | solution.py:175
  10.0 402.2 %all-gather.17.cloned.1.call-start = ((), (), s32[]{:S(2)}) async-start(), calls=%async_computation.12 | async-start | bytes 25952256 | tf_op jit(solution)/shard_map/all_gather | solution.py:200
  10.6 557.2 %all-gather.19.cloned.1.call-start = ((), (), s32[]{:S(2)}) async-start(), calls=%async_computation.13 | async-start | bytes 25952256 | tf_op jit(solution)/shard_map/all_gather | solution.py:201
  11.2 712.3 %all-gather.21.cloned.1.call-start = ((), (), s32[]{:S(2)}) async-start(), calls=%async_computation.14 | async-start | bytes 25952256 | tf_op jit(solution)/shard_map/all_gather | solution.py:202
  11.9 2008.6 %reduce-scatter.25.cloned.1.call-start = ((), (), s32[]{:S(2)}) async-start(), calls=%async_computation.22 | async-start | bytes 811008
  78.1 112.8 %copy-start.20 = (f32[1536]{0:T(1024)}, f32[1536]{0:T(1024)S(1)}, u32[]{:S(2)}) copy-start(f32[1536]{0:T(1024)S(1)} %convert_element_type.108) | copy-start | bytes 18436
  78.1 184.4 %copy-start.26 = (f32[1536]{0:T(1024)}, f32[1536]{0:T(1024)S(1)}, u32[]{:S(2)}) copy-start(f32[1536]{0:T(1024)S(1)} %convert_element_type.118) | copy-start | bytes 18436
  118.7 144.7 %copy-start.23 = (bf16[1536,16]{0,1:T(8,128)(2,1)}, bf16[1536,16]{0,1:T(8,128)(2,1)S(1)}, u32[]{:S(2)}) copy-start(bf16[1536,16]{0,1:T(8,128)(2,1)S(1)} %reshape.604) | copy-start | bytes 147460
  138.3 52.6 %copy-start.28 = (f32[512]{0:T(512)}, f32[512]{0:T(512)S(1)}, u32[]{:S(2)}) copy-start(f32[512]{0:T(512)S(1)} %add_rsqrt_fusion.1) | copy-start | bytes 6148
  139.3 57.0 %copy-start.13 = (f32[512,32]{0,1:T(8,128)}, f32[512,32]{0,1:T(8,128)S(1)}, u32[]{:S(2)}) copy-start(f32[512,32]{0,1:T(8,128)S(1)} %get-tuple-element.377) | copy-start | bytes 196612
  244.8 17.7 copy-start.18
  294.3 431.4 %copy-start.34 = (f32[16,320]{1,0:T(8,128)S(1)}, f32[16,320]{1,0:T(8,128)}, u32[]{:S(2)}) copy-start(f32[16,320]{1,0:T(8,128)} %custom-call.13) | copy-start | bytes 61444
  1175.6 38.1 copy-start.30
  1213.6 617.3 %copy-start.24 = (bf16[1536,16]{0,1:T(8,128)(2,1)S(1)}, bf16[1536,16]{0,1:T(8,128)(2,1)}, u32[]{:S(2)}) copy-start(bf16[1536,16]{0,1:T(8,128)(2,1)} %copy-done.23) | copy-start | bytes 147460
  1213.6 617.3 %copy-start.33 = (f32[512]{0:T(512)S(1)}, f32[512]{0:T(512)}, u32[]{:S(2)}) copy-start(f32[512]{0:T(512)} %copy-done.32) | copy-start | bytes 6148
  1311.0 4.1 copy-start.6
  1387.5 4.1 copy-start.6
  1464.2 4.1 copy-start.6
  1502.5 4.2 copy-start.6
  1534.2 4.1 copy-start.2
  1572.7 4.1 copy-start.2
  1579.6 4.2 copy-start.6
  1694.6 4.1 copy-start.6
  1733.0 4.2 copy-start.6
  1771.6 4.2 copy-start.6
  1831.0 4.7 copy-start.10
  1831.0 5.1 copy-start.11
  1831.0 5.1 copy-start.27
  1831.0 9.3 slice-start
  1836.1 4.2 slice-start.1
  1845.9 80.8 %copy-start.14 = (f32[512,32]{0,1:T(8,128)S(1)}, f32[512,32]{0,1:T(8,128)}, u32[]{:S(2)}) copy-start(f32[512,32]{0,1:T(8,128)} %copy-done.13) | copy-start | bytes 196612
  1845.9 80.8 %copy-start.22 = (f32[512,32]{0,1:T(8,128)S(1)}, f32[512,32]{0,1:T(8,128)}, u32[]{:S(2)}) copy-start(f32[512,32]{0,1:T(8,128)} %get-tuple-element.375) | copy-start | bytes 196612
  1926.6 200.5 %reduce-scatter.13.cloned.1.call-start = ((), (), s32[]{:S(2)}) async-start(), calls=%async_computation.16 | async-start | bytes 3244032 | tf_op jit(solution)/shard_map/reduce_scatter | solution.py:328
  1931.1 302.4 %reduce-scatter.15.cloned.1.call-start = ((), (), s32[]{:S(2)}) async-start(), calls=%async_computation.17 | async-start | bytes 3244032 | tf_op jit(solution)/shard_map/reduce_scatter | solution.py:329
  1934.1 440.5 %reduce-scatter.11.cloned.1.call-start = ((), (), s32[]{:S(2)}) async-start(), calls=%async_computation.15 | async-start | bytes 9732096 | tf_op jit(solution)/shard_map/reduce_scatter | solution.py:327
  1943.6 573.0 %reduce-scatter.17.cloned.1.call-start = ((), (), s32[]{:S(2)}) async-start(), calls=%async_computation.18 | async-start | bytes 9732096 | tf_op jit(solution)/shard_map/reduce_scatter | solution.py:330
  1952.3 1001.8 %reduce-scatter.19.cloned.1.call-start = ((), (), s32[]{:S(2)}) async-start(), calls=%async_computation.19 | async-start | bytes 51904512 | tf_op jit(solution)/shard_map/reduce_scatter | solution.py:285
  1953.1 1438.5 %reduce-scatter.21.cloned.1.call-start = ((), (), s32[]{:S(2)}) async-start(), calls=%async_computation.20 | async-start | bytes 51904512 | tf_op jit(solution)/shard_map/reduce_scatter | solution.py:286
  1953.7 1875.2 %reduce-scatter.23.cloned.1.call-start = ((), (), s32[]{:S(2)}) async-start(), calls=%async_computation.21 | async-start | bytes 51904512 | tf_op jit(solution)/shard_map/reduce_scatter | solution.py:287
  1954.2 5.2 copy-start.15
  (68 other events, 214.5 us)
Sparse Core Ops, SparseCore 0:
  10.9 57.6 all-gather.10
  71.5 53.8 all-gather.8
  128.3 62.5 all-gather.12
  193.6 62.4 all-gather.14
  258.7 153.4 all-gather.16
  415.0 152.8 all-gather.18
  570.7 152.8 all-gather.20
  1926.7 93.7 reduce-scatter.24
  2026.5 100.5 reduce-scatter.12
  2133.0 100.4 reduce-scatter.14
  2240.0 134.6 reduce-scatter.10
  2382.0 134.5 reduce-scatter.16
  2523.6 430.4 reduce-scatter.18
  2960.9 430.5 reduce-scatter.20
  3398.4 430.3 reduce-scatter.22
where the time goes:
time: 3850 us; the launch traced here: 3840 us
  waiting for transfers between devices  2310 us (60%)
  matrix products  664 us (17%)
  other arithmetic  370 us (10%)
  local copies, waits for them, and re-layouts  355 us (9%)
  blocking collectives  122 us (3%)
    reduce_scatter x1, waiting for transfers between devices, shards(): lax.psum_scatter(expert_grads[0], 'fsdp', scatter_dimension=1, tiled=True)  437 us
    reduce_scatter x1, waiting for transfers between devices, shards(): lax.psum_scatter(expert_grads[1], 'fsdp', scatter_dimension=1, tiled=True)  437 us
    reduce_scatter x1, waiting for transfers between devices, shards(): lax.psum_scatter(expert_grads[2], 'fsdp', scatter_dimension=1, tiled=True)  437 us
    dot_general x53, matrix products, matmul(): return jnp.dot(left, right, preferred_element_type=jnp.float32)  197 us
    dot_general x52, matrix products, contract_rows(): lax.dot_general(left, right, (((0,), (0,)), ((), ())), preferred_element_...  194 us
    dot_general x53, matrix products, contract_last(): lax.dot_general(left, right, (((1,), (1,)), ((), ())), preferred_element_...  169 us
    all_gather x1, waiting for transfers between devices, shards(): lax.all_gather(w_down, 'fsdp', axis=1, tiled=True)  156 us
    all_gather x1, waiting for transfers between devices, shards(): lax.all_gather(w_up, 'fsdp', axis=1, tiled=True)  156 us
  transfers between devices with their start and end apart: 15, of which 13 were waited for; matrix products, arithmetic and copies ran while one was open for 5% of the time, Pallas kernels for 0%

commit v1 on v0

v1 whole, which is shorter than its diff:
```python
import functools
import math

import jax
import jax.numpy as jnp
from jax import lax
from jax.experimental import pallas as pl
from jax.experimental.pallas import tpu as pltpu
from jax.sharding import PartitionSpec as P

HQ = 24
HK = 8
HD = 64
E = 16
GROUP = 8
PAIR_E = E // GROUP
LANES = 128
HEADS_STEP = 6

norm_eps = 1e-06
resid_scale = 0.22
score_scale = 0.015625
rope_base = 10000.0
masked_score = -1e30

f32 = jnp.float32
bf16 = jnp.bfloat16


def matmul(left, right):
    return jnp.dot(left, right, preferred_element_type=f32)


def contract_rows(left, right):
    return lax.dot_general(left, right, (((0,), (0,)), ((), ())), preferred_element_type=f32)


def contract_last(left, right):
    return lax.dot_general(left, right, (((1,), (1,)), ((), ())), preferred_element_type=f32)


def norm_back(values, rinv, gain, grad):
    scaled = gain * grad
    return rinv * scaled - values * rinv * rinv * rinv * jnp.mean(
        scaled * values, axis=-1, keepdims=True
    )


def layout(seq_lengths, row_count):
    seq_ends = jnp.cumsum(seq_lengths)
    starts = seq_ends - seq_lengths
    places = jnp.arange(row_count, dtype=jnp.int32)
    member = (places[:, None] >= starts[None, :]) & (places[:, None] < seq_ends[None, :])
    labels = jnp.arange(seq_lengths.shape[0], dtype=jnp.int32)
    segment = jnp.sum(jnp.where(member, labels[None, :], 0), axis=1)
    offset = jnp.sum(jnp.where(member, starts[None, :], 0), axis=1)
    return (segment, places - offset)


def turn_tables(position):
    half_dim = HD // 2
    inv_freq = jnp.exp(
        -(jnp.arange(half_dim, dtype=f32) * (2.0 / HD)) * math.log(rope_base)
    )
    angles = position.astype(f32)[:, None] * inv_freq[None, :]
    cosine, sine_val = jnp.cos(angles), jnp.sin(angles)
    return (
        jnp.concatenate([cosine] * 4, axis=1),
        jnp.concatenate([-sine_val, sine_val] * 2, axis=1),
    )


def swap(value, bit, device_count):
    return lax.ppermute(value, "fsdp", [(i, i ^ bit) for i in range(device_count)])


def group_gather(own, device_count):
    half = own.shape[0] // 2
    from2 = swap(own, 2, device_count)
    from4 = swap(own, 4, device_count)
    from1 = swap(own, 1, device_count)
    from6 = jnp.concatenate(
        [swap(from2[:half], 4, device_count), swap(from4[half:], 2, device_count)], axis=0
    )
    from3 = swap(from2, 1, device_count)
    from5 = swap(from4, 1, device_count)
    from7 = swap(from6, 1, device_count)
    return [own, from1, from2, from3, from4, from5, from6, from7]


def add_low(left, right):
    return (left.astype(f32) + right.astype(f32)).astype(bf16)


def group_sum(parts, device_count):
    half = parts[0].shape[0] // 2
    chip = {j: add_low(parts[j], swap(parts[j + 1], 1, device_count)) for j in (6, 2, 4, 0)}
    low = swap(chip[6][:half], 4, device_count)
    high = swap(chip[6][half:], 2, device_count)
    sum2 = jnp.concatenate([add_low(chip[2][:half], low), chip[2][half:]], axis=0)
    sum4 = jnp.concatenate([chip[4][:half], add_low(chip[4][half:], high)], axis=0)
    return (
        chip[0].astype(f32)
        + swap(sum2, 2, device_count).astype(f32)
        + swap(sum4, 4, device_count).astype(f32)
    )


def turn(values, cosine, sine_val, low_half):
    shifted = jnp.where(low_half, pltpu.roll(values, LANES - 32, 1), pltpu.roll(values, 32, 1))
    return values * cosine + shifted * sine_val


def half_views(pair, scale):
    lane = lax.broadcasted_iota(jnp.int32, pair.shape, 1)
    wide = pair.astype(f32) * scale
    other = pltpu.roll(wide, HD, 1)
    low = lane < HD
    return [
        [jnp.where(low, wide, 0.0).astype(bf16), jnp.where(low, other, 0.0).astype(bf16)],
        [jnp.where(low, 0.0, other).astype(bf16), jnp.where(low, 0.0, wide).astype(bf16)],
    ]


def visible_keys(seg_col, seg_row, row_start, rows, keys):
    query_at = row_start + lax.broadcasted_iota(jnp.int32, (rows, keys), 0)
    key_at = lax.broadcasted_iota(jnp.int32, (rows, keys), 1)
    return (seg_col[row_start : row_start + rows, :] == seg_row[:, :keys]) & (key_at <= query_at)


def attend_kernel(block, normed_ref, wq_ref, wk_ref, wv_ref, cos_ref, sin_ref, segc_ref, segr_ref,
                  q_ref, k_ref, v_ref, out_ref, lse_ref):
    rows_all = normed_ref.shape[0]
    normed = normed_ref[...]
    lane = lax.broadcasted_iota(jnp.int32, (rows_all, LANES), 1)
    first = (lane % HD) < (HD // 2)
    cosine, sine_val = cos_ref[...], sin_ref[...]
    q_pre = matmul(normed, wq_ref[...])
    for t in range(3):
        cols = slice(t * LANES, (t + 1) * LANES)
        q_ref[:, cols] = turn(q_pre[:, cols], cosine, sine_val, first).astype(bf16)
    k_low = turn(matmul(normed, wk_ref[...]), cosine, sine_val, first).astype(bf16)
    v_low = matmul(normed, wv_ref[...]).astype(bf16)
    k_ref[...] = k_low
    v_ref[...] = v_low
    k_views = half_views(k_low, score_scale)
    v_views = half_views(v_low, 1.0)
    seg_col, seg_row = segc_ref[...], segr_ref[...]
    for start in range(0, rows_all, block):
        keys = start + block
        visible = visible_keys(seg_col, seg_row, start, block, keys)
        lane_b = lax.broadcasted_iota(jnp.int32, (block, LANES), 1)
        norms = jnp.zeros((block, LANES), f32)
        for t in range(3):
            cols = slice(t * LANES, (t + 1) * LANES)
            q_tile = q_ref[start : start + block, cols]
            total = jnp.zeros((block, LANES), f32)
            for side in range(2):
                head = 2 * t + side
                kv = head // 3
                scores = contract_last(q_tile, k_views[side][kv][:keys])
                scores = jnp.where(visible, scores, masked_score)
                peak = jnp.max(scores, axis=-1, keepdims=True)
                expo = jnp.exp(scores - peak)
                mass = jnp.sum(expo, axis=-1, keepdims=True)
                probs = (expo * (1.0 / mass)).astype(bf16)
                total = total + matmul(probs, v_views[side][kv][:keys])
                norms = jnp.where(lane_b == head, peak + jnp.log(mass), norms)
            out_ref[start : start + block, cols] = total.astype(bf16)
        lse_ref[0, start : start + block, :] = norms


def attend_forward(normed, packed, cosine, sine_val, segment):
    rows = normed.shape[0]
    width = normed.shape[1]
    steps = HK // 2
    whole = lambda shape: pl.BlockSpec(shape, lambda i: (0, 0))
    return pl.pallas_call(
        functools.partial(attend_kernel, 128),
        grid=(steps,),
        in_specs=[
            whole((rows, width)),
            pl.BlockSpec((width, 3 * LANES), lambda i: (0, i)),
            pl.BlockSpec((width, LANES), lambda i: (0, 24 + i)),
            pl.BlockSpec((width, LANES), lambda i: (0, 28 + i)),
            whole((rows, LANES)),
            whole((rows, LANES)),
            whole((rows, 1)),
            whole((1, rows)),
        ],
        out_specs=[
            pl.BlockSpec((rows, 3 * LANES), lambda i: (0, i)),
            pl.BlockSpec((rows, LANES), lambda i: (0, i)),
            pl.BlockSpec((rows, LANES), lambda i: (0, i)),
            pl.BlockSpec((rows, 3 * LANES), lambda i: (0, i)),
            pl.BlockSpec((1, rows, LANES), lambda i: (i, 0, 0)),
        ],
        out_shape=[
            jax.ShapeDtypeStruct((rows, HQ * HD), bf16),
            jax.ShapeDtypeStruct((rows, HK * HD), bf16),
            jax.ShapeDtypeStruct((rows, HK * HD), bf16),
            jax.ShapeDtypeStruct((rows, HQ * HD), bf16),
            jax.ShapeDtypeStruct((steps, rows, LANES), f32),
        ],
        compiler_params=pltpu.CompilerParams(vmem_limit_bytes=56 * 1024 * 1024),
        cost_estimate=pl.CostEstimate(
            flops=9_000_000_000, bytes_accessed=20_000_000, transcendentals=4_000_000
        ),
    )(normed, packed, packed, packed, cosine, sine_val, segment[:, None], segment[None, :])


def attend_back_kernel(block, q_ref, k_ref, v_ref, grad_ref, lse_ref, cos_ref, sin_ref, segc_ref,
                       segr_ref, dq_ref, dk_ref, dv_ref, qt_ref, gt_ref, dkt_ref, dvt_ref):
    rows_all = q_ref.shape[0]
    lane = lax.broadcasted_iota(jnp.int32, (rows_all, LANES), 1)
    first = (lane % HD) < (HD // 2)
    k_views = half_views(k_ref[...], score_scale)
    v_views = half_views(v_ref[...], 1.0)
    qt_ref[...] = q_ref[...].astype(f32).T.astype(bf16)
    gt_ref[...] = grad_ref[...].astype(f32).T.astype(bf16)
    dkt_ref[...] = jnp.zeros_like(dkt_ref)
    dvt_ref[...] = jnp.zeros_like(dvt_ref)
    seg_col, seg_row = segc_ref[...], segr_ref[...]
    cosine, sine_val = cos_ref[...], -sin_ref[...]
    for start in range(0, rows_all, block):
        keys = start + block
        rows = slice(start, start + block)
        visible = visible_keys(seg_col, seg_row, start, block, keys)
        norms = lse_ref[0, rows, :]
        for t in range(3):
            cols = slice(t * LANES, (t + 1) * LANES)
            q_tile = q_ref[rows, cols]
            g_tile = grad_ref[rows, cols]
            q_turned = qt_ref[cols, rows]
            g_turned = gt_ref[cols, rows]
            dq = jnp.zeros((block, LANES), f32)
            for side in range(2):
                head = 2 * t + side
                kv = head // 3
                scores = contract_last(q_tile, k_views[side][kv][:keys])
                probs = jnp.where(visible, jnp.exp(scores - norms[:, head : head + 1]), 0.0)
                prob_grad = contract_last(g_tile, v_views[side][kv][:keys])
                centre = jnp.sum(probs * prob_grad, axis=-1, keepdims=True)
                score_grad = (probs * (prob_grad - centre)).astype(bf16)
                dq = dq + matmul(score_grad, k_views[side][kv][:keys])
                slot = 2 * side + kv
                dkt_ref[slot, :, :keys] += matmul(q_turned, score_grad)
                dvt_ref[slot, :, :keys] += matmul(g_turned, probs.astype(bf16))
            dq_ref[rows, cols] = turn(dq, cosine[rows], sine_val[rows], first[rows]).astype(bf16)

    def joined(ref):
        low_low, low_high, high_low, high_high = [ref[s].T for s in range(4)]
        is_low = lane < HD
        straight = jnp.where(is_low, low_low, high_high)
        crossed = pltpu.roll(jnp.where(is_low, low_high, high_low), HD, 1)
        return straight + crossed

    dk_ref[...] = turn(joined(dkt_ref) * score_scale, cosine, sine_val, first).astype(bf16)
    dv_ref[...] = joined(dvt_ref).astype(bf16)


def attend_backward(queries, keys, values, grads, norms, cosine, sine_val, segment):
    rows = queries.shape[0]
    steps = HK // 2
    whole = lambda shape: pl.BlockSpec(shape, lambda i: (0, 0))
    wide = pl.BlockSpec((rows, 3 * LANES), lambda i: (0, i))
    thin = pl.BlockSpec((rows, LANES), lambda i: (0, i))
    return pl.pallas_call(
        functools.partial(attend_back_kernel, 128),
        grid=(steps,),
        in_specs=[
            wide,
            thin,
            thin,
            wide,
            pl.BlockSpec((1, rows, LANES), lambda i: (i, 0, 0)),
            whole((rows, LANES)),
            whole((rows, LANES)),
            whole((rows, 1)),
            whole((1, rows)),
        ],
        out_specs=[wide, thin, thin],
        out_shape=[
            jax.ShapeDtypeStruct((rows, HQ * HD), bf16),
            jax.ShapeDtypeStruct((rows, HK * HD), bf16),
            jax.ShapeDtypeStruct((rows, HK * HD), bf16),
        ],
        scratch_shapes=[
            pltpu.VMEM((3 * LANES, rows), bf16),
            pltpu.VMEM((3 * LANES, rows), bf16),
            pltpu.VMEM((4, LANES, rows), f32),
            pltpu.VMEM((4, LANES, rows), f32),
        ],
        compiler_params=pltpu.CompilerParams(vmem_limit_bytes=56 * 1024 * 1024),
        cost_estimate=pl.CostEstimate(
            flops=15_000_000_000, bytes_accessed=10_000_000, transcendentals=4_000_000
        ),
    )(queries, keys, values, grads, norms, cosine, sine_val, segment[:, None], segment[None, :])


def experts_kernel(rows_ref, cot_ref, gate_ref, wgu_ref, wd_ref,
                   out_ref, grad_ref, mix_ref, gate_grad_ref, up_grad_ref, mid_ref):
    rows_in = rows_ref[...]
    cot = cot_ref[...]
    cot_wide = cot.astype(f32)
    width = rows_in.shape[1]
    hidden = wgu_ref.shape[3] // 2
    lane = lax.broadcasted_iota(jnp.int32, mix_ref.shape, 1)
    mixes = jnp.zeros(mix_ref.shape, f32)
    for e in range(PAIR_E):
        gate_row = gate_ref[:, e : e + 1]
        w_gate = wgu_ref[:, e, :, :hidden].reshape(width, hidden)
        w_up = wgu_ref[:, e, :, hidden:].reshape(width, hidden)
        w_down = wd_ref[:, e].reshape(hidden, width)
        gate_proj = matmul(rows_in, w_gate)
        up_proj = matmul(rows_in, w_up)
        sigmoid_g = 1.0 / (1.0 + jnp.exp(-gate_proj))
        active = gate_proj * sigmoid_g
        mid = (active * up_proj).astype(bf16)
        cols = slice(e * hidden, (e + 1) * hidden)
        mid_ref[:, cols] = mid
        out_grad = ((resid_scale * gate_row) * cot_wide).astype(bf16)
        mid_grad = contract_last(out_grad, w_down)
        gate_grad = (
            mid_grad * up_proj * sigmoid_g * (1.0 + gate_proj * (1.0 - sigmoid_g))
        ).astype(bf16)
        up_grad = (mid_grad * active).astype(bf16)
        gate_grad_ref[:, cols] = gate_grad
        up_grad_ref[:, cols] = up_grad
        out_rows = matmul(mid, w_down)
        mix = resid_scale * jnp.sum(cot_wide * out_rows, axis=-1, keepdims=True)
        mixes = jnp.where(lane == e, mix, mixes)
        back = contract_last(gate_grad, w_gate) + contract_last(up_grad, w_up)
        if e == 0:
            total, grads = gate_row * out_rows, back
        else:
            total, grads = total + gate_row * out_rows, grads + back
    out_ref[...] = total.astype(bf16)
    grad_ref[...] = grads.astype(bf16)
    mix_ref[...] = mixes


def run_experts(rows_in, cots, gates, w_gate_up, w_down, tile):
    count, width = rows_in.shape
    hidden = w_gate_up.shape[3] // 2
    once = pl.Buffered(1)
    tall = lambda cols: pl.BlockSpec((tile, cols), lambda i: (i, 0))
    return pl.pallas_call(
        experts_kernel,
        grid=(count // tile,),
        in_specs=[
            tall(width),
            tall(width),
            tall(PAIR_E),
            pl.BlockSpec(w_gate_up.shape, lambda i: (0, 0, 0, 0), pipeline_mode=once),
            pl.BlockSpec(w_down.shape, lambda i: (0, 0, 0, 0), pipeline_mode=once),
        ],
        out_specs=[
            tall(width),
            tall(width),
            tall(PAIR_E),
            tall(PAIR_E * hidden),
            tall(PAIR_E * hidden),
            tall(PAIR_E * hidden),
        ],
        out_shape=[
            jax.ShapeDtypeStruct((count, width), bf16),
            jax.ShapeDtypeStruct((count, width), bf16),
            jax.ShapeDtypeStruct((count, PAIR_E), f32),
            jax.ShapeDtypeStruct((count, PAIR_E * hidden), bf16),
            jax.ShapeDtypeStruct((count, PAIR_E * hidden), bf16),
            jax.ShapeDtypeStruct((count, PAIR_E * hidden), bf16),
        ],
        compiler_params=pltpu.CompilerParams(vmem_limit_bytes=60 * 1024 * 1024),
        cost_estimate=pl.CostEstimate(
            flops=12 * count * width * hidden * PAIR_E,
            bytes_accessed=60_000_000,
            transcendentals=count * hidden * PAIR_E,
        ),
    )(rows_in, cots, gates, w_gate_up, w_down)


def xor_order(stacked, place):
    for bit in (1, 2, 4):
        flipped = jnp.concatenate(
            [stacked[k ^ bit][None] for k in range(GROUP)], axis=0
        )
        stacked = jnp.where((place & bit) != 0, flipped, stacked)
    return stacked


def shards(device_count, hidden_in, lengths, routes, norm_attn, w_query, w_key, w_value, w_out,
           norm_moe, w_router, w_gate, w_up, w_down, cotangent):
    n = device_count
    layers = n // GROUP
    along = [[q + GROUP * j for j in range(layers)] for q in range(GROUP)]
    inside = [[GROUP * j + q for q in range(GROUP)] for j in range(layers)]
    place = lax.axis_index("fsdp") % GROUP
    rows, width = hidden_in.shape
    own_rows = w_query.shape[0]
    hidden = w_gate.shape[2]
    own_hidden = w_down.shape[1]

    extras = jnp.concatenate(
        [w_router, norm_attn[:, None], norm_moe[:, None], jnp.zeros((own_rows, LANES - E - 2), bf16)],
        axis=1,
    )
    packed = lax.all_gather(
        jnp.concatenate([w_query, w_out, w_key, w_value, extras], axis=1), "fsdp", axis=0, tiled=True
    )
    gathered_out = packed[:, width : 2 * width]
    extras_full = packed[:, 2 * width + 2 * HK * HD :]
    router = extras_full[:, :E]
    gains = extras_full[:, E : E + 2].astype(f32).T
    gain_one, gain_two = gains[0:1], gains[1:2]

    gate_up = jnp.concatenate([w_gate, w_up], axis=2)
    gate_up = lax.all_to_all(
        gate_up.reshape(GROUP, PAIR_E, own_rows, 2 * hidden), "fsdp", 0, 0, tiled=True,
        axis_index_groups=inside,
    )
    gate_up = gate_up.transpose(1, 0, 2, 3).reshape(PAIR_E, GROUP * own_rows, 2 * hidden)
    gate_up = lax.all_gather(gate_up, "fsdp", axis=0, axis_index_groups=along)
    down = lax.all_to_all(
        w_down.reshape(GROUP, PAIR_E, own_hidden, width), "fsdp", 0, 0, tiled=True,
        axis_index_groups=inside,
    )
    down = down.transpose(1, 0, 2, 3).reshape(PAIR_E, GROUP * own_hidden, width)
    down = lax.all_gather(down, "fsdp", axis=0, axis_index_groups=along)
    cots = jnp.concatenate(group_gather(cotangent, n), axis=0)

    hidden_f32 = hidden_in.astype(f32)
    cot_f32 = cotangent.astype(f32)
    segment, position = layout(lengths[0], rows)
    cosine, sine_val = turn_tables(position)
    rinv_one = lax.rsqrt(jnp.mean(hidden_f32 * hidden_f32, axis=-1, keepdims=True) + norm_eps)
    normed = (hidden_f32 * rinv_one * gain_one).astype(bf16)
    queries, keys, values, attn_out, norms = attend_forward(
        normed, packed, cosine, sine_val, segment
    )
    middle = hidden_f32 + resid_scale * matmul(attn_out, gathered_out)
    rinv_two = lax.rsqrt(jnp.mean(middle * middle, axis=-1, keepdims=True) + norm_eps)
    inner = (middle * rinv_two * gain_two).astype(bf16)
    all_inner = jnp.concatenate(group_gather(inner, n), axis=0)

    logits = matmul(inner, router)
    named = jnp.any(routes[:, :, None] == jnp.arange(E, dtype=jnp.int32)[None, None, :], axis=1)
    peak = jnp.max(jnp.where(named, logits, masked_score), axis=-1, keepdims=True)
    expo = jnp.where(named, jnp.exp(jnp.where(named, logits - peak, 0.0)), 0.0)
    mix = expo / jnp.sum(expo, axis=-1, keepdims=True)
    mix_turned = mix.T.reshape(GROUP, PAIR_E, rows)
    got = []
    for k in range(GROUP):
        piece = lax.dynamic_index_in_dim(mix_turned, place ^ k, 0, keepdims=False)
        got.append(swap(piece, k, n) if k else piece)
    gates = jnp.concatenate([piece.T for piece in got], axis=0)

    out_part, grad_part, mix_part, gate_grad, up_grad, mid = run_experts(
        all_inner, cots, gates, gate_up, down, rows
    )
    grad_parts = [grad_part[k * rows : (k + 1) * rows] for k in range(GROUP)]
    inner_grad = group_sum(grad_parts, n)
    back = []
    for k in range(GROUP):
        piece = mix_part[k * rows : (k + 1) * rows].T
        back.append(swap(piece, k, n) if k else piece)
    mix_grad = xor_order(jnp.stack(back), place).reshape(E, rows).T

    shared_gate_up, shared_down = [], []
    for e in range(PAIR_E):
        cols = slice(e * hidden, (e + 1) * hidden)
        out_grad = (resid_scale * gates[:, e : e + 1] * cots.astype(f32)).astype(bf16)
        both = jnp.concatenate(
            [contract_rows(all_inner, gate_grad[:, cols]), contract_rows(all_inner, up_grad[:, cols])],
            axis=1,
        ).astype(bf16)
        low = contract_rows(mid[:, cols], out_grad).astype(bf16)
        shared_gate_up.append(
            lax.psum_scatter(both, "fsdp", scatter_dimension=0, tiled=True, axis_index_groups=along)
        )
        shared_down.append(
            lax.psum_scatter(low, "fsdp", scatter_dimension=0, tiled=True, axis_index_groups=along)
        )
    both = jnp.stack([s.reshape(GROUP, own_rows, 2 * hidden) for s in shared_gate_up], axis=1)
    low = jnp.stack([s.reshape(GROUP, own_hidden, width) for s in shared_down], axis=1)
    both = lax.all_to_all(both, "fsdp", 0, 0, tiled=True, axis_index_groups=inside)
    low = lax.all_to_all(low, "fsdp", 0, 0, tiled=True, axis_index_groups=inside)
    both = both.reshape(E, own_rows, 2 * hidden).astype(f32)
    grad_gate, grad_up = both[:, :, :hidden], both[:, :, hidden:]
    grad_down = low.reshape(E, own_hidden, width).astype(f32)

    logit_grad = (
        mix * (mix_grad - jnp.sum(mix * mix_grad, axis=-1, keepdims=True))
    ).astype(bf16)
    grad_router = contract_rows(inner, logit_grad)
    inner_grad = inner_grad + contract_last(logit_grad, router)
    grad_norm_moe = jnp.sum(inner_grad * middle * rinv_two, axis=0)
    middle_grad = cot_f32 + norm_back(middle, rinv_two, gain_two, inner_grad)

    proj_grad = (resid_scale * middle_grad).astype(bf16)
    grad_out = contract_rows(attn_out, proj_grad)
    attn_grad = contract_last(proj_grad, gathered_out).astype(bf16)
    query_grad, key_grad, value_grad = attend_backward(
        queries, keys, values, attn_grad, norms, cosine, sine_val, segment
    )
    inner_grad_b, out_part = lax.optimization_barrier((inner_grad, out_part))
    out_sum = group_sum([out_part[k * rows : (k + 1) * rows] for k in range(GROUP)], n)
    mixed = (middle + resid_scale * out_sum).astype(bf16)

    grad_query = contract_rows(normed, query_grad)
    grad_key = contract_rows(normed, key_grad)
    grad_value = contract_rows(normed, value_grad)
    normed_grad = (
        contract_last(query_grad, packed[:, :width])
        + contract_last(key_grad, packed[:, 2 * width : 2 * width + HK * HD])
        + contract_last(value_grad, packed[:, 2 * width + HK * HD : 2 * width + 2 * HK * HD])
    )
    grad_norm_attn = jnp.sum(normed_grad * hidden_f32 * rinv_one, axis=0)
    input_grad = middle_grad + norm_back(hidden_f32, rinv_one, gain_one, normed_grad)

    extra_grads = jnp.concatenate(
        [
            grad_router,
            grad_norm_attn[:, None],
            grad_norm_moe[:, None],
            jnp.zeros((width, LANES - E - 2), f32),
        ],
        axis=1,
    )
    whole = jnp.concatenate([grad_query, grad_out, grad_key, grad_value, extra_grads], axis=1)
    columns = whole.shape[1]
    whole = whole.astype(bf16).reshape(layers, GROUP, own_rows, columns)
    parts = [
        lax.dynamic_index_in_dim(whole, place ^ k, 1, keepdims=False).reshape(-1, columns)
        for k in range(GROUP)
    ]
    mine = group_sum(parts, n).astype(bf16)
    mine = lax.psum_scatter(
        mine, "fsdp", scatter_dimension=0, tiled=True, axis_index_groups=along
    ).astype(f32)
    kv = HK * HD
    return (
        mixed,
        input_grad,
        mine[:, 2 * width + 2 * kv + E],
        mine[:, :width],
        mine[:, 2 * width : 2 * width + kv],
        mine[:, 2 * width + kv : 2 * width + 2 * kv],
        mine[:, width : 2 * width],
        mine[:, 2 * width + 2 * kv + E + 1],
        mine[:, 2 * width + 2 * kv : 2 * width + 2 * kv + E],
        grad_gate,
        grad_up,
        grad_down,
    )


def solution(mesh):

    in_specs = (
        P("fsdp", None),
        P("fsdp", None),
        P("fsdp", None),
        P("fsdp"),
        P("fsdp", None),
        P("fsdp", None),
        P("fsdp", None),
        P("fsdp", None),
        P("fsdp"),
        P("fsdp", None),
        P(None, "fsdp", None),
        P(None, "fsdp", None),
        P(None, "fsdp", None),
        P("fsdp", None),
    )
    out_specs = (
        P("fsdp", None),
        P("fsdp", None),
        P("fsdp"),
        P("fsdp", None),
        P("fsdp", None),
        P("fsdp", None),
        P("fsdp", None),
        P("fsdp"),
        P("fsdp", None),
        P(None, "fsdp", None),
        P(None, "fsdp", None),
        P(None, "fsdp", None),
    )
    return jax.shard_map(
        functools.partial(shards, mesh.shape["fsdp"]),
        mesh=mesh,
        in_specs=in_specs,
        out_specs=out_specs,
        check_vma=False,
    )
```

time: 3850 us -> 895 us (0.23)
  waiting for transfers between devices: 2310 us -> 318 us
  matrix products: 664 us -> 97.1 us
  other arithmetic: 370 us -> 70.6 us
  local copies, waits for them, and re-layouts: 355 us -> 153 us
  Pallas kernels: 0 us -> 164 us
  blocking collectives: 122 us -> 20.6 us
  starting transfers between devices: 0.59 us -> 49 us
    reduce_scatter x7 -> x5, waiting for transfers between devices: 1810 us -> 0.12 us  [the longest x1 0.08 us: shards(): lax.psum_scatter(mine, 'fsdp', scatter_dimension=0, tiled=True, axis_inde...]
    all_gather x7 -> x3, waiting for transfers between devices: 484 us -> 43.2 us  [the longest x1 43.2 us: shards(): gate_up = lax.all_gather(gate_up, 'fsdp', axis=0, axis_index_groups=along)]
    scatter-add x33 -> x0, other arithmetic: 300 us -> none  [the longest x16 134 us: expert_forward(): totals.at[token_row].add(gate_row[:, None] * out_rows)]
    gather x66 -> x0, local copies, waits for them, and re-layouts: 298 us -> none  [the longest x16 92.9 us: expert_forward(): rows_in = inner_b[token_row]]
    dot_general x109 -> x2, matrix products: 298 us -> 7.18 us  [matmul(): return jnp.dot(left, right, preferred_element_type=f32)]
    ppermute x0 -> x54, waiting for transfers between devices: none -> 236 us  [swap(): lax.ppermute(value, 'fsdp', [(i, i ^ bit) for i in range(device_count)])]
    pallas_call x0 -> x3, Pallas kernels: none -> 164 us  [the longest x1 91.6 us: run_experts(): pl.pallas_call(experts_kernel, grid=(count // tile,), in_specs=[tall(widt...]
    dot_general x53 -> x5, matrix products: 169 us -> 16.2 us  [contract_last(): lax.dot_general(left, right, (((1,), (1,)), ((), ())), preferred_element_...]
  transfers between devices with their start and end apart: 15 -> 65, of which waited for: 13 -> 24; matrix products, arithmetic and copies ran while one was open for 5% -> 34% of each run, Pallas kernels for 0% -> 8%
where the time goes in v1:
time: 895 us; the launch traced here: 888 us
  waiting for transfers between devices  318 us (36%)
  Pallas kernels  164 us (18%)
  local copies, waits for them, and re-layouts  153 us (17%)
  matrix products  97.1 us (11%)
  other arithmetic  70.6 us (8%)
  starting transfers between devices  49 us (5%)
  blocking collectives  20.6 us (2%)
  between operations  15.6 us (2%)
    ppermute x54, waiting for transfers between devices, swap(): lax.ppermute(value, 'fsdp', [(i, i ^ bit) for i in range(device_count)])  236 us
    pallas_call x1, Pallas kernels, run_experts(): pl.pallas_call(experts_kernel, grid=(count // tile,), in_specs=[tall(widt...  91.6 us
    dot_general x11, matrix products, contract_rows(): lax.dot_general(left, right, (((0,), (0,)), ((), ())), preferred_element_...  73.7 us
    unnamed x112, local copies, waits for them, and re-layouts  53.3 us
    all_gather x1, waiting for transfers between devices, shards(): gate_up = lax.all_gather(gate_up, 'fsdp', axis=0, axis_index_groups=along)  43.2 us
    pallas_call x1, Pallas kernels, attend_backward(): pl.pallas_call(functools.partial(attend_back_kernel, 128), grid=(steps,),...  39 us
    ppermute x54, starting transfers between devices, swap(): lax.ppermute(value, 'fsdp', [(i, i ^ bit) for i in range(device_count)])  35.9 us
    pallas_call x1, Pallas kernels, attend_forward(): pl.pallas_call(functools.partial(attend_kernel, 128), grid=(steps,), in_s...  33.4 us
  transfers between devices with their start and end apart: 65, of which 24 were waited for; matrix products, arithmetic and copies ran while one was open for 34% of the time, Pallas kernels for 8%

profile of v1, /device:TPU:0, one launch (start us, length us, event | category | flops | bytes accessed | tf_op | source)
XLA Modules:
  0.0 888.3 jit_solution(2423635669995047934)
XLA Ops:
  11.5 20.6 %all_to_all.20 = bf16[8,2,16,1536]{3,2,1,0:T(8,128)(2,1)S(1)} all-to-all(bf16[8,2,16,1536]{3,2,1,0:T(8,128)(2,1)} %bitcast.169), channel_id=1, replica_groups={{0,1,2,3,4,5,6,7},{8,9,10,11,12,13,14,15},{16,17,18,19,20,21,22,23},{24..., dimensions={0} | all-to-all | bytes 1572864 | tf_op jit(solution)/shard_map/all_to_all | solution.py:424
  37.1 4.3 all-to-all-start
  43.1 39.1 %collective-permute-done.9 = bf16[512,1536]{1,0:T(8,128)(2,1)} collective-permute-done((bf16[512,1536]{1,0:T(8,128)(2,1)S(1)}, bf16[512,1536]{1,0:T(8,128)(2,1)}, u32[]{:S(2)}, u32[]{:S(2)}) %collective-permute-start.9) | collective-permute-done | bytes 1572896 | tf_op jit(solution)/shard_map/ppermute | solution.py:74
  91.0 20.4 %all-to-all-done = bf16[8,2,48,1024]{3,2,1,0:T(8,128)(2,1)} async-done(((bf16[8,2,48,1024]{3,2,1,0:T(8,128)(2,1)}), bf16[8,2,48,1024]{3,2,1,0:T(8,128)(2,1)}, u32[]{:S(2)}, u32[]{:S(2)}) %all-to-all-start) | async-done | bytes 1572896 | tf_op jit(solution)/shard_map/all_to_all | solution.py:418
  117.4 11.2 %collective-permute-done.13 = bf16[256,1536]{1,0:T(8,128)(2,1)} collective-permute-done((bf16[256,1536]{1,0:T(8,128)(2,1)}, bf16[256,1536]{1,0:T(8,128)(2,1)}, u32[]{:S(2)}, u32[]{:S(2)}) %collective-permute-start.13) | collective-permute-done | bytes 786464 | tf_op jit(solution)/shard_map/ppermute | solution.py:74
  128.7 7.4 collective-permute-done.14
  157.4 33.4 %shard_map.229 = (bf16[512,1536]{1,0:T(8,128)(2,1)}, bf16[512,512]{1,0:T(8,128)(2,1)}, bf16[512,512]{1,0:T(8,128)(2,1)}, bf16[512,1536]{1,0:T(8,128)(2,1)}, f32[4,512,128]{2,1,0:T(8,128)}) custom-call(bf16[512,1536]{1,0:T(8,128)(2,1)} %fusion.33.normed_ref, bf16[1536,4224]{1,0:T(8,128)(2,1)} %all-gather.4.cloned.1.call-done.wq_ref.wk_ref.wv_ref, ...), custom_call_target="tpu_custom_call" | custom-call | flops 8999999488 | bytes 20000000 | tf_op jit(solution)/shard_map/pallas_call | solution.py:178
  190.8 5.2 multiply_reduce_fusion.2
  204.3 31.0 %collective-permute-done.17 = f32[2,512]{1,0:T(2,128)S(1)} collective-permute-done((f32[2,512]{1,0:T(2,128)S(1)}, f32[2,512]{1,0:T(2,128)S(1)}, u32[]{:S(2)}, u32[]{:S(2)}) %collective-permute-start.17) | collective-permute-done | bytes 4128 | tf_op jit(solution)/shard_map/ppermute | solution.py:74
  239.9 3.6 collective-permute-done.21
  255.7 9.8 %collective-permute-done.5 = bf16[256,1536]{1,0:T(8,128)(2,1)} collective-permute-done((bf16[256,1536]{1,0:T(8,128)(2,1)}, bf16[256,1536]{1,0:T(8,128)(2,1)}, u32[]{:S(2)}, u32[]{:S(2)}) %collective-permute-start.5) | collective-permute-done | bytes 786464 | tf_op jit(solution)/shard_map/ppermute | solution.py:74
  285.7 43.2 %all-gather.6.cloned.1.call-done.wgu_ref = bf16[4,2,384,1024]{3,2,1,0:T(8,128)(2,1)} async-done(((bf16[1,2,384,1024]{3,2,1,0:T(8,128)(2,1)}), bf16[4,2,384,1024]{3,2,1,0:T(8,128)(2,1)}) %all-gather.6.cloned.1.call-update) | async-done | bytes 6291472 | tf_op jit(solution)/shard_map/all_gather | solution.py:423
  328.9 91.6 %shard_map.230 = (bf16[4096,1536]{1,0:T(8,128)(2,1)}, bf16[4096,1536]{1,0:T(8,128)(2,1)}, f32[4096,2]{1,0:T(8,128)}, bf16[4096,1024]{1,0:T(8,128)(2,1)}, bf16[40...) custom-call(bf16[4096,1536]{1,0:T(8,128)(2,1)} %constant_dynamic-update-slice_fusion.rows_ref, ...), custom_call_target="tpu_custom_call" | custom-call | flops 77309411328 | bytes 60000000 | tf_op jit(solution)/shard_map/pallas_call | solution.py:348
  420.5 6.2 fusion.90
  427.9 11.6 %fusion.44 = bf16[512,1536]{1,0:T(8,128)(2,1)} fusion(bf16[4096,1536]{1,0:T(8,128)(2,1)} %constant_dynamic-update-slice_fusion.9.cot_ref, f32[4096]{0:T(1024)S(1)} %bitcast.183, bf16[4096,1024]{1,0:T(8,128)(2,1)S(1)} %copy-done.33), kind=kOutput, calls=%fused_computation.72 | convolution fusion | flops 6462111744 | bytes 18366464 | tf_op jit(solution)/shard_map/dot_general | solution.py:35
  446.0 7.2 add_convert_fusion.8
  458.6 11.0 %fusion.49 = bf16[512,1536]{1,0:T(8,128)(2,1)} fusion(bf16[4096,1536]{1,0:T(8,128)(2,1)} %constant_dynamic-update-slice_fusion.9.cot_ref, f32[4096]{0:T(1024)S(1)} %bitcast.182, bf16[4096,1024]{1,0:T(8,128)(2,1)S(1)} %bitcast.189), kind=kOutput, calls=%fused_computation.73 | convolution fusion | flops 6462111744 | bytes 18366464 | tf_op jit(solution)/shard_map/dot_general | solution.py:35
  481.7 5.4 collective-permute-done.26
  491.2 8.3 collective-permute-done.29
  503.4 29.4 %collective-permute-done.27 = bf16[512,1536]{1,0:T(8,128)(2,1)} collective-permute-done((bf16[512,1536]{1,0:T(8,128)(2,1)}, bf16[512,1536]{1,0:T(8,128)(2,1)}, u32[]{:S(2)}, u32[]{:S(2)}) %collective-permute-start.27) | collective-permute-done | bytes 1572896 | tf_op jit(solution)/shard_map/ppermute | solution.py:74
  532.9 4.1 collective-permute-done.30
  536.9 5.3 multiply_reduce_fusion
  542.2 4.7 fusion.89
  547.4 8.5 fusion.57
  556.0 5.3 add_convert_fusion.4
  563.2 8.5 fusion.60
  573.7 4.7 copy.265
  587.1 13.6 %collective-permute-done.44 = bf16[256,1536]{1,0:T(8,128)(2,1)S(1)} collective-permute-done((bf16[256,1536]{1,0:T(8,128)(2,1)}, bf16[256,1536]{1,0:T(8,128)(2,1)S(1)}, u32[]{:S(2)}, u32[]{:S(2)}) %collective-permute-start.44) | collective-permute-done | bytes 786464 | tf_op jit(solution)/shard_map/ppermute | solution.py:74
  603.5 12.1 %fusion.63 = bf16[1536,512]{0,1:T(8,128)(2,1)} fusion(bf16[4096,1536]{1,0:T(8,128)(2,1)} %constant_dynamic-update-slice_fusion.rows_ref, bf16[4096,1024]{1,0:T(8,128)(2,1)} %get-tuple-element.39), kind=kOutput, calls=%fused_computation.79 | convolution fusion | flops 6443237376 | bytes 18350080 | tf_op jit(solution)/shard_map/dot_general | solution.py:35
  620.2 13.6 %collective-permute-done.42 = bf16[512,1536]{1,0:T(8,128)(2,1)} collective-permute-done((bf16[512,1536]{1,0:T(8,128)(2,1)}, bf16[512,1536]{1,0:T(8,128)(2,1)}, u32[]{:S(2)}, u32[]{:S(2)}) %collective-permute-start.42) | collective-permute-done | bytes 1572896 | tf_op jit(solution)/shard_map/ppermute | solution.py:74
  633.8 3.8 collective-permute-done.45
  637.6 6.2 subtract_add_fusion
  643.8 7.2 fusion.54.grad_ref
  651.0 39.0 %shard_map.231 = (bf16[512,1536]{1,0:T(8,128)(2,1)}, bf16[512,512]{1,0:T(8,128)(2,1)}, bf16[512,512]{1,0:T(8,128)(2,1)}) custom-call(bf16[512,1536]{1,0:T(8,128)(2,1)} %get-tuple-element.32.q_ref, bf16[512,512]{1,0:T(8,128)(2,1)} %get-tuple-element.33.k_ref, bf16[512,512]{1,0:T(8,128)(2,1)} %get-tuple-element.34.v_ref, bf16[512,1536]{1,0:T(8,128)(2,1)} %fusion.54.grad_ref, ...), custom_call_target="tpu_custom_call" | custom-call | flops 15000000512 | bytes 10000000 | tf_op jit(solution)/shard_map/pallas_call | solution.py:268
  690.0 2.9 convolution_convert_fusion
  696.3 3.1 convolution_convert_fusion.1
  706.1 3.7 fusion.41
  718.2 19.5 %concatenate.108 = bf16[4,8,48,4224]{3,2,0,1:T(8,128)(2,1)} concatenate(bf16[4,8,48,1536]{3,2,0,1:T(8,128)(2,1)} %copy.252, bf16[4,8,48,1536]{3,2,0,1:T(8,128)(2,1)} %copy.253, bf16[4,8,48,512]{3,2,0,1:T(8,128)(2,1)S(1)} %copy.254, bf16[4,8,48,512]{3,2,0,1:T(8,128)(2,1)} %copy.255, bf16[4,8,48,16]{3,2,0,1:T(8,128)(2,1)} %copy.256, bf16[4,8,48,1]{3,2,0,1:T(8,128)(2,1)} %copy.257, ...), dimensions={3} | concatenate | bytes 25952256 | tf_op jit(solution)/shard_map/concatenate | solution.py:530
  737.7 9.2 %constant_dynamic-slice_fusion.6 = (bf16[4,1,48,4224]{3,2,0,1:T(8,128)(2,1)}, bf16[4,1,48,4224]{3,2,0,1:T(8,128)(2,1)}, bf16[4,1,48,4224]{3,2,0,1:T(8,128)(2,1)S...) fusion(bf16[4,8,48,4224]{3,2,0,1:T(8,128)(2,1)} %concatenate.10, ...), kind=kLoop, calls=%fused_computation.189 | loop fusion | bytes 25952288 | tf_op jit(solution)/shard_map/jit(dynamic_index_in_dim)/dynamic_slice | solution.py:534
  747.1 11.1 %fusion.66 = bf16[1536,512]{0,1:T(8,128)(2,1)S(1)} fusion(bf16[4096,1536]{1,0:T(8,128)(2,1)} %constant_dynamic-update-slice_fusion.rows_ref, bf16[4096,1024]{1,0:T(8,128)(2,1)} %get-tuple-element.40), kind=kOutput, calls=%fused_computation.80 | convolution fusion | flops 6443237376 | bytes 18350080 | tf_op jit(solution)/shard_map/dot_general | solution.py:35
  760.1 4.9 copy.267
  774.1 14.6 %collective-permute-done.49 = bf16[96,4224]{1,0:T(8,128)(2,1)S(1)} collective-permute-done((bf16[96,4224]{1,0:T(8,128)(2,1)S(1)}, bf16[96,4224]{1,0:T(8,128)(2,1)S(1)}, u32[]{:S(2)}, u32[]{:S(2)}) %collective-permute-start.49) | collective-permute-done | bytes 811040 | tf_op jit(solution)/shard_map/ppermute | solution.py:74
  796.7 4.2 all-to-all-start.3
  801.0 27.9 %collective-permute-done.50 = bf16[192,4224]{1,0:T(8,128)(2,1)} collective-permute-done((bf16[192,4224]{1,0:T(8,128)(2,1)}, bf16[192,4224]{1,0:T(8,128)(2,1)}, u32[]{:S(2)}, u32[]{:S(2)}) %collective-permute-start.50) | collective-permute-done | bytes 1622048 | tf_op jit(solution)/shard_map/ppermute | solution.py:74
  829.0 6.2 collective-permute-done.53
  835.2 4.4 add_convert_fusion
  842.4 3.7 all-to-all-start.2
  848.6 18.6 %all-to-all-done.2 = bf16[8,2,48,1024]{3,2,1,0:T(8,128)(2,1)S(1)} async-done(((bf16[8,2,48,1024]{3,2,1,0:T(8,128)(2,1)}), bf16[8,2,48,1024]{3,2,1,0:T(8,128)(2,1)S(1)}, u32[]{:S(2)}, u32[]{:S(2)}) %all-to-all-start.2) | async-done | bytes 1572896 | tf_op jit(solution)/shard_map/all_to_all | solution.py:486
  (345 shorter events, 202.0 us)
Async XLA Ops:
  7.2 146.8 %all-gather.4.cloned.1.call-start = ((), (), s32[]{:S(2)}) async-start(), calls=%async_computation.9 | async-start | bytes 13381632 | tf_op jit(solution)/shard_map/all_gather | solution.py:408
  11.5 274.2 %all-gather.8.cloned.1.call-start = ((), (), s32[]{:S(2)}) async-start(), calls=%async_computation.11 | async-start | bytes 3932160 | tf_op jit(solution)/shard_map/all_gather | solution.py:429
  33.2 49.1 %collective-permute-start.9 = (bf16[512,1536]{1,0:T(8,128)(2,1)S(1)}, bf16[512,1536]{1,0:T(8,128)(2,1)}, u32[]{:S(2)}, u32[]{:S(2)}) collective-permute-start(bf16[512,1536]{1,0:T(8,128)(2,1)S(1)} %copy-done.7), channel_id=1, source_target_pairs={{0,2},{1,3},{2,0},{3,1},{4,6},{5,7},{6,4},{7,5},{8,10},{9,11},{10,... | collective-permute-start | bytes 4718600 | tf_op jit(solution)/shard_map/ppermute | solution.py:74
  33.2 52.9 %collective-permute-start.11 = (bf16[512,1536]{1,0:T(8,128)(2,1)S(1)}, bf16[512,1536]{1,0:T(8,128)(2,1)}, u32[]{:S(2)}, u32[]{:S(2)}) collective-permute-start(bf16[512,1536]{1,0:T(8,128)(2,1)S(1)} %copy-done.7), channel_id=1, source_target_pairs={{0,4},{1,5},{2,6},{3,7},{4,0},{5,1},{6,2},{7,3},{8,12},{9,13},{10,... | collective-permute-start | bytes 4718600 | tf_op jit(solution)/shard_map/ppermute | solution.py:74
  34.4 80.4 %collective-permute-start.8 = (bf16[512,1536]{1,0:T(8,128)(2,1)S(1)}, bf16[512,1536]{1,0:T(8,128)(2,1)}, u32[]{:S(2)}, u32[]{:S(2)}) collective-permute-start(bf16[512,1536]{1,0:T(8,128)(2,1)S(1)} %copy-done.7), channel_id=1, source_target_pairs={{0,1},{1,0},{2,3},{3,2},{4,5},{5,4},{6,7},{7,6},{8,9},{9,8},{10,11... | collective-permute-start | bytes 4718600 | tf_op jit(solution)/shard_map/ppermute | solution.py:74
  37.1 74.3 %all-to-all-start = ((bf16[8,2,48,1024]{3,2,1,0:T(8,128)(2,1)}), bf16[8,2,48,1024]{3,2,1,0:T(8,128)(2,1)}, u32[]{:S(2)}, u32[]{:S(2)}) async-start(bf16[8,2,48,1024]{3,2,1,0:T(8,128)(2,1)} %bitcast.160), calls=%async_computation | async-start | bytes 3145728 | tf_op jit(solution)/shard_map/all_to_all | solution.py:418
  41.4 287.5 %all-gather.6.cloned.1.call-start = ((), (), s32[]{:S(2)}) async-start(), calls=%async_computation.10 | async-start | bytes 7864320 | tf_op jit(solution)/shard_map/all_gather | solution.py:423
  82.2 58.0 %collective-permute-start.10 = (bf16[512,1536]{1,0:T(8,128)(2,1)}, bf16[512,1536]{1,0:T(8,128)(2,1)}, u32[]{:S(2)}, u32[]{:S(2)}) collective-permute-start(bf16[512,1536]{1,0:T(8,128)(2,1)} %collective-permute-done.9), channel_id=1, source_target_pairs={{0,1},{1,0},{2,3},{3,2},{4,5},{5,4},{6,7},{7,6},{8,9},{9,8},{10,11... | collective-permute-start | bytes 4718600 | tf_op jit(solution)/shard_map/ppermute | solution.py:74
  85.8 42.9 %collective-permute-start.13 = (bf16[256,1536]{1,0:T(8,128)(2,1)}, bf16[256,1536]{1,0:T(8,128)(2,1)}, u32[]{:S(2)}, u32[]{:S(2)}) collective-permute-start(bf16[256,1536]{1,0:T(8,128)(2,1)} %slice.333), channel_id=1, source_target_pairs={{0,4},{1,5},{2,6},{3,7},{4,0},{5,1},{6,2},{7,3},{8,12},{9,13},{10,... | collective-permute-start | bytes 2359304 | tf_op jit(solution)/shard_map/ppermute | solution.py:74
  88.2 47.9 %collective-permute-start.14 = (bf16[256,1536]{1,0:T(8,128)(2,1)}, bf16[256,1536]{1,0:T(8,128)(2,1)}, u32[]{:S(2)}, u32[]{:S(2)}) collective-permute-start(bf16[256,1536]{1,0:T(8,128)(2,1)} %slice.334), channel_id=1, source_target_pairs={{0,2},{1,3},{2,0},{3,1},{4,6},{5,7},{6,4},{7,5},{8,10},{9,11},{10,... | collective-permute-start | bytes 2359304 | tf_op jit(solution)/shard_map/ppermute | solution.py:74
  91.0 54.7 %collective-permute-start.12 = (bf16[512,1536]{1,0:T(8,128)(2,1)}, bf16[512,1536]{1,0:T(8,128)(2,1)}, u32[]{:S(2)}, u32[]{:S(2)}) collective-permute-start(bf16[512,1536]{1,0:T(8,128)(2,1)} %collective-permute-done.11), channel_id=1, source_target_pairs={{0,1},{1,0},{2,3},{3,2},{4,5},{5,4},{6,7},{7,6},{8,9},{9,8},{10,11... | collective-permute-start | bytes 4718600 | tf_op jit(solution)/shard_map/ppermute | solution.py:74
  114.2 680.5 %reduce-scatter.12.cloned.1.call-start = ((), (), s32[]{:S(2)}) async-start(), calls=%async_computation.13 | async-start | bytes 1966080 | tf_op jit(solution)/shard_map/reduce_scatter | solution.py:482
  198.1 55.0 %collective-permute-start = (bf16[512,1536]{1,0:T(8,128)(2,1)}, bf16[512,1536]{1,0:T(8,128)(2,1)}, u32[]{:S(2)}, u32[]{:S(2)}) collective-permute-start(bf16[512,1536]{1,0:T(8,128)(2,1)} %get-tuple-element.138), channel_id=1, source_target_pairs={{0,1},{1,0},{2,3},{3,2},{4,5},{5,4},{6,7},{7,6},{8,9},{9,8},{10,11... | collective-permute-start | bytes 4718600 | tf_op jit(solution)/shard_map/ppermute | solution.py:74
  198.3 45.3 %collective-permute-start.1 = (bf16[512,1536]{1,0:T(8,128)(2,1)}, bf16[512,1536]{1,0:T(8,128)(2,1)}, u32[]{:S(2)}, u32[]{:S(2)}) collective-permute-start(bf16[512,1536]{1,0:T(8,128)(2,1)} %get-tuple-element.138), channel_id=1, source_target_pairs={{0,2},{1,3},{2,0},{3,1},{4,6},{5,7},{6,4},{7,5},{8,10},{9,11},{10,... | collective-permute-start | bytes 4718600 | tf_op jit(solution)/shard_map/ppermute | solution.py:74
  198.9 48.1 %collective-permute-start.3 = (bf16[512,1536]{1,0:T(8,128)(2,1)}, bf16[512,1536]{1,0:T(8,128)(2,1)}, u32[]{:S(2)}, u32[]{:S(2)}) collective-permute-start(bf16[512,1536]{1,0:T(8,128)(2,1)} %get-tuple-element.138), channel_id=1, source_target_pairs={{0,4},{1,5},{2,6},{3,7},{4,0},{5,1},{6,2},{7,3},{8,12},{9,13},{10,... | collective-permute-start | bytes 4718600 | tf_op jit(solution)/shard_map/ppermute | solution.py:74
  202.0 33.3 %collective-permute-start.17 = (f32[2,512]{1,0:T(2,128)S(1)}, f32[2,512]{1,0:T(2,128)S(1)}, u32[]{:S(2)}, u32[]{:S(2)}) collective-permute-start(f32[2,512]{1,0:T(2,128)S(1)} %get-tuple-element.196), channel_id=1, source_target_pairs={{0,2},{1,3},{2,0},{3,1},{4,6},{5,7},{6,4},{7,5},{8,10},{9,11},{10,... | collective-permute-start | bytes 12296 | tf_op jit(solution)/shard_map/ppermute | solution.py:74
  203.4 32.4 %collective-permute-start.18 = (f32[2,512]{1,0:T(2,128)S(1)}, f32[2,512]{1,0:T(2,128)S(1)}, u32[]{:S(2)}, u32[]{:S(2)}) collective-permute-start(f32[2,512]{1,0:T(2,128)S(1)} %get-tuple-element.195), channel_id=1, source_target_pairs={{0,3},{1,2},{2,1},{3,0},{4,7},{5,6},{6,5},{7,4},{8,11},{9,10},{10,... | collective-permute-start | bytes 12296 | tf_op jit(solution)/shard_map/ppermute | solution.py:74
  245.7 19.8 %collective-permute-start.5 = (bf16[256,1536]{1,0:T(8,128)(2,1)}, bf16[256,1536]{1,0:T(8,128)(2,1)}, u32[]{:S(2)}, u32[]{:S(2)}) collective-permute-start(bf16[256,1536]{1,0:T(8,128)(2,1)} %slice.331), channel_id=1, source_target_pairs={{0,4},{1,5},{2,6},{3,7},{4,0},{5,1},{6,2},{7,3},{8,12},{9,13},{10,... | collective-permute-start | bytes 2359304 | tf_op jit(solution)/shard_map/ppermute | solution.py:74
  249.1 18.8 %collective-permute-start.6 = (bf16[256,1536]{1,0:T(8,128)(2,1)}, bf16[256,1536]{1,0:T(8,128)(2,1)}, u32[]{:S(2)}, u32[]{:S(2)}) collective-permute-start(bf16[256,1536]{1,0:T(8,128)(2,1)} %slice.332), channel_id=1, source_target_pairs={{0,2},{1,3},{2,0},{3,1},{4,6},{5,7},{6,4},{7,5},{8,10},{9,11},{10,... | collective-permute-start | bytes 2359304 | tf_op jit(solution)/shard_map/ppermute | solution.py:74
  250.5 21.7 %collective-permute-start.2 = (bf16[512,1536]{1,0:T(8,128)(2,1)}, bf16[512,1536]{1,0:T(8,128)(2,1)}, u32[]{:S(2)}, u32[]{:S(2)}) collective-permute-start(bf16[512,1536]{1,0:T(8,128)(2,1)} %collective-permute-done.1), channel_id=1, source_target_pairs={{0,1},{1,0},{2,3},{3,2},{4,5},{5,4},{6,7},{7,6},{8,9},{9,8},{10,11... | collective-permute-start | bytes 4718600 | tf_op jit(solution)/shard_map/ppermute | solution.py:74
  250.5 27.0 %collective-permute-start.4 = (bf16[512,1536]{1,0:T(8,128)(2,1)}, bf16[512,1536]{1,0:T(8,128)(2,1)}, u32[]{:S(2)}, u32[]{:S(2)}) collective-permute-start(bf16[512,1536]{1,0:T(8,128)(2,1)} %collective-permute-done.3), channel_id=1, source_target_pairs={{0,1},{1,0},{2,3},{3,2},{4,5},{5,4},{6,7},{7,6},{8,9},{9,8},{10,11... | collective-permute-start | bytes 4718600 | tf_op jit(solution)/shard_map/ppermute | solution.py:74
  427.2 18.1 %collective-permute-start.28 = (bf16[512,1536]{1,0:T(8,128)(2,1)}, bf16[512,1536]{1,0:T(8,128)(2,1)}, u32[]{:S(2)}, u32[]{:S(2)}) collective-permute-start(bf16[512,1536]{1,0:T(8,128)(2,1)} %get-tuple-element.155), channel_id=1, source_target_pairs={{0,1},{1,0},{2,3},{3,2},{4,5},{5,4},{6,7},{7,6},{8,9},{9,8},{10,11... | collective-permute-start | bytes 4718600 | tf_op jit(solution)/shard_map/ppermute | solution.py:74
  439.6 355.1 %reduce-scatter.14.cloned.1.call-start = ((), (), s32[]{:S(2)}) async-start(), calls=%async_computation.14 | async-start | bytes 1966080 | tf_op jit(solution)/shard_map/reduce_scatter | solution.py:482
  444.5 28.5 %collective-permute-start.34 = (f32[2,512]{0,1:T(8,128)}, f32[2,512]{0,1:T(8,128)}, u32[]{:S(2)}, u32[]{:S(2)}) collective-permute-start(f32[2,512]{0,1:T(8,128)} %get-tuple-element.168), channel_id=1, source_target_pairs={{0,5},{1,4},{2,7},{3,6},{4,1},{5,0},{6,3},{7,2},{8,13},{9,12},{10,... | collective-permute-start | bytes 12296 | tf_op jit(solution)/shard_map/ppermute | solution.py:74
  445.3 28.8 %collective-permute-start.35 = (f32[2,512]{0,1:T(8,128)}, f32[2,512]{0,1:T(8,128)}, u32[]{:S(2)}, u32[]{:S(2)}) collective-permute-start(f32[2,512]{0,1:T(8,128)} %get-tuple-element.167), channel_id=1, source_target_pairs={{0,4},{1,5},{2,6},{3,7},{4,0},{5,1},{6,2},{7,3},{8,12},{9,13},{10,... | collective-permute-start | bytes 12296 | tf_op jit(solution)/shard_map/ppermute | solution.py:74
  454.5 20.8 %collective-permute-start.36 = (f32[2,512]{0,1:T(8,128)}, f32[2,512]{0,1:T(8,128)}, u32[]{:S(2)}, u32[]{:S(2)}) collective-permute-start(f32[2,512]{0,1:T(8,128)} %get-tuple-element.166), channel_id=1, source_target_pairs={{0,7},{1,6},{2,5},{3,4},{4,3},{5,2},{6,1},{7,0},{8,15},{9,14},{10,... | collective-permute-start | bytes 12296 | tf_op jit(solution)/shard_map/ppermute | solution.py:74
  456.5 19.8 %collective-permute-start.37 = (f32[2,512]{0,1:T(8,128)}, f32[2,512]{0,1:T(8,128)}, u32[]{:S(2)}, u32[]{:S(2)}) collective-permute-start(f32[2,512]{0,1:T(8,128)} %get-tuple-element.165), channel_id=1, source_target_pairs={{0,6},{1,7},{2,4},{3,5},{4,2},{5,3},{6,0},{7,1},{8,14},{9,15},{10,... | collective-permute-start | bytes 12296 | tf_op jit(solution)/shard_map/ppermute | solution.py:74
  457.2 29.9 %collective-permute-start.26 = (bf16[256,1536]{1,0:T(8,128)(2,1)}, bf16[256,1536]{1,0:T(8,128)(2,1)}, u32[]{:S(2)}, u32[]{:S(2)}) collective-permute-start(bf16[256,1536]{1,0:T(8,128)(2,1)} %get-tuple-element.177), channel_id=1, source_target_pairs={{0,4},{1,5},{2,6},{3,7},{4,0},{5,1},{6,2},{7,3},{8,12},{9,13},{10,... | collective-permute-start | bytes 2359304 | tf_op jit(solution)/shard_map/ppermute | solution.py:74
  469.8 369.8 %reduce-scatter.16.cloned.1.call-start = ((), (), s32[]{:S(2)}) async-start(), calls=%async_computation.15 | async-start | bytes 3932160 | tf_op jit(solution)/shard_map/reduce_scatter | solution.py:479
  473.0 30.4 %collective-permute-start.23 = (bf16[512,1536]{1,0:T(8,128)(2,1)}, bf16[512,1536]{1,0:T(8,128)(2,1)}, u32[]{:S(2)}, u32[]{:S(2)}) collective-permute-start(bf16[512,1536]{1,0:T(8,128)(2,1)} %get-tuple-element.154), channel_id=1, source_target_pairs={{0,1},{1,0},{2,3},{3,2},{4,5},{5,4},{6,7},{7,6},{8,9},{9,8},{10,11... | collective-permute-start | bytes 4718600 | tf_op jit(solution)/shard_map/ppermute | solution.py:74
  478.8 20.6 %collective-permute-start.29 = (bf16[256,1536]{1,0:T(8,128)(2,1)}, bf16[256,1536]{1,0:T(8,128)(2,1)S(1)}, u32[]{:S(2)}, u32[]{:S(2)}) collective-permute-start(bf16[256,1536]{1,0:T(8,128)(2,1)} %get-tuple-element.178), channel_id=1, source_target_pairs={{0,2},{1,3},{2,0},{3,1},{4,6},{5,7},{6,4},{7,5},{8,10},{9,11},{10,... | collective-permute-start | bytes 2359304 | tf_op jit(solution)/shard_map/ppermute | solution.py:74
  489.7 43.1 %collective-permute-start.27 = (bf16[512,1536]{1,0:T(8,128)(2,1)}, bf16[512,1536]{1,0:T(8,128)(2,1)}, u32[]{:S(2)}, u32[]{:S(2)}) collective-permute-start(bf16[512,1536]{1,0:T(8,128)(2,1)} %pad_maximum_fusion.7), channel_id=1, source_target_pairs={{0,2},{1,3},{2,0},{3,1},{4,6},{5,7},{6,4},{7,5},{8,10},{9,11},{10,... | collective-permute-start | bytes 4718600 | tf_op jit(solution)/shard_map/ppermute | solution.py:74
  500.9 36.0 %collective-permute-start.30 = (bf16[512,1536]{1,0:T(8,128)(2,1)}, bf16[512,1536]{1,0:T(8,128)(2,1)}, u32[]{:S(2)}, u32[]{:S(2)}) collective-permute-start(bf16[512,1536]{1,0:T(8,128)(2,1)} %pad_maximum_fusion.8), channel_id=1, source_target_pairs={{0,4},{1,5},{2,6},{3,7},{4,0},{5,1},{6,2},{7,3},{8,12},{9,13},{10,... | collective-permute-start | bytes 4718600 | tf_op jit(solution)/shard_map/ppermute | solution.py:74
  562.5 20.4 %collective-permute-start.41 = (bf16[256,1536]{1,0:T(8,128)(2,1)}, bf16[256,1536]{1,0:T(8,128)(2,1)}, u32[]{:S(2)}, u32[]{:S(2)}) collective-permute-start(bf16[256,1536]{1,0:T(8,128)(2,1)} %get-tuple-element.175), channel_id=1, source_target_pairs={{0,4},{1,5},{2,6},{3,7},{4,0},{5,1},{6,2},{7,3},{8,12},{9,13},{10,... | collective-permute-start | bytes 2359304 | tf_op jit(solution)/shard_map/ppermute | solution.py:74
  578.4 261.2 %reduce-scatter.18.cloned.1.call-start = ((), (), s32[]{:S(2)}) async-start(), calls=%async_computation.16 | async-start | bytes 3932160 | tf_op jit(solution)/shard_map/reduce_scatter | solution.py:479
  578.4 41.8 %collective-permute-start.38 = (bf16[512,1536]{1,0:T(8,128)(2,1)}, bf16[512,1536]{1,0:T(8,128)(2,1)}, u32[]{:S(2)}, u32[]{:S(2)}) collective-permute-start(bf16[512,1536]{1,0:T(8,128)(2,1)} %get-tuple-element.147), channel_id=1, source_target_pairs={{0,1},{1,0},{2,3},{3,2},{4,5},{5,4},{6,7},{7,6},{8,9},{9,8},{10,11... | collective-permute-start | bytes 4718600 | tf_op jit(solution)/shard_map/ppermute | solution.py:74
  580.0 20.6 %collective-permute-start.44 = (bf16[256,1536]{1,0:T(8,128)(2,1)}, bf16[256,1536]{1,0:T(8,128)(2,1)S(1)}, u32[]{:S(2)}, u32[]{:S(2)}) collective-permute-start(bf16[256,1536]{1,0:T(8,128)(2,1)} %get-tuple-element.176), channel_id=1, source_target_pairs={{0,2},{1,3},{2,0},{3,1},{4,6},{5,7},{6,4},{7,5},{8,10},{9,11},{10,... | collective-permute-start | bytes 2359304 | tf_op jit(solution)/shard_map/ppermute | solution.py:74
  585.6 48.2 %collective-permute-start.42 = (bf16[512,1536]{1,0:T(8,128)(2,1)}, bf16[512,1536]{1,0:T(8,128)(2,1)}, u32[]{:S(2)}, u32[]{:S(2)}) collective-permute-start(bf16[512,1536]{1,0:T(8,128)(2,1)} %pad_maximum_fusion.9), channel_id=1, source_target_pairs={{0,2},{1,3},{2,0},{3,1},{4,6},{5,7},{6,4},{7,5},{8,10},{9,11},{10,... | collective-permute-start | bytes 4718600 | tf_op jit(solution)/shard_map/ppermute | solution.py:74
  602.1 35.5 %collective-permute-start.45 = (bf16[512,1536]{1,0:T(8,128)(2,1)}, bf16[512,1536]{1,0:T(8,128)(2,1)}, u32[]{:S(2)}, u32[]{:S(2)}) collective-permute-start(bf16[512,1536]{1,0:T(8,128)(2,1)} %pad_maximum_fusion.10), channel_id=1, source_target_pairs={{0,4},{1,5},{2,6},{3,7},{4,0},{5,1},{6,2},{7,3},{8,12},{9,13},{10,... | collective-permute-start | bytes 4718600 | tf_op jit(solution)/shard_map/ppermute | solution.py:74
  747.0 19.1 %collective-permute-start.48 = (bf16[192,4224]{1,0:T(8,128)(2,1)}, bf16[192,4224]{1,0:T(8,128)(2,1)}, u32[]{:S(2)}, u32[]{:S(2)}) collective-permute-start(bf16[192,4224]{1,0:T(8,128)(2,1)} %bitcast.60), channel_id=1, source_target_pairs={{0,1},{1,0},{2,3},{3,2},{4,5},{5,4},{6,7},{7,6},{8,9},{9,8},{10,11... | collective-permute-start | bytes 4866056 | tf_op jit(solution)/shard_map/ppermute | solution.py:74
  765.7 35.3 %collective-permute-start.46 = (bf16[192,4224]{1,0:T(8,128)(2,1)}, bf16[192,4224]{1,0:T(8,128)(2,1)}, u32[]{:S(2)}, u32[]{:S(2)}) collective-permute-start(bf16[192,4224]{1,0:T(8,128)(2,1)} %bitcast.164), channel_id=1, source_target_pairs={{0,1},{1,0},{2,3},{3,2},{4,5},{5,4},{6,7},{7,6},{8,9},{9,8},{10,11... | collective-permute-start | bytes 4866056 | tf_op jit(solution)/shard_map/ppermute | solution.py:74
  768.7 20.1 %collective-permute-start.49 = (bf16[96,4224]{1,0:T(8,128)(2,1)S(1)}, bf16[96,4224]{1,0:T(8,128)(2,1)S(1)}, u32[]{:S(2)}, u32[]{:S(2)}) collective-permute-start(bf16[96,4224]{1,0:T(8,128)(2,1)S(1)} %get-tuple-element.173), channel_id=1, source_target_pairs={{0,4},{1,5},{2,6},{3,7},{4,0},{5,1},{6,2},{7,3},{8,12},{9,13},{10,... | collective-permute-start | bytes 2433032 | tf_op jit(solution)/shard_map/ppermute | solution.py:74
  770.6 21.1 %collective-permute-start.52 = (bf16[96,4224]{1,0:T(8,128)(2,1)S(1)}, bf16[96,4224]{1,0:T(8,128)(2,1)S(1)}, u32[]{:S(2)}, u32[]{:S(2)}) collective-permute-start(bf16[96,4224]{1,0:T(8,128)(2,1)S(1)} %get-tuple-element.174), channel_id=1, source_target_pairs={{0,2},{1,3},{2,0},{3,1},{4,6},{5,7},{6,4},{7,5},{8,10},{9,11},{10,... | collective-permute-start | bytes 2433032 | tf_op jit(solution)/shard_map/ppermute | solution.py:74
  790.3 38.7 %collective-permute-start.50 = (bf16[192,4224]{1,0:T(8,128)(2,1)}, bf16[192,4224]{1,0:T(8,128)(2,1)}, u32[]{:S(2)}, u32[]{:S(2)}) collective-permute-start(bf16[192,4224]{1,0:T(8,128)(2,1)} %pad_maximum_fusion.2), channel_id=1, source_target_pairs={{0,2},{1,3},{2,0},{3,1},{4,6},{5,7},{6,4},{7,5},{8,10},{9,11},{10,... | collective-permute-start | bytes 4866056 | tf_op jit(solution)/shard_map/ppermute | solution.py:74
  793.3 41.9 %collective-permute-start.53 = (bf16[192,4224]{1,0:T(8,128)(2,1)}, bf16[192,4224]{1,0:T(8,128)(2,1)}, u32[]{:S(2)}, u32[]{:S(2)}) collective-permute-start(bf16[192,4224]{1,0:T(8,128)(2,1)} %pad_maximum_fusion.3), channel_id=1, source_target_pairs={{0,4},{1,5},{2,6},{3,7},{4,0},{5,1},{6,2},{7,3},{8,12},{9,13},{10,... | collective-permute-start | bytes 4866056 | tf_op jit(solution)/shard_map/ppermute | solution.py:74
  796.7 45.7 %all-to-all-start.3 = ((bf16[8,2,16,1536]{3,2,1,0:T(8,128)(2,1)}), bf16[8,2,16,1536]{3,2,1,0:T(8,128)(2,1)}, u32[]{:S(2)}, u32[]{:S(2)}) async-start(bf16[8,2,16,1536]{3,2,1,0:T(8,128)(2,1)} %pad_maximum_fusion.12), calls=%async_computation.6 | async-start | bytes 1572864 | tf_op jit(solution)/shard_map/all_to_all | solution.py:487
  801.0 73.5 %reduce-scatter.10.cloned.1.call-start = ((), (), s32[]{:S(2)}) async-start(), calls=%async_computation.12 | async-start | bytes 2027520 | tf_op jit(solution)/shard_map/reduce_scatter | solution.py:538
  842.4 24.7 %all-to-all-start.2 = ((bf16[8,2,48,1024]{3,2,1,0:T(8,128)(2,1)}), bf16[8,2,48,1024]{3,2,1,0:T(8,128)(2,1)S(1)}, u32[]{:S(2)}, u32[]{:S(2)}) async-start(bf16[8,2,48,1024]{3,2,1,0:T(8,128)(2,1)} %copy.261), calls=%async_computation.3 | async-start | bytes 3145728 | tf_op jit(solution)/shard_map/all_to_all | solution.py:486
  (60 other events, 748.7 us)
Sparse Core Ops, SparseCore 0:
  11.6 138.3 all-gather.3
  151.6 61.6 all-gather.7
  214.9 113.9 all-gather.5
  439.7 33.5 reduce-scatter.11
  475.4 34.2 reduce-scatter.13
  578.5 58.6 reduce-scatter.15
  765.2 58.7 reduce-scatter.17
  839.7 34.7 reduce-scatter.9

commit v2 on v1

v2 whole, which is shorter than its diff:
```python
import functools
import math

import jax
import jax.numpy as jnp
from jax import lax
from jax.experimental import pallas as pl
from jax.experimental.pallas import tpu as pltpu
from jax.sharding import PartitionSpec as P

HQ = 24
HK = 8
HD = 64
E = 16
GROUP = 8
PAIR_E = E // GROUP
LANES = 128
QW = HQ * HD
KW = HK * HD
QKV_WIDE = QW + 2 * KW + LANES
GAIN_ONE = E
GAIN_TWO = E + 1
VMEM_LIMIT = 58 * 1024 * 1024

norm_eps = 1e-06
resid_scale = 0.22
score_scale = 0.015625
rope_base = 10000.0
masked_score = -1e30

f32 = jnp.float32
bf16 = jnp.bfloat16


def matmul(left, right):
    return jnp.dot(left, right, preferred_element_type=f32)


def contract_rows(left, right):
    return lax.dot_general(left, right, (((0,), (0,)), ((), ())), preferred_element_type=f32)


def contract_last(left, right):
    return lax.dot_general(left, right, (((1,), (1,)), ((), ())), preferred_element_type=f32)


def layout(seq_lengths, row_count):
    seq_ends = jnp.cumsum(seq_lengths)
    starts = seq_ends - seq_lengths
    places = jnp.arange(row_count, dtype=jnp.int32)
    member = (places[:, None] >= starts[None, :]) & (places[:, None] < seq_ends[None, :])
    labels = jnp.arange(seq_lengths.shape[0], dtype=jnp.int32)
    segment = jnp.sum(jnp.where(member, labels[None, :], 0), axis=1)
    offset = jnp.sum(jnp.where(member, starts[None, :], 0), axis=1)
    return (segment, places - offset)


def turn_tables(position):
    half_dim = HD // 2
    inv_freq = jnp.exp(
        -(jnp.arange(half_dim, dtype=f32) * (2.0 / HD)) * math.log(rope_base)
    )
    angles = position.astype(f32)[:, None] * inv_freq[None, :]
    cosine, sine_val = jnp.cos(angles), jnp.sin(angles)
    return (
        jnp.concatenate([cosine] * 4, axis=1),
        jnp.concatenate([-sine_val, sine_val] * 2, axis=1),
    )


def swap(value, bit, device_count):
    return lax.ppermute(value, "fsdp", [(i, i ^ bit) for i in range(device_count)])


def shift(value, steps, device_count):
    moved = [(i, (i + GROUP * steps) % device_count) for i in range(device_count)]
    return lax.ppermute(value, "fsdp", moved)


def after(value, *needed):
    return lax.optimization_barrier((value, needed))[0]


def tie(*values):
    return lax.optimization_barrier(values)


def gather_start(own, device_count):
    return swap(own, 2, device_count), swap(own, 4, device_count)


def gather_far(from2, from4, device_count):
    half = from2.shape[0] // 2
    return swap(from2[:half], 4, device_count), swap(from4[half:], 2, device_count)


def gather_cores(own, near, far, device_count):
    other = lambda value: swap(value, 1, device_count)
    return [
        [own], [other(own)], [near[0]], [other(near[0])], [near[1]], [other(near[1])],
        list(far), [other(far[0]), other(far[1])],
    ]


def add_low(left, right):
    return (left.astype(f32) + right.astype(f32)).astype(bf16)


def sum_cores(parts, device_count):
    return add_low(parts[0], swap(parts[1], 1, device_count))


def sum_far(chip, device_count):
    half = chip.shape[0] // 2
    return swap(chip[:half], 4, device_count), swap(chip[half:], 2, device_count)


def sum_near(chip2, chip4, low, high, device_count):
    half = chip2.shape[0] // 2
    sum2 = jnp.concatenate([add_low(chip2[:half], low), chip2[half:]], axis=0)
    sum4 = jnp.concatenate([chip4[:half], add_low(chip4[half:], high)], axis=0)
    return swap(sum2, 2, device_count), swap(sum4, 4, device_count)


def add_up(parts):
    return parts[0].astype(f32) + parts[1].astype(f32) + parts[2].astype(f32)


def layer_start(stacked, layer, layers, device_count):
    pick = lambda at: lax.dynamic_index_in_dim(stacked, at % layers, 0, keepdims=False)
    return [pick(layer)] + [shift(pick(layer + k), k, device_count) for k in range(1, layers)]


def layer_add(blocks):
    total = blocks[0].astype(f32)
    for block in blocks[1:]:
        total = total + block.astype(f32)
    return total


def turn(values, cosine, sine_val, low_half):
    shifted = jnp.where(low_half, pltpu.roll(values, LANES - 32, 1), pltpu.roll(values, 32, 1))
    return values * cosine + shifted * sine_val


def half_views(pair, scale):
    lane = lax.broadcasted_iota(jnp.int32, pair.shape, 1)
    wide = pair.astype(f32) * scale
    other = pltpu.roll(wide, HD, 1)
    low = lane < HD
    return [
        [jnp.where(low, wide, 0.0).astype(bf16), jnp.where(low, other, 0.0).astype(bf16)],
        [jnp.where(low, 0.0, other).astype(bf16), jnp.where(low, 0.0, wide).astype(bf16)],
    ]


def visible_keys(seg_col, seg_row, row_start, rows, keys):
    query_at = row_start + lax.broadcasted_iota(jnp.int32, (rows, keys), 0)
    key_at = lax.broadcasted_iota(jnp.int32, (rows, keys), 1)
    return (seg_col[row_start : row_start + rows, :] == seg_row[:, :keys]) & (key_at <= query_at)


def any_spec():
    return pl.BlockSpec(memory_space=pl.ANY)


def smem_spec():
    return pl.BlockSpec(memory_space=pltpu.SMEM)


def small_cost():
    return pl.CostEstimate(flops=1_000_000, bytes_accessed=100_000, transcendentals=0)


def params():
    return pltpu.CompilerParams(vmem_limit_bytes=VMEM_LIMIT)


def whole_spec(shape):
    zeros = (0,) * len(shape)
    return pl.BlockSpec(shape, lambda *_: zeros, pipeline_mode=pl.Buffered(1))


def gather_copies(plan, refs, table_ref, dst, sems):
    copies = []
    for ref, runs in zip(refs, plan):
        rows = ref.shape[0] // len(runs)
        for number, (member, step) in enumerate(runs):
            start = pl.multiple_of(table_ref[member, step], 16)
            copies.append(
                pltpu.make_async_copy(
                    ref.at[pl.ds(number * rows, rows)],
                    dst.at[pl.ds(start, rows)],
                    sems.at[len(copies)],
                )
            )
    return copies


def spread_copies(src, table_ref, refs, sems):
    copies = []
    members, blocks = table_ref.shape
    rows = src.shape[0] // (members * blocks)
    for member in range(members):
        for block in range(blocks):
            start = pl.multiple_of(table_ref[member, block], 16)
            to = (member // 2 * blocks + block) * rows
            copies.append(
                pltpu.make_async_copy(
                    src.at[pl.ds(start, rows)], refs[member % 2].at[pl.ds(to, rows)], sems.at[len(copies)]
                )
            )
    return copies


def stack_shapes(table, width, full):
    members = table.shape[0]
    stacks = min(members, 2)
    return [jax.ShapeDtypeStruct((width // stacks, full), bf16)] * stacks


def attend_kernel(block, plan, table_ref, x_ref, cos_ref, sin_ref, segc_ref, segr_ref, *refs):
    pair = pl.program_id(0)
    rows_all, width = x_ref.shape
    at = lambda start, wide: pl.ds(pl.multiple_of(start, LANES), wide)
    if plan is None:
        wq_ref, wk_ref, wv_ref, q_ref, k_ref, v_ref, out_ref, lse_ref = refs
        normed_ref = x_ref
        w_q, w_k, w_v = wq_ref[...], wk_ref[...], wv_ref[...]
    else:
        sources = refs[: len(plan)]
        (w_out_ref, normed_ref, turned_ref, q_ref, k_ref, v_ref, out_ref, lse_ref,
         w_ref, sems, save_sem) = refs[len(plan) :]

        @pl.when(pair == 0)
        def _():
            copies = gather_copies(plan, sources, table_ref, w_ref, sems)
            for c in copies:
                c.start()
            x = x_ref[...].astype(f32)
            rinv = lax.rsqrt(jnp.mean(x * x, axis=-1, keepdims=True) + norm_eps)
            for c in copies:
                c.wait()
            pltpu.make_async_copy(w_ref, w_out_ref, save_sem).start()
            gains = w_ref[:, QW + 2 * KW :].astype(f32).T
            scaled = x * rinv * gains[GAIN_ONE : GAIN_ONE + 1, :]
            normed_ref[...] = scaled.astype(bf16)
            turned_ref[...] = scaled.T.astype(bf16)

        w_q = w_ref[:, at(pair * 3 * LANES, 3 * LANES)]
        w_k = w_ref[:, at(QW + pair * LANES, LANES)]
        w_v = w_ref[:, at(QW + KW + pair * LANES, LANES)]

    normed = normed_ref[...]
    lane = lax.broadcasted_iota(jnp.int32, (rows_all, LANES), 1)
    first = (lane % HD) < (HD // 2)
    cosine, sine_val = cos_ref[...], sin_ref[...]
    q_pre = matmul(normed, w_q)
    for t in range(3):
        cols = slice(t * LANES, (t + 1) * LANES)
        q_ref[:, cols] = turn(q_pre[:, cols], cosine, sine_val, first).astype(bf16)
    k_low = turn(matmul(normed, w_k), cosine, sine_val, first).astype(bf16)
    v_low = matmul(normed, w_v).astype(bf16)
    k_ref[...] = k_low
    v_ref[...] = v_low
    k_views = half_views(k_low, score_scale)
    v_views = half_views(v_low, 1.0)
    seg_col, seg_row = segc_ref[...], segr_ref[...]
    for start in range(0, rows_all, block):
        keys = start + block
        visible = visible_keys(seg_col, seg_row, start, block, keys)
        lane_b = lax.broadcasted_iota(jnp.int32, (block, LANES), 1)
        norms = jnp.zeros((block, LANES), f32)
        for t in range(3):
            cols = slice(t * LANES, (t + 1) * LANES)
            q_tile = q_ref[start : start + block, cols]
            total = jnp.zeros((block, LANES), f32)
            for side in range(2):
                head = 2 * t + side
                kv = head // 3
                scores = contract_last(q_tile, k_views[side][kv][:keys])
                scores = jnp.where(visible, scores, masked_score)
                peak = jnp.max(scores, axis=-1, keepdims=True)
                expo = jnp.exp(scores - peak)
                mass = jnp.sum(expo, axis=-1, keepdims=True)
                probs = (expo * (1.0 / mass)).astype(bf16)
                total = total + matmul(probs, v_views[side][kv][:keys])
                norms = jnp.where(lane_b == head, peak + jnp.log(mass), norms)
            out_ref[start : start + block, cols] = total.astype(bf16)
        lse_ref[0, start : start + block, :] = norms

    if plan is not None:
        @pl.when(pair == pl.num_programs(0) - 1)
        def _():
            pltpu.make_async_copy(w_ref, w_out_ref, save_sem).wait()


def attend_forward(base, steps, table, plan, weights, rows_in, cosine, sine_val, segment):
    rows, width = rows_in.shape
    wide = pl.BlockSpec((rows, 3 * LANES), lambda i: (0, i))
    thin = pl.BlockSpec((rows, LANES), lambda i: (0, i))
    in_specs = [
        smem_spec(),
        whole_spec((rows, width)),
        whole_spec((rows, LANES)),
        whole_spec((rows, LANES)),
        whole_spec((rows, 1)),
        whole_spec((1, rows)),
    ]
    out_specs = [wide, thin, thin, wide, pl.BlockSpec((1, rows, LANES), lambda i: (i, 0, 0))]
    out_shape = [
        jax.ShapeDtypeStruct((rows, 3 * LANES * steps), bf16),
        jax.ShapeDtypeStruct((rows, LANES * steps), bf16),
        jax.ShapeDtypeStruct((rows, LANES * steps), bf16),
        jax.ShapeDtypeStruct((rows, 3 * LANES * steps), bf16),
        jax.ShapeDtypeStruct((steps, rows, LANES), f32),
    ]
    if plan is None:
        in_specs += [
            pl.BlockSpec((width, 3 * LANES), lambda i: (0, base + i)),
            pl.BlockSpec((width, LANES), lambda i: (0, QW // LANES + base + i)),
            pl.BlockSpec((width, LANES), lambda i: (0, (QW + KW) // LANES + base + i)),
        ]
        weights = [weights] * 3
        scratch = []
    else:
        in_specs += [any_spec()] * len(weights)
        out_specs = [any_spec(), whole_spec((rows, width)), whole_spec((width, rows))] + out_specs
        out_shape = [
            jax.ShapeDtypeStruct((width, QKV_WIDE), bf16),
            jax.ShapeDtypeStruct((rows, width), bf16),
            jax.ShapeDtypeStruct((width, rows), bf16),
        ] + out_shape
        scratch = [
            pltpu.VMEM((width, QKV_WIDE), bf16),
            pltpu.SemaphoreType.DMA((sum(len(r) for r in plan),)),
            pltpu.SemaphoreType.DMA(()),
        ]
    return pl.pallas_call(
        functools.partial(attend_kernel, 128, plan),
        grid=(steps,),
        in_specs=in_specs,
        out_specs=out_specs,
        out_shape=out_shape,
        scratch_shapes=scratch,
        compiler_params=params(),
        cost_estimate=small_cost(),
    )(table, rows_in, cosine, sine_val, segment[:, None], segment[None, :], *weights)


def middle_kernel(plan, table_ref, x_ref, attn0_ref, attn1_ref, extras_ref, routes_ref, *refs):
    sources = refs[: len(plan)]
    w_out_ref, middle_ref, inner_ref, mix_ref, w_ref, sems, save_sem = refs[len(plan) :]
    copies = gather_copies(plan, sources, table_ref, w_ref, sems)
    for c in copies:
        c.start()
    extras = extras_ref[...]
    gains = extras.astype(f32).T
    rows, width = x_ref.shape
    for c in copies:
        c.wait()
    save = pltpu.make_async_copy(w_ref, w_out_ref, save_sem)
    save.start()
    half = attn0_ref.shape[1]
    product = matmul(attn0_ref[...], w_ref[:half]) + matmul(attn1_ref[...], w_ref[half:])
    middle = x_ref[...].astype(f32) + resid_scale * product
    middle_ref[...] = middle
    rinv = lax.rsqrt(jnp.mean(middle * middle, axis=-1, keepdims=True) + norm_eps)
    inner = (middle * rinv * gains[GAIN_TWO : GAIN_TWO + 1, :]).astype(bf16)
    inner_ref[:, :width] = inner
    logits = matmul(inner, extras)
    lane = lax.broadcasted_iota(jnp.int32, logits.shape, 1)
    routes = routes_ref[...]
    named = lane == routes[:, 0:1]
    for k in range(1, routes.shape[1]):
        named = named | (lane == routes[:, k : k + 1])
    chosen = jnp.where(named, logits, masked_score)
    peak = jnp.max(chosen, axis=-1, keepdims=True)
    expo = jnp.where(named, jnp.exp(chosen - peak), 0.0)
    mix = expo / jnp.sum(expo, axis=-1, keepdims=True)
    mix_ref[...] = mix
    high = mix.astype(bf16).astype(f32)
    rest = (mix - high).astype(bf16).astype(f32)
    low = mix - high - rest
    spread = high + pltpu.roll(rest, E, 1) + pltpu.roll(low, 2 * E, 1)
    inner_ref[:, width:] = spread.astype(bf16)
    save.wait()


def to_middle(table, plan, pieces, hidden_in, attn_out, extras, routes):
    rows, width = hidden_in.shape
    vmem = pl.BlockSpec(memory_space=pltpu.VMEM)
    return pl.pallas_call(
        functools.partial(middle_kernel, plan),
        in_specs=[smem_spec()] + [vmem] * 5 + [any_spec()] * len(pieces),
        out_specs=[any_spec(), vmem, vmem, vmem],
        out_shape=[
            jax.ShapeDtypeStruct((QW, width), bf16),
            jax.ShapeDtypeStruct((rows, width), f32),
            jax.ShapeDtypeStruct((rows, width + LANES), bf16),
            jax.ShapeDtypeStruct((rows, LANES), f32),
        ],
        scratch_shapes=[
            pltpu.VMEM((QW, width), bf16),
            pltpu.SemaphoreType.DMA((sum(len(r) for r in plan),)),
            pltpu.SemaphoreType.DMA(()),
        ],
        compiler_params=params(),
        cost_estimate=small_cost(),
    )(table, hidden_in, *attn_out, extras, routes, *pieces)


def middle_back_kernel(blocks, table_ref, sum0_ref, sum1_ref, sum2_ref, inner_ref, mix_ref, middle_ref,
                       cot_ref, extras_ref, attn0_ref, attn1_ref, w_ref, *refs):
    dests = refs[:blocks]
    grad_ref, attn_grad0_ref, attn_grad1_ref, wgrad_ref, sems = refs[blocks:]
    rows, width = middle_ref.shape
    total = sum0_ref[...].astype(f32) + sum1_ref[...].astype(f32) + sum2_ref[...].astype(f32)
    inner_grad, tail = total[:, :width], total[:, width:]
    lane = lax.broadcasted_iota(jnp.int32, tail.shape, 1)
    mix = mix_ref[...]
    mix_grad = tail + pltpu.roll(tail, LANES - E, 1) + pltpu.roll(tail, LANES - 2 * E, 1)
    mix_grad = jnp.where(lane < E, mix_grad, 0.0)
    logit_grad = mix * (mix_grad - jnp.sum(mix * mix_grad, axis=-1, keepdims=True))
    logit_grad = logit_grad.astype(bf16)
    extras = extras_ref[...]
    gain = extras.astype(f32).T[GAIN_TWO : GAIN_TWO + 1, :]
    inner_grad = inner_grad + contract_last(logit_grad, extras)
    middle = middle_ref[...]
    rinv = lax.rsqrt(jnp.mean(middle * middle, axis=-1, keepdims=True) + norm_eps)
    scaled = gain * inner_grad
    back = rinv * scaled - middle * (rinv * rinv * rinv * jnp.mean(scaled * middle, axis=-1, keepdims=True))
    middle_grad = cot_ref[...].astype(f32) + back
    grad_ref[...] = middle_grad
    proj_grad = (resid_scale * middle_grad).astype(bf16)
    half = attn0_ref.shape[1]
    attn_grad0_ref[...] = contract_last(proj_grad, w_ref[:half]).astype(bf16)
    attn_grad1_ref[...] = contract_last(proj_grad, w_ref[half:]).astype(bf16)
    wgrad_ref[:half, :width] = contract_rows(attn0_ref[...], proj_grad).astype(bf16)
    wgrad_ref[half:, :width] = contract_rows(attn1_ref[...], proj_grad).astype(bf16)
    wgrad_ref[:, width:] = contract_rows(inner_ref[:, :width], logit_grad).astype(bf16)
    copies = spread_copies(wgrad_ref, table_ref, dests, sems)
    for c in copies:
        c.start()
    for c in copies:
        c.wait()


def middle_back(table, sums, inner, mix, middle, cotangent, extras, attn_out, w_out):
    rows, width = middle.shape
    members, layers = table.shape
    vmem = pl.BlockSpec(memory_space=pltpu.VMEM)
    full = width + LANES
    return pl.pallas_call(
        functools.partial(middle_back_kernel, min(members, 2)),
        in_specs=[smem_spec()] + [vmem] * 11,
        out_specs=[any_spec()] * min(members, 2) + [vmem] * 3,
        out_shape=stack_shapes(table, width, full)
        + [jax.ShapeDtypeStruct((rows, width), f32)]
        + [jax.ShapeDtypeStruct((rows, QW // 2), bf16)] * 2,
        scratch_shapes=[
            pltpu.VMEM((width, full), bf16),
            pltpu.SemaphoreType.DMA((members * layers,)),
        ],
        compiler_params=params(),
        cost_estimate=small_cost(),
    )(table, *sums, inner, mix, middle, cotangent, extras, *attn_out, w_out)


def attend_back_kernel(block, blocks, table_ref, turned_ref, q_ref, k_ref, v_ref, grad_ref, lse_ref,
                       cos_ref, sin_ref, segc_ref, segr_ref, *refs):
    dests = refs[:blocks]
    dq_ref, dk_ref, dv_ref, qt_ref, gt_ref, dkt_ref, dvt_ref, wgrad_ref, sems = refs[blocks:]
    step = pl.program_id(0)
    width, rows_all = turned_ref.shape
    lane = lax.broadcasted_iota(jnp.int32, (rows_all, LANES), 1)
    first = (lane % HD) < (HD // 2)
    k_views = half_views(k_ref[...], score_scale)
    v_views = half_views(v_ref[...], 1.0)

    qt_ref[...] = q_ref[...].astype(f32).T.astype(bf16)
    gt_ref[...] = grad_ref[...].astype(f32).T.astype(bf16)
    dkt_ref[...] = jnp.zeros_like(dkt_ref)
    dvt_ref[...] = jnp.zeros_like(dvt_ref)
    seg_col, seg_row = segc_ref[...], segr_ref[...]
    cosine, sine_val = cos_ref[...], -sin_ref[...]
    for start in range(0, rows_all, block):
        keys = start + block
        rows = slice(start, start + block)
        visible = visible_keys(seg_col, seg_row, start, block, keys)
        norms = lse_ref[0, rows, :]
        for t in range(3):
            cols = slice(t * LANES, (t + 1) * LANES)
            q_tile = q_ref[rows, cols]
            g_tile = grad_ref[rows, cols]
            q_turned = qt_ref[cols, rows]
            g_turned = gt_ref[cols, rows]
            dq = jnp.zeros((block, LANES), f32)
            for side in range(2):
                head = 2 * t + side
                kv = head // 3
                scores = contract_last(q_tile, k_views[side][kv][:keys])
                probs = jnp.where(visible, jnp.exp(scores - norms[:, head : head + 1]), 0.0)
                prob_grad = contract_last(g_tile, v_views[side][kv][:keys])
                centre = jnp.sum(probs * prob_grad, axis=-1, keepdims=True)
                score_grad = (probs * (prob_grad - centre)).astype(bf16)
                dq = dq + matmul(score_grad, k_views[side][kv][:keys])
                slot = 2 * side + kv
                dkt_ref[slot, :, :keys] += matmul(q_turned, score_grad)
                dvt_ref[slot, :, :keys] += matmul(g_turned, probs.astype(bf16))
            dq_ref[rows, cols] = turn(dq, cosine[rows], sine_val[rows], first[rows]).astype(bf16)

    def joined(ref):
        low_low, low_high, high_low, high_high = [ref[s].T for s in range(4)]
        is_low = lane < HD
        straight = jnp.where(is_low, low_low, high_high)
        crossed = pltpu.roll(jnp.where(is_low, low_high, high_low), HD, 1)
        return straight + crossed

    dk_ref[...] = turn(joined(dkt_ref) * score_scale, cosine, sine_val, first).astype(bf16)
    dv_ref[...] = joined(dvt_ref).astype(bf16)
    at = lambda start, wide: pl.ds(pl.multiple_of(start, LANES), wide)
    normed_turned = turned_ref[...]
    count = wgrad_ref.shape[1] // (5 * LANES)
    wgrad_ref[:, at(step * 3 * LANES, 3 * LANES)] = matmul(normed_turned, dq_ref[...]).astype(bf16)
    wgrad_ref[:, at((3 * count + step) * LANES, LANES)] = matmul(normed_turned, dk_ref[...]).astype(bf16)
    wgrad_ref[:, at((4 * count + step) * LANES, LANES)] = matmul(normed_turned, dv_ref[...]).astype(bf16)

    @pl.when(step == pl.num_programs(0) - 1)
    def _():
        copies = spread_copies(wgrad_ref, table_ref, dests, sems)
        for c in copies:
            c.start()
        for c in copies:
            c.wait()


def attend_backward(base, steps, table, turned, queries, keys, values, grads, norms, cosine, sine_val,
                    segment):
    width, rows = turned.shape
    members, layers = table.shape
    full = 5 * steps * LANES
    wide = pl.BlockSpec((rows, 3 * LANES), lambda i: (0, base + i))
    thin = pl.BlockSpec((rows, LANES), lambda i: (0, base + i))
    out_wide = pl.BlockSpec((rows, 3 * LANES), lambda i: (0, i))
    out_thin = pl.BlockSpec((rows, LANES), lambda i: (0, i))
    return pl.pallas_call(
        functools.partial(attend_back_kernel, 128, min(members, 2)),
        grid=(steps,),
        in_specs=[
            smem_spec(),
            whole_spec((width, rows)),
            wide,
            thin,
            thin,
            wide,
            pl.BlockSpec((1, rows, LANES), lambda i: (base + i, 0, 0)),
            whole_spec((rows, LANES)),
            whole_spec((rows, LANES)),
            whole_spec((rows, 1)),
            whole_spec((1, rows)),
        ],
        out_specs=[any_spec()] * min(members, 2) + [out_wide, out_thin, out_thin],
        out_shape=stack_shapes(table, width, full)
        + [jax.ShapeDtypeStruct((rows, k * LANES * steps), bf16) for k in (3, 1, 1)],
        scratch_shapes=[
            pltpu.VMEM((3 * LANES, rows), bf16),
            pltpu.VMEM((3 * LANES, rows), bf16),
            pltpu.VMEM((4, LANES, rows), f32),
            pltpu.VMEM((4, LANES, rows), f32),
            pltpu.VMEM((width, full), bf16),
            pltpu.SemaphoreType.DMA((members * layers,)),
        ],
        compiler_params=params(),
        cost_estimate=small_cost(),
    )(table, turned, queries, keys, values, grads, norms, cosine, sine_val, segment[:, None],
      segment[None, :])


def input_kernel(x_ref, mgrad_ref, w_ref, *refs):
    *grads, out_ref = refs
    x = x_ref[...].astype(f32)
    rinv = lax.rsqrt(jnp.mean(x * x, axis=-1, keepdims=True) + norm_eps)
    gain = w_ref[:, QW + 2 * KW :].astype(f32).T[GAIN_ONE : GAIN_ONE + 1, :]
    start = [0, QW, QW + KW]
    total = None
    for number, ref in enumerate(grads):
        wide = ref.shape[1]
        kind = number % 3
        product = contract_last(ref[...], w_ref[:, start[kind] : start[kind] + wide])
        start[kind] += wide
        total = product if total is None else total + product
    scaled = gain * total
    back = rinv * scaled - x * (rinv * rinv * rinv * jnp.mean(scaled * x, axis=-1, keepdims=True))
    out_ref[...] = mgrad_ref[...] + back


def to_input(hidden_in, middle_grad, w_qkv, grads):
    vmem = pl.BlockSpec(memory_space=pltpu.VMEM)
    return pl.pallas_call(
        input_kernel,
        in_specs=[vmem] * (3 + len(grads)),
        out_specs=vmem,
        out_shape=jax.ShapeDtypeStruct(hidden_in.shape, f32),
        compiler_params=params(),
        cost_estimate=small_cost(),
    )(hidden_in, middle_grad, w_qkv, *grads)


def experts_kernel(tiles, expert, packed, has_prev, has_sums, last, *refs):
    refs = list(refs)
    take = lambda count: [refs.pop(0) for _ in range(count)]
    (place_ref,) = take(1)
    x_src = [take(len(t)) for t in tiles]
    c_src = [take(len(t)) for t in tiles]
    weights = take(1 if packed else 3)
    prev_src = [take(2) for _ in tiles] if has_prev else None
    sums_src = take(3) if has_sums else None
    dest = [take(2) for _ in tiles]
    sums_dst = take(1 if packed and last else 3)
    xs, cs, og_out, og_grad = take(4)
    prevs = take(2) if has_prev else None
    acc = take(3)
    held = take(3) if packed else weights
    sem_in, sem_out, sem_sum, sem_w = take(4)
    i = pl.program_id(0)
    count = len(tiles)
    width = cs.shape[2]
    hidden = acc[0].shape[1]

    def weight_loads():
        own, low = held[0].shape[2], held[2].shape[2]
        src = weights[0]
        pairs = [(src.at[:, :, pl.ds(0, own)], held[0]), (src.at[:, :, pl.ds(own, own)], held[1])]
        for third in range(width // hidden):
            pairs.append(
                (
                    src.at[:, :, pl.ds(2 * own + third * low, low)],
                    held[2].at[:, :, :, pl.ds(third * hidden, hidden)],
                )
            )
        return [pltpu.make_async_copy(a, b, sem_w.at[q]) for q, (a, b) in enumerate(pairs)]

    def loads(t):
        out = []
        slot = t % 2
        number = 0
        for srcs, dst in ((x_src[t], xs), (c_src[t], cs)):
            row = 0
            for r in srcs:
                rows = r.shape[0]
                out.append(pltpu.make_async_copy(r, dst.at[slot, pl.ds(row, rows)], sem_in.at[slot, number]))
                row += rows
                number += 1
        if has_prev:
            for r, dst in zip(prev_src[t], prevs):
                out.append(pltpu.make_async_copy(r, dst.at[slot], sem_in.at[slot, number]))
                number += 1
        return out

    def stores(t):
        slot = t % 2
        return [
            pltpu.make_async_copy(og_out.at[slot], dest[t][0], sem_out.at[slot, 0]),
            pltpu.make_async_copy(og_grad.at[slot], dest[t][1], sem_out.at[slot, 1]),
        ]

    def sum_loads():
        return [pltpu.make_async_copy(s, a, sem_sum.at[q]) for q, (s, a) in enumerate(zip(sums_src, acc))]

    @pl.when(i == 0)
    def _():
        for c in loads(0):
            c.start()
        if packed:
            for c in weight_loads():
                c.start()
        if has_sums:
            for c in sum_loads():
                c.start()
        else:
            for a in acc:
                a[...] = jnp.zeros_like(a)
        if packed:
            for c in weight_loads():
                c.wait()

    for t in range(count):
        @pl.when(i == t)
        def _(t=t):
            for c in loads(t):
                c.wait()
            if t + 1 < count:
                for c in loads(t + 1):
                    c.start()
            if t >= 2:
                for c in stores(t - 2):
                    c.wait()

    slot = lax.rem(i, 2)
    rows_in = xs[slot, :, :width]
    extra = xs[slot, :, width:].astype(f32)
    lane = lax.broadcasted_iota(jnp.int32, extra.shape, 1)
    mine = place_ref[0] * PAIR_E + expert
    gate_row = jnp.sum(jnp.where((lane < 3 * E) & (lax.rem(lane, E) == mine), extra, 0.0), axis=-1, keepdims=True)
    cot_wide = cs[slot].astype(f32)
    w_gate = held[0][...].reshape(width, hidden)
    w_up = held[1][...].reshape(width, hidden)
    w_down = held[2][...].reshape(hidden, width)
    gate_proj = matmul(rows_in, w_gate)
    up_proj = matmul(rows_in, w_up)
    sigmoid_g = 1.0 / (1.0 + jnp.exp(-gate_proj))
    active = gate_proj * sigmoid_g
    mid = (active * up_proj).astype(bf16)
    out_grad = ((resid_scale * gate_row) * cot_wide).astype(bf16)
    mid_grad = contract_last(out_grad, w_down)
    gate_grad = (mid_grad * up_proj * sigmoid_g * (1.0 + gate_proj * (1.0 - sigmoid_g))).astype(bf16)
    up_grad = (mid_grad * active).astype(bf16)
    out_rows = matmul(mid, w_down)
    mix = resid_scale * jnp.sum(cot_wide * out_rows, axis=-1, keepdims=True)
    mixed = gate_row * out_rows
    if has_prev:
        mixed = mixed + prevs[0][slot].astype(f32)
    og_out[slot] = mixed.astype(bf16)
    back = contract_last(gate_grad, w_gate) + contract_last(up_grad, w_up)
    if has_prev:
        back = back + prevs[1][slot, :, :width].astype(f32)
    og_grad[slot, :, :width] = back.astype(bf16)
    high = mix.astype(bf16).astype(f32)
    middle = (mix - high).astype(bf16).astype(f32)
    low = mix - high - middle
    spread = jnp.where(lane == mine, high, jnp.where(lane == mine + E, middle, jnp.where(lane == mine + 2 * E, low, 0.0)))
    if has_prev:
        spread = spread + prevs[1][slot, :, width:].astype(f32)
    og_grad[slot, :, width:] = spread.astype(bf16)
    for t in range(count):
        @pl.when(i == t)
        def _(t=t):
            for c in stores(t):
                c.start()
    if has_sums:
        @pl.when(i == 0)
        def _():
            for c in sum_loads():
                c.wait()
    acc[0][...] += contract_rows(rows_in, gate_grad)
    acc[1][...] += contract_rows(rows_in, up_grad)
    acc[2][...] += contract_rows(mid, out_grad)

    @pl.when(i == count - 1)
    def _():
        if last and packed:
            out = sums_dst[0]
            layers, members, own, _ = held[0].shape
            low = held[2].shape[2]
            out[:, :, :own] = acc[0][...].astype(bf16).reshape(layers, members, own, hidden)
            out[:, :, own : 2 * own] = acc[1][...].astype(bf16).reshape(layers, members, own, hidden)
            for third in range(width // hidden):
                piece = acc[2][:, third * hidden : (third + 1) * hidden].astype(bf16)
                start = 2 * own + third * low
                out[:, :, start : start + low] = piece.reshape(layers, members, low, hidden)
        elif last:
            for a, d in zip(acc, sums_dst):
                d[...] = a[...].astype(bf16)
        else:
            copies = [pltpu.make_async_copy(a, d, sem_sum.at[q]) for q, (a, d) in enumerate(zip(acc, sums_dst))]
            for c in copies:
                c.start()
            for c in copies:
                c.wait()
        for t in range(max(0, count - 2), count):
            for c in stores(t):
                c.wait()


def experts_call(place, expert, xs, cs, weights, own, prev, sums, last):
    tiles = [x if isinstance(x, (list, tuple)) else [x] for x in xs]
    cots = [c if isinstance(c, (list, tuple)) else [c] for c in cs]
    rows = sum(a.shape[0] for a in tiles[0])
    full = tiles[0][0].shape[1]
    packed = len(weights) == 1
    width, hidden = cots[0][0].shape[1], weights[0].shape[-1] if packed else weights[0].shape[1]
    anyspace = pl.BlockSpec(memory_space=pl.ANY)
    resident = lambda a: pl.BlockSpec(a.shape, lambda i: (0, 0), pipeline_mode=pl.Buffered(1))
    args, specs = [jnp.asarray(place, jnp.int32).reshape(1)], [pl.BlockSpec(memory_space=pltpu.SMEM)]
    for group in tiles + cots:
        args += group
        specs += [anyspace] * len(group)
    args += list(weights)
    specs += [anyspace] if packed else [resident(w) for w in weights]
    if prev is not None:
        for pair in prev:
            args += list(pair)
            specs += [anyspace] * 2
    if sums is not None:
        args += list(sums)
        specs += [anyspace] * 3
    shapes, out_specs = [], []
    for _ in tiles:
        shapes += [jax.ShapeDtypeStruct((rows, width), bf16), jax.ShapeDtypeStruct((rows, full), bf16)]
        out_specs += [anyspace] * 2
    sum_shapes = ((width, hidden), (width, hidden), (hidden, width))
    if packed and last:
        shapes.append(jax.ShapeDtypeStruct(weights[0].shape, bf16))
        out_specs.append(whole_spec(weights[0].shape))
        sum_shapes = ()
    for shape in sum_shapes:
        shapes.append(jax.ShapeDtypeStruct(shape, bf16 if last else f32))
        out_specs.append(pl.BlockSpec(shape, lambda i: (0, 0), pipeline_mode=pl.Buffered(1)) if last else anyspace)
    scratch = [
        pltpu.VMEM((2, rows, full), bf16), pltpu.VMEM((2, rows, width), bf16),
        pltpu.VMEM((2, rows, width), bf16), pltpu.VMEM((2, rows, full), bf16),
    ]
    if prev is not None:
        scratch += [pltpu.VMEM((2, rows, width), bf16), pltpu.VMEM((2, rows, full), bf16)]
    scratch += [pltpu.VMEM((width, hidden), f32), pltpu.VMEM((width, hidden), f32), pltpu.VMEM((hidden, width), f32)]
    if packed:
        layers = weights[0].shape[0]
        low = hidden // (layers * GROUP)
        scratch += [
            pltpu.VMEM((layers, GROUP, own, hidden), bf16),
            pltpu.VMEM((layers, GROUP, own, hidden), bf16),
            pltpu.VMEM((layers, GROUP, low, width), bf16),
        ]
    scratch += [pltpu.SemaphoreType.DMA(shape) for shape in ((2, 6), (2, 2), (3,), (2 + width // hidden,))]
    out = pl.pallas_call(
        functools.partial(experts_kernel, [[0] * len(t) for t in tiles], expert, packed,
                          prev is not None, sums is not None, last),
        grid=(len(tiles),),
        in_specs=specs,
        out_specs=out_specs,
        out_shape=shapes,
        scratch_shapes=scratch,
        compiler_params=pltpu.CompilerParams(vmem_limit_bytes=60 * 1024 * 1024),
        cost_estimate=small_cost(),
    )(*args)
    parts = [(out[2 * t], out[2 * t + 1]) for t in range(len(tiles))]
    return parts, tuple(out[2 * len(tiles) :])


def shards(device_count, hidden_in, lengths, routes, norm_attn, w_query, w_key, w_value, w_out,
           norm_moe, w_router, w_gate, w_up, w_down, cotangent):
    n = device_count
    layers = n // GROUP
    along = [[q + GROUP * j for j in range(layers)] for q in range(GROUP)]
    inside = [[GROUP * j + q for q in range(GROUP)] for j in range(layers)]
    me = lax.axis_index("fsdp")
    place, layer = me % GROUP, me // GROUP
    rows, width = hidden_in.shape
    own_rows = w_query.shape[0]
    hidden = w_gate.shape[2]
    own_hidden = w_down.shape[1]
    split = own_rows % 16 == 0
    thirds = width // hidden
    members = jnp.arange(GROUP, dtype=jnp.int32) ^ place
    steps = jnp.arange(layers, dtype=jnp.int32)

    extras = jnp.concatenate(
        [w_router, norm_attn[:, None], norm_moe[:, None], jnp.zeros((own_rows, LANES - E - 2), bf16)],
        axis=1,
    )
    own_attn = jnp.concatenate([w_query, w_key, w_value, extras, w_out], axis=1)
    if split:
        column = lax.all_gather(own_attn, "fsdp", axis=0, tiled=True, axis_index_groups=along)
    else:
        column = lax.all_gather(own_attn, "fsdp", axis=0, tiled=True)

    down_rows = jnp.concatenate(
        [w_down[:, :, t * hidden : (t + 1) * hidden] for t in range(thirds)], axis=1
    )
    expert_rows = jnp.concatenate([w_gate, w_up, down_rows], axis=1)
    per_expert = expert_rows.shape[1]
    expert_rows = expert_rows.reshape(GROUP, PAIR_E, per_expert, hidden).transpose(1, 0, 2, 3)
    expert_rows = lax.all_to_all(expert_rows, "fsdp", 1, 1, tiled=True, axis_index_groups=inside)
    column, expert_rows = tie(column, expert_rows)
    column, out_column = column[:, :QKV_WIDE], column[:, QKV_WIDE:]
    gathered_first = lax.all_gather(expert_rows[0], "fsdp", axis=0, axis_index_groups=along)
    gathered_second = lax.all_gather(expert_rows[1], "fsdp", axis=0, axis_index_groups=along)

    aligned = own_rows % 16 == 0 and own_hidden % 16 == 0

    def expert_parts(gathered):
        if aligned:
            return (gathered,)
        gate = gathered[:, :, :own_rows].reshape(width, hidden)
        up = gathered[:, :, own_rows : 2 * own_rows].reshape(width, hidden)
        low = gathered[:, :, 2 * own_rows :].reshape(layers, GROUP, thirds, own_hidden, hidden)
        return gate, up, low.transpose(0, 1, 3, 2, 4).reshape(hidden, width)

    def flat(pieces):
        for k, group in enumerate(pieces):
            if layers % len(group):
                pieces[k] = [jnp.concatenate(group, axis=0)]
        runs = []
        for k, group in enumerate(pieces):
            per = layers // len(group)
            runs += [[(k, c * per + j) for j in range(per)] for c in range(len(group))]
        return runs, [a for group in pieces for a in group]

    if split:
        near = gather_start(column, n)
        plan, pieces = flat(gather_cores(column, near, gather_far(*near, n), n))
        table = own_rows * (GROUP * steps[None, :] + members[:, None])
    else:
        plan, pieces = [[(0, 0)]], [column]
        table = jnp.zeros((1, 1), jnp.int32)
    table = table.astype(jnp.int32)

    core = lambda value: swap(value, 1, n)
    pieces, out_column, cotangent = tie(pieces, out_column, cotangent)
    if split:
        near = gather_start(out_column, n)
    cots_near = gather_start(cotangent, n)
    segment, position = layout(lengths[0], rows)
    cosine, sine_val = turn_tables(position)
    half = HK // 4
    w_qkv, normed, turned, *first_half = attend_forward(
        0, half, table, plan, pieces, hidden_in, cosine, sine_val, segment
    )
    extras_full = w_qkv[:, QW + 2 * KW :]
    if split:
        near, normed = tie(near, normed)
        out_far = gather_far(*near, n)
        out_other = [core(v) for v in (out_column, *near)]
    second_half = attend_forward(half, half, table, None, w_qkv, normed, cosine, sine_val, segment)
    attn_out = (first_half[3], second_half[3])
    if split:
        attn_out, out_far, out_other, cots_near = tie(attn_out, out_far, out_other, cots_near)
        _, out_pieces = flat(
            [[out_column], [out_other[0]], [near[0]], [out_other[1]], [near[1]], [out_other[2]],
             list(out_far), [core(v) for v in out_far]]
        )
    else:
        out_pieces = [out_column]

    cots_core = [core(cotangent), core(cots_near[0]), core(cots_near[1])]
    w_out_full, middle, inner, mix = to_middle(
        table, plan, out_pieces, hidden_in, attn_out, extras_full, routes
    )
    cots_core = after(cots_core, inner)

    def expert_sums(sums):
        if len(sums) == 1:
            return lax.psum_scatter(
                sums[0], "fsdp", scatter_dimension=0, tiled=True, axis_index_groups=along
            )[0]
        gate, up, low = sums
        low = low.reshape(layers, GROUP, own_hidden, thirds, hidden).transpose(0, 1, 3, 2, 4)
        joined = jnp.concatenate(
            [
                gate.reshape(layers, GROUP, own_rows, hidden),
                up.reshape(layers, GROUP, own_rows, hidden),
                low.reshape(layers, GROUP, thirds * own_hidden, hidden),
            ],
            axis=2,
        )
        return lax.psum_scatter(
            joined, "fsdp", scatter_dimension=0, tiled=True, axis_index_groups=along
        )[0]

    first = expert_parts(gathered_first)
    second = expert_parts(gathered_second)
    part = {}

    def run(expert, tiles, xs, cs, weights, sums, last):
        done, sums = experts_call(
            place, expert, xs, cs, weights, own_rows, [part[k] for k in tiles] if expert else None, sums, last
        )
        part.update(zip(tiles, done))
        return sums

    inner_near = gather_start(inner, n)
    x_own, c_own = [[inner], [core(inner)]], [[cotangent], [cots_core[0]]]
    sums = run(0, [0, 1], x_own, c_own, first, None, False)
    inner_near = after(inner_near, sums)
    inner_far = gather_far(*inner_near, n)
    cots_far = gather_far(*tie(*cots_near, *inner_near)[:2], n)
    x_near = [[inner_near[0]], [core(inner_near[0])], [inner_near[1]], [core(inner_near[1])]]
    c_near = [[cots_near[0]], [cots_core[1]], [cots_near[1]], [cots_core[2]]]
    sums = run(0, [2, 3, 4, 5], x_near, c_near, first, sums, False)
    inner_far, cots_far = after((inner_far, cots_far), sums)
    x_far = [list(inner_far), [core(v) for v in inner_far]]
    c_far = [list(cots_far), [core(v) for v in cots_far]]
    sums0 = run(0, [6, 7], x_far, c_far, first, sums, True)
    shared0 = expert_sums(sums0)

    sums = run(1, [6, 7], x_far, c_far, second, None, False)
    chip6, out6 = [sum_cores([part[6][i], part[7][i]], n) for i in (1, 0)]
    x_near[0], chip6, out6 = tie(x_near[0], chip6, out6)
    far_sums, out_far = sum_far(chip6, n), sum_far(out6, n)
    sums = run(1, [2, 3, 4, 5], x_near, c_near, second, sums, False)
    done = [part[k] for k in (2, 3, 4, 5)]
    far_sums, out_far, sums, done = tie(far_sums, out_far, sums, done)
    part.update(zip((2, 3, 4, 5), done))
    chip2, chip4 = [sum_cores([part[k][1], part[k + 1][1]], n) for k in (2, 4)]
    x_own[0], chip2, chip4, shared0 = tie(x_own[0], chip2, chip4, shared0)
    inner_two, inner_four = sum_near(chip2, chip4, *far_sums, n)
    out_core = [core(part[3][0]), core(part[5][0])]
    sums = run(1, [0, 1], x_own, c_own, second, sums, True)
    inner_two, inner_four, out_core, sums, part[0], part[1] = tie(
        inner_two, inner_four, out_core, sums, part[0], part[1]
    )
    shared1 = expert_sums(sums)
    inner_chip = sum_cores([part[0][1], part[1][1]], n)
    out_chips = [add_low(part[k][0], other) for k, other in zip((2, 4), out_core)]
    out_chips, inner_chip = tie(out_chips, inner_chip)
    out_near = sum_near(*out_chips, *out_far, n)
    out_other = core(part[1][0])
    *out_grads, middle_grad, attn_grad0, attn_grad1 = middle_back(
        table, (inner_chip, inner_two, inner_four), inner, mix, middle, cotangent, extras_full, attn_out,
        w_out_full,
    )

    def chips_of(stacks):
        return add_low(stacks[0], core(stacks[1])) if split else stacks[0]

    def far_of(chips):
        rows_each = chips.shape[0] // 4
        return sum_far(chips[3 * rows_each :], n) if split else ()

    def near_of(chips, far):
        rows_each = chips.shape[0] // 4
        if not split:
            return ()
        return sum_near(chips[rows_each : 2 * rows_each], chips[2 * rows_each : 3 * rows_each], *far, n)

    def owned(chips, near):
        return add_up([chips[: chips.shape[0] // 4], *near]).astype(bf16)

    def over_layers(pairs):
        if not split:
            sums = [
                lax.psum_scatter(chips, "fsdp", scatter_dimension=0, tiled=True) for chips, _ in pairs
            ]
            return [jnp.concatenate(sums, axis=1)]
        total = jnp.concatenate([owned(*pair) for pair in pairs], axis=1)
        return layer_start(total.reshape(layers, own_rows, -1), layer, layers, n)

    def back(base, steps, half_set, grads):
        return attend_backward(
            base, steps, table, turned, *half_set[:3], grads, half_set[4], cosine, sine_val, segment
        )

    wo_chips = chips_of(out_grads)
    attn_grad0, wo_chips = tie(attn_grad0, wo_chips)
    wo_far = far_of(wo_chips)
    to_owner = lambda block: lax.all_to_all(
        block, "fsdp", 0, 0, tiled=True, axis_index_groups=inside
    )
    owned0 = to_owner(shared0)
    *stacks0, dq0, dk0, dv0 = back(0, half, first_half, attn_grad0)
    owned0, out_other, wo_far, stacks0, dq0 = tie(owned0, out_other, wo_far, stacks0, dq0)

    chips0 = chips_of(stacks0)
    attn_grad1, chips0, shared1 = tie(attn_grad1, chips0, shared1)
    wo_near, far0 = near_of(wo_chips, wo_far), far_of(chips0)
    *stacks1, dq1, dk1, dv1 = back(0, half // 2, second_half, attn_grad1)
    wo_near, far0, stacks1, dq1, out_near = tie(wo_near, far0, stacks1, dq1, out_near)

    chips1 = chips_of(stacks1)
    attn_grad1, chips1 = tie(attn_grad1, chips1)
    near0, far1 = near_of(chips0, far0), far_of(chips1)
    *stacks2, dq2, dk2, dv2 = back(half // 2, half - half // 2, second_half, attn_grad1)
    near0, far1, stacks2, dq2, wo_near = tie(near0, far1, stacks2, dq2, wo_near)

    chips2 = chips_of(stacks2)
    dq2, chips2 = tie(dq2, chips2)
    near1, far2 = near_of(chips1, far1), far_of(chips2)
    early = over_layers([(wo_chips, wo_near), (chips0, near0)])
    input_grad = to_input(
        hidden_in, middle_grad, w_qkv, (dq0, dk0, dv0, dq1, dk1, dv1, dq2, dk2, dv2)
    )
    near1, far2, early, input_grad = tie(near1, far2, early, input_grad)
    near2 = near_of(chips2, far2)
    owned1 = to_owner(after(shared1, near2))
    out_own = add_low(part[0][0], out_other)
    mixed = (middle + resid_scale * add_up([out_own, *out_near])).astype(bf16)
    early = layer_add(early)
    mine_out = early[:, : width + LANES]
    late = layer_add(over_layers([(chips1, near1), (chips2, near2)]))
    unit1, unit2 = chips1.shape[1], chips2.shape[1]
    mine = [early[:, width + LANES :], late[:, :unit1], late[:, unit1 : unit1 + unit2]]

    shared = jnp.stack([owned0, owned1], axis=1).reshape(E, per_expert, hidden).astype(f32)
    grad_gate, grad_up = shared[:, :own_rows], shared[:, own_rows : 2 * own_rows]
    grad_down = jnp.concatenate(
        [
            shared[:, 2 * own_rows + t * own_hidden : 2 * own_rows + (t + 1) * own_hidden]
            for t in range(thirds)
        ],
        axis=2,
    )
    def joined(kind):
        pieces = []
        for part_grads in mine:
            unit = part_grads.shape[1] // 5
            start, wide = ((0, 3 * unit), (3 * unit, unit), (4 * unit, unit))[kind]
            pieces.append(part_grads[:, start : start + wide])
        return jnp.concatenate(pieces, axis=1)

    grad_query, grad_key, grad_value = joined(0), joined(1), joined(2)
    grad_router = mine_out[:, width : width + E]

    def row_sums(weight, grad):
        return jnp.sum(weight.astype(f32) * grad, axis=-1)

    grad_norm_attn = (
        row_sums(w_query, grad_query) + row_sums(w_key, grad_key) + row_sums(w_value, grad_value)
    ) / norm_attn.astype(f32)
    grad_norm_moe = (
        jnp.sum(row_sums(w_gate, grad_gate) + row_sums(w_up, grad_up), axis=0)
        + row_sums(w_router, grad_router)
    ) / norm_moe.astype(f32)
    return (
        mixed,
        input_grad,
        grad_norm_attn,
        grad_query,
        grad_key,
        grad_value,
        mine_out[:, :width],
        grad_norm_moe,
        grad_router,
        grad_gate,
        grad_up,
        grad_down,
    )


def solution(mesh):

    in_specs = (
        P("fsdp", None),
        P("fsdp", None),
        P("fsdp", None),
        P("fsdp"),
        P("fsdp", None),
        P("fsdp", None),
        P("fsdp", None),
        P("fsdp", None),
        P("fsdp"),
        P("fsdp", None),
        P(None, "fsdp", None),
        P(None, "fsdp", None),
        P(None, "fsdp", None),
        P("fsdp", None),
    )
    out_specs = (
        P("fsdp", None),
        P("fsdp", None),
        P("fsdp"),
        P("fsdp", None),
        P("fsdp", None),
        P("fsdp", None),
        P("fsdp", None),
        P("fsdp"),
        P("fsdp", None),
        P(None, "fsdp", None),
        P(None, "fsdp", None),
        P(None, "fsdp", None),
    )
    return jax.shard_map(
        functools.partial(shards, mesh.shape["fsdp"]),
        mesh=mesh,
        in_specs=in_specs,
        out_specs=out_specs,
        check_vma=False,
    )
```

time: 895 us -> 688 us (0.77)
  waiting for transfers between devices: 318 us -> 151 us
  Pallas kernels: 164 us -> 308 us
  local copies, waits for them, and re-layouts: 153 us -> 44.5 us
  matrix products: 97.1 us -> 0 us
  starting transfers between devices: 49 us -> 70 us
  other arithmetic: 70.6 us -> 56.1 us
  blocking collectives: 20.6 us -> 34.4 us
    pallas_call x3 -> x14, Pallas kernels: 164 us -> 308 us  [the longest x6 168 us: experts_call(): pl.pallas_call(functools.partial(experts_kernel, [[0] * len(t) for t in t...]
    ppermute x54 -> x72, waiting for transfers between devices: 236 us -> 123 us  [swap(): lax.ppermute(value, 'fsdp', [(i, i ^ bit) for i in range(device_count)])]
    dot_general x18 -> x0, matrix products: 97.1 us -> none  [the longest x11 73.7 us: contract_rows(): lax.dot_general(left, right, (((0,), (0,)), ((), ())), preferred_element_...]
    unnamed x112 -> x121, local copies, waits for them, and re-layouts: 53.3 us -> 14.3 us
    all_gather x3, waiting for transfers between devices: 43.2 us -> 5.22 us  [the longest x1 5.2 us: shards(): lax.all_gather(own_attn, 'fsdp', axis=0, tiled=True, axis_index_groups=al...]
    concatenate x17 -> x2, local copies, waits for them, and re-layouts: 37 us -> 1.89 us  [the longest x1 1.87 us: shards(): own_attn = jnp.concatenate([w_query, w_key, w_value, extras, w_out], axis=1)]
    all_to_all x3 -> x2, waiting for transfers between devices: 39 us -> 9.39 us  [shards(): lax.all_to_all(block, 'fsdp', 0, 0, tiled=True, axis_index_groups=inside)]
    ppermute x54 -> x72, starting transfers between devices: 35.9 us -> 51.2 us  [swap(): lax.ppermute(value, 'fsdp', [(i, i ^ bit) for i in range(device_count)])]
  transfers between devices with their start and end apart: 65 -> 85, of which waited for: 24 -> 30; matrix products, arithmetic and copies ran while one was open for 34% -> 11% of each run, Pallas kernels for 8% -> 45%
where the time goes in v2:
time: 688 us; the launch traced here: 679 us
  Pallas kernels  308 us (45%)
  waiting for transfers between devices  151 us (22%)
  starting transfers between devices  70 us (10%)
  other arithmetic  56.1 us (8%)
  local copies, waits for them, and re-layouts  44.5 us (6%)
  blocking collectives  34.4 us (5%)
  between operations  15.1 us (2%)
    pallas_call x6, Pallas kernels, experts_call(): pl.pallas_call(functools.partial(experts_kernel, [[0] * len(t) for t in t...  168 us
    ppermute x72, waiting for transfers between devices, swap(): lax.ppermute(value, 'fsdp', [(i, i ^ bit) for i in range(device_count)])  123 us
    pallas_call x3, Pallas kernels, attend_backward(): pl.pallas_call(functools.partial(attend_back_kernel, 128, min(members, 2)...  54.8 us
    ppermute x72, starting transfers between devices, swap(): lax.ppermute(value, 'fsdp', [(i, i ^ bit) for i in range(device_count)])  51.2 us
    pallas_call x2, Pallas kernels, attend_forward(): pl.pallas_call(functools.partial(attend_kernel, 128, plan), grid=(steps,)...  41.6 us
    all_to_all x1, blocking collectives, shards(): lax.all_to_all(expert_rows, 'fsdp', 1, 1, tiled=True, axis_index_groups=i...  34.4 us
    convert_element_type x19, other arithmetic, add_low(): return (left.astype(f32) + right.astype(f32)).astype(bf16)  22.9 us
    pallas_call x1, Pallas kernels, middle_back(): pl.pallas_call(functools.partial(middle_back_kernel, min(members, 2)), in...  18.7 us
  transfers between devices with their start and end apart: 85, of which 30 were waited for; matrix products, arithmetic and copies ran while one was open for 11% of the time, Pallas kernels for 45%

profile of v2, /device:TPU:0, one launch (start us, length us, event | category | flops | bytes accessed | tf_op | source)
XLA Modules:
  0.0 679.3 jit_solution(17642018739361622784)
XLA Ops:
  12.7 34.4 %all_to_all.15 = bf16[2,8,144,512]{3,2,0,1:T(8,128)(2,1)S(1)} all-to-all(bf16[2,8,144,512]{3,2,0,1:T(8,128)(2,1)S(1)} %bitcast.48), channel_id=1, replica_groups={{0,1,2,3,4,5,6,7},{8,9,10,11,12,13,14,15},{16,17,18,19,20,21,22,23},{24..., dimensions={1} | all-to-all | bytes 4718592 | tf_op jit(solution)/shard_map/all_to_all | solution.py:874
  47.1 5.2 all-gather.4.cloned.1.call-done
  58.3 21.6 %collective-permute-done.3.refs_4_ = bf16[192,2688]{1,0:T(8,128)(2,1)} collective-permute-done((bf16[192,2688]{1,0:T(8,128)(2,1)S(1)}, bf16[192,2688]{1,0:T(8,128)(2,1)}, u32[]{:S(2)}, u32[]{:S(2)}) %collective-permute-start.3) | collective-permute-done | bytes 1032224 | tf_op jit(solution)/shard_map/ppermute | solution.py:72
  87.3 7.2 %collective-permute-done.6.refs_7_ = bf16[96,2688]{1,0:T(8,128)(2,1)S(1)} collective-permute-done((bf16[96,2688]{1,0:T(8,128)(2,1)}, bf16[96,2688]{1,0:T(8,128)(2,1)S(1)}, u32[]{:S(2)}, u32[]{:S(2)}) %collective-permute-start.6) | collective-permute-done | bytes 516128 | tf_op jit(solution)/shard_map/ppermute | solution.py:72
  94.5 3.2 collective-permute-done.5.refs_6_
  106.1 2.8 pad_maximum_fusion.12
  108.9 7.5 %collective-permute-done.10.refs_4_ = bf16[192,1536]{1,0:T(8,128)(2,1)} collective-permute-done((bf16[192,1536]{1,0:T(8,128)(2,1)}, bf16[192,1536]{1,0:T(8,128)(2,1)}, u32[]{:S(2)}, u32[]{:S(2)}) %collective-permute-start.10) | collective-permute-done | bytes 589856 | tf_op jit(solution)/shard_map/ppermute | solution.py:72
  117.9 23.2 %shard_map.229 = (bf16[1536,2688]{1,0:T(8,128)(2,1)}, bf16[512,1536]{1,0:T(8,128)(2,1)}, bf16[1536,512]{1,0:T(8,128)(2,1)}, bf16[512,768]{1,0:T(8,128)(2,1)}, bf...) custom-call(s32[8,4]{1,0:T(8,128)} %add_multiply_fusion.table_ref, ...), custom_call_target="tpu_custom_call" | custom-call | flops 1000000 | bytes 100000 | tf_op jit(solution)/shard_map/pallas_call | solution.py:339
  145.3 12.1 %collective-permute-done.12.refs_7_ = bf16[96,1536]{1,0:T(8,128)(2,1)S(1)} collective-permute-done((bf16[96,1536]{1,0:T(8,128)(2,1)S(1)}, bf16[96,1536]{1,0:T(8,128)(2,1)S(1)}, u32[]{:S(2)}, u32[]{:S(2)}) %collective-permute-start.12) | collective-permute-done | bytes 294944 | tf_op jit(solution)/shard_map/ppermute | solution.py:72
  157.9 18.4 %shard_map.230 = (bf16[512,768]{1,0:T(8,128)(2,1)}, bf16[512,256]{1,0:T(8,128)(2,1)}, bf16[512,256]{1,0:T(8,128)(2,1)}, bf16[512,768]{1,0:T(8,128)(2,1)}, f32[2,512,128]{2,1,0:T(8,128)}) custom-call(s32[8,4]{1,0:T(8,128)} %add_multiply_fusion.table_ref, bf16[512,1536]{1,0:T(8,128)(2,1)} %get-tuple-element.224.x_ref, f32[512,128]{1,0:T(8,128)} %get-tuple-element.535.cos_ref, ...), custom_call_target="tpu_custom_call" | custom-call | flops 1000000 | bytes 100000 | tf_op jit(solution)/shard_map/pallas_call | solution.py:339
  180.6 11.8 %shard_map.231 = (bf16[1536,1536]{1,0:T(8,128)(2,1)}, f32[512,1536]{1,0:T(8,128)}, bf16[512,1664]{1,0:T(8,128)(2,1)}, f32[512,128]{1,0:T(8,128)}) custom-call(s32[8,4]{1,0:T(8,128)} %add_multiply_fusion.table_ref, bf16[512,1536]{1,0:T(8,128)(2,1)} %x_ref.5, bf16[512,768]{1,0:T(8,128)(2,1)} %get-tuple-element.230.attn0_ref, ...), custom_call_target="tpu_custom_call" | custom-call | flops 1000000 | bytes 100000 | tf_op jit(solution)/shard_map/pallas_call | solution.py:393
  194.3 4.4 collective-permute-done.24.refs_6_
  198.7 2.2 collective-permute-done.25.refs_8_
  200.9 21.7 %shard_map.232 = (bf16[512,1536]{1,0:T(8,128)(2,1)}, bf16[512,1664]{1,0:T(8,128)(2,1)}, bf16[512,1536]{1,0:T(8,128)(2,1)}, bf16[512,1664]{1,0:T(8,128)(2,1)}, f3...) custom-call(s32[1]{0:T(128)} %bitcast.10.refs_0_, ...), custom_call_target="tpu_custom_call" | custom-call | flops 1000000 | bytes 100000 | tf_op jit(solution)/shard_map/pallas_call | solution.py:826
  222.6 9.7 %collective-permute-done.21.refs_3_ = bf16[512,1664]{1,0:T(8,128)(2,1)S(1)} collective-permute-done((bf16[512,1664]{1,0:T(8,128)(2,1)}, bf16[512,1664]{1,0:T(8,128)(2,1)S(1)}, u32[]{:S(2)}, u32[]{:S(2)}) %collective-permute-start.21) | collective-permute-done | bytes 1703968 | tf_op jit(solution)/shard_map/ppermute | solution.py:72
  233.2 2.1 slice.278
  238.5 2.1 slice.280
  244.2 38.1 %shard_map.233 = (bf16[512,1536]{1,0:T(8,128)(2,1)}, bf16[512,1664]{1,0:T(8,128)(2,1)}, bf16[512,1536]{1,0:T(8,128)(2,1)}, bf16[512,1664]{1,0:T(8,128)(2,1)}, bf...) custom-call(s32[1]{0:T(128)} %bitcast.10.refs_0_, ...), custom_call_target="tpu_custom_call" | custom-call | flops 1000000 | bytes 100000 | tf_op jit(solution)/shard_map/pallas_call | solution.py:826
  283.4 3.9 collective-permute-done.34.refs_7_
  290.5 22.3 %shard_map.234 = (bf16[512,1536]{1,0:T(8,128)(2,1)}, bf16[512,1664]{1,0:T(8,128)(2,1)}, bf16[512,1536]{1,0:T(8,128)(2,1)}, bf16[512,1664]{1,0:T(8,128)(2,1)}, bf16[4,8,144,512]{3,2,1,0:T(8,128)(2,1)}) custom-call(s32[1]{0:T(128)} %bitcast.10.refs_0_, bf16[256,1664]{1,0:T(8,128)(2,1)} %collective-permute-done.26.refs_1_, ...), custom_call_target="tpu_custom_call" | custom-call | flops 1000000 | bytes 100000 | tf_op jit(solution)/shard_map/pallas_call | solution.py:826
  312.9 23.1 %shard_map.235 = (bf16[512,1536]{1,0:T(8,128)(2,1)}, bf16[512,1664]{1,0:T(8,128)(2,1)}, bf16[512,1536]{1,0:T(8,128)(2,1)}, bf16[512,1664]{1,0:T(8,128)(2,1)}, f3...) custom-call(s32[1]{0:T(128)} %bitcast.10.refs_0_, bf16[256,1664]{1,0:T(8,128)(2,1)} %collective-permute-done.26.refs_1_, ...), custom_call_target="tpu_custom_call" | custom-call | flops 1000000 | bytes 100000 | tf_op jit(solution)/shard_map/pallas_call | solution.py:826
  336.6 3.1 collective-permute-done.37
  348.1 39.1 %shard_map.236 = (bf16[512,1536]{1,0:T(8,128)(2,1)}, bf16[512,1664]{1,0:T(8,128)(2,1)}, bf16[512,1536]{1,0:T(8,128)(2,1)}, bf16[512,1664]{1,0:T(8,128)(2,1)}, bf...) custom-call(s32[1]{0:T(128)} %bitcast.10.refs_0_, ...), custom_call_target="tpu_custom_call" | custom-call | flops 1000000 | bytes 100000 | tf_op jit(solution)/shard_map/pallas_call | solution.py:826
  388.4 2.7 collective-permute-done.42
  394.0 2.1 reduce-scatter.3.cloned.1.call-done
  402.5 23.7 %shard_map.237 = (bf16[512,1536]{1,0:T(8,128)(2,1)}, bf16[512,1664]{1,0:T(8,128)(2,1)}, bf16[512,1536]{1,0:T(8,128)(2,1)}, bf16[512,1664]{1,0:T(8,128)(2,1)}, bf16[4,8,144,512]{3,2,1,0:T(8,128)(2,1)}) custom-call(s32[1]{0:T(128)} %bitcast.10.refs_0_, bf16[512,1664]{1,0:T(8,128)(2,1)} %get-tuple-element.303.refs_1_.inner_ref, ...), custom_call_target="tpu_custom_call" | custom-call | flops 1000000 | bytes 100000 | tf_op jit(solution)/shard_map/pallas_call | solution.py:826
  426.2 11.7 %collective-permute-done.45.sum2_ref = bf16[512,1664]{1,0:T(8,128)(2,1)} collective-permute-done((bf16[512,1664]{1,0:T(8,128)(2,1)S(1)}, bf16[512,1664]{1,0:T(8,128)(2,1)}, u32[]{:S(2)}, u32[]{:S(2)}) %collective-permute-start.45) | collective-permute-done | bytes 1703968 | tf_op jit(solution)/shard_map/ppermute | solution.py:72
  442.6 2.4 add_convert_fusion.9
  446.7 18.7 %shard_map.238 = (bf16[768,1664]{1,0:T(8,128)(2,1)}, bf16[768,1664]{1,0:T(8,128)(2,1)}, f32[512,1536]{1,0:T(8,128)}, bf16[512,768]{1,0:T(8,128)(2,1)}, bf16[512,768]{1,0:T(8,128)(2,1)}) custom-call(s32[8,4]{1,0:T(8,128)} %add_multiply_fusion.table_ref, bf16[512,1664]{1,0:T(8,128)(2,1)} %add_convert_fusion.2.sum0_ref, ...), custom_call_target="tpu_custom_call" | custom-call | flops 1000000 | bytes 100000 | tf_op jit(solution)/shard_map/pallas_call | solution.py:454
  465.5 4.5 all-to-all-start.1
  471.7 2.4 add_convert_fusion
  478.7 2.2 add_convert_fusion.15
  480.9 25.6 %shard_map.239 = (bf16[768,1280]{1,0:T(8,128)(2,1)}, bf16[768,1280]{1,0:T(8,128)(2,1)}, bf16[512,768]{1,0:T(8,128)(2,1)}, bf16[512,256]{1,0:T(8,128)(2,1)}, bf16[512,256]{1,0:T(8,128)(2,1)}) custom-call(s32[8,4]{1,0:T(8,128)} %add_multiply_fusion.table_ref, bf16[1536,512]{1,0:T(8,128)(2,1)} %get-tuple-element.334.turned_ref, ...), custom_call_target="tpu_custom_call" | custom-call | flops 1000000 | bytes 100000 | tf_op jit(solution)/shard_map/pallas_call | solution.py:547
  506.7 2.5 pad_maximum_fusion.3
  520.7 4.3 reduce-scatter.5.cloned.1.call-done
  528.0 18.8 %collective-permute-done.59 = bf16[512,1536]{1,0:T(8,128)(2,1)} collective-permute-done((bf16[512,1536]{1,0:T(8,128)(2,1)}, bf16[512,1536]{1,0:T(8,128)(2,1)}, u32[]{:S(2)}, u32[]{:S(2)}) %collective-permute-start.59) | collective-permute-done | bytes 1572896 | tf_op jit(solution)/shard_map/ppermute | solution.py:72
  547.3 14.3 %shard_map.240 = (bf16[768,640]{1,0:T(8,128)(2,1)}, bf16[768,640]{1,0:T(8,128)(2,1)}, bf16[512,384]{1,0:T(8,128)(2,1)}, bf16[512,128]{1,0:T(8,128)(2,1)}, bf16[512,128]{1,0:T(8,128)(2,1)}) custom-call(s32[8,4]{1,0:T(8,128)} %add_multiply_fusion.table_ref, bf16[1536,512]{1,0:T(8,128)(2,1)} %get-tuple-element.334.turned_ref, ...), custom_call_target="tpu_custom_call" | custom-call | flops 1000000 | bytes 100000 | tf_op jit(solution)/shard_map/pallas_call | solution.py:547
  563.5 4.4 collective-permute-done.57
  576.0 14.8 %shard_map.241 = (bf16[768,640]{1,0:T(8,128)(2,1)}, bf16[768,640]{1,0:T(8,128)(2,1)}, bf16[512,384]{1,0:T(8,128)(2,1)}, bf16[512,128]{1,0:T(8,128)(2,1)}, bf16[512,128]{1,0:T(8,128)(2,1)}) custom-call(s32[8,4]{1,0:T(8,128)} %add_multiply_fusion.table_ref, bf16[1536,512]{1,0:T(8,128)(2,1)} %get-tuple-element.334.turned_ref, ...), custom_call_target="tpu_custom_call" | custom-call | flops 1000000 | bytes 100000 | tf_op jit(solution)/shard_map/pallas_call | solution.py:547
  598.1 3.0 collective-permute-start.72
  606.3 4.6 add_convert_fusion.6
  610.9 13.5 %shard_map.242 = f32[512,1536]{1,0:T(8,128)} custom-call(bf16[512,1536]{1,0:T(8,128)(2,1)} %x_ref.5, f32[512,1536]{1,0:T(8,128)} %get-tuple-element.386.mgrad_ref, bf16[1536,2688]{1,0:T(8,128)(2,1)} %get-tuple-element.225.refs_0_.refs_1_.refs_2_.w_ref, bf16[512,768]{1,0:T(8,128)(2,1)} %get-tuple-element.387.refs_0_, ...), custom_call_target="tpu_custom_call" | custom-call | flops 1000000 | bytes 100000 | tf_op jit(solution)/shard_map/pallas_call | solution.py:600
  624.3 2.5 collective-permute-done.71
  633.7 3.2 collective-permute-done.74
  640.4 2.7 collective-permute-start.77
  644.4 4.0 all-to-all-start.2
  648.5 4.4 collective-permute-done.76
  655.9 9.4 %all-to-all-done.2 = bf16[8,144,512]{2,1,0:T(8,128)(2,1)S(1)} async-done(((bf16[8,144,512]{2,1,0:T(8,128)(2,1)}), bf16[8,144,512]{2,1,0:T(8,128)(2,1)S(1)}, u32[]{:S(2)}, u32[]{:S(2)}) %all-to-all-start.2) | async-done | bytes 1179680 | tf_op jit(solution)/shard_map/all_to_all | solution.py:1047
  (364 shorter events, 142.5 us)
Async XLA Ops:
  7.2 45.1 %all-gather.4.cloned.1.call-start = ((), (), s32[]{:S(2)}) async-start(), calls=%async_computation.5 | async-start | bytes 2027520 | tf_op jit(solution)/shard_map/all_gather | solution.py:864
  11.6 189.4 %all-gather.6.cloned.1.call-start = ((), (), s32[]{:S(2)}) async-start(), calls=%async_computation.6 | async-start | bytes 5898240 | tf_op jit(solution)/shard_map/all_gather | solution.py:877
  53.9 259.0 %all-gather.8.cloned.1.call-start = ((), (), s32[]{:S(2)}) async-start(), calls=%async_computation.7 | async-start | bytes 5898240 | tf_op jit(solution)/shard_map/all_gather | solution.py:878
  55.3 24.6 %collective-permute-start.3 = (bf16[192,2688]{1,0:T(8,128)(2,1)S(1)}, bf16[192,2688]{1,0:T(8,128)(2,1)}, u32[]{:S(2)}, u32[]{:S(2)}) collective-permute-start(bf16[192,2688]{1,0:T(8,128)(2,1)S(1)} %slice.270.refs_0_), channel_id=1, source_target_pairs={{0,4},{1,5},{2,6},{3,7},{4,0},{5,1},{6,2},{7,3},{8,12},{9,13},{10,... | collective-permute-start | bytes 3096584 | tf_op jit(solution)/shard_map/ppermute | solution.py:72
  56.8 26.4 %collective-permute-start.1 = (bf16[192,2688]{1,0:T(8,128)(2,1)S(1)}, bf16[192,2688]{1,0:T(8,128)(2,1)}, u32[]{:S(2)}, u32[]{:S(2)}) collective-permute-start(bf16[192,2688]{1,0:T(8,128)(2,1)S(1)} %slice.270.refs_0_), channel_id=1, source_target_pairs={{0,2},{1,3},{2,0},{3,1},{4,6},{5,7},{6,4},{7,5},{8,10},{9,11},{10,... | collective-permute-start | bytes 3096584 | tf_op jit(solution)/shard_map/ppermute | solution.py:72
  99.8 296.3 %reduce-scatter.3.cloned.1.call-start = ((), (), s32[]{:S(2)}) async-start(), calls=%async_computation.8 | async-start | bytes 5898240 | tf_op jit(solution)/shard_map/reduce_scatter | solution.py:944
  99.9 16.5 %collective-permute-start.10 = (bf16[192,1536]{1,0:T(8,128)(2,1)}, bf16[192,1536]{1,0:T(8,128)(2,1)}, u32[]{:S(2)}, u32[]{:S(2)}) collective-permute-start(bf16[192,1536]{1,0:T(8,128)(2,1)} %slice.273.refs_0_), channel_id=1, source_target_pairs={{0,4},{1,5},{2,6},{3,7},{4,0},{5,1},{6,2},{7,3},{8,12},{9,13},{10,... | collective-permute-start | bytes 1769480 | tf_op jit(solution)/shard_map/ppermute | solution.py:72
  101.4 42.4 %collective-permute-start.13 = (bf16[192,1536]{1,0:T(8,128)(2,1)}, bf16[192,1536]{1,0:T(8,128)(2,1)}, u32[]{:S(2)}, u32[]{:S(2)}) collective-permute-start(bf16[192,1536]{1,0:T(8,128)(2,1)} %slice.273.refs_0_), channel_id=1, source_target_pairs={{0,1},{1,0},{2,3},{3,2},{4,5},{5,4},{6,7},{7,6},{8,9},{9,8},{10,11... | collective-permute-start | bytes 1769480 | tf_op jit(solution)/shard_map/ppermute | solution.py:72
  101.7 39.4 %collective-permute-start.9 = (bf16[192,1536]{1,0:T(8,128)(2,1)}, bf16[192,1536]{1,0:T(8,128)(2,1)}, u32[]{:S(2)}, u32[]{:S(2)}) collective-permute-start(bf16[192,1536]{1,0:T(8,128)(2,1)} %slice.273.refs_0_), channel_id=1, source_target_pairs={{0,2},{1,3},{2,0},{3,1},{4,6},{5,7},{6,4},{7,5},{8,10},{9,11},{10,... | collective-permute-start | bytes 1769480 | tf_op jit(solution)/shard_map/ppermute | solution.py:72
  102.4 74.0 %collective-permute-start.17 = (bf16[512,1536]{1,0:T(8,128)(2,1)S(1)}, bf16[512,1536]{1,0:T(8,128)(2,1)S(1)}, u32[]{:S(2)}, u32[]{:S(2)}) collective-permute-start(bf16[512,1536]{1,0:T(8,128)(2,1)S(1)} %copy-done), channel_id=1, source_target_pairs={{0,4},{1,5},{2,6},{3,7},{4,0},{5,1},{6,2},{7,3},{8,12},{9,13},{10,... | collective-permute-start | bytes 4718600 | tf_op jit(solution)/shard_map/ppermute | solution.py:72
  102.9 73.5 %collective-permute-start.16 = (bf16[512,1536]{1,0:T(8,128)(2,1)S(1)}, bf16[512,1536]{1,0:T(8,128)(2,1)}, u32[]{:S(2)}, u32[]{:S(2)}) collective-permute-start(bf16[512,1536]{1,0:T(8,128)(2,1)S(1)} %copy-done), channel_id=1, source_target_pairs={{0,2},{1,3},{2,0},{3,1},{4,6},{5,7},{6,4},{7,5},{8,10},{9,11},{10,... | collective-permute-start | bytes 4718600 | tf_op jit(solution)/shard_map/ppermute | solution.py:72
  116.4 77.4 %collective-permute-start.23 = (bf16[512,1536]{1,0:T(8,128)(2,1)S(1)}, bf16[512,1536]{1,0:T(8,128)(2,1)}, u32[]{:S(2)}, u32[]{:S(2)}) collective-permute-start(bf16[512,1536]{1,0:T(8,128)(2,1)S(1)} %copy-done), channel_id=1, source_target_pairs={{0,1},{1,0},{2,3},{3,2},{4,5},{5,4},{6,7},{7,6},{8,9},{9,8},{10,11... | collective-permute-start | bytes 4718600 | tf_op jit(solution)/shard_map/ppermute | solution.py:72
  157.4 19.0 %collective-permute-start.14 = (bf16[192,1536]{1,0:T(8,128)(2,1)}, bf16[192,1536]{1,0:T(8,128)(2,1)S(1)}, u32[]{:S(2)}, u32[]{:S(2)}) collective-permute-start(bf16[192,1536]{1,0:T(8,128)(2,1)} %collective-permute-done.9.refs_2_), channel_id=1, source_target_pairs={{0,1},{1,0},{2,3},{3,2},{4,5},{5,4},{6,7},{7,6},{8,9},{9,8},{10,11... | collective-permute-start | bytes 1769480 | tf_op jit(solution)/shard_map/ppermute | solution.py:72
  157.4 19.0 %collective-permute-start.15 = (bf16[192,1536]{1,0:T(8,128)(2,1)}, bf16[192,1536]{1,0:T(8,128)(2,1)S(1)}, u32[]{:S(2)}, u32[]{:S(2)}) collective-permute-start(bf16[192,1536]{1,0:T(8,128)(2,1)} %collective-permute-done.10.refs_4_), channel_id=1, source_target_pairs={{0,1},{1,0},{2,3},{3,2},{4,5},{5,4},{6,7},{7,6},{8,9},{9,8},{10,11... | collective-permute-start | bytes 1769480 | tf_op jit(solution)/shard_map/ppermute | solution.py:72
  192.6 39.8 %collective-permute-start.21 = (bf16[512,1664]{1,0:T(8,128)(2,1)}, bf16[512,1664]{1,0:T(8,128)(2,1)S(1)}, u32[]{:S(2)}, u32[]{:S(2)}) collective-permute-start(bf16[512,1664]{1,0:T(8,128)(2,1)} %get-tuple-element.303.refs_1_.inner_ref), channel_id=1, source_target_pairs={{0,4},{1,5},{2,6},{3,7},{4,0},{5,1},{6,2},{7,3},{8,12},{9,13},{10,... | collective-permute-start | bytes 5111816 | tf_op jit(solution)/shard_map/ppermute | solution.py:72
  193.1 39.6 %collective-permute-start.20 = (bf16[512,1664]{1,0:T(8,128)(2,1)}, bf16[512,1664]{1,0:T(8,128)(2,1)}, u32[]{:S(2)}, u32[]{:S(2)}) collective-permute-start(bf16[512,1664]{1,0:T(8,128)(2,1)} %get-tuple-element.303.refs_1_.inner_ref), channel_id=1, source_target_pairs={{0,2},{1,3},{2,0},{3,1},{4,6},{5,7},{6,4},{7,5},{8,10},{9,11},{10,... | collective-permute-start | bytes 5111816 | tf_op jit(solution)/shard_map/ppermute | solution.py:72
  236.4 45.9 %collective-permute-start.27 = (bf16[256,1664]{1,0:T(8,128)(2,1)}, bf16[256,1664]{1,0:T(8,128)(2,1)}, u32[]{:S(2)}, u32[]{:S(2)}) collective-permute-start(bf16[256,1664]{1,0:T(8,128)(2,1)} %slice.279), channel_id=1, source_target_pairs={{0,2},{1,3},{2,0},{3,1},{4,6},{5,7},{6,4},{7,5},{8,10},{9,11},{10,... | collective-permute-start | bytes 2555912 | tf_op jit(solution)/shard_map/ppermute | solution.py:72
  237.0 45.3 %collective-permute-start.26 = (bf16[256,1664]{1,0:T(8,128)(2,1)}, bf16[256,1664]{1,0:T(8,128)(2,1)}, u32[]{:S(2)}, u32[]{:S(2)}) collective-permute-start(bf16[256,1664]{1,0:T(8,128)(2,1)} %slice.278), channel_id=1, source_target_pairs={{0,4},{1,5},{2,6},{3,7},{4,0},{5,1},{6,2},{7,3},{8,12},{9,13},{10,... | collective-permute-start | bytes 2555912 | tf_op jit(solution)/shard_map/ppermute | solution.py:72
  241.6 40.7 %collective-permute-start.29 = (bf16[256,1536]{1,0:T(8,128)(2,1)}, bf16[256,1536]{1,0:T(8,128)(2,1)}, u32[]{:S(2)}, u32[]{:S(2)}) collective-permute-start(bf16[256,1536]{1,0:T(8,128)(2,1)} %slice.281), channel_id=1, source_target_pairs={{0,2},{1,3},{2,0},{3,1},{4,6},{5,7},{6,4},{7,5},{8,10},{9,11},{10,... | collective-permute-start | bytes 2359304 | tf_op jit(solution)/shard_map/ppermute | solution.py:72
  242.9 39.4 %collective-permute-start.28 = (bf16[256,1536]{1,0:T(8,128)(2,1)}, bf16[256,1536]{1,0:T(8,128)(2,1)}, u32[]{:S(2)}, u32[]{:S(2)}) collective-permute-start(bf16[256,1536]{1,0:T(8,128)(2,1)} %slice.280), channel_id=1, source_target_pairs={{0,4},{1,5},{2,6},{3,7},{4,0},{5,1},{6,2},{7,3},{8,12},{9,13},{10,... | collective-permute-start | bytes 2359304 | tf_op jit(solution)/shard_map/ppermute | solution.py:72
  312.8 212.2 %reduce-scatter.5.cloned.1.call-start = ((), (), s32[]{:S(2)}) async-start(), calls=%async_computation.9 | async-start | bytes 5898240 | tf_op jit(solution)/shard_map/reduce_scatter | solution.py:944
  342.7 44.5 %collective-permute-start.39 = (bf16[256,1664]{1,0:T(8,128)(2,1)S(1)}, bf16[256,1664]{1,0:T(8,128)(2,1)S(1)}, u32[]{:S(2)}, u32[]{:S(2)}) collective-permute-start(bf16[256,1664]{1,0:T(8,128)(2,1)S(1)} %get-tuple-element.499), channel_id=1, source_target_pairs={{0,2},{1,3},{2,0},{3,1},{4,6},{5,7},{6,4},{7,5},{8,10},{9,11},{10,... | collective-permute-start | bytes 2555912 | tf_op jit(solution)/shard_map/ppermute | solution.py:72
  342.9 44.4 %collective-permute-start.38 = (bf16[256,1664]{1,0:T(8,128)(2,1)S(1)}, bf16[256,1664]{1,0:T(8,128)(2,1)S(1)}, u32[]{:S(2)}, u32[]{:S(2)}) collective-permute-start(bf16[256,1664]{1,0:T(8,128)(2,1)S(1)} %get-tuple-element.500), channel_id=1, source_target_pairs={{0,4},{1,5},{2,6},{3,7},{4,0},{5,1},{6,2},{7,3},{8,12},{9,13},{10,... | collective-permute-start | bytes 2555912 | tf_op jit(solution)/shard_map/ppermute | solution.py:72
  344.9 42.3 %collective-permute-start.41 = (bf16[256,1536]{1,0:T(8,128)(2,1)}, bf16[256,1536]{1,0:T(8,128)(2,1)}, u32[]{:S(2)}, u32[]{:S(2)}) collective-permute-start(bf16[256,1536]{1,0:T(8,128)(2,1)} %get-tuple-element.501), channel_id=1, source_target_pairs={{0,2},{1,3},{2,0},{3,1},{4,6},{5,7},{6,4},{7,5},{8,10},{9,11},{10,... | collective-permute-start | bytes 2359304 | tf_op jit(solution)/shard_map/ppermute | solution.py:72
  346.2 41.0 %collective-permute-start.40 = (bf16[256,1536]{1,0:T(8,128)(2,1)}, bf16[256,1536]{1,0:T(8,128)(2,1)}, u32[]{:S(2)}, u32[]{:S(2)}) collective-permute-start(bf16[256,1536]{1,0:T(8,128)(2,1)} %get-tuple-element.502), channel_id=1, source_target_pairs={{0,4},{1,5},{2,6},{3,7},{4,0},{5,1},{6,2},{7,3},{8,12},{9,13},{10,... | collective-permute-start | bytes 2359304 | tf_op jit(solution)/shard_map/ppermute | solution.py:72
  398.8 39.2 %collective-permute-start.45 = (bf16[512,1664]{1,0:T(8,128)(2,1)S(1)}, bf16[512,1664]{1,0:T(8,128)(2,1)}, u32[]{:S(2)}, u32[]{:S(2)}) collective-permute-start(bf16[512,1664]{1,0:T(8,128)(2,1)S(1)} %pad_maximum_fusion.1), channel_id=1, source_target_pairs={{0,4},{1,5},{2,6},{3,7},{4,0},{5,1},{6,2},{7,3},{8,12},{9,13},{10,... | collective-permute-start | bytes 5111816 | tf_op jit(solution)/shard_map/ppermute | solution.py:72
  400.4 38.9 %collective-permute-start.44 = (bf16[512,1664]{1,0:T(8,128)(2,1)S(1)}, bf16[512,1664]{1,0:T(8,128)(2,1)}, u32[]{:S(2)}, u32[]{:S(2)}) collective-permute-start(bf16[512,1664]{1,0:T(8,128)(2,1)S(1)} %pad_maximum_fusion), channel_id=1, source_target_pairs={{0,2},{1,3},{2,0},{3,1},{4,6},{5,7},{6,4},{7,5},{8,10},{9,11},{10,... | collective-permute-start | bytes 5111816 | tf_op jit(solution)/shard_map/ppermute | solution.py:72
  402.0 24.2 %collective-permute-start.46 = (bf16[512,1536]{1,0:T(8,128)(2,1)}, bf16[512,1536]{1,0:T(8,128)(2,1)}, u32[]{:S(2)}, u32[]{:S(2)}) collective-permute-start(bf16[512,1536]{1,0:T(8,128)(2,1)} %get-tuple-element.301), channel_id=1, source_target_pairs={{0,1},{1,0},{2,3},{3,2},{4,5},{5,4},{6,7},{7,6},{8,9},{9,8},{10,11... | collective-permute-start | bytes 4718600 | tf_op jit(solution)/shard_map/ppermute | solution.py:72
  402.0 24.2 %collective-permute-start.47 = (bf16[512,1536]{1,0:T(8,128)(2,1)}, bf16[512,1536]{1,0:T(8,128)(2,1)}, u32[]{:S(2)}, u32[]{:S(2)}) collective-permute-start(bf16[512,1536]{1,0:T(8,128)(2,1)} %get-tuple-element.302), channel_id=1, source_target_pairs={{0,1},{1,0},{2,3},{3,2},{4,5},{5,4},{6,7},{7,6},{8,9},{9,8},{10,11... | collective-permute-start | bytes 4718600 | tf_op jit(solution)/shard_map/ppermute | solution.py:72
  465.5 41.1 %all-to-all-start.1 = ((bf16[8,144,512]{2,1,0:T(8,128)(2,1)}), bf16[8,144,512]{2,1,0:T(8,128)(2,1)}, u32[]{:S(2)}, u32[]{:S(2)}) async-start(bf16[8,144,512]{2,1,0:T(8,128)(2,1)} %bitcast.51), calls=%async_computation.2 | async-start | bytes 2359296 | tf_op jit(solution)/shard_map/all_to_all | solution.py:1047
  470.0 36.6 %collective-permute-start.48 = (bf16[512,1536]{1,0:T(8,128)(2,1)}, bf16[512,1536]{1,0:T(8,128)(2,1)}, u32[]{:S(2)}, u32[]{:S(2)}) collective-permute-start(bf16[512,1536]{1,0:T(8,128)(2,1)} %get-tuple-element.318), channel_id=1, source_target_pairs={{0,1},{1,0},{2,3},{3,2},{4,5},{5,4},{6,7},{7,6},{8,9},{9,8},{10,11... | collective-permute-start | bytes 4718600 | tf_op jit(solution)/shard_map/ppermute | solution.py:72
  475.2 31.3 %collective-permute-start.52 = (bf16[96,1664]{1,0:T(8,128)(2,1)}, bf16[96,1664]{1,0:T(8,128)(2,1)}, u32[]{:S(2)}, u32[]{:S(2)}) collective-permute-start(bf16[96,1664]{1,0:T(8,128)(2,1)} %get-tuple-element.487), channel_id=1, source_target_pairs={{0,2},{1,3},{2,0},{3,1},{4,6},{5,7},{6,4},{7,5},{8,10},{9,11},{10,... | collective-permute-start | bytes 958472 | tf_op jit(solution)/shard_map/ppermute | solution.py:72
  477.2 29.4 %collective-permute-start.51 = (bf16[96,1664]{1,0:T(8,128)(2,1)}, bf16[96,1664]{1,0:T(8,128)(2,1)}, u32[]{:S(2)}, u32[]{:S(2)}) collective-permute-start(bf16[96,1664]{1,0:T(8,128)(2,1)} %get-tuple-element.488), channel_id=1, source_target_pairs={{0,4},{1,5},{2,6},{3,7},{4,0},{5,1},{6,2},{7,3},{8,12},{9,13},{10,... | collective-permute-start | bytes 958472 | tf_op jit(solution)/shard_map/ppermute | solution.py:72
  509.2 37.6 %collective-permute-start.59 = (bf16[512,1536]{1,0:T(8,128)(2,1)}, bf16[512,1536]{1,0:T(8,128)(2,1)}, u32[]{:S(2)}, u32[]{:S(2)}) collective-permute-start(bf16[512,1536]{1,0:T(8,128)(2,1)} %pad_maximum_fusion.3), channel_id=1, source_target_pairs={{0,4},{1,5},{2,6},{3,7},{4,0},{5,1},{6,2},{7,3},{8,12},{9,13},{10,... | collective-permute-start | bytes 4718600 | tf_op jit(solution)/shard_map/ppermute | solution.py:72
  512.4 49.2 %collective-permute-start.58 = (bf16[512,1536]{1,0:T(8,128)(2,1)}, bf16[512,1536]{1,0:T(8,128)(2,1)}, u32[]{:S(2)}, u32[]{:S(2)}) collective-permute-start(bf16[512,1536]{1,0:T(8,128)(2,1)} %pad_maximum_fusion.2), channel_id=1, source_target_pairs={{0,2},{1,3},{2,0},{3,1},{4,6},{5,7},{6,4},{7,5},{8,10},{9,11},{10,... | collective-permute-start | bytes 4718600 | tf_op jit(solution)/shard_map/ppermute | solution.py:72
  514.8 48.7 %collective-permute-start.53 = (bf16[192,1664]{1,0:T(8,128)(2,1)}, bf16[192,1664]{1,0:T(8,128)(2,1)S(1)}, u32[]{:S(2)}, u32[]{:S(2)}) collective-permute-start(bf16[192,1664]{1,0:T(8,128)(2,1)} %pad_maximum_fusion.6), channel_id=1, source_target_pairs={{0,2},{1,3},{2,0},{3,1},{4,6},{5,7},{6,4},{7,5},{8,10},{9,11},{10,... | collective-permute-start | bytes 1916936 | tf_op jit(solution)/shard_map/ppermute | solution.py:72
  517.5 46.1 %collective-permute-start.54 = (bf16[192,1664]{1,0:T(8,128)(2,1)}, bf16[192,1664]{1,0:T(8,128)(2,1)}, u32[]{:S(2)}, u32[]{:S(2)}) collective-permute-start(bf16[192,1664]{1,0:T(8,128)(2,1)} %pad_maximum_fusion.7), channel_id=1, source_target_pairs={{0,4},{1,5},{2,6},{3,7},{4,0},{5,1},{6,2},{7,3},{8,12},{9,13},{10,... | collective-permute-start | bytes 1916936 | tf_op jit(solution)/shard_map/ppermute | solution.py:72
  526.4 41.5 %collective-permute-start.57 = (bf16[96,1280]{1,0:T(8,128)(2,1)S(1)}, bf16[96,1280]{1,0:T(8,128)(2,1)S(1)}, u32[]{:S(2)}, u32[]{:S(2)}) collective-permute-start(bf16[96,1280]{1,0:T(8,128)(2,1)S(1)} %get-tuple-element.495), channel_id=1, source_target_pairs={{0,2},{1,3},{2,0},{3,1},{4,6},{5,7},{6,4},{7,5},{8,10},{9,11},{10,... | collective-permute-start | bytes 737288 | tf_op jit(solution)/shard_map/ppermute | solution.py:72
  546.7 21.2 %collective-permute-start.56 = (bf16[96,1280]{1,0:T(8,128)(2,1)S(1)}, bf16[96,1280]{1,0:T(8,128)(2,1)S(1)}, u32[]{:S(2)}, u32[]{:S(2)}) collective-permute-start(bf16[96,1280]{1,0:T(8,128)(2,1)S(1)} %get-tuple-element.496), channel_id=1, source_target_pairs={{0,4},{1,5},{2,6},{3,7},{4,0},{5,1},{6,2},{7,3},{8,12},{9,13},{10,... | collective-permute-start | bytes 737288 | tf_op jit(solution)/shard_map/ppermute | solution.py:72
  570.0 20.8 %collective-permute-start.61 = (bf16[192,1280]{1,0:T(8,128)(2,1)}, bf16[192,1280]{1,0:T(8,128)(2,1)}, u32[]{:S(2)}, u32[]{:S(2)}) collective-permute-start(bf16[192,1280]{1,0:T(8,128)(2,1)} %pad_maximum_fusion.8), channel_id=1, source_target_pairs={{0,2},{1,3},{2,0},{3,1},{4,6},{5,7},{6,4},{7,5},{8,10},{9,11},{10,... | collective-permute-start | bytes 1474568 | tf_op jit(solution)/shard_map/ppermute | solution.py:72
  571.2 19.6 %collective-permute-start.62 = (bf16[192,1280]{1,0:T(8,128)(2,1)}, bf16[192,1280]{1,0:T(8,128)(2,1)}, u32[]{:S(2)}, u32[]{:S(2)}) collective-permute-start(bf16[192,1280]{1,0:T(8,128)(2,1)} %pad_maximum_fusion.9), channel_id=1, source_target_pairs={{0,4},{1,5},{2,6},{3,7},{4,0},{5,1},{6,2},{7,3},{8,12},{9,13},{10,... | collective-permute-start | bytes 1474568 | tf_op jit(solution)/shard_map/ppermute | solution.py:72
  573.9 16.9 %collective-permute-start.64 = (bf16[96,640]{1,0:T(8,128)(2,1)}, bf16[96,640]{1,0:T(8,128)(2,1)}, u32[]{:S(2)}, u32[]{:S(2)}) collective-permute-start(bf16[96,640]{1,0:T(8,128)(2,1)} %get-tuple-element.515), channel_id=1, source_target_pairs={{0,2},{1,3},{2,0},{3,1},{4,6},{5,7},{6,4},{7,5},{8,10},{9,11},{10,... | collective-permute-start | bytes 368648 | tf_op jit(solution)/shard_map/ppermute | solution.py:72
  598.1 26.2 %collective-permute-start.72 = (bf16[48,2944]{1,0:T(8,128)(2,1)}, bf16[48,2944]{1,0:T(8,128)(2,1)S(1)}, u32[]{:S(2)}, u32[]{:S(2)}) collective-permute-start(bf16[48,2944]{1,0:T(8,128)(2,1)} %get-tuple-element.503), channel_id=1, source_target_pairs={{0,24},{1,25},{2,26},{3,27},{4,28},{5,29},{6,30},{7,31},{8,0},{9,1... | collective-permute-start | bytes 847880 | tf_op jit(solution)/shard_map/ppermute | solution.py:77
  601.2 25.7 %collective-permute-start.71 = (bf16[48,2944]{1,0:T(8,128)(2,1)}, bf16[48,2944]{1,0:T(8,128)(2,1)}, u32[]{:S(2)}, u32[]{:S(2)}) collective-permute-start(bf16[48,2944]{1,0:T(8,128)(2,1)} %get-tuple-element.504), channel_id=1, source_target_pairs={{0,16},{1,17},{2,18},{3,19},{4,20},{5,21},{6,22},{7,23},{8,24},{9,... | collective-permute-start | bytes 847880 | tf_op jit(solution)/shard_map/ppermute | solution.py:77
  601.2 25.7 %collective-permute-start.70 = (bf16[48,2944]{1,0:T(8,128)(2,1)}, bf16[48,2944]{1,0:T(8,128)(2,1)}, u32[]{:S(2)}, u32[]{:S(2)}) collective-permute-start(bf16[48,2944]{1,0:T(8,128)(2,1)} %get-tuple-element.505), channel_id=1, source_target_pairs={{0,8},{1,9},{2,10},{3,11},{4,12},{5,13},{6,14},{7,15},{8,16},{9,17... | collective-permute-start | bytes 847880 | tf_op jit(solution)/shard_map/ppermute | solution.py:77
  603.5 23.4 %collective-permute-start.69 = (bf16[96,640]{1,0:T(8,128)(2,1)S(1)}, bf16[96,640]{1,0:T(8,128)(2,1)S(1)}, u32[]{:S(2)}, u32[]{:S(2)}) collective-permute-start(bf16[96,640]{1,0:T(8,128)(2,1)S(1)} %get-tuple-element.511), channel_id=1, source_target_pairs={{0,2},{1,3},{2,0},{3,1},{4,6},{5,7},{6,4},{7,5},{8,10},{9,11},{10,... | collective-permute-start | bytes 368648 | tf_op jit(solution)/shard_map/ppermute | solution.py:72
  605.7 21.2 %collective-permute-start.68 = (bf16[96,640]{1,0:T(8,128)(2,1)S(1)}, bf16[96,640]{1,0:T(8,128)(2,1)S(1)}, u32[]{:S(2)}, u32[]{:S(2)}) collective-permute-start(bf16[96,640]{1,0:T(8,128)(2,1)S(1)} %get-tuple-element.512), channel_id=1, source_target_pairs={{0,4},{1,5},{2,6},{3,7},{4,0},{5,1},{6,2},{7,3},{8,12},{9,13},{10,... | collective-permute-start | bytes 368648 | tf_op jit(solution)/shard_map/ppermute | solution.py:72
  644.4 20.8 %all-to-all-start.2 = ((bf16[8,144,512]{2,1,0:T(8,128)(2,1)}), bf16[8,144,512]{2,1,0:T(8,128)(2,1)S(1)}, u32[]{:S(2)}, u32[]{:S(2)}) async-start(bf16[8,144,512]{2,1,0:T(8,128)(2,1)} %bitcast.14), calls=%async_computation.4 | async-start | bytes 2359296 | tf_op jit(solution)/shard_map/all_to_all | solution.py:1047
  (98 other events, 782.8 us)
Sparse Core Ops, SparseCore 0:
  11.7 40.5 all-gather.3
  54.4 88.2 all-gather.5
  144.3 87.8 all-gather.7
  312.9 83.0 reduce-scatter.2
  439.5 85.5 reduce-scatter.4

commit v3 on v2

--- a/solution.py
+++ b/solution.py
@@ -14,6 +14,7 @@
 E = 16
 GROUP = 8
 PAIR_E = E // GROUP
+HEADS_STEP = 2 * HQ // HK
 LANES = 128
 QW = HQ * HD
 KW = HK * HD
@@ -85,6 +86,29 @@
     return lax.optimization_barrier(values)
 
 
+def ring_start(own, layers, device_count):
+    blocks = {0: own}
+    ahead, behind = own, own
+    for step in range(1, (layers - 1) // 2 + 1):
+        ahead, behind = shift(ahead, 1, device_count), shift(behind, -1, device_count)
+        blocks[step], blocks[layers - step] = ahead, behind
+    return blocks
+
+
+def ring_end(blocks, layers, device_count):
+    if layers % 2 == 0:
+        ahead, behind = blocks[layers // 2 - 1], blocks[(layers // 2 + 1) % layers]
+        half = ahead.shape[1] // 2 // LANES * LANES
+        blocks[layers // 2] = jnp.concatenate(
+            [shift(ahead[:, :half], 1, device_count), shift(behind[:, half:], -1, device_count)], axis=1
+        )
+    return blocks
+
+
+def joined_rows(blocks, places):
+    return jnp.concatenate([blocks[j] for j in places], axis=0)
+
+
 def gather_start(own, device_count):
     return swap(own, 2, device_count), swap(own, 4, device_count)
 
@@ -102,30 +126,6 @@
     ]
 
 
-def add_low(left, right):
-    return (left.astype(f32) + right.astype(f32)).astype(bf16)
-
-
-def sum_cores(parts, device_count):
-    return add_low(parts[0], swap(parts[1], 1, device_count))
-
-
-def sum_far(chip, device_count):
-    half = chip.shape[0] // 2
-    return swap(chip[:half], 4, device_count), swap(chip[half:], 2, device_count)
-
-
-def sum_near(chip2, chip4, low, high, device_count):
-    half = chip2.shape[0] // 2
-    sum2 = jnp.concatenate([add_low(chip2[:half], low), chip2[half:]], axis=0)
-    sum4 = jnp.concatenate([chip4[:half], add_low(chip4[half:], high)], axis=0)
-    return swap(sum2, 2, device_count), swap(sum4, 4, device_count)
-
-
-def add_up(parts):
-    return parts[0].astype(f32) + parts[1].astype(f32) + parts[2].astype(f32)
-
-
 def layer_start(stacked, layer, layers, device_count):
     pick = lambda at: lax.dynamic_index_in_dim(stacked, at % layers, 0, keepdims=False)
     return [pick(layer)] + [shift(pick(layer + k), k, device_count) for k in range(1, layers)]
@@ -145,12 +145,15 @@
 
 def half_views(pair, scale):
     lane = lax.broadcasted_iota(jnp.int32, pair.shape, 1)
-    wide = pair.astype(f32) * scale
-    other = pltpu.roll(wide, HD, 1)
+    scaled = pair.astype(f32) * scale
     low = lane < HD
+    return jnp.where(low, scaled, 0.0).astype(bf16), jnp.where(low, 0.0, scaled).astype(bf16)
+
+
+def head_tiles(tiles):
     return [
-        [jnp.where(low, wide, 0.0).astype(bf16), jnp.where(low, other, 0.0).astype(bf16)],
-        [jnp.where(low, 0.0, other).astype(bf16), jnp.where(low, 0.0, wide).astype(bf16)],
+        tiles[head // 2] if head % 2 == head // 3 else pltpu.roll(tiles[head // 2], HD, 1)
+        for head in range(HEADS_STEP)
     ]
 
 
@@ -219,6 +222,119 @@
     return [jax.ShapeDtypeStruct((width // stacks, full), bf16)] * stacks
 
 
+def far_kernel(*refs):
+    count = len(refs) // 4
+    for q in range(count):
+        left, right = refs[2 * q : 2 * q + 2]
+        low, high = refs[2 * count + 2 * q : 2 * count + 2 * q + 2]
+        total = (left[...].astype(f32) + right[...].astype(f32)).astype(bf16)
+        low[...] = total[0]
+        high[...] = total[1]
+
+
+def sums_for_far(pairs):
+    rows = pairs[0][0].shape[0]
+    tile = rows // 8
+    args, in_specs, out_specs, shapes = [], [], [], []
+    for pair in pairs:
+        width = pair[0].shape[1]
+        args += [value.reshape(2, rows // 2, width) for value in pair]
+        in_specs += [pl.BlockSpec((2, tile, width), lambda i: (0, i, 0))] * 2
+        out_specs += [pl.BlockSpec((tile, width), lambda i: (i, 0))] * 2
+        shapes += [jax.ShapeDtypeStruct((rows // 2, width), bf16)] * 2
+    out = pl.pallas_call(
+        far_kernel, grid=(4,), in_specs=in_specs, out_specs=out_specs, out_shape=shapes,
+        compiler_params=params(), cost_estimate=small_cost(),
+    )(*args)
+    return [out[2 * q : 2 * q + 2] for q in range(len(pairs))]
+
+
+def near_kernel(a2_ref, b2_ref, a4_ref, b4_ref, low_ref, high_ref, sum2_ref, sum4_ref):
+    two = a2_ref[...].astype(f32) + b2_ref[...].astype(f32)
+    four = a4_ref[...].astype(f32) + b4_ref[...].astype(f32)
+    sum2_ref[0] = (two[0] + low_ref[...].astype(f32)).astype(bf16)
+    sum2_ref[1] = two[1].astype(bf16)
+    sum4_ref[0] = four[0].astype(bf16)
+    sum4_ref[1] = (four[1] + high_ref[...].astype(f32)).astype(bf16)
+
+
+def sums_for_near(a2, b2, a4, b4, low, high):
+    rows, width = a2.shape
+    tile = rows // 8
+    pair = pl.BlockSpec((2, tile, width), lambda i: (0, i, 0))
+    single = pl.BlockSpec((tile, width), lambda i: (i, 0))
+    out = pl.pallas_call(
+        near_kernel, grid=(4,), in_specs=[pair] * 4 + [single] * 2, out_specs=[pair] * 2,
+        out_shape=[jax.ShapeDtypeStruct((2, rows // 2, width), bf16)] * 2,
+        compiler_params=params(), cost_estimate=small_cost(),
+    )(*[value.reshape(2, rows // 2, width) for value in (a2, b2, a4, b4)], low, high)
+    return [value.reshape(rows, width) for value in out]
+
+
+def half_kernel(more_for, a2_ref, b2_ref, a4_ref, b4_ref, more_ref, sum2_ref, sum4_ref):
+    two = a2_ref[...].astype(f32) + b2_ref[...].astype(f32)
+    four = a4_ref[...].astype(f32) + b4_ref[...].astype(f32)
+    more = more_ref[...].astype(f32)
+    sum2_ref[...] = (two + more if more_for == 2 else two).astype(bf16)
+    sum4_ref[...] = (four + more if more_for == 4 else four).astype(bf16)
+
+
+def half_for_near(which, a2, b2, a4, b4, more):
+    rows, width = a2.shape
+    tile = rows // 8
+    picked = pl.BlockSpec((tile, width), lambda i: (4 * which + i, 0))
+    single = pl.BlockSpec((tile, width), lambda i: (i, 0))
+    return pl.pallas_call(
+        functools.partial(half_kernel, (2, 4)[which]), grid=(4,), in_specs=[picked] * 4 + [single],
+        out_specs=[single] * 2, out_shape=[jax.ShapeDtypeStruct((rows // 2, width), bf16)] * 2,
+        compiler_params=params(), cost_estimate=small_cost(),
+    )(a2, b2, a4, b4, more)
+
+
+def stack_kernel(even_ref, odd_ref, own_ref, two_ref, four_ref, low_ref, high_ref):
+    rows = own_ref.shape[0]
+    half = rows // 2
+    spots = ((own_ref, 0, rows), (two_ref, rows, rows), (four_ref, 2 * rows, rows), (low_ref, 3 * rows, half),
+             (high_ref, 3 * rows + half, half))
+    for ref, start, count in spots:
+        at = slice(start, start + count)
+        ref[...] = (even_ref[at].astype(f32) + odd_ref[at].astype(f32)).astype(bf16)
+
+
+def sums_of_stack(even, odd):
+    rows, width = even.shape[0] // 4, even.shape[1]
+    vmem = pl.BlockSpec(memory_space=pltpu.VMEM)
+    return pl.pallas_call(
+        stack_kernel, in_specs=[vmem] * 2, out_specs=[vmem] * 5,
+        out_shape=[jax.ShapeDtypeStruct((r, width), bf16) for r in (rows, rows, rows, rows // 2, rows // 2)],
+        compiler_params=params(), cost_estimate=small_cost(),
+    )(even, odd)
+
+
+def stack_near_kernel(*refs):
+    *sources, sum2_ref, sum4_ref = refs
+    start = 0
+    for q in range(0, len(sources), 4):
+        two_ref, four_ref, low_ref, high_ref = sources[q : q + 4]
+        half = low_ref.shape[0]
+        at = slice(start, start + two_ref.shape[1])
+        sum2_ref[:half, at] = (two_ref[:half].astype(f32) + low_ref[...].astype(f32)).astype(bf16)
+        sum2_ref[half:, at] = two_ref[half:]
+        sum4_ref[:half, at] = four_ref[:half]
+        sum4_ref[half:, at] = (four_ref[half:].astype(f32) + high_ref[...].astype(f32)).astype(bf16)
+        start += two_ref.shape[1]
+
+
+def stack_near(sets):
+    vmem = pl.BlockSpec(memory_space=pltpu.VMEM)
+    shape = (sets[0][0].shape[0], sum(one[0].shape[1] for one in sets))
+    return pl.pallas_call(
+        stack_near_kernel, in_specs=[vmem] * (4 * len(sets)), out_specs=[vmem] * 2,
+        out_shape=[jax.ShapeDtypeStruct(shape, bf16)] * 2,
+        compiler_params=params(), cost_estimate=small_cost(),
+    )(*[value for one in sets for value in one])
+
+
 def attend_kernel(block, plan, table_ref, x_ref, cos_ref, sin_ref, segc_ref, segr_ref, *refs):
     pair = pl.program_id(0)
     rows_all, width = x_ref.shape
@@ -256,9 +372,12 @@
     first = (lane % HD) < (HD // 2)
     cosine, sine_val = cos_ref[...], sin_ref[...]
     q_pre = matmul(normed, w_q)
+    tiles = []
     for t in range(3):
         cols = slice(t * LANES, (t + 1) * LANES)
-        q_ref[:, cols] = turn(q_pre[:, cols], cosine, sine_val, first).astype(bf16)
+        tiles.append(turn(q_pre[:, cols], cosine, sine_val, first))
+        q_ref[:, cols] = tiles[t].astype(bf16)
+    heads = [tile.astype(bf16) for tile in head_tiles(tiles)]
     k_low = turn(matmul(normed, w_k), cosine, sine_val, first).astype(bf16)
     v_low = matmul(normed, w_v).astype(bf16)
     k_ref[...] = k_low
@@ -266,28 +385,32 @@
     k_views = half_views(k_low, score_scale)
     v_views = half_views(v_low, 1.0)
     seg_col, seg_row = segc_ref[...], segr_ref[...]
+    lane_b = lax.broadcasted_iota(jnp.int32, (block, LANES), 1)
     for start in range(0, rows_all, block):
         keys = start + block
+        rows = slice(start, keys)
         visible = visible_keys(seg_col, seg_row, start, block, keys)
-        lane_b = lax.broadcasted_iota(jnp.int32, (block, LANES), 1)
         norms = jnp.zeros((block, LANES), f32)
+        outs = []
+        for kv in range(2):
+            q_rows = jnp.concatenate([heads[3 * kv + j][rows] for j in range(3)], axis=0)
+            scores = contract_last(q_rows, k_views[kv][:keys]).reshape(3, block, keys)
+            scores = jnp.where(visible[None], scores, masked_score)
+            peak = jnp.max(scores, axis=-1, keepdims=True)
+            expo = jnp.exp(scores - peak)
+            mass = jnp.sum(expo, axis=-1, keepdims=True)
+            probs = (expo * (1.0 / mass)).astype(bf16)
+            total = matmul(probs.reshape(3 * block, keys), v_views[kv][:keys])
+            norm = peak + jnp.log(mass)
+            for j in range(3):
+                outs.append(total[j * block : (j + 1) * block])
+                norms = jnp.where(lane_b == 3 * kv + j, norm[j], norms)
         for t in range(3):
-            cols = slice(t * LANES, (t + 1) * LANES)
-            q_tile = q_ref[start : start + block, cols]
-            total = jnp.zeros((block, LANES), f32)
-            for side in range(2):
-                head = 2 * t + side
-                kv = head // 3
-                scores = contract_last(q_tile, k_views[side][kv][:keys])
-                scores = jnp.where(visible, scores, masked_score)
-                peak = jnp.max(scores, axis=-1, keepdims=True)
-                expo = jnp.exp(scores - peak)
-                mass = jnp.sum(expo, axis=-1, keepdims=True)
-                probs = (expo * (1.0 / mass)).astype(bf16)
-                total = total + matmul(probs, v_views[side][kv][:keys])
-                norms = jnp.where(lane_b == head, peak + jnp.log(mass), norms)
-            out_ref[start : start + block, cols] = total.astype(bf16)
-        lse_ref[0, start : start + block, :] = norms
+            low, high = outs[2 * t], outs[2 * t + 1]
+            low = pltpu.roll(low, HD, 1) if t == 2 else low
+            high = pltpu.roll(high, HD, 1) if t == 0 else high
+            out_ref[rows, t * LANES : (t + 1) * LANES] = (low + high).astype(bf16)
+        lse_ref[0, rows, :] = norms
 
     if plan is not None:
         @pl.when(pair == pl.num_programs(0) - 1)
@@ -410,18 +533,19 @@
     )(table, hidden_in, *attn_out, extras, routes, *pieces)
 
 
-def middle_back_kernel(blocks, table_ref, sum0_ref, sum1_ref, sum2_ref, inner_ref, mix_ref, middle_ref,
+def middle_back_kernel(blocks, table_ref, own0_ref, own1_ref, near2_ref, near4_ref, inner_ref, mix_ref, middle_ref,
                        cot_ref, extras_ref, attn0_ref, attn1_ref, w_ref, *refs):
     dests = refs[:blocks]
     grad_ref, attn_grad0_ref, attn_grad1_ref, wgrad_ref, sems = refs[blocks:]
     rows, width = middle_ref.shape
-    total = sum0_ref[...].astype(f32) + sum1_ref[...].astype(f32) + sum2_ref[...].astype(f32)
+    total = own0_ref[...].astype(f32) + own1_ref[...].astype(f32)
+    total = total + near2_ref[...].astype(f32) + near4_ref[...].astype(f32)
     inner_grad, tail = total[:, :width], total[:, width:]
     lane = lax.broadcasted_iota(jnp.int32, tail.shape, 1)
     mix = mix_ref[...]
     mix_grad = tail + pltpu.roll(tail, LANES - E, 1) + pltpu.roll(tail, LANES - 2 * E, 1)
     mix_grad = jnp.where(lane < E, mix_grad, 0.0)
-    logit_grad = mix * (mix_grad - jnp.sum(mix * mix_grad, axis=-1, keepdims=True))
+    logit_grad = mix_grad - mix * jnp.sum(mix_grad, axis=-1, keepdims=True)
     logit_grad = logit_grad.astype(bf16)
     extras = extras_ref[...]
     gain = extras.astype(f32).T[GAIN_TWO : GAIN_TWO + 1, :]
@@ -453,7 +577,7 @@
     full = width + LANES
     return pl.pallas_call(
         functools.partial(middle_back_kernel, min(members, 2)),
-        in_specs=[smem_spec()] + [vmem] * 11,
+        in_specs=[smem_spec()] + [vmem] * 12,
         out_specs=[any_spec()] * min(members, 2) + [vmem] * 3,
         out_shape=stack_shapes(table, width, full)
         + [jax.ShapeDtypeStruct((rows, width), f32)]
@@ -470,52 +594,65 @@
 def attend_back_kernel(block, blocks, table_ref, turned_ref, q_ref, k_ref, v_ref, grad_ref, lse_ref,
                        cos_ref, sin_ref, segc_ref, segr_ref, *refs):
     dests = refs[:blocks]
-    dq_ref, dk_ref, dv_ref, qt_ref, gt_ref, dkt_ref, dvt_ref, wgrad_ref, sems = refs[blocks:]
+    dq_ref, dk_ref, dv_ref, dkt_ref, dvt_ref, wgrad_ref, sems = refs[blocks:]
     step = pl.program_id(0)
     width, rows_all = turned_ref.shape
     lane = lax.broadcasted_iota(jnp.int32, (rows_all, LANES), 1)
     first = (lane % HD) < (HD // 2)
     k_views = half_views(k_ref[...], score_scale)
     v_views = half_views(v_ref[...], 1.0)
-
-    qt_ref[...] = q_ref[...].astype(f32).T.astype(bf16)
-    gt_ref[...] = grad_ref[...].astype(f32).T.astype(bf16)
+    tile_cols = [slice(t * LANES, (t + 1) * LANES) for t in range(3)]
+    q_tiles = [q_ref[:, cols].astype(f32) for cols in tile_cols]
+    g_tiles = [grad_ref[:, cols].astype(f32) for cols in tile_cols]
+    q_heads = [tile.astype(bf16) for tile in head_tiles(q_tiles)]
+    g_heads = [tile.astype(bf16) for tile in head_tiles(g_tiles)]
+
+    def turned_heads(tiles):
+        out = []
+        for head in range(HEADS_STEP):
+            tile = tiles[head // 2].T
+            if head % 2 != head // 3:
+                tile = jnp.concatenate([tile[HD:], tile[:HD]], axis=0)
+            out.append(tile.astype(bf16))
+        return out
+
+    q_turned, g_turned = turned_heads(q_tiles), turned_heads(g_tiles)
     dkt_ref[...] = jnp.zeros_like(dkt_ref)
     dvt_ref[...] = jnp.zeros_like(dvt_ref)
     seg_col, seg_row = segc_ref[...], segr_ref[...]
     cosine, sine_val = cos_ref[...], -sin_ref[...]
     for start in range(0, rows_all, block):
         keys = start + block
-        rows = slice(start, start + block)
+        rows = slice(start, keys)
         visible = visible_keys(seg_col, seg_row, start, block, keys)
         norms = lse_ref[0, rows, :]
+        parts = []
+        for kv in range(2):
+            three = [3 * kv + j for j in range(3)]
+            q_rows = jnp.concatenate([q_heads[h][rows] for h in three], axis=0)
+            g_rows = jnp.concatenate([g_heads[h][rows] for h in three], axis=0)
+            norm = jnp.concatenate([norms[:, h : h + 1] for h in three], axis=0).reshape(3, block, 1)
+            scores = contract_last(q_rows, k_views[kv][:keys]).reshape(3, block, keys)
+            probs = jnp.where(visible[None], jnp.exp(scores - norm), 0.0)
+            prob_grad = contract_last(g_rows, v_views[kv][:keys]).reshape(3, block, keys)
+            centre = jnp.sum(probs * prob_grad, axis=-1, keepdims=True)
+            score_grad = (probs * (prob_grad - centre)).astype(bf16).reshape(3 * block, keys)
+            probs = probs.astype(bf16).reshape(3 * block, keys)
+            dq = matmul(score_grad, k_views[kv][:keys])
+            parts += [dq[j * block : (j + 1) * block] for j in range(3)]
+            q_across = jnp.concatenate([q_turned[h][:, rows] for h in three], axis=1)
+            g_across = jnp.concatenate([g_turned[h][:, rows] for h in three], axis=1)
+            dkt_ref[kv, :, :keys] += matmul(q_across, score_grad)
+            dvt_ref[kv, :, :keys] += matmul(g_across, probs)
         for t in range(3):
-            cols = slice(t * LANES, (t + 1) * LANES)
-            q_tile = q_ref[rows, cols]
-            g_tile = grad_ref[rows, cols]
-            q_turned = qt_ref[cols, rows]
-            g_turned = gt_ref[cols, rows]
-            dq = jnp.zeros((block, LANES), f32)
-            for side in range(2):
-                head = 2 * t + side
-                kv = head // 3
-                scores = contract_last(q_tile, k_views[side][kv][:keys])
-                probs = jnp.where(visible, jnp.exp(scores - norms[:, head : head + 1]), 0.0)
-                prob_grad = contract_last(g_tile, v_views[side][kv][:keys])
-                centre = jnp.sum(probs * prob_grad, axis=-1, keepdims=True)
-                score_grad = (probs * (prob_grad - centre)).astype(bf16)
-                dq = dq + matmul(score_grad, k_views[side][kv][:keys])
-                slot = 2 * side + kv
-                dkt_ref[slot, :, :keys] += matmul(q_turned, score_grad)
-                dvt_ref[slot, :, :keys] += matmul(g_turned, probs.astype(bf16))
-            dq_ref[rows, cols] = turn(dq, cosine[rows], sine_val[rows], first[rows]).astype(bf16)
+            low, high = parts[2 * t], parts[2 * t + 1]
+            low = pltpu.roll(low, HD, 1) if t == 2 else low
+            high = pltpu.roll(high, HD, 1) if t == 0 else high
+            turned_back = turn(low + high, cosine[rows], sine_val[rows], first[rows])
+            dq_ref[rows, tile_cols[t]] = turned_back.astype(bf16)
 
     def joined(ref):
-        low_low, low_high, high_low, high_high = [ref[s].T for s in range(4)]
-        is_low = lane < HD
-        straight = jnp.where(is_low, low_low, high_high)
-        crossed = pltpu.roll(jnp.where(is_low, low_high, high_low), HD, 1)
-        return straight + crossed
+        return jnp.where(lane < HD, ref[0].T, ref[1].T)
 
     dk_ref[...] = turn(joined(dkt_ref) * score_scale, cosine, sine_val, first).astype(bf16)
     dv_ref[...] = joined(dvt_ref).astype(bf16)
@@ -564,10 +701,8 @@
         out_shape=stack_shapes(table, width, full)
         + [jax.ShapeDtypeStruct((rows, k * LANES * steps), bf16) for k in (3, 1, 1)],
         scratch_shapes=[
-            pltpu.VMEM((3 * LANES, rows), bf16),
-            pltpu.VMEM((3 * LANES, rows), bf16),
-            pltpu.VMEM((4, LANES, rows), f32),
-            pltpu.VMEM((4, LANES, rows), f32),
+            pltpu.VMEM((2, LANES, rows), f32),
+            pltpu.VMEM((2, LANES, rows), f32),
             pltpu.VMEM((width, full), bf16),
             pltpu.SemaphoreType.DMA((members * layers,)),
         ],
@@ -607,16 +742,16 @@
     )(hidden_in, middle_grad, w_qkv, *grads)
 
 
-def experts_kernel(tiles, expert, packed, has_prev, has_sums, last, *refs):
+def experts_kernel(x_counts, c_counts, expert, packed, has_prev, has_sums, last, *refs):
     refs = list(refs)
     take = lambda count: [refs.pop(0) for _ in range(count)]
     (place_ref,) = take(1)
-    x_src = [take(len(t)) for t in tiles]
-    c_src = [take(len(t)) for t in tiles]
+    x_src = [take(c) for c in x_counts]
+    c_src = [take(c) for c in c_counts]
     weights = take(1 if packed else 3)
-    prev_src = [take(2) for _ in tiles] if has_prev else None
+    prev_src = [take(2) for _ in x_counts] if has_prev else None
     sums_src = take(3) if has_sums else None
-    dest = [take(2) for _ in tiles]
+    dest = [take(2) for _ in x_counts]
     sums_dst = take(1 if packed and last else 3)
     xs, cs, og_out, og_grad = take(4)
     prevs = take(2) if has_prev else None
@@ -624,7 +759,7 @@
     held = take(3) if packed else weights
     sem_in, sem_out, sem_sum, sem_w = take(4)
     i = pl.program_id(0)
-    count = len(tiles)
+    count = len(x_counts)
     width = cs.shape[2]
     hidden = acc[0].shape[1]
 
@@ -717,7 +852,7 @@
     gate_grad = (mid_grad * up_proj * sigmoid_g * (1.0 + gate_proj * (1.0 - sigmoid_g))).astype(bf16)
     up_grad = (mid_grad * active).astype(bf16)
     out_rows = matmul(mid, w_down)
-    mix = resid_scale * jnp.sum(cot_wide * out_rows, axis=-1, keepdims=True)
+    mix = jnp.sum(mid.astype(f32) * mid_grad, axis=-1, keepdims=True)
     mixed = gate_row * out_rows
     if has_prev:
         mixed = mixed + prevs[0][slot].astype(f32)
@@ -824,7 +959,7 @@
         ]
     scratch += [pltpu.SemaphoreType.DMA(shape) for shape in ((2, 6), (2, 2), (3,), (2 + width // hidden,))]
     out = pl.pallas_call(
-        functools.partial(experts_kernel, [[0] * len(t) for t in tiles], expert, packed,
+        functools.partial(experts_kernel, [len(t) for t in tiles], [len(c) for c in cots], expert, packed,
                           prev is not None, sums is not None, last),
         grid=(len(tiles),),
         in_specs=specs,
@@ -846,6 +981,7 @@
     inside = [[GROUP * j + q for q in range(GROUP)] for j in range(layers)]
     me = lax.axis_index("fsdp")
     place, layer = me % GROUP, me // GROUP
+    core = lambda value: swap(value, 1, n)
     rows, width = hidden_in.shape
     own_rows = w_query.shape[0]
     hidden = w_gate.shape[2]
@@ -859,11 +995,7 @@
         [w_router, norm_attn[:, None], norm_moe[:, None], jnp.zeros((own_rows, LANES - E - 2), bf16)],
         axis=1,
     )
-    own_attn = jnp.concatenate([w_query, w_key, w_value, extras, w_out], axis=1)
-    if split:
-        column = lax.all_gather(own_attn, "fsdp", axis=0, tiled=True, axis_index_groups=along)
-    else:
-        column = lax.all_gather(own_attn, "fsdp", axis=0, tiled=True)
+    own_qkv = jnp.concatenate([w_query, w_key, w_value, extras], axis=1)
 
     down_rows = jnp.concatenate(
         [w_down[:, :, t * hidden : (t + 1) * hidden] for t in range(thirds)], axis=1
@@ -871,11 +1003,11 @@
     expert_rows = jnp.concatenate([w_gate, w_up, down_rows], axis=1)
     per_expert = expert_rows.shape[1]
     expert_rows = expert_rows.reshape(GROUP, PAIR_E, per_expert, hidden).transpose(1, 0, 2, 3)
+
     expert_rows = lax.all_to_all(expert_rows, "fsdp", 1, 1, tiled=True, axis_index_groups=inside)
-    column, expert_rows = tie(column, expert_rows)
-    column, out_column = column[:, :QKV_WIDE], column[:, QKV_WIDE:]
-    gathered_first = lax.all_gather(expert_rows[0], "fsdp", axis=0, axis_index_groups=along)
-    gathered_second = lax.all_gather(expert_rows[1], "fsdp", axis=0, axis_index_groups=along)
+
+    def over_all(block):
+        return lax.all_gather(block, "fsdp", axis=0, axis_index_groups=along)
 
     aligned = own_rows % 16 == 0 and own_hidden % 16 == 0
 
@@ -887,57 +1019,77 @@
         low = gathered[:, :, 2 * own_rows :].reshape(layers, GROUP, thirds, own_hidden, hidden)
         return gate, up, low.transpose(0, 1, 3, 2, 4).reshape(hidden, width)
 
-    def flat(pieces):
-        for k, group in enumerate(pieces):
-            if layers % len(group):
-                pieces[k] = [jnp.concatenate(group, axis=0)]
-        runs = []
-        for k, group in enumerate(pieces):
-            per = layers // len(group)
-            runs += [[(k, c * per + j) for j in range(per)] for c in range(len(group))]
-        return runs, [a for group in pieces for a in group]
-
-    if split:
-        near = gather_start(column, n)
-        plan, pieces = flat(gather_cores(column, near, gather_far(*near, n), n))
-        table = own_rows * (GROUP * steps[None, :] + members[:, None])
-    else:
-        plan, pieces = [[(0, 0)]], [column]
-        table = jnp.zeros((1, 1), jnp.int32)
-    table = table.astype(jnp.int32)
-
-    core = lambda value: swap(value, 1, n)
-    pieces, out_column, cotangent = tie(pieces, out_column, cotangent)
-    if split:
-        near = gather_start(out_column, n)
-    cots_near = gather_start(cotangent, n)
     segment, position = layout(lengths[0], rows)
     cosine, sine_val = turn_tables(position)
     half = HK // 4
+    c_low, c_high = cotangent[: rows // 2], cotangent[rows // 2 :]
+    near = lambda block: (swap(block, 2, n), swap(block, 4, n))
+    cores = lambda *values: [core(value) for value in values]
+    if split:
+        ring = list(range(layers))
+        plan = [[(k, j) for j in ring] for k in range(6)]
+        upper = (layers + 1) // 2
+        plan += [[(k, j) for j in part] for k in (6, 7) for part in (ring[:upper], ring[upper:]) if part]
+        cut = upper * own_rows
+        blocks = ring_start(own_qkv, layers, n)
+        column = joined_rows(ring_end(blocks, layers, n), ring)
+        column, expert_rows, w_out = tie(column, expert_rows, w_out)
+
+        def far_ways(pair):
+            ways = [swap(pair[0][:cut], 4, n)]
+            return ways + ([swap(pair[1][cut:], 2, n)] if layers > 1 else [])
+
+        def in_order(own, other, near_two, far):
+            return [own, other[0], near_two[0], other[1], near_two[1], other[2], *far, *cores(*far)]
+
+        near_qkv = near(column)
+        wo_blocks = ring_start(w_out, layers, n)
+        near_qkv, wo_blocks, cosine, sine_val = tie(near_qkv, wo_blocks, cosine, sine_val)
+        far = far_ways(near_qkv)
+        other = cores(column, *near_qkv)
+        other, wo_blocks = tie(other, wo_blocks)
+        wo_column = joined_rows(ring_end(wo_blocks, layers, n), ring)
+        far, other, wo_column = tie(far, other, wo_column)
+        pieces = in_order(column, other, near_qkv, far)
+        pieces, wo_column = tie(pieces, wo_column)
+        wo_near, wo_other = near(wo_column), core(wo_column)
+        table = own_rows * (GROUP * steps[None, :] + members[:, None])
+        ring_table = own_rows * (GROUP * ((layer - steps[None, :]) % layers) + members[:, None])
+    else:
+        pieces = [lax.all_gather(own_qkv, "fsdp", axis=0, tiled=True)]
+        plan = [[(0, 0)]]
+        table = ring_table = jnp.zeros((1, 1), jnp.int32)
+    table, ring_table = table.astype(jnp.int32), ring_table.astype(jnp.int32)
+
+    gathered_first, gathered_second = over_all(expert_rows[0]), over_all(expert_rows[1])
     w_qkv, normed, turned, *first_half = attend_forward(
-        0, half, table, plan, pieces, hidden_in, cosine, sine_val, segment
+        0, half, ring_table, plan, pieces, hidden_in, cosine, sine_val, segment
     )
     extras_full = w_qkv[:, QW + 2 * KW :]
+    normed, c_low = tie(normed, c_low)
     if split:
-        near, normed = tie(near, normed)
-        out_far = gather_far(*near, n)
-        out_other = [core(v) for v in (out_column, *near)]
+        wo_near, wo_other, normed = tie(wo_near, wo_other, normed)
+        wo_far = far_ways(wo_near)
+    c_near_low = near(c_low)
     second_half = attend_forward(half, half, table, None, w_qkv, normed, cosine, sine_val, segment)
     attn_out = (first_half[3], second_half[3])
     if split:
-        attn_out, out_far, out_other, cots_near = tie(attn_out, out_far, out_other, cots_near)
-        _, out_pieces = flat(
-            [[out_column], [out_other[0]], [near[0]], [out_other[1]], [near[1]], [out_other[2]],
-             list(out_far), [core(v) for v in out_far]]
-        )
+        attn_out, c_near_low, c_high, wo_far, wo_near = tie(attn_out, c_near_low, c_high, wo_far, wo_near)
     else:
-        out_pieces = [out_column]
-
-    cots_core = [core(cotangent), core(cots_near[0]), core(cots_near[1])]
+        attn_out, c_near_low, c_high = tie(attn_out, c_near_low, c_high)
+    if split:
+        out_pieces = in_order(wo_column, [wo_other, *cores(*wo_near)], wo_near, wo_far)
+        out_pieces, c_high = tie(out_pieces, c_high)
+    else:
+        out_pieces = [lax.all_gather(w_out, "fsdp", axis=0, tiled=True)]
+
+    c_near_high = near(c_high)
+    c_other = [cores(c_low, *c_near_low)]
     w_out_full, middle, inner, mix = to_middle(
-        table, plan, out_pieces, hidden_in, attn_out, extras_full, routes
-    )
-    cots_core = after(cots_core, inner)
+        ring_table, plan, out_pieces, hidden_in, attn_out, extras_full, routes
+    )
+    c_near_high, c_other, inner = tie(c_near_high, c_other, inner)
+    c_other.append(cores(c_high, *c_near_high))
 
     def expert_sums(sums):
         if len(sums) == 1:
@@ -970,13 +1122,16 @@
         return sums
 
     inner_near = gather_start(inner, n)
-    x_own, c_own = [[inner], [core(inner)]], [[cotangent], [cots_core[0]]]
+    x_own, c_own = [[inner], [core(inner)]], [[cotangent], [c_other[0][0], c_other[1][0]]]
     sums = run(0, [0, 1], x_own, c_own, first, None, False)
     inner_near = after(inner_near, sums)
     inner_far = gather_far(*inner_near, n)
-    cots_far = gather_far(*tie(*cots_near, *inner_near)[:2], n)
+    c_near_low, c_near_high, sums = tie(c_near_low, c_near_high, sums)
+    cots_far = swap(c_near_low[0], 4, n), swap(c_near_high[1], 2, n)
     x_near = [[inner_near[0]], [core(inner_near[0])], [inner_near[1]], [core(inner_near[1])]]
-    c_near = [[cots_near[0]], [cots_core[1]], [cots_near[1]], [cots_core[2]]]
+    c_near = []
+    for q in (0, 1):
+        c_near += [[c_near_low[q], c_near_high[q]], [c_other[0][1 + q], c_other[1][1 + q]]]
     sums = run(0, [2, 3, 4, 5], x_near, c_near, first, sums, False)
     inner_far, cots_far = after((inner_far, cots_far), sums)
     x_far = [list(inner_far), [core(v) for v in inner_far]]
@@ -985,55 +1140,62 @@
     shared0 = expert_sums(sums0)
 
     sums = run(1, [6, 7], x_far, c_far, second, None, False)
-    chip6, out6 = [sum_cores([part[6][i], part[7][i]], n) for i in (1, 0)]
-    x_near[0], chip6, out6 = tie(x_near[0], chip6, out6)
-    far_sums, out_far = sum_far(chip6, n), sum_far(out6, n)
+    both_ways = lambda low, high: (swap(low, 4, n), swap(high, 2, n))
+    halves, out_halves = sums_for_far([(part[6][i], core(part[7][i])) for i in (1, 0)])
+    x_near[0], halves, out_halves = tie(x_near[0], halves, out_halves)
+    far_sums, out_far = both_ways(*halves), both_ways(*out_halves)
     sums = run(1, [2, 3, 4, 5], x_near, c_near, second, sums, False)
     done = [part[k] for k in (2, 3, 4, 5)]
     far_sums, out_far, sums, done = tie(far_sums, out_far, sums, done)
     part.update(zip((2, 3, 4, 5), done))
-    chip2, chip4 = [sum_cores([part[k][1], part[k + 1][1]], n) for k in (2, 4)]
-    x_own[0], chip2, chip4, shared0 = tie(x_own[0], chip2, chip4, shared0)
-    inner_two, inner_four = sum_near(chip2, chip4, *far_sums, n)
+    near_sums = sums_for_near(part[2][1], core(part[3][1]), part[4][1], core(part[5][1]), *far_sums)
+    x_own[0], near_sums, shared0 = tie(x_own[0], near_sums, shared0)
+    inner_near = [swap(value, bit, n) for value, bit in zip(near_sums, (2, 4))]
     out_core = [core(part[3][0]), core(part[5][0])]
     sums = run(1, [0, 1], x_own, c_own, second, sums, True)
-    inner_two, inner_four, out_core, sums, part[0], part[1] = tie(
-        inner_two, inner_four, out_core, sums, part[0], part[1]
-    )
+    inner_near, out_core, sums, part[0], part[1] = tie(inner_near, out_core, sums, part[0], part[1])
     shared1 = expert_sums(sums)
-    inner_chip = sum_cores([part[0][1], part[1][1]], n)
-    out_chips = [add_low(part[k][0], other) for k, other in zip((2, 4), out_core)]
-    out_chips, inner_chip = tie(out_chips, inner_chip)
-    out_near = sum_near(*out_chips, *out_far, n)
+    inner_other = core(part[1][1])
+    out_blocks = (part[2][0], out_core[0], part[4][0], out_core[1])
+    out_sums = half_for_near(0, *out_blocks, out_far[0])
+    out_sums, inner_other = tie(out_sums, inner_other)
+    out_low = [swap(out_sums[0], 2, n), swap(out_sums[1], 4, n)]
     out_other = core(part[1][0])
     *out_grads, middle_grad, attn_grad0, attn_grad1 = middle_back(
-        table, (inner_chip, inner_two, inner_four), inner, mix, middle, cotangent, extras_full, attn_out,
+        table, (part[0][1], inner_other, *inner_near), inner, mix, middle, cotangent, extras_full, attn_out,
         w_out_full,
     )
+    out_low, out_other, out_grads, middle_grad, attn_grad0, attn_grad1 = tie(
+        out_low, out_other, out_grads, middle_grad, attn_grad0, attn_grad1
+    )
+
+    wide = lambda value: value.astype(f32)
 
     def chips_of(stacks):
-        return add_low(stacks[0], core(stacks[1])) if split else stacks[0]
+        return sums_of_stack(stacks[0], core(stacks[1])) if split else [stacks[0]]
 
     def far_of(chips):
-        rows_each = chips.shape[0] // 4
-        return sum_far(chips[3 * rows_each :], n) if split else ()
-
-    def near_of(chips, far):
-        rows_each = chips.shape[0] // 4
+        return both_ways(*chips[3:]) if split else ()
+
+    def near_of(*sets):
         if not split:
             return ()
-        return sum_near(chips[rows_each : 2 * rows_each], chips[2 * rows_each : 3 * rows_each], *far, n)
-
-    def owned(chips, near):
-        return add_up([chips[: chips.shape[0] // 4], *near]).astype(bf16)
-
-    def over_layers(pairs):
+        sum2, sum4 = stack_near([(*chips[1:3], *far) for chips, far in sets])
+        return swap(sum2, 2, n), swap(sum4, 4, n)
+
+    def over_layers(sets):
         if not split:
             sums = [
-                lax.psum_scatter(chips, "fsdp", scatter_dimension=0, tiled=True) for chips, _ in pairs
+                lax.psum_scatter(chips[0], "fsdp", scatter_dimension=0, tiled=True)
+                for group, _ in sets
+                for chips in group
             ]
             return [jnp.concatenate(sums, axis=1)]
-        total = jnp.concatenate([owned(*pair) for pair in pairs], axis=1)
+        total = []
+        for group, near_sums in sets:
+            own = jnp.concatenate([chips[0] for chips in group], axis=1)
+            total.append((wide(own) + wide(near_sums[0]) + wide(near_sums[1])).astype(bf16))
+        total = jnp.concatenate(total, axis=1)
         return layer_start(total.reshape(layers, own_rows, -1), layer, layers, n)
 
     def back(base, steps, half_set, grads):
@@ -1042,43 +1204,48 @@
         )
 
     wo_chips = chips_of(out_grads)
-    attn_grad0, wo_chips = tie(attn_grad0, wo_chips)
+    out_sums = half_for_near(1, *tie(*out_blocks, middle_grad)[:4], out_far[1])
+    attn_grad0, wo_chips, out_sums = tie(attn_grad0, wo_chips, out_sums)
+    out_high = [swap(value, bit, n) for value, bit in zip(out_sums, (2, 4))]
     wo_far = far_of(wo_chips)
+    *stacks0, dq0, dk0, dv0 = back(0, half, first_half, attn_grad0)
+    out_high, wo_far, stacks0, dq0, dk0, dv0 = tie(out_high, wo_far, stacks0, dq0, dk0, dv0)
+
+    chips0 = chips_of(stacks0)
+    attn_grad1, chips0 = tie(attn_grad1, chips0)
+    wo_near, far0 = near_of((wo_chips, wo_far)), far_of(chips0)
+    *stacks1, dq1, dk1, dv1 = back(0, half // 2, second_half, attn_grad1)
+    wo_near, far0, stacks1, dq1, dk1, dv1 = tie(wo_near, far0, stacks1, dq1, dk1, dv1)
+
+    chips1 = chips_of(stacks1)
+    attn_grad1, chips1, dq1, shared1 = tie(attn_grad1, chips1, dq1, shared1)
+    near0, far1 = near_of((chips0, far0)), far_of(chips1)
+    *stacks2, dq2, dk2, dv2 = back(half // 2, half - half // 2, second_half, attn_grad1)
+    near0, far1, stacks2, dq2, dk2, dv2, wo_near = tie(near0, far1, stacks2, dq2, dk2, dv2, wo_near)
+
     to_owner = lambda block: lax.all_to_all(
         block, "fsdp", 0, 0, tiled=True, axis_index_groups=inside
     )
-    owned0 = to_owner(shared0)
-    *stacks0, dq0, dk0, dv0 = back(0, half, first_half, attn_grad0)
-    owned0, out_other, wo_far, stacks0, dq0 = tie(owned0, out_other, wo_far, stacks0, dq0)
-
-    chips0 = chips_of(stacks0)
-    attn_grad1, chips0, shared1 = tie(attn_grad1, chips0, shared1)
-    wo_near, far0 = near_of(wo_chips, wo_far), far_of(chips0)
-    *stacks1, dq1, dk1, dv1 = back(0, half // 2, second_half, attn_grad1)
-    wo_near, far0, stacks1, dq1, out_near = tie(wo_near, far0, stacks1, dq1, out_near)
-
-    chips1 = chips_of(stacks1)
-    attn_grad1, chips1 = tie(attn_grad1, chips1)
-    near0, far1 = near_of(chips0, far0), far_of(chips1)
-    *stacks2, dq2, dk2, dv2 = back(half // 2, half - half // 2, second_half, attn_grad1)
-    near0, far1, stacks2, dq2, wo_near = tie(near0, far1, stacks2, dq2, wo_near)
-
     chips2 = chips_of(stacks2)
     dq2, chips2 = tie(dq2, chips2)
-    near1, far2 = near_of(chips1, far1), far_of(chips2)
-    early = over_layers([(wo_chips, wo_near), (chips0, near0)])
+    far2 = far_of(chips2)
+    owned0 = to_owner(shared0)
+    early = over_layers([([wo_chips], wo_near), ([chips0], near0)])
     input_grad = to_input(
         hidden_in, middle_grad, w_qkv, (dq0, dk0, dv0, dq1, dk1, dv1, dq2, dk2, dv2)
     )
-    near1, far2, early, input_grad = tie(near1, far2, early, input_grad)
-    near2 = near_of(chips2, far2)
-    owned1 = to_owner(after(shared1, near2))
-    out_own = add_low(part[0][0], out_other)
-    mixed = (middle + resid_scale * add_up([out_own, *out_near])).astype(bf16)
+    far2, early, input_grad, owned0 = tie(far2, early, input_grad, owned0)
+    near12 = near_of((chips1, far1), (chips2, far2))
+    owned1 = to_owner(after(shared1, near12))
+    out_low, near12 = tie(out_low, near12)
+    out_total = wide(part[0][0]) + wide(out_other) + jnp.concatenate(
+        [wide(out_low[0]) + wide(out_low[1]), wide(out_high[0]) + wide(out_high[1])], axis=0
+    )
+    mixed = (middle + resid_scale * out_total).astype(bf16)
     early = layer_add(early)
     mine_out = early[:, : width + LANES]
-    late = layer_add(over_layers([(chips1, near1), (chips2, near2)]))
-    unit1, unit2 = chips1.shape[1], chips2.shape[1]
+    late = layer_add(over_layers([([chips1, chips2], near12)]))
+    unit1, unit2 = chips1[0].shape[1], chips2[0].shape[1]
     mine = [early[:, width + LANES :], late[:, :unit1], late[:, unit1 : unit1 + unit2]]
 
     shared = jnp.stack([owned0, owned1], axis=1).reshape(E, per_expert, hidden).astype(f32)

time: 688 us -> 635 us (0.923)
  blocking collectives: 34.4 us -> 0 us
  other arithmetic: 56.1 us -> 23.4 us
  starting transfers between devices: 70 us -> 95.8 us
  waiting for transfers between devices: 151 us -> 133 us
  Pallas kernels: 308 us -> 321 us
    pallas_call x6 -> x17, Pallas kernels: 168 us -> 206 us  [the longest x6 167 us: experts_call(): pl.pallas_call(functools.partial(experts_kernel, [len(t) for t in tiles],...]
    all_to_all x1 -> x0, blocking collectives: 34.4 us -> none  [shards(): lax.all_to_all(expert_rows, 'fsdp', 1, 1, tiled=True, axis_index_groups=i...]
    ppermute x72 -> x77, waiting for transfers between devices: 123 us -> 90.1 us  [swap(): lax.ppermute(value, 'fsdp', [(i, i ^ bit) for i in range(device_count)])]
    ppermute x6 -> x14, waiting for transfers between devices: 6.92 us -> 38 us  [shift(): return lax.ppermute(value, 'fsdp', moved)]
    convert_element_type x24 -> x4, other arithmetic: 32.6 us -> 6.88 us  [the longest x1 3.65 us: shards(): mixed = (middle + resid_scale * out_total).astype(bf16)]
    ppermute x6 -> x14, starting transfers between devices: 10.2 us -> 26.6 us  [shift(): return lax.ppermute(value, 'fsdp', moved)]
    pallas_call x3, Pallas kernels: 54.8 us -> 40.1 us  [attend_backward(): pl.pallas_call(functools.partial(attend_back_kernel, 128, min(members, 2)...]
    pallas_call x2, Pallas kernels: 41.6 us -> 30 us  [attend_forward(): pl.pallas_call(functools.partial(attend_kernel, 128, plan), grid=(steps,)...]
  transfers between devices with their start and end apart: 85 -> 98, of which waited for: 30 -> 38; matrix products, arithmetic and copies ran while one was open for 11% -> 5% of each run, Pallas kernels for 45% -> 51%
where the time goes in v3:
time: 635 us; the launch traced here: 626 us
  Pallas kernels  321 us (51%)
  waiting for transfers between devices  133 us (21%)
  starting transfers between devices  95.8 us (15%)
  local copies, waits for them, and re-layouts  37.8 us (6%)
  other arithmetic  23.4 us (4%)
  between operations  15.5 us (2%)
    pallas_call x6, Pallas kernels, experts_call(): pl.pallas_call(functools.partial(experts_kernel, [len(t) for t in tiles],...  167 us
    ppermute x77, waiting for transfers between devices, swap(): lax.ppermute(value, 'fsdp', [(i, i ^ bit) for i in range(device_count)])  90.1 us
    ppermute x77, starting transfers between devices, swap(): lax.ppermute(value, 'fsdp', [(i, i ^ bit) for i in range(device_count)])  55.5 us
    pallas_call x3, Pallas kernels, attend_backward(): pl.pallas_call(functools.partial(attend_back_kernel, 128, min(members, 2)...  40.1 us
    ppermute x14, waiting for transfers between devices, shift(): return lax.ppermute(value, 'fsdp', moved)  38 us
    pallas_call x2, Pallas kernels, attend_forward(): pl.pallas_call(functools.partial(attend_kernel, 128, plan), grid=(steps,)...  30 us
    ppermute x14, starting transfers between devices, shift(): return lax.ppermute(value, 'fsdp', moved)  26.6 us
    unnamed x163, local copies, waits for them, and re-layouts  21.3 us
  transfers between devices with their start and end apart: 98, of which 38 were waited for; matrix products, arithmetic and copies ran while one was open for 5% of the time, Pallas kernels for 51%

profile of v3, /device:TPU:0, one launch (start us, length us, event | category | flops | bytes accessed | tf_op | source)
XLA Modules:
  0.0 626.4 jit_solution(5752503190962041764)
XLA Ops:
  10.3 5.3 all-to-all-start
  16.1 3.7 collective-permute-start.2
  19.8 6.6 %collective-permute-done.2 = bf16[48,2688]{1,0:T(8,128)(2,1)S(1)} collective-permute-done((bf16[48,2688]{1,0:T(8,128)(2,1)S(1)}, bf16[48,2688]{1,0:T(8,128)(2,1)S(1)}, u32[]{:S(2)}, u32[]{:S(2)}) %collective-permute-start.2) | collective-permute-done | bytes 258080 | tf_op jit(solution)/shard_map/ppermute | solution.py:78
  26.4 4.3 collective-permute-start.3
  34.5 5.1 collective-permute-done.1
  40.6 4.5 all-to-all-done
  48.2 3.7 collective-permute-start.7
  54.2 3.2 collective-permute-done.7
  57.3 4.7 collective-permute-done.6
  62.1 6.7 %collective-permute-done.5.refs_4_ = bf16[192,2688]{1,0:T(8,128)(2,1)} collective-permute-done((bf16[192,2688]{1,0:T(8,128)(2,1)S(1)}, bf16[192,2688]{1,0:T(8,128)(2,1)}, u32[]{:S(2)}, u32[]{:S(2)}) %collective-permute-start.5) | collective-permute-done | bytes 1032224 | tf_op jit(solution)/shard_map/ppermute | solution.py:73
  78.4 3.6 collective-permute-start.14
  82.0 6.6 %collective-permute-done.14 = bf16[48,768]{1,0:T(8,128)(2,1)S(1)} collective-permute-done((bf16[48,768]{1,0:T(8,128)(2,1)S(1)}, bf16[48,768]{1,0:T(8,128)(2,1)S(1)}, u32[]{:S(2)}, u32[]{:S(2)}) %collective-permute-start.14) | collective-permute-done | bytes 73760 | tf_op jit(solution)/shard_map/ppermute | solution.py:78
  96.8 17.5 %shard_map.229 = (bf16[1536,2688]{1,0:T(8,128)(2,1)}, bf16[512,1536]{1,0:T(8,128)(2,1)}, bf16[1536,512]{1,0:T(8,128)(2,1)}, bf16[512,768]{1,0:T(8,128)(2,1)}, bf...) custom-call(s32[8,4]{1,0:T(8,128)} %get-tuple-element.744.table_ref, ...), custom_call_target="tpu_custom_call" | custom-call | flops 1000000 | bytes 100000 | tf_op jit(solution)/shard_map/pallas_call | solution.py:462
  121.0 12.5 %shard_map.230 = (bf16[512,768]{1,0:T(8,128)(2,1)}, bf16[512,256]{1,0:T(8,128)(2,1)}, bf16[512,256]{1,0:T(8,128)(2,1)}, bf16[512,768]{1,0:T(8,128)(2,1)}, f32[2,512,128]{2,1,0:T(8,128)}) custom-call(s32[8,4]{1,0:T(8,128)} %get-tuple-element.743.table_ref, bf16[512,1536]{1,0:T(8,128)(2,1)} %get-tuple-element.362.x_ref, ...), custom_call_target="tpu_custom_call" | custom-call | flops 1000000 | bytes 100000 | tf_op jit(solution)/shard_map/pallas_call | solution.py:462
  136.3 4.7 collective-permute-done.23.refs_7_
  150.8 11.8 %shard_map.231 = (bf16[1536,1536]{1,0:T(8,128)(2,1)}, f32[512,1536]{1,0:T(8,128)}, bf16[512,1664]{1,0:T(8,128)(2,1)}, f32[512,128]{1,0:T(8,128)}) custom-call(s32[8,4]{1,0:T(8,128)} %get-tuple-element.744.table_ref, bf16[512,1536]{1,0:T(8,128)(2,1)} %x_ref.5, bf16[512,768]{1,0:T(8,128)(2,1)} %get-tuple-element.368.attn0_ref, ...), custom_call_target="tpu_custom_call" | custom-call | flops 1000000 | bytes 100000 | tf_op jit(solution)/shard_map/pallas_call | solution.py:516
  171.8 21.7 %shard_map.232 = (bf16[512,1536]{1,0:T(8,128)(2,1)}, bf16[512,1664]{1,0:T(8,128)(2,1)}, bf16[512,1536]{1,0:T(8,128)(2,1)}, bf16[512,1664]{1,0:T(8,128)(2,1)}, f3...) custom-call(s32[1]{0:T(128)} %bitcast.10.refs_0_, ...), custom_call_target="tpu_custom_call" | custom-call | flops 1000000 | bytes 100000 | tf_op jit(solution)/shard_map/pallas_call | solution.py:961
  193.5 12.6 %collective-permute-done.34.refs_3_ = bf16[512,1664]{1,0:T(8,128)(2,1)S(1)} collective-permute-done((bf16[512,1664]{1,0:T(8,128)(2,1)}, bf16[512,1664]{1,0:T(8,128)(2,1)S(1)}, u32[]{:S(2)}, u32[]{:S(2)}) %collective-permute-start.34) | collective-permute-done | bytes 1703968 | tf_op jit(solution)/shard_map/ppermute | solution.py:73
  219.3 37.7 %shard_map.233 = (bf16[512,1536]{1,0:T(8,128)(2,1)}, bf16[512,1664]{1,0:T(8,128)(2,1)}, bf16[512,1536]{1,0:T(8,128)(2,1)}, bf16[512,1664]{1,0:T(8,128)(2,1)}, bf...) custom-call(s32[1]{0:T(128)} %bitcast.10.refs_0_, ...), custom_call_target="tpu_custom_call" | custom-call | flops 1000000 | bytes 100000 | tf_op jit(solution)/shard_map/pallas_call | solution.py:961
  258.2 5.0 collective-permute-done.47.refs_7_
  266.0 22.5 %shard_map.234 = (bf16[512,1536]{1,0:T(8,128)(2,1)}, bf16[512,1664]{1,0:T(8,128)(2,1)}, bf16[512,1536]{1,0:T(8,128)(2,1)}, bf16[512,1664]{1,0:T(8,128)(2,1)}, bf16[4,8,144,512]{3,2,1,0:T(8,128)(2,1)}) custom-call(s32[1]{0:T(128)} %bitcast.10.refs_0_, bf16[256,1664]{1,0:T(8,128)(2,1)} %collective-permute-done.37.refs_1_, ...), custom_call_target="tpu_custom_call" | custom-call | flops 1000000 | bytes 100000 | tf_op jit(solution)/shard_map/pallas_call | solution.py:961
  288.6 22.7 %shard_map.235 = (bf16[512,1536]{1,0:T(8,128)(2,1)}, bf16[512,1664]{1,0:T(8,128)(2,1)}, bf16[512,1536]{1,0:T(8,128)(2,1)}, bf16[512,1664]{1,0:T(8,128)(2,1)}, f3...) custom-call(s32[1]{0:T(128)} %bitcast.10.refs_0_, bf16[256,1664]{1,0:T(8,128)(2,1)} %collective-permute-done.37.refs_1_, ...), custom_call_target="tpu_custom_call" | custom-call | flops 1000000 | bytes 100000 | tf_op jit(solution)/shard_map/pallas_call | solution.py:961
  311.8 5.5 collective-permute-done.50
  319.1 5.0 shard_map.236
  328.1 38.7 %shard_map.237 = (bf16[512,1536]{1,0:T(8,128)(2,1)}, bf16[512,1664]{1,0:T(8,128)(2,1)}, bf16[512,1536]{1,0:T(8,128)(2,1)}, bf16[512,1664]{1,0:T(8,128)(2,1)}, bf...) custom-call(s32[1]{0:T(128)} %bitcast.10.refs_0_, ...), custom_call_target="tpu_custom_call" | custom-call | flops 1000000 | bytes 100000 | tf_op jit(solution)/shard_map/pallas_call | solution.py:961
  368.2 3.3 collective-permute-done.55
  375.2 5.8 shard_map.238
  383.1 23.3 %shard_map.239 = (bf16[512,1536]{1,0:T(8,128)(2,1)}, bf16[512,1664]{1,0:T(8,128)(2,1)}, bf16[512,1536]{1,0:T(8,128)(2,1)}, bf16[512,1664]{1,0:T(8,128)(2,1)}, bf16[4,8,144,512]{3,2,1,0:T(8,128)(2,1)}) custom-call(s32[1]{0:T(128)} %bitcast.10.refs_0_, bf16[512,1664]{1,0:T(8,128)(2,1)} %get-tuple-element.469.refs_1_.inner_ref, ...), custom_call_target="tpu_custom_call" | custom-call | flops 1000000 | bytes 100000 | tf_op jit(solution)/shard_map/pallas_call | solution.py:961
  406.5 14.1 %collective-permute-done.57.near2_ref = bf16[512,1664]{1,0:T(8,128)(2,1)} collective-permute-done((bf16[512,1664]{1,0:T(8,128)(2,1)}, bf16[512,1664]{1,0:T(8,128)(2,1)}, u32[]{:S(2)}, u32[]{:S(2)}) %collective-permute-start.57) | collective-permute-done | bytes 1703968 | tf_op jit(solution)/shard_map/ppermute | solution.py:73
  421.4 4.6 shard_map.240
  428.8 19.4 %shard_map.241 = (bf16[768,1664]{1,0:T(8,128)(2,1)}, bf16[768,1664]{1,0:T(8,128)(2,1)}, f32[512,1536]{1,0:T(8,128)}, bf16[512,768]{1,0:T(8,128)(2,1)}, bf16[512,768]{1,0:T(8,128)(2,1)}) custom-call(s32[8,4]{1,0:T(8,128)} %get-tuple-element.743.table_ref, bf16[512,1664]{1,0:T(8,128)(2,1)} %get-tuple-element.494.own0_ref, bf16[512,1664]{1,0:T(8,128)(2,1)} %copy-done.30, ...), custom_call_target="tpu_custom_call" | custom-call | flops 1000000 | bytes 100000 | tf_op jit(solution)/shard_map/pallas_call | solution.py:578
  449.3 4.2 shard_map.243
  455.9 4.3 shard_map.242
  464.2 18.4 %shard_map.244 = (bf16[768,1280]{1,0:T(8,128)(2,1)}, bf16[768,1280]{1,0:T(8,128)(2,1)}, bf16[512,768]{1,0:T(8,128)(2,1)}, bf16[512,256]{1,0:T(8,128)(2,1)}, bf16[512,256]{1,0:T(8,128)(2,1)}) custom-call(s32[8,4]{1,0:T(8,128)} %get-tuple-element.743.table_ref, bf16[1536,512]{1,0:T(8,128)(2,1)} %get-tuple-element.529.turned_ref, ...), custom_call_target="tpu_custom_call" | custom-call | flops 1000000 | bytes 100000 | tf_op jit(solution)/shard_map/pallas_call | solution.py:684
  482.6 4.4 collective-permute-done.68.refs_2_
  494.3 3.5 shard_map.245
  499.7 10.8 %shard_map.247 = (bf16[768,640]{1,0:T(8,128)(2,1)}, bf16[768,640]{1,0:T(8,128)(2,1)}, bf16[512,384]{1,0:T(8,128)(2,1)}, bf16[512,128]{1,0:T(8,128)(2,1)}, bf16[512,128]{1,0:T(8,128)(2,1)}) custom-call(s32[8,4]{1,0:T(8,128)} %get-tuple-element.743.table_ref, bf16[1536,512]{1,0:T(8,128)(2,1)} %get-tuple-element.529.turned_ref, ...), custom_call_target="tpu_custom_call" | custom-call | flops 1000000 | bytes 100000 | tf_op jit(solution)/shard_map/pallas_call | solution.py:684
  510.6 3.3 collective-permute-done.73.refs_2_
  524.5 3.8 all-to-all-start.1
  528.3 10.8 %shard_map.250 = (bf16[768,640]{1,0:T(8,128)(2,1)}, bf16[768,640]{1,0:T(8,128)(2,1)}, bf16[512,384]{1,0:T(8,128)(2,1)}, bf16[512,128]{1,0:T(8,128)(2,1)}, bf16[512,128]{1,0:T(8,128)(2,1)}) custom-call(s32[8,4]{1,0:T(8,128)} %get-tuple-element.743.table_ref, bf16[1536,512]{1,0:T(8,128)(2,1)} %get-tuple-element.529.turned_ref, ...), custom_call_target="tpu_custom_call" | custom-call | flops 1000000 | bytes 100000 | tf_op jit(solution)/shard_map/pallas_call | solution.py:684
  542.5 3.4 collective-permute-start.85
  554.2 13.6 %shard_map.252 = f32[512,1536]{1,0:T(8,128)} custom-call(bf16[512,1536]{1,0:T(8,128)(2,1)} %x_ref.5, f32[512,1536]{1,0:T(8,128)} %get-tuple-element.517.mgrad_ref, bf16[1536,2688]{1,0:T(8,128)(2,1)} %get-tuple-element.363.refs_0_.refs_1_.refs_2_.w_ref, bf16[512,768]{1,0:T(8,128)(2,1)} %get-tuple-element.612.refs_0_, ...), custom_call_target="tpu_custom_call" | custom-call | flops 1000000 | bytes 100000 | tf_op jit(solution)/shard_map/pallas_call | solution.py:735
  567.8 3.0 collective-permute-done.84
  579.5 6.7 %collective-permute-done.86 = bf16[192,1280]{1,0:T(8,128)(2,1)} collective-permute-done((bf16[192,1280]{1,0:T(8,128)(2,1)}, bf16[192,1280]{1,0:T(8,128)(2,1)}, u32[]{:S(2)}, u32[]{:S(2)}) %collective-permute-start.86) | collective-permute-done | bytes 491552 | tf_op jit(solution)/shard_map/ppermute | solution.py:73
  587.6 4.3 all-to-all-start.2
  594.5 3.0 collective-permute-start.90
  599.8 3.7 fusion.2
  603.5 5.4 collective-permute-done.89
  (400 shorter events, 157.9 us)
Async XLA Ops:
  10.3 34.8 %all-to-all-start = ((bf16[2,8,144,512]{3,2,0,1:T(8,128)(2,1)}), bf16[2,8,144,512]{3,2,0,1:T(8,128)(2,1)S(1)}, u32[]{:S(2)}, u32[]{:S(2)}) async-start(bf16[2,8,144,512]{3,2,0,1:T(8,128)(2,1)} %bitcast.58), calls=%async_computation | async-start | bytes 4718592 | tf_op jit(solution)/shard_map/all_to_all | solution.py:1007
  15.6 156.2 %all-gather.3.cloned.1.call-start = ((), (), s32[]{:S(2)}) async-start(), calls=%async_computation.5 | async-start | bytes 5898240 | tf_op jit(solution)/shard_map/all_gather | solution.py:1010
  46.7 241.9 %all-gather.5.cloned.1.call-start = ((), (), s32[]{:S(2)}) async-start(), calls=%async_computation.6 | async-start | bytes 5898240 | tf_op jit(solution)/shard_map/all_gather | solution.py:1010
  46.9 21.9 %collective-permute-start.5 = (bf16[192,2688]{1,0:T(8,128)(2,1)S(1)}, bf16[192,2688]{1,0:T(8,128)(2,1)}, u32[]{:S(2)}, u32[]{:S(2)}) collective-permute-start(bf16[192,2688]{1,0:T(8,128)(2,1)S(1)} %pad_maximum_fusion.2.refs_0_), channel_id=1, source_target_pairs={{0,4},{1,5},{2,6},{3,7},{4,0},{5,1},{6,2},{7,3},{8,12},{9,13},{10,... | collective-permute-start | bytes 3096584 | tf_op jit(solution)/shard_map/ppermute | solution.py:73
  47.5 23.2 %collective-permute-start.4 = (bf16[192,2688]{1,0:T(8,128)(2,1)S(1)}, bf16[192,2688]{1,0:T(8,128)(2,1)}, u32[]{:S(2)}, u32[]{:S(2)}) collective-permute-start(bf16[192,2688]{1,0:T(8,128)(2,1)S(1)} %pad_maximum_fusion.2.refs_0_), channel_id=1, source_target_pairs={{0,2},{1,3},{2,0},{3,1},{4,6},{5,7},{6,4},{7,5},{8,10},{9,11},{10,... | collective-permute-start | bytes 3096584 | tf_op jit(solution)/shard_map/ppermute | solution.py:73
  54.2 24.2 %collective-permute-start.10 = (bf16[192,2688]{1,0:T(8,128)(2,1)S(1)}, bf16[192,2688]{1,0:T(8,128)(2,1)}, u32[]{:S(2)}, u32[]{:S(2)}) collective-permute-start(bf16[192,2688]{1,0:T(8,128)(2,1)S(1)} %pad_maximum_fusion.2.refs_0_), channel_id=1, source_target_pairs={{0,1},{1,0},{2,3},{3,2},{4,5},{5,4},{6,7},{7,6},{8,9},{9,8},{10,11... | collective-permute-start | bytes 3096584 | tf_op jit(solution)/shard_map/ppermute | solution.py:73
  93.9 23.6 %collective-permute-start.19 = (bf16[192,1536]{1,0:T(8,128)(2,1)S(1)}, bf16[192,1536]{1,0:T(8,128)(2,1)S(1)}, u32[]{:S(2)}, u32[]{:S(2)}) collective-permute-start(bf16[192,1536]{1,0:T(8,128)(2,1)S(1)} %pad_maximum_fusion.3.refs_0_), channel_id=1, source_target_pairs={{0,1},{1,0},{2,3},{3,2},{4,5},{5,4},{6,7},{7,6},{8,9},{9,8},{10,11... | collective-permute-start | bytes 1769480 | tf_op jit(solution)/shard_map/ppermute | solution.py:73
  94.1 23.5 %collective-permute-start.18 = (bf16[192,1536]{1,0:T(8,128)(2,1)S(1)}, bf16[192,1536]{1,0:T(8,128)(2,1)}, u32[]{:S(2)}, u32[]{:S(2)}) collective-permute-start(bf16[192,1536]{1,0:T(8,128)(2,1)S(1)} %pad_maximum_fusion.3.refs_0_), channel_id=1, source_target_pairs={{0,4},{1,5},{2,6},{3,7},{4,0},{5,1},{6,2},{7,3},{8,12},{9,13},{10,... | collective-permute-start | bytes 1769480 | tf_op jit(solution)/shard_map/ppermute | solution.py:73
  95.0 22.5 %collective-permute-start.17 = (bf16[192,1536]{1,0:T(8,128)(2,1)S(1)}, bf16[192,1536]{1,0:T(8,128)(2,1)}, u32[]{:S(2)}, u32[]{:S(2)}) collective-permute-start(bf16[192,1536]{1,0:T(8,128)(2,1)S(1)} %pad_maximum_fusion.3.refs_0_), channel_id=1, source_target_pairs={{0,2},{1,3},{2,0},{3,1},{4,6},{5,7},{6,4},{7,5},{8,10},{9,11},{10,... | collective-permute-start | bytes 1769480 | tf_op jit(solution)/shard_map/ppermute | solution.py:73
  114.3 20.7 %collective-permute-start.21 = (bf16[256,1536]{1,0:T(8,128)(2,1)}, bf16[256,1536]{1,0:T(8,128)(2,1)S(1)}, u32[]{:S(2)}, u32[]{:S(2)}) collective-permute-start(bf16[256,1536]{1,0:T(8,128)(2,1)} %get-tuple-element.365), channel_id=1, source_target_pairs={{0,4},{1,5},{2,6},{3,7},{4,0},{5,1},{6,2},{7,3},{8,12},{9,13},{10,... | collective-permute-start | bytes 2359304 | tf_op jit(solution)/shard_map/ppermute | solution.py:73
  115.5 20.8 %collective-permute-start.20 = (bf16[256,1536]{1,0:T(8,128)(2,1)}, bf16[256,1536]{1,0:T(8,128)(2,1)}, u32[]{:S(2)}, u32[]{:S(2)}) collective-permute-start(bf16[256,1536]{1,0:T(8,128)(2,1)} %get-tuple-element.365), channel_id=1, source_target_pairs={{0,2},{1,3},{2,0},{3,1},{4,6},{5,7},{6,4},{7,5},{8,10},{9,11},{10,... | collective-permute-start | bytes 2359304 | tf_op jit(solution)/shard_map/ppermute | solution.py:73
  117.3 263.7 %reduce-scatter.3.cloned.1.call-start = ((), (), s32[]{:S(2)}) async-start(), calls=%async_computation.7 | async-start | bytes 5898240 | tf_op jit(solution)/shard_map/reduce_scatter | solution.py:1096
  119.7 21.3 %collective-permute-start.23 = (bf16[96,1536]{1,0:T(8,128)(2,1)S(1)}, bf16[96,1536]{1,0:T(8,128)(2,1)S(1)}, u32[]{:S(2)}, u32[]{:S(2)}) collective-permute-start(bf16[96,1536]{1,0:T(8,128)(2,1)S(1)} %slice.129), channel_id=1, source_target_pairs={{0,2},{1,3},{2,0},{3,1},{4,6},{5,7},{6,4},{7,5},{8,10},{9,11},{10,... | collective-permute-start | bytes 884744 | tf_op jit(solution)/shard_map/ppermute | solution.py:73
  120.1 21.0 %collective-permute-start.22 = (bf16[96,1536]{1,0:T(8,128)(2,1)S(1)}, bf16[96,1536]{1,0:T(8,128)(2,1)S(1)}, u32[]{:S(2)}, u32[]{:S(2)}) collective-permute-start(bf16[96,1536]{1,0:T(8,128)(2,1)S(1)} %slice.128), channel_id=1, source_target_pairs={{0,4},{1,5},{2,6},{3,7},{4,0},{5,1},{6,2},{7,3},{8,12},{9,13},{10,... | collective-permute-start | bytes 884744 | tf_op jit(solution)/shard_map/ppermute | solution.py:73
  142.1 20.5 %collective-permute-start.30 = (bf16[256,1536]{1,0:T(8,128)(2,1)}, bf16[256,1536]{1,0:T(8,128)(2,1)S(1)}, u32[]{:S(2)}, u32[]{:S(2)}) collective-permute-start(bf16[256,1536]{1,0:T(8,128)(2,1)} %get-tuple-element.365), channel_id=1, source_target_pairs={{0,1},{1,0},{2,3},{3,2},{4,5},{5,4},{6,7},{7,6},{8,9},{9,8},{10,11... | collective-permute-start | bytes 2359304 | tf_op jit(solution)/shard_map/ppermute | solution.py:73
  145.6 20.1 %collective-permute-start.29 = (bf16[256,1536]{1,0:T(8,128)(2,1)}, bf16[256,1536]{1,0:T(8,128)(2,1)}, u32[]{:S(2)}, u32[]{:S(2)}) collective-permute-start(bf16[256,1536]{1,0:T(8,128)(2,1)} %get-tuple-element.387), channel_id=1, source_target_pairs={{0,4},{1,5},{2,6},{3,7},{4,0},{5,1},{6,2},{7,3},{8,12},{9,13},{10,... | collective-permute-start | bytes 2359304 | tf_op jit(solution)/shard_map/ppermute | solution.py:73
  146.5 19.8 %collective-permute-start.28 = (bf16[256,1536]{1,0:T(8,128)(2,1)}, bf16[256,1536]{1,0:T(8,128)(2,1)}, u32[]{:S(2)}, u32[]{:S(2)}) collective-permute-start(bf16[256,1536]{1,0:T(8,128)(2,1)} %get-tuple-element.387), channel_id=1, source_target_pairs={{0,2},{1,3},{2,0},{3,1},{4,6},{5,7},{6,4},{7,5},{8,10},{9,11},{10,... | collective-permute-start | bytes 2359304 | tf_op jit(solution)/shard_map/ppermute | solution.py:73
  166.3 39.8 %collective-permute-start.34 = (bf16[512,1664]{1,0:T(8,128)(2,1)}, bf16[512,1664]{1,0:T(8,128)(2,1)S(1)}, u32[]{:S(2)}, u32[]{:S(2)}) collective-permute-start(bf16[512,1664]{1,0:T(8,128)(2,1)} %get-tuple-element.469.refs_1_.inner_ref), channel_id=1, source_target_pairs={{0,4},{1,5},{2,6},{3,7},{4,0},{5,1},{6,2},{7,3},{8,12},{9,13},{10,... | collective-permute-start | bytes 5111816 | tf_op jit(solution)/shard_map/ppermute | solution.py:73
  167.5 39.5 %collective-permute-start.33 = (bf16[512,1664]{1,0:T(8,128)(2,1)}, bf16[512,1664]{1,0:T(8,128)(2,1)S(1)}, u32[]{:S(2)}, u32[]{:S(2)}) collective-permute-start(bf16[512,1664]{1,0:T(8,128)(2,1)} %get-tuple-element.469.refs_1_.inner_ref), channel_id=1, source_target_pairs={{0,2},{1,3},{2,0},{3,1},{4,6},{5,7},{6,4},{7,5},{8,10},{9,11},{10,... | collective-permute-start | bytes 5111816 | tf_op jit(solution)/shard_map/ppermute | solution.py:73
  209.9 47.2 %collective-permute-start.38 = (bf16[256,1664]{1,0:T(8,128)(2,1)}, bf16[256,1664]{1,0:T(8,128)(2,1)}, u32[]{:S(2)}, u32[]{:S(2)}) collective-permute-start(bf16[256,1664]{1,0:T(8,128)(2,1)} %slice.133), channel_id=1, source_target_pairs={{0,2},{1,3},{2,0},{3,1},{4,6},{5,7},{6,4},{7,5},{8,10},{9,11},{10,... | collective-permute-start | bytes 2555912 | tf_op jit(solution)/shard_map/ppermute | solution.py:73
  214.3 42.8 %collective-permute-start.37 = (bf16[256,1664]{1,0:T(8,128)(2,1)}, bf16[256,1664]{1,0:T(8,128)(2,1)}, u32[]{:S(2)}, u32[]{:S(2)}) collective-permute-start(bf16[256,1664]{1,0:T(8,128)(2,1)} %slice.132), channel_id=1, source_target_pairs={{0,4},{1,5},{2,6},{3,7},{4,0},{5,1},{6,2},{7,3},{8,12},{9,13},{10,... | collective-permute-start | bytes 2555912 | tf_op jit(solution)/shard_map/ppermute | solution.py:73
  215.5 41.6 %collective-permute-start.39 = (bf16[256,1536]{1,0:T(8,128)(2,1)}, bf16[256,1536]{1,0:T(8,128)(2,1)}, u32[]{:S(2)}, u32[]{:S(2)}) collective-permute-start(bf16[256,1536]{1,0:T(8,128)(2,1)} %collective-permute-done.20.refs_5_), channel_id=1, source_target_pairs={{0,4},{1,5},{2,6},{3,7},{4,0},{5,1},{6,2},{7,3},{8,12},{9,13},{10,... | collective-permute-start | bytes 2359304 | tf_op jit(solution)/shard_map/ppermute | solution.py:73
  217.6 39.5 %collective-permute-start.40 = (bf16[256,1536]{1,0:T(8,128)(2,1)}, bf16[256,1536]{1,0:T(8,128)(2,1)S(1)}, u32[]{:S(2)}, u32[]{:S(2)}) collective-permute-start(bf16[256,1536]{1,0:T(8,128)(2,1)} %collective-permute-done.29.refs_10_), channel_id=1, source_target_pairs={{0,2},{1,3},{2,0},{3,1},{4,6},{5,7},{6,4},{7,5},{8,10},{9,11},{10,... | collective-permute-start | bytes 2359304 | tf_op jit(solution)/shard_map/ppermute | solution.py:73
  288.5 233.8 %reduce-scatter.5.cloned.1.call-start = ((), (), s32[]{:S(2)}) async-start(), calls=%async_computation.8 | async-start | bytes 5898240 | tf_op jit(solution)/shard_map/reduce_scatter | solution.py:1096
  324.0 42.8 %collective-permute-start.51 = (bf16[256,1664]{1,0:T(8,128)(2,1)}, bf16[256,1664]{1,0:T(8,128)(2,1)S(1)}, u32[]{:S(2)}, u32[]{:S(2)}) collective-permute-start(bf16[256,1664]{1,0:T(8,128)(2,1)} %get-tuple-element.429), channel_id=1, source_target_pairs={{0,4},{1,5},{2,6},{3,7},{4,0},{5,1},{6,2},{7,3},{8,12},{9,13},{10,... | collective-permute-start | bytes 2555912 | tf_op jit(solution)/shard_map/ppermute | solution.py:73
  325.1 41.7 %collective-permute-start.52 = (bf16[256,1664]{1,0:T(8,128)(2,1)}, bf16[256,1664]{1,0:T(8,128)(2,1)S(1)}, u32[]{:S(2)}, u32[]{:S(2)}) collective-permute-start(bf16[256,1664]{1,0:T(8,128)(2,1)} %get-tuple-element.430), channel_id=1, source_target_pairs={{0,2},{1,3},{2,0},{3,1},{4,6},{5,7},{6,4},{7,5},{8,10},{9,11},{10,... | collective-permute-start | bytes 2555912 | tf_op jit(solution)/shard_map/ppermute | solution.py:73
  325.5 41.3 %collective-permute-start.53 = (bf16[256,1536]{1,0:T(8,128)(2,1)}, bf16[256,1536]{1,0:T(8,128)(2,1)S(1)}, u32[]{:S(2)}, u32[]{:S(2)}) collective-permute-start(bf16[256,1536]{1,0:T(8,128)(2,1)} %get-tuple-element.431), channel_id=1, source_target_pairs={{0,4},{1,5},{2,6},{3,7},{4,0},{5,1},{6,2},{7,3},{8,12},{9,13},{10,... | collective-permute-start | bytes 2359304 | tf_op jit(solution)/shard_map/ppermute | solution.py:73
  326.4 40.4 %collective-permute-start.54 = (bf16[256,1536]{1,0:T(8,128)(2,1)}, bf16[256,1536]{1,0:T(8,128)(2,1)S(1)}, u32[]{:S(2)}, u32[]{:S(2)}) collective-permute-start(bf16[256,1536]{1,0:T(8,128)(2,1)} %get-tuple-element.432), channel_id=1, source_target_pairs={{0,2},{1,3},{2,0},{3,1},{4,6},{5,7},{6,4},{7,5},{8,10},{9,11},{10,... | collective-permute-start | bytes 2359304 | tf_op jit(solution)/shard_map/ppermute | solution.py:73
  381.0 39.6 %collective-permute-start.57 = (bf16[512,1664]{1,0:T(8,128)(2,1)}, bf16[512,1664]{1,0:T(8,128)(2,1)}, u32[]{:S(2)}, u32[]{:S(2)}) collective-permute-start(bf16[512,1664]{1,0:T(8,128)(2,1)} %bitcast.80), channel_id=1, source_target_pairs={{0,2},{1,3},{2,0},{3,1},{4,6},{5,7},{6,4},{7,5},{8,10},{9,11},{10,... | collective-permute-start | bytes 5111816 | tf_op jit(solution)/shard_map/ppermute | solution.py:73
  381.5 39.3 %collective-permute-start.58 = (bf16[512,1664]{1,0:T(8,128)(2,1)}, bf16[512,1664]{1,0:T(8,128)(2,1)}, u32[]{:S(2)}, u32[]{:S(2)}) collective-permute-start(bf16[512,1664]{1,0:T(8,128)(2,1)} %bitcast.79), channel_id=1, source_target_pairs={{0,4},{1,5},{2,6},{3,7},{4,0},{5,1},{6,2},{7,3},{8,12},{9,13},{10,... | collective-permute-start | bytes 5111816 | tf_op jit(solution)/shard_map/ppermute | solution.py:73
  382.6 23.8 %collective-permute-start.59 = (bf16[512,1536]{1,0:T(8,128)(2,1)}, bf16[512,1536]{1,0:T(8,128)(2,1)S(1)}, u32[]{:S(2)}, u32[]{:S(2)}) collective-permute-start(bf16[512,1536]{1,0:T(8,128)(2,1)} %get-tuple-element.467), channel_id=1, source_target_pairs={{0,1},{1,0},{2,3},{3,2},{4,5},{5,4},{6,7},{7,6},{8,9},{9,8},{10,11... | collective-permute-start | bytes 4718600 | tf_op jit(solution)/shard_map/ppermute | solution.py:73
  382.6 23.9 %collective-permute-start.60 = (bf16[512,1536]{1,0:T(8,128)(2,1)}, bf16[512,1536]{1,0:T(8,128)(2,1)S(1)}, u32[]{:S(2)}, u32[]{:S(2)}) collective-permute-start(bf16[512,1536]{1,0:T(8,128)(2,1)} %get-tuple-element.468), channel_id=1, source_target_pairs={{0,1},{1,0},{2,3},{3,2},{4,5},{5,4},{6,7},{7,6},{8,9},{9,8},{10,11... | collective-permute-start | bytes 4718600 | tf_op jit(solution)/shard_map/ppermute | solution.py:73
  420.9 27.3 %collective-permute-start.64 = (bf16[512,1536]{1,0:T(8,128)(2,1)}, bf16[512,1536]{1,0:T(8,128)(2,1)S(1)}, u32[]{:S(2)}, u32[]{:S(2)}) collective-permute-start(bf16[512,1536]{1,0:T(8,128)(2,1)} %get-tuple-element.493), channel_id=1, source_target_pairs={{0,1},{1,0},{2,3},{3,2},{4,5},{5,4},{6,7},{7,6},{8,9},{9,8},{10,11... | collective-permute-start | bytes 4718600 | tf_op jit(solution)/shard_map/ppermute | solution.py:73
  426.0 22.2 %collective-permute-start.62 = (bf16[256,1536]{1,0:T(8,128)(2,1)}, bf16[256,1536]{1,0:T(8,128)(2,1)S(1)}, u32[]{:S(2)}, u32[]{:S(2)}) collective-permute-start(bf16[256,1536]{1,0:T(8,128)(2,1)} %get-tuple-element.491), channel_id=1, source_target_pairs={{0,2},{1,3},{2,0},{3,1},{4,6},{5,7},{6,4},{7,5},{8,10},{9,11},{10,... | collective-permute-start | bytes 2359304 | tf_op jit(solution)/shard_map/ppermute | solution.py:73
  427.7 20.5 %collective-permute-start.63 = (bf16[256,1536]{1,0:T(8,128)(2,1)}, bf16[256,1536]{1,0:T(8,128)(2,1)S(1)}, u32[]{:S(2)}, u32[]{:S(2)}) collective-permute-start(bf16[256,1536]{1,0:T(8,128)(2,1)} %get-tuple-element.492), channel_id=1, source_target_pairs={{0,4},{1,5},{2,6},{3,7},{4,0},{5,1},{6,2},{7,3},{8,12},{9,13},{10,... | collective-permute-start | bytes 2359304 | tf_op jit(solution)/shard_map/ppermute | solution.py:73
  460.1 26.9 %collective-permute-start.66 = (bf16[256,1536]{1,0:T(8,128)(2,1)S(1)}, bf16[256,1536]{1,0:T(8,128)(2,1)S(1)}, u32[]{:S(2)}, u32[]{:S(2)}) collective-permute-start(bf16[256,1536]{1,0:T(8,128)(2,1)S(1)} %copy-done.76), channel_id=1, source_target_pairs={{0,2},{1,3},{2,0},{3,1},{4,6},{5,7},{6,4},{7,5},{8,10},{9,11},{10,... | collective-permute-start | bytes 2359304 | tf_op jit(solution)/shard_map/ppermute | solution.py:73
  460.8 26.2 %collective-permute-start.67 = (bf16[256,1536]{1,0:T(8,128)(2,1)S(1)}, bf16[256,1536]{1,0:T(8,128)(2,1)S(1)}, u32[]{:S(2)}, u32[]{:S(2)}) collective-permute-start(bf16[256,1536]{1,0:T(8,128)(2,1)S(1)} %copy-done.75), channel_id=1, source_target_pairs={{0,4},{1,5},{2,6},{3,7},{4,0},{5,1},{6,2},{7,3},{8,12},{9,13},{10,... | collective-permute-start | bytes 2359304 | tf_op jit(solution)/shard_map/ppermute | solution.py:73
  462.0 25.0 %collective-permute-start.68 = (bf16[96,1664]{1,0:T(8,128)(2,1)}, bf16[96,1664]{1,0:T(8,128)(2,1)S(1)}, u32[]{:S(2)}, u32[]{:S(2)}) collective-permute-start(bf16[96,1664]{1,0:T(8,128)(2,1)} %get-tuple-element.527), channel_id=1, source_target_pairs={{0,4},{1,5},{2,6},{3,7},{4,0},{5,1},{6,2},{7,3},{8,12},{9,13},{10,... | collective-permute-start | bytes 958472 | tf_op jit(solution)/shard_map/ppermute | solution.py:73
  462.9 24.1 %collective-permute-start.69 = (bf16[96,1664]{1,0:T(8,128)(2,1)}, bf16[96,1664]{1,0:T(8,128)(2,1)S(1)}, u32[]{:S(2)}, u32[]{:S(2)}) collective-permute-start(bf16[96,1664]{1,0:T(8,128)(2,1)} %get-tuple-element.528), channel_id=1, source_target_pairs={{0,2},{1,3},{2,0},{3,1},{4,6},{5,7},{6,4},{7,5},{8,10},{9,11},{10,... | collective-permute-start | bytes 958472 | tf_op jit(solution)/shard_map/ppermute | solution.py:73
  490.7 19.8 %collective-permute-start.71 = (bf16[192,1664]{1,0:T(8,128)(2,1)}, bf16[192,1664]{1,0:T(8,128)(2,1)S(1)}, u32[]{:S(2)}, u32[]{:S(2)}) collective-permute-start(bf16[192,1664]{1,0:T(8,128)(2,1)} %get-tuple-element.552), channel_id=1, source_target_pairs={{0,2},{1,3},{2,0},{3,1},{4,6},{5,7},{6,4},{7,5},{8,10},{9,11},{10,... | collective-permute-start | bytes 1916936 | tf_op jit(solution)/shard_map/ppermute | solution.py:73
  517.0 22.2 %collective-permute-start.76 = (bf16[192,1280]{1,0:T(8,128)(2,1)}, bf16[192,1280]{1,0:T(8,128)(2,1)}, u32[]{:S(2)}, u32[]{:S(2)}) collective-permute-start(bf16[192,1280]{1,0:T(8,128)(2,1)} %get-tuple-element.580), channel_id=1, source_target_pairs={{0,2},{1,3},{2,0},{3,1},{4,6},{5,7},{6,4},{7,5},{8,10},{9,11},{10,... | collective-permute-start | bytes 1474568 | tf_op jit(solution)/shard_map/ppermute | solution.py:73
  517.7 21.5 %collective-permute-start.77 = (bf16[192,1280]{1,0:T(8,128)(2,1)}, bf16[192,1280]{1,0:T(8,128)(2,1)}, u32[]{:S(2)}, u32[]{:S(2)}) collective-permute-start(bf16[192,1280]{1,0:T(8,128)(2,1)} %get-tuple-element.581), channel_id=1, source_target_pairs={{0,4},{1,5},{2,6},{3,7},{4,0},{5,1},{6,2},{7,3},{8,12},{9,13},{10,... | collective-permute-start | bytes 1474568 | tf_op jit(solution)/shard_map/ppermute | solution.py:73
  524.5 43.4 %all-to-all-start.1 = ((bf16[8,144,512]{2,1,0:T(8,128)(2,1)}), bf16[8,144,512]{2,1,0:T(8,128)(2,1)S(1)}, u32[]{:S(2)}, u32[]{:S(2)}) async-start(bf16[8,144,512]{2,1,0:T(8,128)(2,1)} %bitcast.23), calls=%async_computation.3 | async-start | bytes 2359296 | tf_op jit(solution)/shard_map/all_to_all | solution.py:1226
  542.5 25.3 %collective-permute-start.85 = (bf16[48,2944]{1,0:T(8,128)(2,1)}, bf16[48,2944]{1,0:T(8,128)(2,1)}, u32[]{:S(2)}, u32[]{:S(2)}) collective-permute-start(bf16[48,2944]{1,0:T(8,128)(2,1)} %get-tuple-element.723), channel_id=1, source_target_pairs={{0,24},{1,25},{2,26},{3,27},{4,28},{5,29},{6,30},{7,31},{8,0},{9,1... | collective-permute-start | bytes 847880 | tf_op jit(solution)/shard_map/ppermute | solution.py:78
  545.9 24.9 %collective-permute-start.84 = (bf16[48,2944]{1,0:T(8,128)(2,1)}, bf16[48,2944]{1,0:T(8,128)(2,1)}, u32[]{:S(2)}, u32[]{:S(2)}) collective-permute-start(bf16[48,2944]{1,0:T(8,128)(2,1)} %get-tuple-element.724), channel_id=1, source_target_pairs={{0,16},{1,17},{2,18},{3,19},{4,20},{5,21},{6,22},{7,23},{8,24},{9,... | collective-permute-start | bytes 847880 | tf_op jit(solution)/shard_map/ppermute | solution.py:78
  545.9 24.9 %collective-permute-start.83 = (bf16[48,2944]{1,0:T(8,128)(2,1)}, bf16[48,2944]{1,0:T(8,128)(2,1)}, u32[]{:S(2)}, u32[]{:S(2)}) collective-permute-start(bf16[48,2944]{1,0:T(8,128)(2,1)} %get-tuple-element.725), channel_id=1, source_target_pairs={{0,8},{1,9},{2,10},{3,11},{4,12},{5,13},{6,14},{7,15},{8,16},{9,17... | collective-permute-start | bytes 847880 | tf_op jit(solution)/shard_map/ppermute | solution.py:78
  550.7 20.1 %collective-permute-start.81 = (bf16[96,640]{1,0:T(8,128)(2,1)}, bf16[96,640]{1,0:T(8,128)(2,1)}, u32[]{:S(2)}, u32[]{:S(2)}) collective-permute-start(bf16[96,640]{1,0:T(8,128)(2,1)} %get-tuple-element.604), channel_id=1, source_target_pairs={{0,4},{1,5},{2,6},{3,7},{4,0},{5,1},{6,2},{7,3},{8,12},{9,13},{10,... | collective-permute-start | bytes 368648 | tf_op jit(solution)/shard_map/ppermute | solution.py:73
  587.6 24.4 %all-to-all-start.2 = ((bf16[8,144,512]{2,1,0:T(8,128)(2,1)}), bf16[8,144,512]{2,1,0:T(8,128)(2,1)}, u32[]{:S(2)}, u32[]{:S(2)}) async-start(bf16[8,144,512]{2,1,0:T(8,128)(2,1)} %bitcast.69), calls=%async_computation.4 | async-start | bytes 2359296 | tf_op jit(solution)/shard_map/all_to_all | solution.py:1226
  (129 other events, 956.7 us)
Sparse Core Ops, SparseCore 0:
  46.8 92.0 all-gather.2
  140.5 87.9 all-gather.4
  288.6 84.9 reduce-scatter.2
  420.9 86.0 reduce-scatter.4

commit v4 on v3

--- a/solution.py
+++ b/solution.py
@@ -173,6 +173,10 @@
 
 def small_cost():
     return pl.CostEstimate(flops=1_000_000, bytes_accessed=100_000, transcendentals=0)
+
+
+def extras_spec(width):
+    return pl.BlockSpec((width, LANES), lambda *_: (0, (QW + 2 * KW) // LANES))
 
 
 def params():
@@ -515,7 +519,8 @@
     vmem = pl.BlockSpec(memory_space=pltpu.VMEM)
     return pl.pallas_call(
         functools.partial(middle_kernel, plan),
-        in_specs=[smem_spec()] + [vmem] * 5 + [any_spec()] * len(pieces),
+        grid=(1,),
+        in_specs=[smem_spec()] + [vmem] * 3 + [extras_spec(width), vmem] + [any_spec()] * len(pieces),
         out_specs=[any_spec(), vmem, vmem, vmem],
         out_shape=[
             jax.ShapeDtypeStruct((QW, width), bf16),
@@ -534,10 +539,17 @@
 
 
 def middle_back_kernel(blocks, table_ref, own0_ref, own1_ref, near2_ref, near4_ref, inner_ref, mix_ref, middle_ref,
-                       cot_ref, extras_ref, attn0_ref, attn1_ref, w_ref, *refs):
+                       cot_ref, extras_ref, attn0_src, attn1_src, w_src, *refs):
     dests = refs[:blocks]
-    grad_ref, attn_grad0_ref, attn_grad1_ref, wgrad_ref, sems = refs[blocks:]
+    (grad_ref, attn_grad0_ref, attn_grad1_ref, wgrad_ref, attn0_ref, attn1_ref, w_ref, sems,
+     load_sems) = refs[blocks:]
     rows, width = middle_ref.shape
+    loads = [
+        pltpu.make_async_copy(a, b, load_sems.at[q])
+        for q, (a, b) in enumerate(((w_src, w_ref), (attn0_src, attn0_ref), (attn1_src, attn1_ref)))
+    ]
+    for c in loads:
+        c.start()
     total = own0_ref[...].astype(f32) + own1_ref[...].astype(f32)
     total = total + near2_ref[...].astype(f32) + near4_ref[...].astype(f32)
     inner_grad, tail = total[:, :width], total[:, width:]
@@ -558,6 +570,8 @@
     grad_ref[...] = middle_grad
     proj_grad = (resid_scale * middle_grad).astype(bf16)
     half = attn0_ref.shape[1]
+    for c in loads:
+        c.wait()
     attn_grad0_ref[...] = contract_last(proj_grad, w_ref[:half]).astype(bf16)
     attn_grad1_ref[...] = contract_last(proj_grad, w_ref[half:]).astype(bf16)
     wgrad_ref[:half, :width] = contract_rows(attn0_ref[...], proj_grad).astype(bf16)
@@ -577,14 +591,19 @@
     full = width + LANES
     return pl.pallas_call(
         functools.partial(middle_back_kernel, min(members, 2)),
-        in_specs=[smem_spec()] + [vmem] * 12,
+        grid=(1,),
+        in_specs=[smem_spec()] + [vmem] * 8 + [extras_spec(width)] + [any_spec()] * 3,
         out_specs=[any_spec()] * min(members, 2) + [vmem] * 3,
         out_shape=stack_shapes(table, width, full)
         + [jax.ShapeDtypeStruct((rows, width), f32)]
         + [jax.ShapeDtypeStruct((rows, QW // 2), bf16)] * 2,
         scratch_shapes=[
             pltpu.VMEM((width, full), bf16),
+            pltpu.VMEM((rows, QW // 2), bf16),
+            pltpu.VMEM((rows, QW // 2), bf16),
+            pltpu.VMEM(w_out.shape, bf16),
             pltpu.SemaphoreType.DMA((members * layers,)),
+            pltpu.SemaphoreType.DMA((3,)),
         ],
         compiler_params=params(),
         cost_estimate=small_cost(),
@@ -757,6 +776,7 @@
     prevs = take(2) if has_prev else None
     acc = take(3)
     held = take(3) if packed else weights
+    (staged,) = take(1) if packed and last else (None,)
     sem_in, sem_out, sem_sum, sem_w = take(4)
     i = pl.program_id(0)
     count = len(x_counts)
@@ -787,11 +807,23 @@
                 out.append(pltpu.make_async_copy(r, dst.at[slot, pl.ds(row, rows)], sem_in.at[slot, number]))
                 row += rows
                 number += 1
-        if has_prev:
-            for r, dst in zip(prev_src[t], prevs):
-                out.append(pltpu.make_async_copy(r, dst.at[slot], sem_in.at[slot, number]))
-                number += 1
         return out
+
+    def prev_loads(t):
+        if not has_prev:
+            return []
+        slot = t % 2
+        return [
+            pltpu.make_async_copy(r, dst.at[slot], sem_in.at[slot, 4 + q])
+            for q, (r, dst) in enumerate(zip(prev_src[t], prevs))
+        ]
+
+    def sum_stores():
+        if last and packed:
+            return [pltpu.make_async_copy(staged, sums_dst[0], sem_sum.at[0])]
+        if last:
+            return []
+        return [pltpu.make_async_copy(a, d, sem_sum.at[q]) for q, (a, d) in enumerate(zip(acc, sums_dst))]
 
     def stores(t):
         slot = t % 2
@@ -810,6 +842,8 @@
         if packed:
             for c in weight_loads():
                 c.start()
+        for c in prev_loads(0):
+            c.start()
         if has_sums:
             for c in sum_loads():
                 c.start()
@@ -826,7 +860,7 @@
             for c in loads(t):
                 c.wait()
             if t + 1 < count:
-                for c in loads(t + 1):
+                for c in loads(t + 1) + prev_loads(t + 1):
                     c.start()
             if t >= 2:
                 for c in stores(t - 2):
@@ -851,9 +885,40 @@
     mid_grad = contract_last(out_grad, w_down)
     gate_grad = (mid_grad * up_proj * sigmoid_g * (1.0 + gate_proj * (1.0 - sigmoid_g))).astype(bf16)
     up_grad = (mid_grad * active).astype(bf16)
-    out_rows = matmul(mid, w_down)
     mix = jnp.sum(mid.astype(f32) * mid_grad, axis=-1, keepdims=True)
-    mixed = gate_row * out_rows
+    if has_sums:
+        @pl.when(i == 0)
+        def _():
+            for c in sum_loads():
+                c.wait()
+    acc[0][...] += contract_rows(rows_in, gate_grad)
+    acc[1][...] += contract_rows(rows_in, up_grad)
+    acc[2][...] += contract_rows(mid, out_grad)
+
+    @pl.when(i == count - 1)
+    def _():
+        if last and packed:
+            layers, members, own, _ = held[0].shape
+            low = held[2].shape[2]
+            staged[:, :, :own] = acc[0][...].astype(bf16).reshape(layers, members, own, hidden)
+            staged[:, :, own : 2 * own] = acc[1][...].astype(bf16).reshape(layers, members, own, hidden)
+            for third in range(width // hidden):
+                piece = acc[2][:, third * hidden : (third + 1) * hidden].astype(bf16)
+                start = 2 * own + third * low
+                staged[:, :, start : start + low] = piece.reshape(layers, members, low, hidden)
+        elif last:
+            for a, d in zip(acc, sums_dst):
+                d[...] = a[...].astype(bf16)
+        for c in sum_stores():
+            c.start()
+
+    if has_prev:
+        for t in range(count):
+            @pl.when(i == t)
+            def _(t=t):
+                for c in prev_loads(t):
+                    c.wait()
+    mixed = gate_row * matmul(mid, w_down)
     if has_prev:
         mixed = mixed + prevs[0][slot].astype(f32)
     og_out[slot] = mixed.astype(bf16)
@@ -873,36 +938,11 @@
         def _(t=t):
             for c in stores(t):
                 c.start()
-    if has_sums:
-        @pl.when(i == 0)
-        def _():
-            for c in sum_loads():
-                c.wait()
-    acc[0][...] += contract_rows(rows_in, gate_grad)
-    acc[1][...] += contract_rows(rows_in, up_grad)
-    acc[2][...] += contract_rows(mid, out_grad)
 
     @pl.when(i == count - 1)
     def _():
-        if last and packed:
-            out = sums_dst[0]
-            layers, members, own, _ = held[0].shape
-            low = held[2].shape[2]
-            out[:, :, :own] = acc[0][...].astype(bf16).reshape(layers, members, own, hidden)
-            out[:, :, own : 2 * own] = acc[1][...].astype(bf16).reshape(layers, members, own, hidden)
-            for third in range(width // hidden):
-                piece = acc[2][:, third * hidden : (third + 1) * hidden].astype(bf16)
-                start = 2 * own + third * low
-                out[:, :, start : start + low] = piece.reshape(layers, members, low, hidden)
-        elif last:
-            for a, d in zip(acc, sums_dst):
-                d[...] = a[...].astype(bf16)
-        else:
-            copies = [pltpu.make_async_copy(a, d, sem_sum.at[q]) for q, (a, d) in enumerate(zip(acc, sums_dst))]
-            for c in copies:
-                c.start()
-            for c in copies:
-                c.wait()
+        for c in sum_stores():
+            c.wait()
         for t in range(max(0, count - 2), count):
             for c in stores(t):
                 c.wait()
@@ -937,7 +977,7 @@
     sum_shapes = ((width, hidden), (width, hidden), (hidden, width))
     if packed and last:
         shapes.append(jax.ShapeDtypeStruct(weights[0].shape, bf16))
-        out_specs.append(whole_spec(weights[0].shape))
+        out_specs.append(anyspace)
         sum_shapes = ()
     for shape in sum_shapes:
         shapes.append(jax.ShapeDtypeStruct(shape, bf16 if last else f32))
@@ -957,6 +997,8 @@
             pltpu.VMEM((layers, GROUP, own, hidden), bf16),
             pltpu.VMEM((layers, GROUP, low, width), bf16),
         ]
+    if packed and last:
+        scratch.append(pltpu.VMEM(weights[0].shape, bf16))
     scratch += [pltpu.SemaphoreType.DMA(shape) for shape in ((2, 6), (2, 2), (3,), (2 + width // hidden,))]
     out = pl.pallas_call(
         functools.partial(experts_kernel, [len(t) for t in tiles], [len(c) for c in cots], expert, packed,
@@ -1062,11 +1104,11 @@
     table, ring_table = table.astype(jnp.int32), ring_table.astype(jnp.int32)
 
     gathered_first, gathered_second = over_all(expert_rows[0]), over_all(expert_rows[1])
+    c_own = cores(c_low, c_high)
     w_qkv, normed, turned, *first_half = attend_forward(
         0, half, ring_table, plan, pieces, hidden_in, cosine, sine_val, segment
     )
-    extras_full = w_qkv[:, QW + 2 * KW :]
-    normed, c_low = tie(normed, c_low)
+    normed, c_low, c_own = tie(normed, c_low, c_own)
     if split:
         wo_near, wo_other, normed = tie(wo_near, wo_other, normed)
         wo_far = far_ways(wo_near)
@@ -1074,22 +1116,19 @@
     second_half = attend_forward(half, half, table, None, w_qkv, normed, cosine, sine_val, segment)
     attn_out = (first_half[3], second_half[3])
     if split:
-        attn_out, c_near_low, c_high, wo_far, wo_near = tie(attn_out, c_near_low, c_high, wo_far, wo_near)
-    else:
-        attn_out, c_near_low, c_high = tie(attn_out, c_near_low, c_high)
-    if split:
+        attn_out, c_high, wo_far, wo_near = tie(attn_out, c_high, wo_far, wo_near)
         out_pieces = in_order(wo_column, [wo_other, *cores(*wo_near)], wo_near, wo_far)
         out_pieces, c_high = tie(out_pieces, c_high)
     else:
+        attn_out, c_high = tie(attn_out, c_high)
         out_pieces = [lax.all_gather(w_out, "fsdp", axis=0, tiled=True)]
 
     c_near_high = near(c_high)
-    c_other = [cores(c_low, *c_near_low)]
     w_out_full, middle, inner, mix = to_middle(
-        ring_table, plan, out_pieces, hidden_in, attn_out, extras_full, routes
+        ring_table, plan, out_pieces, hidden_in, attn_out, w_qkv, routes
     )
-    c_near_high, c_other, inner = tie(c_near_high, c_other, inner)
-    c_other.append(cores(c_high, *c_near_high))
+    c_near_low, inner = tie(c_near_low, inner)
+    c_core_low = cores(*c_near_low)
 
     def expert_sums(sums):
         if len(sums) == 1:
@@ -1122,16 +1161,18 @@
         return sums
 
     inner_near = gather_start(inner, n)
-    x_own, c_own = [[inner], [core(inner)]], [[cotangent], [c_other[0][0], c_other[1][0]]]
+    inner_other = core(inner)
+    inner_other, c_core_low = tie(inner_other, c_core_low)
+    x_own, c_own = [[inner], [inner_other]], [[cotangent], c_own]
     sums = run(0, [0, 1], x_own, c_own, first, None, False)
-    inner_near = after(inner_near, sums)
+    inner_near, c_near_high, sums = tie(inner_near, c_near_high, sums)
+    c_core_high = cores(*c_near_high)
     inner_far = gather_far(*inner_near, n)
-    c_near_low, c_near_high, sums = tie(c_near_low, c_near_high, sums)
     cots_far = swap(c_near_low[0], 4, n), swap(c_near_high[1], 2, n)
     x_near = [[inner_near[0]], [core(inner_near[0])], [inner_near[1]], [core(inner_near[1])]]
     c_near = []
     for q in (0, 1):
-        c_near += [[c_near_low[q], c_near_high[q]], [c_other[0][1 + q], c_other[1][1 + q]]]
+        c_near += [[c_near_low[q], c_near_high[q]], [c_core_low[q], c_core_high[q]]]
     sums = run(0, [2, 3, 4, 5], x_near, c_near, first, sums, False)
     inner_far, cots_far = after((inner_far, cots_far), sums)
     x_far = [list(inner_far), [core(v) for v in inner_far]]
@@ -1150,7 +1191,8 @@
     part.update(zip((2, 3, 4, 5), done))
     near_sums = sums_for_near(part[2][1], core(part[3][1]), part[4][1], core(part[5][1]), *far_sums)
     x_own[0], near_sums, shared0 = tie(x_own[0], near_sums, shared0)
-    inner_near = [swap(value, bit, n) for value, bit in zip(near_sums, (2, 4))]
+    ways = lambda two, four: [swap(two, 2, n), swap(four, 4, n)]
+    inner_near = ways(*near_sums)
     out_core = [core(part[3][0]), core(part[5][0])]
     sums = run(1, [0, 1], x_own, c_own, second, sums, True)
     inner_near, out_core, sums, part[0], part[1] = tie(inner_near, out_core, sums, part[0], part[1])
@@ -1159,10 +1201,10 @@
     out_blocks = (part[2][0], out_core[0], part[4][0], out_core[1])
     out_sums = half_for_near(0, *out_blocks, out_far[0])
     out_sums, inner_other = tie(out_sums, inner_other)
-    out_low = [swap(out_sums[0], 2, n), swap(out_sums[1], 4, n)]
+    out_low = ways(*out_sums)
     out_other = core(part[1][0])
     *out_grads, middle_grad, attn_grad0, attn_grad1 = middle_back(
-        table, (part[0][1], inner_other, *inner_near), inner, mix, middle, cotangent, extras_full, attn_out,
+        table, (part[0][1], inner_other, *inner_near), inner, mix, middle, cotangent, w_qkv, attn_out,
         w_out_full,
     )
     out_low, out_other, out_grads, middle_grad, attn_grad0, attn_grad1 = tie(
@@ -1183,21 +1225,6 @@
         sum2, sum4 = stack_near([(*chips[1:3], *far) for chips, far in sets])
         return swap(sum2, 2, n), swap(sum4, 4, n)
 
-    def over_layers(sets):
-        if not split:
-            sums = [
-                lax.psum_scatter(chips[0], "fsdp", scatter_dimension=0, tiled=True)
-                for group, _ in sets
-                for chips in group
-            ]
-            return [jnp.concatenate(sums, axis=1)]
-        total = []
-        for group, near_sums in sets:
-            own = jnp.concatenate([chips[0] for chips in group], axis=1)
-            total.append((wide(own) + wide(near_sums[0]) + wide(near_sums[1])).astype(bf16))
-        total = jnp.concatenate(total, axis=1)
-        return layer_start(total.reshape(layers, own_rows, -1), layer, layers, n)
-
     def back(base, steps, half_set, grads):
         return attend_backward(
             base, steps, table, turned, *half_set[:3], grads, half_set[4], cosine, sine_val, segment
@@ -1206,7 +1233,7 @@
     wo_chips = chips_of(out_grads)
     out_sums = half_for_near(1, *tie(*out_blocks, middle_grad)[:4], out_far[1])
     attn_grad0, wo_chips, out_sums = tie(attn_grad0, wo_chips, out_sums)
-    out_high = [swap(value, bit, n) for value, bit in zip(out_sums, (2, 4))]
+    out_high = ways(*out_sums)
     wo_far = far_of(wo_chips)
     *stacks0, dq0, dk0, dv0 = back(0, half, first_half, attn_grad0)
     out_high, wo_far, stacks0, dq0, dk0, dv0 = tie(out_high, wo_far, stacks0, dq0, dk0, dv0)
@@ -1214,41 +1241,51 @@
     chips0 = chips_of(stacks0)
     attn_grad1, chips0 = tie(attn_grad1, chips0)
     wo_near, far0 = near_of((wo_chips, wo_far)), far_of(chips0)
-    *stacks1, dq1, dk1, dv1 = back(0, half // 2, second_half, attn_grad1)
-    wo_near, far0, stacks1, dq1, dk1, dv1 = tie(wo_near, far0, stacks1, dq1, dk1, dv1)
+    *stacks1, dq1, dk1, dv1 = back(0, half, second_half, attn_grad1)
+    wo_near, far0, stacks1, dq1, dk1, dv1, shared1 = tie(wo_near, far0, stacks1, dq1, dk1, dv1, shared1)
+
+    def to_owner(block):
+        return lax.all_to_all(block, "fsdp", 0, 0, tiled=True, axis_index_groups=inside)
+
+    def summed(group, near_sums):
+        own = jnp.concatenate([chips[0] for chips in group], axis=1)
+        return (wide(own) + wide(near_sums[0]) + wide(near_sums[1])).astype(bf16)
 
     chips1 = chips_of(stacks1)
-    attn_grad1, chips1, dq1, shared1 = tie(attn_grad1, chips1, dq1, shared1)
+    dq1, chips1 = tie(dq1, chips1)
     near0, far1 = near_of((chips0, far0)), far_of(chips1)
-    *stacks2, dq2, dk2, dv2 = back(half // 2, half - half // 2, second_half, attn_grad1)
-    near0, far1, stacks2, dq2, dk2, dv2, wo_near = tie(near0, far1, stacks2, dq2, dk2, dv2, wo_near)
-
-    to_owner = lambda block: lax.all_to_all(
-        block, "fsdp", 0, 0, tiled=True, axis_index_groups=inside
-    )
-    chips2 = chips_of(stacks2)
-    dq2, chips2 = tie(dq2, chips2)
-    far2 = far_of(chips2)
-    owned0 = to_owner(shared0)
-    early = over_layers([([wo_chips], wo_near), ([chips0], near0)])
-    input_grad = to_input(
-        hidden_in, middle_grad, w_qkv, (dq0, dk0, dv0, dq1, dk1, dv1, dq2, dk2, dv2)
-    )
-    far2, early, input_grad, owned0 = tie(far2, early, input_grad, owned0)
-    near12 = near_of((chips1, far1), (chips2, far2))
-    owned1 = to_owner(after(shared1, near12))
-    out_low, near12 = tie(out_low, near12)
+    if split:
+        wo_shared = lax.psum_scatter(
+            summed([wo_chips], wo_near), "fsdp", scatter_dimension=0, tiled=True, axis_index_groups=along
+        )
+    else:
+        wo_shared = lax.psum_scatter(wo_chips[0], "fsdp", scatter_dimension=0, tiled=True)
+    input_grad = to_input(hidden_in, middle_grad, w_qkv, (dq0, dk0, dv0, dq1, dk1, dv1))
+    near0, far1, input_grad = tie(near0, far1, input_grad)
+    near1 = near_of((chips1, far1))
+    owned = to_owner(jnp.stack([shared0, after(shared1, near1)], axis=1))
+    out_low, near1, wo_shared = tie(out_low, near1, wo_shared)
+    mine_out = wide(wo_shared)
     out_total = wide(part[0][0]) + wide(out_other) + jnp.concatenate(
         [wide(out_low[0]) + wide(out_low[1]), wide(out_high[0]) + wide(out_high[1])], axis=0
     )
     mixed = (middle + resid_scale * out_total).astype(bf16)
-    early = layer_add(early)
-    mine_out = early[:, : width + LANES]
-    late = layer_add(over_layers([([chips1, chips2], near12)]))
-    unit1, unit2 = chips1[0].shape[1], chips2[0].shape[1]
-    mine = [early[:, width + LANES :], late[:, :unit1], late[:, unit1 : unit1 + unit2]]
-
-    shared = jnp.stack([owned0, owned1], axis=1).reshape(E, per_expert, hidden).astype(f32)
+    if split:
+        total = jnp.concatenate([summed([chips0], near0), summed([chips1], near1)], axis=1)
+        late, owned = tie(layer_start(total.reshape(layers, own_rows, -1), layer, layers, n), owned)
+        late = layer_add(late)
+    else:
+        late = jnp.concatenate(
+            [
+                wide(lax.psum_scatter(chips[0], "fsdp", scatter_dimension=0, tiled=True))
+                for chips in (chips0, chips1)
+            ],
+            axis=1,
+        )
+    unit = chips0[0].shape[1]
+    mine = [late[:, :unit], late[:, unit:]]
+
+    shared = owned.reshape(E, per_expert, hidden).astype(f32)
     grad_gate, grad_up = shared[:, :own_rows], shared[:, own_rows : 2 * own_rows]
     grad_down = jnp.concatenate(
         [

time: 635 us -> 620 us (0.976)
  starting transfers between devices: 95.8 us -> 79.5 us
  waiting for transfers between devices: 133 us -> 143 us
    ppermute x14 -> x11, waiting for transfers between devices: 38 us -> 46 us  [shift(): return lax.ppermute(value, 'fsdp', moved)]
    ppermute x14 -> x11, starting transfers between devices: 26.6 us -> 20.3 us  [shift(): return lax.ppermute(value, 'fsdp', moved)]
    ppermute x77 -> x74, starting transfers between devices: 55.5 us -> 49.8 us  [swap(): lax.ppermute(value, 'fsdp', [(i, i ^ bit) for i in range(device_count)])]
    unnamed x163 -> x173, local copies, waits for them, and re-layouts: 21.3 us -> 26.4 us
    pallas_call x3 -> x2, Pallas kernels: 40.1 us -> 36.5 us  [attend_backward(): pl.pallas_call(functools.partial(attend_back_kernel, 128, min(members, 2)...]
    pallas_call x4 -> x3, Pallas kernels: 12.7 us -> 11.4 us  [sums_of_stack(): pl.pallas_call(stack_kernel, in_specs=[vmem] * 2, out_specs=[vmem] * 5, o...]
    ppermute x77 -> x74, waiting for transfers between devices: 90.1 us -> 90.8 us  [swap(): lax.ppermute(value, 'fsdp', [(i, i ^ bit) for i in range(device_count)])]
  transfers between devices with their start and end apart: 98 -> 92, of which waited for: 38 -> 33; matrix products, arithmetic and copies ran while one was open for 5% -> 5% of each run, Pallas kernels for 51% -> 51%
where the time goes in v4:
time: 620 us; the launch traced here: 616 us
  Pallas kernels  315 us (51%)
  waiting for transfers between devices  143 us (23%)
  starting transfers between devices  79.5 us (13%)
  local copies, waits for them, and re-layouts  38.7 us (6%)
  other arithmetic  24.4 us (4%)
  between operations  15.5 us (2%)
    pallas_call x6, Pallas kernels, experts_call(): pl.pallas_call(functools.partial(experts_kernel, [len(t) for t in tiles],...  167 us
    ppermute x74, waiting for transfers between devices, swap(): lax.ppermute(value, 'fsdp', [(i, i ^ bit) for i in range(device_count)])  90.8 us
    ppermute x74, starting transfers between devices, swap(): lax.ppermute(value, 'fsdp', [(i, i ^ bit) for i in range(device_count)])  49.8 us
    ppermute x11, waiting for transfers between devices, shift(): return lax.ppermute(value, 'fsdp', moved)  46 us
    pallas_call x2, Pallas kernels, attend_backward(): pl.pallas_call(functools.partial(attend_back_kernel, 128, min(members, 2)...  36.5 us
    pallas_call x2, Pallas kernels, attend_forward(): pl.pallas_call(functools.partial(attend_kernel, 128, plan), grid=(steps,)...  30.4 us
    unnamed x173, local copies, waits for them, and re-layouts  26.4 us
    ppermute x11, starting transfers between devices, shift(): return lax.ppermute(value, 'fsdp', moved)  20.3 us
  transfers between devices with their start and end apart: 92, of which 33 were waited for; matrix products, arithmetic and copies ran while one was open for 5% of the time, Pallas kernels for 51%

profile of v4, /device:TPU:0, one launch (start us, length us, event | category | flops | bytes accessed | tf_op | source)
XLA Modules:
  0.0 615.9 jit_solution(433298176291111057)
XLA Ops:
  10.3 5.3 all-to-all-start
  16.1 3.7 collective-permute-start.2
  19.8 6.6 %collective-permute-done.2 = bf16[48,2688]{1,0:T(8,128)(2,1)S(1)} collective-permute-done((bf16[48,2688]{1,0:T(8,128)(2,1)S(1)}, bf16[48,2688]{1,0:T(8,128)(2,1)S(1)}, u32[]{:S(2)}, u32[]{:S(2)}) %collective-permute-start.2) | collective-permute-done | bytes 258080 | tf_op jit(solution)/shard_map/ppermute | solution.py:78
  26.4 4.3 collective-permute-start.3
  34.5 5.1 collective-permute-done.1
  40.6 4.5 all-to-all-done
  48.2 3.7 collective-permute-start.7
  54.2 3.2 collective-permute-done.7
  57.3 4.7 collective-permute-done.6
  62.1 6.6 %collective-permute-done.5.refs_4_ = bf16[192,2688]{1,0:T(8,128)(2,1)S(1)} collective-permute-done((bf16[192,2688]{1,0:T(8,128)(2,1)S(1)}, bf16[192,2688]{1,0:T(8,128)(2,1)S(1)}, u32[]{:S(2)}, u32[]{:S(2)}) %collective-permute-start.5) | collective-permute-done | bytes 1032224 | tf_op jit(solution)/shard_map/ppermute | solution.py:73
  77.5 3.6 collective-permute-start.14
  81.4 6.6 %collective-permute-done.14 = bf16[48,768]{1,0:T(8,128)(2,1)S(1)} collective-permute-done((bf16[48,768]{1,0:T(8,128)(2,1)S(1)}, bf16[48,768]{1,0:T(8,128)(2,1)S(1)}, u32[]{:S(2)}, u32[]{:S(2)}) %collective-permute-start.14) | collective-permute-done | bytes 73760 | tf_op jit(solution)/shard_map/ppermute | solution.py:78
  95.7 17.5 %shard_map.229 = (bf16[1536,2688]{1,0:T(8,128)(2,1)}, bf16[512,1536]{1,0:T(8,128)(2,1)}, bf16[1536,512]{1,0:T(8,128)(2,1)}, bf16[512,768]{1,0:T(8,128)(2,1)}, bf...) custom-call(s32[8,4]{1,0:T(8,128)} %get-tuple-element.683.table_ref, ...), custom_call_target="tpu_custom_call" | custom-call | flops 1000000 | bytes 100000 | tf_op jit(solution)/shard_map/pallas_call | solution.py:466
  118.7 12.8 %shard_map.230 = (bf16[512,768]{1,0:T(8,128)(2,1)}, bf16[512,256]{1,0:T(8,128)(2,1)}, bf16[512,256]{1,0:T(8,128)(2,1)}, bf16[512,768]{1,0:T(8,128)(2,1)}, f32[2,512,128]{2,1,0:T(8,128)}) custom-call(s32[8,4]{1,0:T(8,128)} %get-tuple-element.682.table_ref, bf16[512,1536]{1,0:T(8,128)(2,1)} %get-tuple-element.335.x_ref, ...), custom_call_target="tpu_custom_call" | custom-call | flops 1000000 | bytes 100000 | tf_op jit(solution)/shard_map/pallas_call | solution.py:466
  137.1 11.8 %shard_map.231 = (bf16[1536,1536]{1,0:T(8,128)(2,1)}, f32[512,1536]{1,0:T(8,128)}, bf16[512,1664]{1,0:T(8,128)(2,1)}, f32[512,128]{1,0:T(8,128)}) custom-call(s32[8,4]{1,0:T(8,128)} %get-tuple-element.683.table_ref, bf16[512,1536]{1,0:T(8,128)(2,1)} %x_ref.5, bf16[512,768]{1,0:T(8,128)(2,1)} %get-tuple-element.340.attn0_ref.attn0_src, ...), custom_call_target="tpu_custom_call" | custom-call | flops 1000000 | bytes 100000 | tf_op jit(solution)/shard_map/pallas_call | solution.py:520
  158.0 21.4 %shard_map.232 = (bf16[512,1536]{1,0:T(8,128)(2,1)}, bf16[512,1664]{1,0:T(8,128)(2,1)}, bf16[512,1536]{1,0:T(8,128)(2,1)}, bf16[512,1664]{1,0:T(8,128)(2,1)}, f3...) custom-call(s32[1]{0:T(128)} %bitcast.10.refs_0_, ...), custom_call_target="tpu_custom_call" | custom-call | flops 1000000 | bytes 100000 | tf_op jit(solution)/shard_map/pallas_call | solution.py:1003
  179.4 27.2 %collective-permute-done.33.refs_10_ = bf16[256,1536]{1,0:T(8,128)(2,1)} collective-permute-done((bf16[256,1536]{1,0:T(8,128)(2,1)}, bf16[256,1536]{1,0:T(8,128)(2,1)}, u32[]{:S(2)}, u32[]{:S(2)}) %collective-permute-start.33) | collective-permute-done | bytes 786464 | tf_op jit(solution)/shard_map/ppermute | solution.py:73
  212.5 2.7 collective-permute-done.43.refs_8_
  220.2 38.1 %shard_map.233 = (bf16[512,1536]{1,0:T(8,128)(2,1)}, bf16[512,1664]{1,0:T(8,128)(2,1)}, bf16[512,1536]{1,0:T(8,128)(2,1)}, bf16[512,1664]{1,0:T(8,128)(2,1)}, bf...) custom-call(s32[1]{0:T(128)} %bitcast.10.refs_0_, ...), custom_call_target="tpu_custom_call" | custom-call | flops 1000000 | bytes 100000 | tf_op jit(solution)/shard_map/pallas_call | solution.py:1003
  259.4 5.0 collective-permute-done.47.refs_7_
  267.2 22.4 %shard_map.234 = (bf16[512,1536]{1,0:T(8,128)(2,1)}, bf16[512,1664]{1,0:T(8,128)(2,1)}, bf16[512,1536]{1,0:T(8,128)(2,1)}, bf16[512,1664]{1,0:T(8,128)(2,1)}, bf16[4,8,144,512]{3,2,1,0:T(8,128)(2,1)}) custom-call(s32[1]{0:T(128)} %bitcast.10.refs_0_, bf16[256,1664]{1,0:T(8,128)(2,1)} %collective-permute-done.37.refs_1_, ...), custom_call_target="tpu_custom_call" | custom-call | flops 1000000 | bytes 100000 | tf_op jit(solution)/shard_map/pallas_call | solution.py:1003
  289.7 21.7 %shard_map.235 = (bf16[512,1536]{1,0:T(8,128)(2,1)}, bf16[512,1664]{1,0:T(8,128)(2,1)}, bf16[512,1536]{1,0:T(8,128)(2,1)}, bf16[512,1664]{1,0:T(8,128)(2,1)}, f3...) custom-call(s32[1]{0:T(128)} %bitcast.10.refs_0_, bf16[256,1664]{1,0:T(8,128)(2,1)} %collective-permute-done.37.refs_1_, ...), custom_call_target="tpu_custom_call" | custom-call | flops 1000000 | bytes 100000 | tf_op jit(solution)/shard_map/pallas_call | solution.py:1003
  312.0 5.5 collective-permute-done.50
  319.3 5.0 shard_map.236
  328.3 39.9 %shard_map.237 = (bf16[512,1536]{1,0:T(8,128)(2,1)}, bf16[512,1664]{1,0:T(8,128)(2,1)}, bf16[512,1536]{1,0:T(8,128)(2,1)}, bf16[512,1664]{1,0:T(8,128)(2,1)}, bf...) custom-call(s32[1]{0:T(128)} %bitcast.10.refs_0_, ...), custom_call_target="tpu_custom_call" | custom-call | flops 1000000 | bytes 100000 | tf_op jit(solution)/shard_map/pallas_call | solution.py:1003
  369.8 3.3 collective-permute-done.55
  373.1 2.4 collective-permute-done.56
  376.8 5.8 shard_map.238
  384.7 23.6 %shard_map.239 = (bf16[512,1536]{1,0:T(8,128)(2,1)}, bf16[512,1664]{1,0:T(8,128)(2,1)}, bf16[512,1536]{1,0:T(8,128)(2,1)}, bf16[512,1664]{1,0:T(8,128)(2,1)}, bf16[4,8,144,512]{3,2,1,0:T(8,128)(2,1)}) custom-call(s32[1]{0:T(128)} %bitcast.10.refs_0_, bf16[512,1664]{1,0:T(8,128)(2,1)} %get-tuple-element.440.refs_1_.inner_ref, ...), custom_call_target="tpu_custom_call" | custom-call | flops 1000000 | bytes 100000 | tf_op jit(solution)/shard_map/pallas_call | solution.py:1003
  408.3 14.0 %collective-permute-done.57.near2_ref = bf16[512,1664]{1,0:T(8,128)(2,1)} collective-permute-done((bf16[512,1664]{1,0:T(8,128)(2,1)}, bf16[512,1664]{1,0:T(8,128)(2,1)}, u32[]{:S(2)}, u32[]{:S(2)}) %collective-permute-start.57) | collective-permute-done | bytes 1703968 | tf_op jit(solution)/shard_map/ppermute | solution.py:73
  423.1 4.3 shard_map.240
  430.2 18.2 %shard_map.241 = (bf16[768,1664]{1,0:T(8,128)(2,1)}, bf16[768,1664]{1,0:T(8,128)(2,1)}, f32[512,1536]{1,0:T(8,128)}, bf16[512,768]{1,0:T(8,128)(2,1)}, bf16[512,768]{1,0:T(8,128)(2,1)}) custom-call(s32[8,4]{1,0:T(8,128)} %get-tuple-element.682.table_ref, bf16[512,1664]{1,0:T(8,128)(2,1)} %get-tuple-element.465.own0_ref, bf16[512,1664]{1,0:T(8,128)(2,1)} %copy-done.29, ...), custom_call_target="tpu_custom_call" | custom-call | flops 1000000 | bytes 100000 | tf_op jit(solution)/shard_map/pallas_call | solution.py:592
  449.6 4.2 shard_map.243
  456.1 4.2 shard_map.242
  464.3 18.2 %shard_map.244 = (bf16[768,1280]{1,0:T(8,128)(2,1)}, bf16[768,1280]{1,0:T(8,128)(2,1)}, bf16[512,768]{1,0:T(8,128)(2,1)}, bf16[512,256]{1,0:T(8,128)(2,1)}, bf16[512,256]{1,0:T(8,128)(2,1)}) custom-call(s32[8,4]{1,0:T(8,128)} %get-tuple-element.682.table_ref, bf16[1536,512]{1,0:T(8,128)(2,1)} %get-tuple-element.501.turned_ref, ...), custom_call_target="tpu_custom_call" | custom-call | flops 1000000 | bytes 100000 | tf_op jit(solution)/shard_map/pallas_call | solution.py:703
  482.6 4.4 collective-permute-done.68.refs_2_
  487.8 2.7 shard_map.245
  494.2 3.6 shard_map.246
  499.4 18.3 %shard_map.247 = (bf16[768,1280]{1,0:T(8,128)(2,1)}, bf16[768,1280]{1,0:T(8,128)(2,1)}, bf16[512,768]{1,0:T(8,128)(2,1)}, bf16[512,256]{1,0:T(8,128)(2,1)}, bf16[512,256]{1,0:T(8,128)(2,1)}) custom-call(s32[8,4]{1,0:T(8,128)} %get-tuple-element.682.table_ref, bf16[1536,512]{1,0:T(8,128)(2,1)} %get-tuple-element.501.turned_ref, ...), custom_call_target="tpu_custom_call" | custom-call | flops 1000000 | bytes 100000 | tf_op jit(solution)/shard_map/pallas_call | solution.py:703
  517.9 2.5 add_convert_fusion
  520.5 2.4 shard_map.249
  526.6 3.6 shard_map.248
  533.2 12.4 %shard_map.250 = f32[512,1536]{1,0:T(8,128)} custom-call(bf16[512,1536]{1,0:T(8,128)(2,1)} %x_ref.5, f32[512,1536]{1,0:T(8,128)} %get-tuple-element.487.mgrad_ref, bf16[1536,2688]{1,0:T(8,128)(2,1)} %get-tuple-element.336.refs_0_.refs_1_.refs_2_.extras_ref.w_ref, bf16[512,768]{1,0:T(8,128)(2,1)} %get-tuple-element.555.refs_0_, ...), custom_call_target="tpu_custom_call" | custom-call | flops 1000000 | bytes 100000 | tf_op jit(solution)/shard_map/pallas_call | solution.py:754
  547.1 2.3 shard_map.251
  553.2 8.8 %collective-permute-done.80 = bf16[192,1280]{1,0:T(8,128)(2,1)S(1)} collective-permute-done((bf16[192,1280]{1,0:T(8,128)(2,1)}, bf16[192,1280]{1,0:T(8,128)(2,1)S(1)}, u32[]{:S(2)}, u32[]{:S(2)}) %collective-permute-start.80) | collective-permute-done | bytes 491552 | tf_op jit(solution)/shard_map/ppermute | solution.py:73
  565.7 3.7 all-to-all-start.1
  571.9 2.8 collective-permute-start.84
  581.4 15.6 %collective-permute-done.83 = bf16[48,2560]{1,0:T(8,128)(2,1)} collective-permute-done((bf16[48,2560]{1,0:T(8,128)(2,1)}, bf16[48,2560]{1,0:T(8,128)(2,1)}, u32[]{:S(2)}, u32[]{:S(2)}) %collective-permute-start.83) | collective-permute-done | bytes 245792 | tf_op jit(solution)/shard_map/ppermute | solution.py:78
  (394 shorter events, 130.0 us)
Async XLA Ops:
  10.3 34.8 %all-to-all-start = ((bf16[2,8,144,512]{3,2,0,1:T(8,128)(2,1)}), bf16[2,8,144,512]{3,2,0,1:T(8,128)(2,1)S(1)}, u32[]{:S(2)}, u32[]{:S(2)}) async-start(bf16[2,8,144,512]{3,2,0,1:T(8,128)(2,1)} %bitcast.46), calls=%async_computation | async-start | bytes 4718592 | tf_op jit(solution)/shard_map/all_to_all | solution.py:1049
  15.6 142.4 %all-gather.3.cloned.1.call-start = ((), (), s32[]{:S(2)}) async-start(), calls=%async_computation.5 | async-start | bytes 5898240 | tf_op jit(solution)/shard_map/all_gather | solution.py:1052
  46.7 243.0 %all-gather.5.cloned.1.call-start = ((), (), s32[]{:S(2)}) async-start(), calls=%async_computation.6 | async-start | bytes 5898240 | tf_op jit(solution)/shard_map/all_gather | solution.py:1052
  46.9 21.8 %collective-permute-start.5 = (bf16[192,2688]{1,0:T(8,128)(2,1)S(1)}, bf16[192,2688]{1,0:T(8,128)(2,1)S(1)}, u32[]{:S(2)}, u32[]{:S(2)}) collective-permute-start(bf16[192,2688]{1,0:T(8,128)(2,1)S(1)} %pad_maximum_fusion.2.refs_0_), channel_id=1, source_target_pairs={{0,4},{1,5},{2,6},{3,7},{4,0},{5,1},{6,2},{7,3},{8,12},{9,13},{10,... | collective-permute-start | bytes 3096584 | tf_op jit(solution)/shard_map/ppermute | solution.py:73
  47.5 23.1 %collective-permute-start.4 = (bf16[192,2688]{1,0:T(8,128)(2,1)S(1)}, bf16[192,2688]{1,0:T(8,128)(2,1)S(1)}, u32[]{:S(2)}, u32[]{:S(2)}) collective-permute-start(bf16[192,2688]{1,0:T(8,128)(2,1)S(1)} %pad_maximum_fusion.2.refs_0_), channel_id=1, source_target_pairs={{0,2},{1,3},{2,0},{3,1},{4,6},{5,7},{6,4},{7,5},{8,10},{9,11},{10,... | collective-permute-start | bytes 3096584 | tf_op jit(solution)/shard_map/ppermute | solution.py:73
  54.2 22.0 %collective-permute-start.10 = (bf16[192,2688]{1,0:T(8,128)(2,1)S(1)}, bf16[192,2688]{1,0:T(8,128)(2,1)S(1)}, u32[]{:S(2)}, u32[]{:S(2)}) collective-permute-start(bf16[192,2688]{1,0:T(8,128)(2,1)S(1)} %pad_maximum_fusion.2.refs_0_), channel_id=1, source_target_pairs={{0,1},{1,0},{2,3},{3,2},{4,5},{5,4},{6,7},{7,6},{8,9},{9,8},{10,11... | collective-permute-start | bytes 3096584 | tf_op jit(solution)/shard_map/ppermute | solution.py:73
  81.1 301.6 %reduce-scatter.4.cloned.1.call-start = ((), (), s32[]{:S(2)}) async-start(), calls=%async_computation.7 | async-start | bytes 5898240 | tf_op jit(solution)/shard_map/reduce_scatter | solution.py:1135
  91.9 21.4 %collective-permute-start.21 = (bf16[256,1536]{1,0:T(8,128)(2,1)}, bf16[256,1536]{1,0:T(8,128)(2,1)S(1)}, u32[]{:S(2)}, u32[]{:S(2)}) collective-permute-start(bf16[256,1536]{1,0:T(8,128)(2,1)} %get-tuple-element.362), channel_id=1, source_target_pairs={{0,1},{1,0},{2,3},{3,2},{4,5},{5,4},{6,7},{7,6},{8,9},{9,8},{10,11... | collective-permute-start | bytes 2359304 | tf_op jit(solution)/shard_map/ppermute | solution.py:73
  92.0 21.3 %collective-permute-start.20 = (bf16[256,1536]{1,0:T(8,128)(2,1)}, bf16[256,1536]{1,0:T(8,128)(2,1)S(1)}, u32[]{:S(2)}, u32[]{:S(2)}) collective-permute-start(bf16[256,1536]{1,0:T(8,128)(2,1)} %get-tuple-element.359), channel_id=1, source_target_pairs={{0,1},{1,0},{2,3},{3,2},{4,5},{5,4},{6,7},{7,6},{8,9},{9,8},{10,11... | collective-permute-start | bytes 2359304 | tf_op jit(solution)/shard_map/ppermute | solution.py:73
  93.0 20.4 %collective-permute-start.19 = (bf16[192,1536]{1,0:T(8,128)(2,1)S(1)}, bf16[192,1536]{1,0:T(8,128)(2,1)}, u32[]{:S(2)}, u32[]{:S(2)}) collective-permute-start(bf16[192,1536]{1,0:T(8,128)(2,1)S(1)} %pad_maximum_fusion.4.refs_0_), channel_id=1, source_target_pairs={{0,1},{1,0},{2,3},{3,2},{4,5},{5,4},{6,7},{7,6},{8,9},{9,8},{10,11... | collective-permute-start | bytes 1769480 | tf_op jit(solution)/shard_map/ppermute | solution.py:73
  93.2 20.1 %collective-permute-start.18 = (bf16[192,1536]{1,0:T(8,128)(2,1)S(1)}, bf16[192,1536]{1,0:T(8,128)(2,1)S(1)}, u32[]{:S(2)}, u32[]{:S(2)}) collective-permute-start(bf16[192,1536]{1,0:T(8,128)(2,1)S(1)} %pad_maximum_fusion.4.refs_0_), channel_id=1, source_target_pairs={{0,4},{1,5},{2,6},{3,7},{4,0},{5,1},{6,2},{7,3},{8,12},{9,13},{10,... | collective-permute-start | bytes 1769480 | tf_op jit(solution)/shard_map/ppermute | solution.py:73
  93.8 19.6 %collective-permute-start.17 = (bf16[192,1536]{1,0:T(8,128)(2,1)S(1)}, bf16[192,1536]{1,0:T(8,128)(2,1)}, u32[]{:S(2)}, u32[]{:S(2)}) collective-permute-start(bf16[192,1536]{1,0:T(8,128)(2,1)S(1)} %pad_maximum_fusion.4.refs_0_), channel_id=1, source_target_pairs={{0,2},{1,3},{2,0},{3,1},{4,6},{5,7},{6,4},{7,5},{8,10},{9,11},{10,... | collective-permute-start | bytes 1769480 | tf_op jit(solution)/shard_map/ppermute | solution.py:73
  117.8 31.2 %collective-permute-start.29 = (bf16[256,1536]{1,0:T(8,128)(2,1)}, bf16[256,1536]{1,0:T(8,128)(2,1)S(1)}, u32[]{:S(2)}, u32[]{:S(2)}) collective-permute-start(bf16[256,1536]{1,0:T(8,128)(2,1)} %get-tuple-element.359), channel_id=1, source_target_pairs={{0,4},{1,5},{2,6},{3,7},{4,0},{5,1},{6,2},{7,3},{8,12},{9,13},{10,... | collective-permute-start | bytes 2359304 | tf_op jit(solution)/shard_map/ppermute | solution.py:73
  118.3 30.7 %collective-permute-start.28 = (bf16[256,1536]{1,0:T(8,128)(2,1)}, bf16[256,1536]{1,0:T(8,128)(2,1)}, u32[]{:S(2)}, u32[]{:S(2)}) collective-permute-start(bf16[256,1536]{1,0:T(8,128)(2,1)} %get-tuple-element.359), channel_id=1, source_target_pairs={{0,2},{1,3},{2,0},{3,1},{4,6},{5,7},{6,4},{7,5},{8,10},{9,11},{10,... | collective-permute-start | bytes 2359304 | tf_op jit(solution)/shard_map/ppermute | solution.py:73
  150.0 57.7 %collective-permute-start.31 = (bf16[512,1664]{1,0:T(8,128)(2,1)}, bf16[512,1664]{1,0:T(8,128)(2,1)S(1)}, u32[]{:S(2)}, u32[]{:S(2)}) collective-permute-start(bf16[512,1664]{1,0:T(8,128)(2,1)} %get-tuple-element.440.refs_1_.inner_ref), channel_id=1, source_target_pairs={{0,4},{1,5},{2,6},{3,7},{4,0},{5,1},{6,2},{7,3},{8,12},{9,13},{10,... | collective-permute-start | bytes 5111816 | tf_op jit(solution)/shard_map/ppermute | solution.py:73
  151.3 56.4 %collective-permute-start.30 = (bf16[512,1664]{1,0:T(8,128)(2,1)}, bf16[512,1664]{1,0:T(8,128)(2,1)S(1)}, u32[]{:S(2)}, u32[]{:S(2)}) collective-permute-start(bf16[512,1664]{1,0:T(8,128)(2,1)} %get-tuple-element.440.refs_1_.inner_ref), channel_id=1, source_target_pairs={{0,2},{1,3},{2,0},{3,1},{4,6},{5,7},{6,4},{7,5},{8,10},{9,11},{10,... | collective-permute-start | bytes 5111816 | tf_op jit(solution)/shard_map/ppermute | solution.py:73
  155.7 50.9 %collective-permute-start.33 = (bf16[256,1536]{1,0:T(8,128)(2,1)}, bf16[256,1536]{1,0:T(8,128)(2,1)}, u32[]{:S(2)}, u32[]{:S(2)}) collective-permute-start(bf16[256,1536]{1,0:T(8,128)(2,1)} %get-tuple-element.362), channel_id=1, source_target_pairs={{0,4},{1,5},{2,6},{3,7},{4,0},{5,1},{6,2},{7,3},{8,12},{9,13},{10,... | collective-permute-start | bytes 2359304 | tf_op jit(solution)/shard_map/ppermute | solution.py:73
  156.8 50.9 %collective-permute-start.32 = (bf16[256,1536]{1,0:T(8,128)(2,1)}, bf16[256,1536]{1,0:T(8,128)(2,1)}, u32[]{:S(2)}, u32[]{:S(2)}) collective-permute-start(bf16[256,1536]{1,0:T(8,128)(2,1)} %get-tuple-element.362), channel_id=1, source_target_pairs={{0,2},{1,3},{2,0},{3,1},{4,6},{5,7},{6,4},{7,5},{8,10},{9,11},{10,... | collective-permute-start | bytes 2359304 | tf_op jit(solution)/shard_map/ppermute | solution.py:73
  210.8 47.5 %collective-permute-start.38 = (bf16[256,1664]{1,0:T(8,128)(2,1)}, bf16[256,1664]{1,0:T(8,128)(2,1)}, u32[]{:S(2)}, u32[]{:S(2)}) collective-permute-start(bf16[256,1664]{1,0:T(8,128)(2,1)} %slice.113), channel_id=1, source_target_pairs={{0,2},{1,3},{2,0},{3,1},{4,6},{5,7},{6,4},{7,5},{8,10},{9,11},{10,... | collective-permute-start | bytes 2555912 | tf_op jit(solution)/shard_map/ppermute | solution.py:73
  215.2 43.1 %collective-permute-start.37 = (bf16[256,1664]{1,0:T(8,128)(2,1)}, bf16[256,1664]{1,0:T(8,128)(2,1)}, u32[]{:S(2)}, u32[]{:S(2)}) collective-permute-start(bf16[256,1664]{1,0:T(8,128)(2,1)} %slice.112), channel_id=1, source_target_pairs={{0,4},{1,5},{2,6},{3,7},{4,0},{5,1},{6,2},{7,3},{8,12},{9,13},{10,... | collective-permute-start | bytes 2555912 | tf_op jit(solution)/shard_map/ppermute | solution.py:73
  216.3 41.9 %collective-permute-start.39 = (bf16[256,1536]{1,0:T(8,128)(2,1)}, bf16[256,1536]{1,0:T(8,128)(2,1)}, u32[]{:S(2)}, u32[]{:S(2)}) collective-permute-start(bf16[256,1536]{1,0:T(8,128)(2,1)} %collective-permute-done.28.refs_5_), channel_id=1, source_target_pairs={{0,4},{1,5},{2,6},{3,7},{4,0},{5,1},{6,2},{7,3},{8,12},{9,13},{10,... | collective-permute-start | bytes 2359304 | tf_op jit(solution)/shard_map/ppermute | solution.py:73
  218.4 39.8 %collective-permute-start.40 = (bf16[256,1536]{1,0:T(8,128)(2,1)}, bf16[256,1536]{1,0:T(8,128)(2,1)S(1)}, u32[]{:S(2)}, u32[]{:S(2)}) collective-permute-start(bf16[256,1536]{1,0:T(8,128)(2,1)} %collective-permute-done.33.refs_10_), channel_id=1, source_target_pairs={{0,2},{1,3},{2,0},{3,1},{4,6},{5,7},{6,4},{7,5},{8,10},{9,11},{10,... | collective-permute-start | bytes 2359304 | tf_op jit(solution)/shard_map/ppermute | solution.py:73
  289.6 228.1 %reduce-scatter.6.cloned.1.call-start = ((), (), s32[]{:S(2)}) async-start(), calls=%async_computation.8 | async-start | bytes 5898240 | tf_op jit(solution)/shard_map/reduce_scatter | solution.py:1135
  324.3 44.0 %collective-permute-start.51 = (bf16[256,1664]{1,0:T(8,128)(2,1)}, bf16[256,1664]{1,0:T(8,128)(2,1)S(1)}, u32[]{:S(2)}, u32[]{:S(2)}) collective-permute-start(bf16[256,1664]{1,0:T(8,128)(2,1)} %get-tuple-element.400), channel_id=1, source_target_pairs={{0,4},{1,5},{2,6},{3,7},{4,0},{5,1},{6,2},{7,3},{8,12},{9,13},{10,... | collective-permute-start | bytes 2555912 | tf_op jit(solution)/shard_map/ppermute | solution.py:73
  325.4 42.9 %collective-permute-start.52 = (bf16[256,1664]{1,0:T(8,128)(2,1)}, bf16[256,1664]{1,0:T(8,128)(2,1)S(1)}, u32[]{:S(2)}, u32[]{:S(2)}) collective-permute-start(bf16[256,1664]{1,0:T(8,128)(2,1)} %get-tuple-element.401), channel_id=1, source_target_pairs={{0,2},{1,3},{2,0},{3,1},{4,6},{5,7},{6,4},{7,5},{8,10},{9,11},{10,... | collective-permute-start | bytes 2555912 | tf_op jit(solution)/shard_map/ppermute | solution.py:73
  325.7 42.6 %collective-permute-start.53 = (bf16[256,1536]{1,0:T(8,128)(2,1)}, bf16[256,1536]{1,0:T(8,128)(2,1)S(1)}, u32[]{:S(2)}, u32[]{:S(2)}) collective-permute-start(bf16[256,1536]{1,0:T(8,128)(2,1)} %get-tuple-element.402), channel_id=1, source_target_pairs={{0,4},{1,5},{2,6},{3,7},{4,0},{5,1},{6,2},{7,3},{8,12},{9,13},{10,... | collective-permute-start | bytes 2359304 | tf_op jit(solution)/shard_map/ppermute | solution.py:73
  326.6 41.7 %collective-permute-start.54 = (bf16[256,1536]{1,0:T(8,128)(2,1)}, bf16[256,1536]{1,0:T(8,128)(2,1)S(1)}, u32[]{:S(2)}, u32[]{:S(2)}) collective-permute-start(bf16[256,1536]{1,0:T(8,128)(2,1)} %get-tuple-element.403), channel_id=1, source_target_pairs={{0,2},{1,3},{2,0},{3,1},{4,6},{5,7},{6,4},{7,5},{8,10},{9,11},{10,... | collective-permute-start | bytes 2359304 | tf_op jit(solution)/shard_map/ppermute | solution.py:73
  382.7 39.6 %collective-permute-start.57 = (bf16[512,1664]{1,0:T(8,128)(2,1)}, bf16[512,1664]{1,0:T(8,128)(2,1)}, u32[]{:S(2)}, u32[]{:S(2)}) collective-permute-start(bf16[512,1664]{1,0:T(8,128)(2,1)} %bitcast.67), channel_id=1, source_target_pairs={{0,2},{1,3},{2,0},{3,1},{4,6},{5,7},{6,4},{7,5},{8,10},{9,11},{10,... | collective-permute-start | bytes 5111816 | tf_op jit(solution)/shard_map/ppermute | solution.py:73
  383.0 39.4 %collective-permute-start.58 = (bf16[512,1664]{1,0:T(8,128)(2,1)}, bf16[512,1664]{1,0:T(8,128)(2,1)}, u32[]{:S(2)}, u32[]{:S(2)}) collective-permute-start(bf16[512,1664]{1,0:T(8,128)(2,1)} %bitcast.66), channel_id=1, source_target_pairs={{0,4},{1,5},{2,6},{3,7},{4,0},{5,1},{6,2},{7,3},{8,12},{9,13},{10,... | collective-permute-start | bytes 5111816 | tf_op jit(solution)/shard_map/ppermute | solution.py:73
  384.2 24.1 %collective-permute-start.59 = (bf16[512,1536]{1,0:T(8,128)(2,1)}, bf16[512,1536]{1,0:T(8,128)(2,1)S(1)}, u32[]{:S(2)}, u32[]{:S(2)}) collective-permute-start(bf16[512,1536]{1,0:T(8,128)(2,1)} %get-tuple-element.438), channel_id=1, source_target_pairs={{0,1},{1,0},{2,3},{3,2},{4,5},{5,4},{6,7},{7,6},{8,9},{9,8},{10,11... | collective-permute-start | bytes 4718600 | tf_op jit(solution)/shard_map/ppermute | solution.py:73
  384.2 24.2 %collective-permute-start.60 = (bf16[512,1536]{1,0:T(8,128)(2,1)}, bf16[512,1536]{1,0:T(8,128)(2,1)S(1)}, u32[]{:S(2)}, u32[]{:S(2)}) collective-permute-start(bf16[512,1536]{1,0:T(8,128)(2,1)} %get-tuple-element.439), channel_id=1, source_target_pairs={{0,1},{1,0},{2,3},{3,2},{4,5},{5,4},{6,7},{7,6},{8,9},{9,8},{10,11... | collective-permute-start | bytes 4718600 | tf_op jit(solution)/shard_map/ppermute | solution.py:73
  422.4 143.3 %reduce-scatter.8.cloned.1.call-start = ((), (), s32[]{:S(2)}) async-start(), calls=%async_computation.9 | async-start | bytes 798720 | tf_op jit(solution)/shard_map/reduce_scatter | solution.py:1258
  422.6 25.9 %collective-permute-start.64 = (bf16[512,1536]{1,0:T(8,128)(2,1)}, bf16[512,1536]{1,0:T(8,128)(2,1)S(1)}, u32[]{:S(2)}, u32[]{:S(2)}) collective-permute-start(bf16[512,1536]{1,0:T(8,128)(2,1)} %get-tuple-element.464), channel_id=1, source_target_pairs={{0,1},{1,0},{2,3},{3,2},{4,5},{5,4},{6,7},{7,6},{8,9},{9,8},{10,11... | collective-permute-start | bytes 4718600 | tf_op jit(solution)/shard_map/ppermute | solution.py:73
  427.4 21.0 %collective-permute-start.62 = (bf16[256,1536]{1,0:T(8,128)(2,1)}, bf16[256,1536]{1,0:T(8,128)(2,1)S(1)}, u32[]{:S(2)}, u32[]{:S(2)}) collective-permute-start(bf16[256,1536]{1,0:T(8,128)(2,1)} %get-tuple-element.462), channel_id=1, source_target_pairs={{0,2},{1,3},{2,0},{3,1},{4,6},{5,7},{6,4},{7,5},{8,10},{9,11},{10,... | collective-permute-start | bytes 2359304 | tf_op jit(solution)/shard_map/ppermute | solution.py:73
  429.1 19.5 %collective-permute-start.63 = (bf16[256,1536]{1,0:T(8,128)(2,1)}, bf16[256,1536]{1,0:T(8,128)(2,1)S(1)}, u32[]{:S(2)}, u32[]{:S(2)}) collective-permute-start(bf16[256,1536]{1,0:T(8,128)(2,1)} %get-tuple-element.463), channel_id=1, source_target_pairs={{0,4},{1,5},{2,6},{3,7},{4,0},{5,1},{6,2},{7,3},{8,12},{9,13},{10,... | collective-permute-start | bytes 2359304 | tf_op jit(solution)/shard_map/ppermute | solution.py:73
  460.3 26.7 %collective-permute-start.66 = (bf16[256,1536]{1,0:T(8,128)(2,1)}, bf16[256,1536]{1,0:T(8,128)(2,1)S(1)}, u32[]{:S(2)}, u32[]{:S(2)}) collective-permute-start(bf16[256,1536]{1,0:T(8,128)(2,1)} %get-tuple-element.497), channel_id=1, source_target_pairs={{0,2},{1,3},{2,0},{3,1},{4,6},{5,7},{6,4},{7,5},{8,10},{9,11},{10,... | collective-permute-start | bytes 2359304 | tf_op jit(solution)/shard_map/ppermute | solution.py:73
  460.9 26.2 %collective-permute-start.67 = (bf16[256,1536]{1,0:T(8,128)(2,1)S(1)}, bf16[256,1536]{1,0:T(8,128)(2,1)S(1)}, u32[]{:S(2)}, u32[]{:S(2)}) collective-permute-start(bf16[256,1536]{1,0:T(8,128)(2,1)S(1)} %copy-done.81), channel_id=1, source_target_pairs={{0,4},{1,5},{2,6},{3,7},{4,0},{5,1},{6,2},{7,3},{8,12},{9,13},{10,... | collective-permute-start | bytes 2359304 | tf_op jit(solution)/shard_map/ppermute | solution.py:73
  462.1 24.9 %collective-permute-start.68 = (bf16[96,1664]{1,0:T(8,128)(2,1)}, bf16[96,1664]{1,0:T(8,128)(2,1)S(1)}, u32[]{:S(2)}, u32[]{:S(2)}) collective-permute-start(bf16[96,1664]{1,0:T(8,128)(2,1)} %get-tuple-element.499), channel_id=1, source_target_pairs={{0,4},{1,5},{2,6},{3,7},{4,0},{5,1},{6,2},{7,3},{8,12},{9,13},{10,... | collective-permute-start | bytes 958472 | tf_op jit(solution)/shard_map/ppermute | solution.py:73
  462.9 24.1 %collective-permute-start.69 = (bf16[96,1664]{1,0:T(8,128)(2,1)}, bf16[96,1664]{1,0:T(8,128)(2,1)S(1)}, u32[]{:S(2)}, u32[]{:S(2)}) collective-permute-start(bf16[96,1664]{1,0:T(8,128)(2,1)} %get-tuple-element.500), channel_id=1, source_target_pairs={{0,2},{1,3},{2,0},{3,1},{4,6},{5,7},{6,4},{7,5},{8,10},{9,11},{10,... | collective-permute-start | bytes 958472 | tf_op jit(solution)/shard_map/ppermute | solution.py:73
  490.5 27.2 %collective-permute-start.70 = (bf16[192,1664]{1,0:T(8,128)(2,1)}, bf16[192,1664]{1,0:T(8,128)(2,1)}, u32[]{:S(2)}, u32[]{:S(2)}) collective-permute-start(bf16[192,1664]{1,0:T(8,128)(2,1)} %get-tuple-element.514), channel_id=1, source_target_pairs={{0,2},{1,3},{2,0},{3,1},{4,6},{5,7},{6,4},{7,5},{8,10},{9,11},{10,... | collective-permute-start | bytes 1916936 | tf_op jit(solution)/shard_map/ppermute | solution.py:73
  491.9 25.8 %collective-permute-start.71 = (bf16[192,1664]{1,0:T(8,128)(2,1)}, bf16[192,1664]{1,0:T(8,128)(2,1)}, u32[]{:S(2)}, u32[]{:S(2)}) collective-permute-start(bf16[192,1664]{1,0:T(8,128)(2,1)} %get-tuple-element.515), channel_id=1, source_target_pairs={{0,4},{1,5},{2,6},{3,7},{4,0},{5,1},{6,2},{7,3},{8,12},{9,13},{10,... | collective-permute-start | bytes 1916936 | tf_op jit(solution)/shard_map/ppermute | solution.py:73
  497.8 19.9 %collective-permute-start.73 = (bf16[96,1280]{1,0:T(8,128)(2,1)}, bf16[96,1280]{1,0:T(8,128)(2,1)}, u32[]{:S(2)}, u32[]{:S(2)}) collective-permute-start(bf16[96,1280]{1,0:T(8,128)(2,1)} %get-tuple-element.524), channel_id=1, source_target_pairs={{0,4},{1,5},{2,6},{3,7},{4,0},{5,1},{6,2},{7,3},{8,12},{9,13},{10,... | collective-permute-start | bytes 737288 | tf_op jit(solution)/shard_map/ppermute | solution.py:73
  498.9 18.8 %collective-permute-start.74 = (bf16[96,1280]{1,0:T(8,128)(2,1)}, bf16[96,1280]{1,0:T(8,128)(2,1)}, u32[]{:S(2)}, u32[]{:S(2)}) collective-permute-start(bf16[96,1280]{1,0:T(8,128)(2,1)} %get-tuple-element.525), channel_id=1, source_target_pairs={{0,2},{1,3},{2,0},{3,1},{4,6},{5,7},{6,4},{7,5},{8,10},{9,11},{10,... | collective-permute-start | bytes 737288 | tf_op jit(solution)/shard_map/ppermute | solution.py:73
  522.8 22.8 %collective-permute-start.76 = (bf16[192,1280]{1,0:T(8,128)(2,1)}, bf16[192,1280]{1,0:T(8,128)(2,1)}, u32[]{:S(2)}, u32[]{:S(2)}) collective-permute-start(bf16[192,1280]{1,0:T(8,128)(2,1)} %get-tuple-element.551), channel_id=1, source_target_pairs={{0,2},{1,3},{2,0},{3,1},{4,6},{5,7},{6,4},{7,5},{8,10},{9,11},{10,... | collective-permute-start | bytes 1474568 | tf_op jit(solution)/shard_map/ppermute | solution.py:73
  524.4 21.3 %collective-permute-start.77 = (bf16[192,1280]{1,0:T(8,128)(2,1)}, bf16[192,1280]{1,0:T(8,128)(2,1)}, u32[]{:S(2)}, u32[]{:S(2)}) collective-permute-start(bf16[192,1280]{1,0:T(8,128)(2,1)} %get-tuple-element.552), channel_id=1, source_target_pairs={{0,4},{1,5},{2,6},{3,7},{4,0},{5,1},{6,2},{7,3},{8,12},{9,13},{10,... | collective-permute-start | bytes 1474568 | tf_op jit(solution)/shard_map/ppermute | solution.py:73
  565.7 33.1 %all-to-all-start.1 = ((bf16[8,2,144,512]{3,2,1,0:T(8,128)(2,1)}), bf16[8,2,144,512]{3,2,1,0:T(8,128)(2,1)S(1)}, u32[]{:S(2)}, u32[]{:S(2)}) async-start(bf16[8,2,144,512]{3,2,1,0:T(8,128)(2,1)} %copy.81), calls=%async_computation.4 | async-start | bytes 4718592 | tf_op jit(solution)/shard_map/all_to_all | solution.py:1248
  574.8 22.3 %collective-permute-start.83 = (bf16[48,2560]{1,0:T(8,128)(2,1)}, bf16[48,2560]{1,0:T(8,128)(2,1)}, u32[]{:S(2)}, u32[]{:S(2)}) collective-permute-start(bf16[48,2560]{1,0:T(8,128)(2,1)} %get-tuple-element.670), channel_id=1, source_target_pairs={{0,16},{1,17},{2,18},{3,19},{4,20},{5,21},{6,22},{7,23},{8,24},{9,... | collective-permute-start | bytes 737288 | tf_op jit(solution)/shard_map/ppermute | solution.py:78
  574.8 22.3 %collective-permute-start.82 = (bf16[48,2560]{1,0:T(8,128)(2,1)S(1)}, bf16[48,2560]{1,0:T(8,128)(2,1)}, u32[]{:S(2)}, u32[]{:S(2)}) collective-permute-start(bf16[48,2560]{1,0:T(8,128)(2,1)S(1)} %get-tuple-element.671), channel_id=1, source_target_pairs={{0,8},{1,9},{2,10},{3,11},{4,12},{5,13},{6,14},{7,15},{8,16},{9,17... | collective-permute-start | bytes 737288 | tf_op jit(solution)/shard_map/ppermute | solution.py:78
  (127 other events, 826.1 us)
Sparse Core Ops, SparseCore 0:
  46.8 92.0 all-gather.2
  140.5 87.9 all-gather.4
  289.7 84.6 reduce-scatter.3
  422.5 85.4 reduce-scatter.5
  520.5 22.6 reduce-scatter.7

commit v5 on v4

--- a/solution.py
+++ b/solution.py
@@ -16,6 +16,7 @@
 PAIR_E = E // GROUP
 HEADS_STEP = 2 * HQ // HK
 LANES = 128
+ROW_TILES = 2
 QW = HQ * HD
 KW = HK * HD
 QKV_WIDE = QW + 2 * KW + LANES
@@ -477,23 +478,27 @@
 
 def middle_kernel(plan, table_ref, x_ref, attn0_ref, attn1_ref, extras_ref, routes_ref, *refs):
     sources = refs[: len(plan)]
-    w_out_ref, middle_ref, inner_ref, mix_ref, w_ref, sems, save_sem = refs[len(plan) :]
-    copies = gather_copies(plan, sources, table_ref, w_ref, sems)
-    for c in copies:
-        c.start()
+    w_out_ref, middle_ref, inner_ref, mix_ref, w_ref, gain_ref, sems, save_sem = refs[len(plan) :]
+    step = pl.program_id(0)
+    rows, width = x_ref.shape
+
+    @pl.when(step == 0)
+    def _():
+        copies = gather_copies(plan, sources, table_ref, w_ref, sems)
+        for c in copies:
+            c.start()
+        gain_ref[...] = extras_ref[...].astype(f32).T[GAIN_TWO : GAIN_TWO + 1, :]
+        for c in copies:
+            c.wait()
+        pltpu.make_async_copy(w_ref, w_out_ref, save_sem).start()
+
     extras = extras_ref[...]
-    gains = extras.astype(f32).T
-    rows, width = x_ref.shape
-    for c in copies:
-        c.wait()
-    save = pltpu.make_async_copy(w_ref, w_out_ref, save_sem)
-    save.start()
     half = attn0_ref.shape[1]
     product = matmul(attn0_ref[...], w_ref[:half]) + matmul(attn1_ref[...], w_ref[half:])
     middle = x_ref[...].astype(f32) + resid_scale * product
     middle_ref[...] = middle
     rinv = lax.rsqrt(jnp.mean(middle * middle, axis=-1, keepdims=True) + norm_eps)
-    inner = (middle * rinv * gains[GAIN_TWO : GAIN_TWO + 1, :]).astype(bf16)
+    inner = (middle * rinv * gain_ref[...]).astype(bf16)
     inner_ref[:, :width] = inner
     logits = matmul(inner, extras)
     lane = lax.broadcasted_iota(jnp.int32, logits.shape, 1)
@@ -511,17 +516,22 @@
     low = mix - high - rest
     spread = high + pltpu.roll(rest, E, 1) + pltpu.roll(low, 2 * E, 1)
     inner_ref[:, width:] = spread.astype(bf16)
-    save.wait()
+
+    @pl.when(step == pl.num_programs(0) - 1)
+    def _():
+        pltpu.make_async_copy(w_ref, w_out_ref, save_sem).wait()
 
 
 def to_middle(table, plan, pieces, hidden_in, attn_out, extras, routes):
     rows, width = hidden_in.shape
-    vmem = pl.BlockSpec(memory_space=pltpu.VMEM)
+    tall = functools.partial(row_tiles, rows)
     return pl.pallas_call(
         functools.partial(middle_kernel, plan),
-        grid=(1,),
-        in_specs=[smem_spec()] + [vmem] * 3 + [extras_spec(width), vmem] + [any_spec()] * len(pieces),
-        out_specs=[any_spec(), vmem, vmem, vmem],
+        grid=(ROW_TILES,),
+        in_specs=[smem_spec(), tall(width), tall(QW // 2), tall(QW // 2), extras_spec(width)]
+        + [tall(routes.shape[1])]
+        + [any_spec()] * len(pieces),
+        out_specs=[any_spec(), tall(width), tall(width + LANES), tall(LANES)],
         out_shape=[
             jax.ShapeDtypeStruct((QW, width), bf16),
             jax.ShapeDtypeStruct((rows, width), f32),
@@ -530,6 +540,7 @@
         ],
         scratch_shapes=[
             pltpu.VMEM((QW, width), bf16),
+            pltpu.VMEM((1, width), f32),
             pltpu.SemaphoreType.DMA((sum(len(r) for r in plan),)),
             pltpu.SemaphoreType.DMA(()),
         ],
@@ -732,10 +743,15 @@
 
 
 def input_kernel(x_ref, mgrad_ref, w_ref, *refs):
-    *grads, out_ref = refs
+    *grads, out_ref, gain_ref = refs
+
+    @pl.when(pl.program_id(0) == 0)
+    def _():
+        gain_ref[...] = w_ref[:, QW + 2 * KW :].astype(f32).T[GAIN_ONE : GAIN_ONE + 1, :]
+
     x = x_ref[...].astype(f32)
     rinv = lax.rsqrt(jnp.mean(x * x, axis=-1, keepdims=True) + norm_eps)
-    gain = w_ref[:, QW + 2 * KW :].astype(f32).T[GAIN_ONE : GAIN_ONE + 1, :]
+    gain = gain_ref[...]
     start = [0, QW, QW + KW]
     total = None
     for number, ref in enumerate(grads):
@@ -749,13 +765,20 @@
     out_ref[...] = mgrad_ref[...] + back
 
 
+def row_tiles(rows, width):
+    return pl.BlockSpec((rows // ROW_TILES, width), lambda i: (i, 0))
+
+
 def to_input(hidden_in, middle_grad, w_qkv, grads):
-    vmem = pl.BlockSpec(memory_space=pltpu.VMEM)
+    rows, width = hidden_in.shape
+    tall = row_tiles(rows, width)
     return pl.pallas_call(
         input_kernel,
-        in_specs=[vmem] * (3 + len(grads)),
-        out_specs=vmem,
+        grid=(ROW_TILES,),
+        in_specs=[tall, tall, whole_spec(w_qkv.shape)] + [row_tiles(rows, g.shape[1]) for g in grads],
+        out_specs=tall,
         out_shape=jax.ShapeDtypeStruct(hidden_in.shape, f32),
+        scratch_shapes=[pltpu.VMEM((1, width), f32)],
         compiler_params=params(),
         cost_estimate=small_cost(),
     )(hidden_in, middle_grad, w_qkv, *grads)
@@ -814,7 +837,7 @@
             return []
         slot = t % 2
         return [
-            pltpu.make_async_copy(r, dst.at[slot], sem_in.at[slot, 4 + q])
+            pltpu.make_async_copy(r, dst.at[slot], sem_in.at[slot, 6 + q])
             for q, (r, dst) in enumerate(zip(prev_src[t], prevs))
         ]
 
@@ -999,7 +1022,7 @@
         ]
     if packed and last:
         scratch.append(pltpu.VMEM(weights[0].shape, bf16))
-    scratch += [pltpu.SemaphoreType.DMA(shape) for shape in ((2, 6), (2, 2), (3,), (2 + width // hidden,))]
+    scratch += [pltpu.SemaphoreType.DMA(shape) for shape in ((2, 8), (2, 2), (3,), (2 + width // hidden,))]
     out = pl.pallas_call(
         functools.partial(experts_kernel, [len(t) for t in tiles], [len(c) for c in cots], expert, packed,
                           prev is not None, sums is not None, last),
@@ -1064,7 +1087,8 @@
     segment, position = layout(lengths[0], rows)
     cosine, sine_val = turn_tables(position)
     half = HK // 4
-    c_low, c_high = cotangent[: rows // 2], cotangent[rows // 2 :]
+    c_parts = [cotangent[: rows // 4], cotangent[rows // 4 : rows // 2], cotangent[rows // 2 :]]
+    c_own = core(cotangent)
     near = lambda block: (swap(block, 2, n), swap(block, 4, n))
     cores = lambda *values: [core(value) for value in values]
     if split:
@@ -1086,14 +1110,16 @@
 
         near_qkv = near(column)
         wo_blocks = ring_start(w_out, layers, n)
-        near_qkv, wo_blocks, cosine, sine_val = tie(near_qkv, wo_blocks, cosine, sine_val)
+        near_qkv, wo_blocks, cosine, sine_val, c_own, c_parts = tie(
+            near_qkv, wo_blocks, cosine, sine_val, c_own, c_parts
+        )
         far = far_ways(near_qkv)
         other = cores(column, *near_qkv)
         other, wo_blocks = tie(other, wo_blocks)
         wo_column = joined_rows(ring_end(wo_blocks, layers, n), ring)
         far, other, wo_column = tie(far, other, wo_column)
         pieces = in_order(column, other, near_qkv, far)
-        pieces, wo_column = tie(pieces, wo_column)
+        pieces, wo_column, c_parts = tie(pieces, wo_column, c_parts)
         wo_near, wo_other = near(wo_column), core(wo_column)
         table = own_rows * (GROUP * steps[None, :] + members[:, None])
         ring_table = own_rows * (GROUP * ((layer - steps[None, :]) % layers) + members[:, None])
@@ -1104,31 +1130,34 @@
     table, ring_table = table.astype(jnp.int32), ring_table.astype(jnp.int32)
 
     gathered_first, gathered_second = over_all(expert_rows[0]), over_all(expert_rows[1])
-    c_own = cores(c_low, c_high)
+    c_near = [near(c_parts[0])]
     w_qkv, normed, turned, *first_half = attend_forward(
         0, half, ring_table, plan, pieces, hidden_in, cosine, sine_val, segment
     )
-    normed, c_low, c_own = tie(normed, c_low, c_own)
+    normed, c_near, c_parts = tie(normed, c_near, c_parts)
     if split:
         wo_near, wo_other, normed = tie(wo_near, wo_other, normed)
         wo_far = far_ways(wo_near)
-    c_near_low = near(c_low)
+    c_near.append(near(c_parts[1]))
     second_half = attend_forward(half, half, table, None, w_qkv, normed, cosine, sine_val, segment)
     attn_out = (first_half[3], second_half[3])
     if split:
-        attn_out, c_high, wo_far, wo_near = tie(attn_out, c_high, wo_far, wo_near)
+        attn_out, c_parts, wo_far, wo_near, c_near = tie(attn_out, c_parts, wo_far, wo_near, c_near)
         out_pieces = in_order(wo_column, [wo_other, *cores(*wo_near)], wo_near, wo_far)
-        out_pieces, c_high = tie(out_pieces, c_high)
     else:
-        attn_out, c_high = tie(attn_out, c_high)
+        attn_out, c_parts, c_near = tie(attn_out, c_parts, c_near)
         out_pieces = [lax.all_gather(w_out, "fsdp", axis=0, tiled=True)]
 
-    c_near_high = near(c_high)
+    c_near.append(near(c_parts[2]))
     w_out_full, middle, inner, mix = to_middle(
         ring_table, plan, out_pieces, hidden_in, attn_out, w_qkv, routes
     )
-    c_near_low, inner = tie(c_near_low, inner)
-    c_core_low = cores(*c_near_low)
+    inner_near = gather_start(inner, n)
+    inner_other = core(inner)
+    c_core = [cores(*pair) for pair in c_near[:2]]
+    inner_here, c_near[2] = tie(inner, c_near[2])
+    c_core.append(cores(*c_near[2]))
+    inner_here, inner_other, c_core[:2] = tie(inner_here, inner_other, c_core[:2])
 
     def expert_sums(sums):
         if len(sums) == 1:
@@ -1160,20 +1189,16 @@
         part.update(zip(tiles, done))
         return sums
 
-    inner_near = gather_start(inner, n)
-    inner_other = core(inner)
-    inner_other, c_core_low = tie(inner_other, c_core_low)
-    x_own, c_own = [[inner], [inner_other]], [[cotangent], c_own]
+    x_own, c_own = [[inner_here], [inner_other]], [[cotangent], [c_own]]
     sums = run(0, [0, 1], x_own, c_own, first, None, False)
-    inner_near, c_near_high, sums = tie(inner_near, c_near_high, sums)
-    c_core_high = cores(*c_near_high)
+    inner_near, c_core[2], sums = tie(inner_near, c_core[2], sums)
     inner_far = gather_far(*inner_near, n)
-    cots_far = swap(c_near_low[0], 4, n), swap(c_near_high[1], 2, n)
+    cots_far = swap(c_near[0][0], 4, n), swap(c_near[1][0], 4, n), swap(c_near[2][1], 2, n)
     x_near = [[inner_near[0]], [core(inner_near[0])], [inner_near[1]], [core(inner_near[1])]]
-    c_near = []
+    c_all = []
     for q in (0, 1):
-        c_near += [[c_near_low[q], c_near_high[q]], [c_core_low[q], c_core_high[q]]]
-    sums = run(0, [2, 3, 4, 5], x_near, c_near, first, sums, False)
+        c_all += [[pair[q] for pair in c_near], [pair[q] for pair in c_core]]
+    sums = run(0, [2, 3, 4, 5], x_near, c_all, first, sums, False)
     inner_far, cots_far = after((inner_far, cots_far), sums)
     x_far = [list(inner_far), [core(v) for v in inner_far]]
     c_far = [list(cots_far), [core(v) for v in cots_far]]
@@ -1185,7 +1210,7 @@
     halves, out_halves = sums_for_far([(part[6][i], core(part[7][i])) for i in (1, 0)])
     x_near[0], halves, out_halves = tie(x_near[0], halves, out_halves)
     far_sums, out_far = both_ways(*halves), both_ways(*out_halves)
-    sums = run(1, [2, 3, 4, 5], x_near, c_near, second, sums, False)
+    sums = run(1, [2, 3, 4, 5], x_near, c_all, second, sums, False)
     done = [part[k] for k in (2, 3, 4, 5)]
     far_sums, out_far, sums, done = tie(far_sums, out_far, sums, done)
     part.update(zip((2, 3, 4, 5), done))
@@ -1202,13 +1227,17 @@
     out_sums = half_for_near(0, *out_blocks, out_far[0])
     out_sums, inner_other = tie(out_sums, inner_other)
     out_low = ways(*out_sums)
+    def to_owner(block):
+        return lax.all_to_all(block, "fsdp", 0, 0, tiled=True, axis_index_groups=inside)
+
+    owned0 = to_owner(shared0)
     out_other = core(part[1][0])
     *out_grads, middle_grad, attn_grad0, attn_grad1 = middle_back(
         table, (part[0][1], inner_other, *inner_near), inner, mix, middle, cotangent, w_qkv, attn_out,
         w_out_full,
     )
-    out_low, out_other, out_grads, middle_grad, attn_grad0, attn_grad1 = tie(
-        out_low, out_other, out_grads, middle_grad, attn_grad0, attn_grad1
+    out_low, out_other, owned0, out_grads, middle_grad, attn_grad0, attn_grad1 = tie(
+        out_low, out_other, owned0, out_grads, middle_grad, attn_grad0, attn_grad1
     )
 
     wide = lambda value: value.astype(f32)
@@ -1219,11 +1248,11 @@
     def far_of(chips):
         return both_ways(*chips[3:]) if split else ()
 
-    def near_of(*sets):
-        if not split:
-            return ()
-        sum2, sum4 = stack_near([(*chips[1:3], *far) for chips, far in sets])
-        return swap(sum2, 2, n), swap(sum4, 4, n)
+    def near_sums_of(chips, far):
+        return stack_near([(*chips[1:3], *far)]) if split else ()
+
+    def near_of(chips, far):
+        return [swap(value, bit, n) for value, bit in zip(near_sums_of(chips, far), (2, 4))]
 
     def back(base, steps, half_set, grads):
         return attend_backward(
@@ -1240,12 +1269,9 @@
 
     chips0 = chips_of(stacks0)
     attn_grad1, chips0 = tie(attn_grad1, chips0)
-    wo_near, far0 = near_of((wo_chips, wo_far)), far_of(chips0)
+    wo_near, far0 = near_of(wo_chips, wo_far), far_of(chips0)
     *stacks1, dq1, dk1, dv1 = back(0, half, second_half, attn_grad1)
     wo_near, far0, stacks1, dq1, dk1, dv1, shared1 = tie(wo_near, far0, stacks1, dq1, dk1, dv1, shared1)
-
-    def to_owner(block):
-        return lax.all_to_all(block, "fsdp", 0, 0, tiled=True, axis_index_groups=inside)
 
     def summed(group, near_sums):
         own = jnp.concatenate([chips[0] for chips in group], axis=1)
@@ -1253,7 +1279,7 @@
 
     chips1 = chips_of(stacks1)
     dq1, chips1 = tie(dq1, chips1)
-    near0, far1 = near_of((chips0, far0)), far_of(chips1)
+    near0, far1 = near_of(chips0, far0), far_of(chips1)
     if split:
         wo_shared = lax.psum_scatter(
             summed([wo_chips], wo_near), "fsdp", scatter_dimension=0, tiled=True, axis_index_groups=along
@@ -1262,30 +1288,27 @@
         wo_shared = lax.psum_scatter(wo_chips[0], "fsdp", scatter_dimension=0, tiled=True)
     input_grad = to_input(hidden_in, middle_grad, w_qkv, (dq0, dk0, dv0, dq1, dk1, dv1))
     near0, far1, input_grad = tie(near0, far1, input_grad)
-    near1 = near_of((chips1, far1))
-    owned = to_owner(jnp.stack([shared0, after(shared1, near1)], axis=1))
-    out_low, near1, wo_shared = tie(out_low, near1, wo_shared)
+    near1, near0 = tie(near_sums_of(chips1, far1), near0)
+    near1 = [swap(value, bit, n) for value, bit in zip(near1, (2, 4))]
+
+    def over_layers(chips, near_sums):
+        if not split:
+            return [lax.psum_scatter(chips[0], "fsdp", scatter_dimension=0, tiled=True)]
+        total = summed([chips], near_sums)
+        return layer_start(total.reshape(layers, own_rows, -1), layer, layers, n)
+
+    late0 = over_layers(chips0, near0)
+    owned1 = to_owner(after(shared1, near1))
+    out_low, near1, wo_shared, late0 = tie(out_low, near1, wo_shared, late0)
     mine_out = wide(wo_shared)
     out_total = wide(part[0][0]) + wide(out_other) + jnp.concatenate(
         [wide(out_low[0]) + wide(out_low[1]), wide(out_high[0]) + wide(out_high[1])], axis=0
     )
     mixed = (middle + resid_scale * out_total).astype(bf16)
-    if split:
-        total = jnp.concatenate([summed([chips0], near0), summed([chips1], near1)], axis=1)
-        late, owned = tie(layer_start(total.reshape(layers, own_rows, -1), layer, layers, n), owned)
-        late = layer_add(late)
-    else:
-        late = jnp.concatenate(
-            [
-                wide(lax.psum_scatter(chips[0], "fsdp", scatter_dimension=0, tiled=True))
-                for chips in (chips0, chips1)
-            ],
-            axis=1,
-        )
-    unit = chips0[0].shape[1]
-    mine = [late[:, :unit], late[:, unit:]]
-
-    shared = owned.reshape(E, per_expert, hidden).astype(f32)
+    late1, owned1 = tie(over_layers(chips1, near1), owned1)
+    mine = [layer_add(late0), layer_add(late1)]
+
+    shared = jnp.stack([owned0, owned1], axis=1).reshape(E, per_expert, hidden).astype(f32)
     grad_gate, grad_up = shared[:, :own_rows], shared[:, own_rows : 2 * own_rows]
     grad_down = jnp.concatenate(
         [

time: 620 us -> 612 us (0.987)
  waiting for transfers between devices: 143 us -> 123 us
  starting transfers between devices: 79.5 us -> 92.2 us
    ppermute x11 -> x14, waiting for transfers between devices: 46 us -> 32.9 us  [shift(): return lax.ppermute(value, 'fsdp', moved)]
    ppermute x11 -> x14, starting transfers between devices: 20.3 us -> 27.1 us  [shift(): return lax.ppermute(value, 'fsdp', moved)]
    ppermute x74 -> x79, waiting for transfers between devices: 90.8 us -> 85.6 us  [swap(): lax.ppermute(value, 'fsdp', [(i, i ^ bit) for i in range(device_count)])]
    unnamed x173 -> x181, local copies, waits for them, and re-layouts: 26.4 us -> 23.6 us
    ppermute x74 -> x79, starting transfers between devices: 49.8 us -> 51.6 us  [swap(): lax.ppermute(value, 'fsdp', [(i, i ^ bit) for i in range(device_count)])]
  transfers between devices with their start and end apart: 92 -> 101, of which waited for: 33 -> 38; matrix products, arithmetic and copies ran while one was open for 5% -> 4% of each run, Pallas kernels for 51% -> 51%
where the time goes in v5:
time: 612 us; the launch traced here: 607 us
  Pallas kernels  313 us (51%)
  waiting for transfers between devices  123 us (20%)
  starting transfers between devices  92.2 us (15%)
  local copies, waits for them, and re-layouts  37.6 us (6%)
  other arithmetic  26 us (4%)
  between operations  15.4 us (3%)
    pallas_call x6, Pallas kernels, experts_call(): pl.pallas_call(functools.partial(experts_kernel, [len(t) for t in tiles],...  167 us
    ppermute x79, waiting for transfers between devices, swap(): lax.ppermute(value, 'fsdp', [(i, i ^ bit) for i in range(device_count)])  85.6 us
    ppermute x79, starting transfers between devices, swap(): lax.ppermute(value, 'fsdp', [(i, i ^ bit) for i in range(device_count)])  51.6 us
    pallas_call x2, Pallas kernels, attend_backward(): pl.pallas_call(functools.partial(attend_back_kernel, 128, min(members, 2)...  36.4 us
    ppermute x14, waiting for transfers between devices, shift(): return lax.ppermute(value, 'fsdp', moved)  32.9 us
    pallas_call x2, Pallas kernels, attend_forward(): pl.pallas_call(functools.partial(attend_kernel, 128, plan), grid=(steps,)...  30 us
    ppermute x14, starting transfers between devices, shift(): return lax.ppermute(value, 'fsdp', moved)  27.1 us
    unnamed x181, local copies, waits for them, and re-layouts  23.6 us
  transfers between devices with their start and end apart: 101, of which 38 were waited for; matrix products, arithmetic and copies ran while one was open for 4% of the time, Pallas kernels for 51%

profile of v5, /device:TPU:0, one launch (start us, length us, event | category | flops | bytes accessed | tf_op | source)
XLA Modules:
  0.0 607.2 jit_solution(102366871216543283)
XLA Ops:
  12.5 5.3 all-to-all-start
  18.3 4.3 collective-permute-start.2
  22.7 6.6 %collective-permute-done.2 = bf16[48,2688]{1,0:T(8,128)(2,1)S(1)} collective-permute-done((bf16[48,2688]{1,0:T(8,128)(2,1)S(1)}, bf16[48,2688]{1,0:T(8,128)(2,1)S(1)}, u32[]{:S(2)}, u32[]{:S(2)}) %collective-permute-start.2) | collective-permute-done | bytes 258080 | tf_op jit(solution)/shard_map/ppermute | solution.py:79
  29.3 4.3 collective-permute-start.3
  37.3 5.1 collective-permute-done.1
  43.5 3.9 all-to-all-done
  47.4 3.2 slice_bitcast_fusion
  53.3 4.1 collective-permute-start.7
  60.7 3.4 collective-permute-done.7
  64.2 5.3 collective-permute-done.6
  69.5 7.1 %collective-permute-done.5.refs_4_ = bf16[192,2688]{1,0:T(8,128)(2,1)S(1)} collective-permute-done((bf16[192,2688]{1,0:T(8,128)(2,1)}, bf16[192,2688]{1,0:T(8,128)(2,1)S(1)}, u32[]{:S(2)}, u32[]{:S(2)}) %collective-permute-start.5) | collective-permute-done | bytes 1032224 | tf_op jit(solution)/shard_map/ppermute | solution.py:74
  82.3 4.1 collective-permute-start.15
  86.7 3.9 collective-permute-done.15
  90.7 3.8 collective-permute-done.14
  104.6 17.5 %shard_map.229 = (bf16[1536,2688]{1,0:T(8,128)(2,1)}, bf16[512,1536]{1,0:T(8,128)(2,1)}, bf16[1536,512]{1,0:T(8,128)(2,1)}, bf16[512,768]{1,0:T(8,128)(2,1)}, bf...) custom-call(s32[8,4]{1,0:T(8,128)} %get-tuple-element.713.table_ref, ...), custom_call_target="tpu_custom_call" | custom-call | flops 1000000 | bytes 100000 | tf_op jit(solution)/shard_map/pallas_call | solution.py:467
  127.4 12.4 %shard_map.230 = (bf16[512,768]{1,0:T(8,128)(2,1)}, bf16[512,256]{1,0:T(8,128)(2,1)}, bf16[512,256]{1,0:T(8,128)(2,1)}, bf16[512,768]{1,0:T(8,128)(2,1)}, f32[2,512,128]{2,1,0:T(8,128)}) custom-call(s32[8,4]{1,0:T(8,128)} %get-tuple-element.712.table_ref, bf16[512,1536]{1,0:T(8,128)(2,1)} %get-tuple-element.355.x_ref, ...), custom_call_target="tpu_custom_call" | custom-call | flops 1000000 | bytes 100000 | tf_op jit(solution)/shard_map/pallas_call | solution.py:467
  149.4 10.8 %shard_map.231 = (bf16[1536,1536]{1,0:T(8,128)(2,1)}, f32[512,1536]{1,0:T(8,128)}, bf16[512,1664]{1,0:T(8,128)(2,1)}, f32[512,128]{1,0:T(8,128)}) custom-call(s32[8,4]{1,0:T(8,128)} %get-tuple-element.713.table_ref, bf16[512,1536]{1,0:T(8,128)(2,1)} %x_ref.5, bf16[512,768]{1,0:T(8,128)(2,1)} %get-tuple-element.364.attn0_ref.attn0_src, ...), custom_call_target="tpu_custom_call" | custom-call | flops 1000000 | bytes 100000 | tf_op jit(solution)/shard_map/pallas_call | solution.py:528
  161.9 4.3 collective-permute-done.32.refs_13_
  169.2 21.1 %shard_map.232 = (bf16[512,1536]{1,0:T(8,128)(2,1)}, bf16[512,1664]{1,0:T(8,128)(2,1)}, bf16[512,1536]{1,0:T(8,128)(2,1)}, bf16[512,1664]{1,0:T(8,128)(2,1)}, f3...) custom-call(s32[1]{0:T(128)} %bitcast.10.refs_0_, ...), custom_call_target="tpu_custom_call" | custom-call | flops 1000000 | bytes 100000 | tf_op jit(solution)/shard_map/pallas_call | solution.py:1026
  190.3 11.5 %collective-permute-done.39.refs_3_ = bf16[512,1664]{1,0:T(8,128)(2,1)S(1)} collective-permute-done((bf16[512,1664]{1,0:T(8,128)(2,1)}, bf16[512,1664]{1,0:T(8,128)(2,1)S(1)}, u32[]{:S(2)}, u32[]{:S(2)}) %collective-permute-start.39) | collective-permute-done | bytes 1703968 | tf_op jit(solution)/shard_map/ppermute | solution.py:74
  211.3 38.2 %shard_map.233 = (bf16[512,1536]{1,0:T(8,128)(2,1)}, bf16[512,1664]{1,0:T(8,128)(2,1)}, bf16[512,1536]{1,0:T(8,128)(2,1)}, bf16[512,1664]{1,0:T(8,128)(2,1)}, bf...) custom-call(s32[1]{0:T(128)} %bitcast.10.refs_0_, ...), custom_call_target="tpu_custom_call" | custom-call | flops 1000000 | bytes 100000 | tf_op jit(solution)/shard_map/pallas_call | solution.py:1026
  257.9 22.7 %shard_map.234 = (bf16[512,1536]{1,0:T(8,128)(2,1)}, bf16[512,1664]{1,0:T(8,128)(2,1)}, bf16[512,1536]{1,0:T(8,128)(2,1)}, bf16[512,1664]{1,0:T(8,128)(2,1)}, bf16[4,8,144,512]{3,2,1,0:T(8,128)(2,1)}) custom-call(s32[1]{0:T(128)} %bitcast.10.refs_0_, bf16[256,1664]{1,0:T(8,128)(2,1)} %collective-permute-done.42.refs_1_, ...), custom_call_target="tpu_custom_call" | custom-call | flops 1000000 | bytes 100000 | tf_op jit(solution)/shard_map/pallas_call | solution.py:1026
  280.8 21.6 %shard_map.235 = (bf16[512,1536]{1,0:T(8,128)(2,1)}, bf16[512,1664]{1,0:T(8,128)(2,1)}, bf16[512,1536]{1,0:T(8,128)(2,1)}, bf16[512,1664]{1,0:T(8,128)(2,1)}, f3...) custom-call(s32[1]{0:T(128)} %bitcast.10.refs_0_, bf16[256,1664]{1,0:T(8,128)(2,1)} %collective-permute-done.42.refs_1_, ...), custom_call_target="tpu_custom_call" | custom-call | flops 1000000 | bytes 100000 | tf_op jit(solution)/shard_map/pallas_call | solution.py:1026
  303.0 5.5 collective-permute-done.55
  310.2 5.0 shard_map.236
  319.3 39.9 %shard_map.237 = (bf16[512,1536]{1,0:T(8,128)(2,1)}, bf16[512,1664]{1,0:T(8,128)(2,1)}, bf16[512,1536]{1,0:T(8,128)(2,1)}, bf16[512,1664]{1,0:T(8,128)(2,1)}, bf...) custom-call(s32[1]{0:T(128)} %bitcast.10.refs_0_, ...), custom_call_target="tpu_custom_call" | custom-call | flops 1000000 | bytes 100000 | tf_op jit(solution)/shard_map/pallas_call | solution.py:1026
  360.7 3.3 collective-permute-done.60
  367.6 5.8 shard_map.238
  376.7 23.4 %shard_map.239 = (bf16[512,1536]{1,0:T(8,128)(2,1)}, bf16[512,1664]{1,0:T(8,128)(2,1)}, bf16[512,1536]{1,0:T(8,128)(2,1)}, bf16[512,1664]{1,0:T(8,128)(2,1)}, bf16[4,8,144,512]{3,2,1,0:T(8,128)(2,1)}) custom-call(s32[1]{0:T(128)} %bitcast.10.refs_0_, bf16[512,1664]{1,0:T(8,128)(2,1)} %get-tuple-element.459.refs_1_.inner_ref, ...), custom_call_target="tpu_custom_call" | custom-call | flops 1000000 | bytes 100000 | tf_op jit(solution)/shard_map/pallas_call | solution.py:1026
  400.2 12.9 %collective-permute-done.62.near2_ref = bf16[512,1664]{1,0:T(8,128)(2,1)} collective-permute-done((bf16[512,1664]{1,0:T(8,128)(2,1)}, bf16[512,1664]{1,0:T(8,128)(2,1)}, u32[]{:S(2)}, u32[]{:S(2)}) %collective-permute-start.62) | collective-permute-done | bytes 1703968 | tf_op jit(solution)/shard_map/ppermute | solution.py:74
  414.9 3.6 all-to-all-start.1
  418.5 5.0 shard_map.240
  426.9 18.2 %shard_map.241 = (bf16[768,1664]{1,0:T(8,128)(2,1)}, bf16[768,1664]{1,0:T(8,128)(2,1)}, f32[512,1536]{1,0:T(8,128)}, bf16[512,768]{1,0:T(8,128)(2,1)}, bf16[512,768]{1,0:T(8,128)(2,1)}) custom-call(s32[8,4]{1,0:T(8,128)} %get-tuple-element.712.table_ref, bf16[512,1664]{1,0:T(8,128)(2,1)} %get-tuple-element.485.own0_ref, ...), custom_call_target="tpu_custom_call" | custom-call | flops 1000000 | bytes 100000 | tf_op jit(solution)/shard_map/pallas_call | solution.py:603
  445.2 6.0 collective-permute-done.67
  451.2 4.1 shard_map.243
  457.7 4.2 shard_map.242
  466.0 18.2 %shard_map.244 = (bf16[768,1280]{1,0:T(8,128)(2,1)}, bf16[768,1280]{1,0:T(8,128)(2,1)}, bf16[512,768]{1,0:T(8,128)(2,1)}, bf16[512,256]{1,0:T(8,128)(2,1)}, bf16[512,256]{1,0:T(8,128)(2,1)}) custom-call(s32[8,4]{1,0:T(8,128)} %get-tuple-element.712.table_ref, bf16[1536,512]{1,0:T(8,128)(2,1)} %get-tuple-element.521.turned_ref, ...), custom_call_target="tpu_custom_call" | custom-call | flops 1000000 | bytes 100000 | tf_op jit(solution)/shard_map/pallas_call | solution.py:714
  484.2 5.6 collective-permute-done.73.refs_2_
  491.2 2.6 shard_map.245
  497.2 3.5 shard_map.246
  502.8 18.3 %shard_map.247 = (bf16[768,1280]{1,0:T(8,128)(2,1)}, bf16[768,1280]{1,0:T(8,128)(2,1)}, bf16[512,768]{1,0:T(8,128)(2,1)}, bf16[512,256]{1,0:T(8,128)(2,1)}, bf16[512,256]{1,0:T(8,128)(2,1)}) custom-call(s32[8,4]{1,0:T(8,128)} %get-tuple-element.712.table_ref, bf16[1536,512]{1,0:T(8,128)(2,1)} %get-tuple-element.521.turned_ref, ...), custom_call_target="tpu_custom_call" | custom-call | flops 1000000 | bytes 100000 | tf_op jit(solution)/shard_map/pallas_call | solution.py:714
  526.1 3.6 shard_map.248
  532.9 11.5 %shard_map.250 = f32[512,1536]{1,0:T(8,128)} custom-call(bf16[512,1536]{1,0:T(8,128)(2,1)} %x_ref.5, f32[512,1536]{1,0:T(8,128)} %get-tuple-element.507.mgrad_ref, bf16[1536,2688]{1,0:T(8,128)(2,1)} %get-tuple-element.356.refs_0_.refs_1_.refs_2_.extras_ref.w_ref, bf16[512,768]{1,0:T(8,128)(2,1)} %get-tuple-element.575.refs_0_, ...), custom_call_target="tpu_custom_call" | custom-call | flops 1000000 | bytes 100000 | tf_op jit(solution)/shard_map/pallas_call | solution.py:775
  549.8 3.3 collective-permute-start.89
  556.0 9.3 %collective-permute-done.85 = bf16[192,1280]{1,0:T(8,128)(2,1)} collective-permute-done((bf16[192,1280]{1,0:T(8,128)(2,1)S(1)}, bf16[192,1280]{1,0:T(8,128)(2,1)}, u32[]{:S(2)}, u32[]{:S(2)}) %collective-permute-start.85) | collective-permute-done | bytes 491552 | tf_op jit(solution)/shard_map/ppermute | solution.py:74
  567.7 4.3 all-to-all-start.2
  572.0 3.3 collective-permute-start.92
  579.4 4.3 fusion.2
  (425 shorter events, 142.3 us)
Async XLA Ops:
  12.5 34.9 %all-to-all-start = ((bf16[2,8,144,512]{3,2,0,1:T(8,128)(2,1)}), bf16[2,8,144,512]{3,2,0,1:T(8,128)(2,1)}, u32[]{:S(2)}, u32[]{:S(2)}) async-start(bf16[2,8,144,512]{3,2,0,1:T(8,128)(2,1)} %bitcast.3), calls=%async_computation | async-start | bytes 4718592 | tf_op jit(solution)/shard_map/all_to_all | solution.py:1072
  17.8 151.3 %all-gather.3.cloned.1.call-start = ((), (), s32[]{:S(2)}) async-start(), calls=%async_computation.6 | async-start | bytes 5898240 | tf_op jit(solution)/shard_map/all_gather | solution.py:1075
  50.6 230.1 %all-gather.5.cloned.1.call-start = ((), (), s32[]{:S(2)}) async-start(), calls=%async_computation.7 | async-start | bytes 5898240 | tf_op jit(solution)/shard_map/all_gather | solution.py:1075
  51.1 25.5 %collective-permute-start.5 = (bf16[192,2688]{1,0:T(8,128)(2,1)}, bf16[192,2688]{1,0:T(8,128)(2,1)S(1)}, u32[]{:S(2)}, u32[]{:S(2)}) collective-permute-start(bf16[192,2688]{1,0:T(8,128)(2,1)} %pad_maximum_fusion.1.refs_0_), channel_id=1, source_target_pairs={{0,4},{1,5},{2,6},{3,7},{4,0},{5,1},{6,2},{7,3},{8,12},{9,13},{10,... | collective-permute-start | bytes 3096584 | tf_op jit(solution)/shard_map/ppermute | solution.py:74
  51.7 25.1 %collective-permute-start.4 = (bf16[192,2688]{1,0:T(8,128)(2,1)}, bf16[192,2688]{1,0:T(8,128)(2,1)S(1)}, u32[]{:S(2)}, u32[]{:S(2)}) collective-permute-start(bf16[192,2688]{1,0:T(8,128)(2,1)} %pad_maximum_fusion.1.refs_0_), channel_id=1, source_target_pairs={{0,2},{1,3},{2,0},{3,1},{4,6},{5,7},{6,4},{7,5},{8,10},{9,11},{10,... | collective-permute-start | bytes 3096584 | tf_op jit(solution)/shard_map/ppermute | solution.py:74
  60.7 20.3 %collective-permute-start.11 = (bf16[192,2688]{1,0:T(8,128)(2,1)S(1)}, bf16[192,2688]{1,0:T(8,128)(2,1)S(1)}, u32[]{:S(2)}, u32[]{:S(2)}) collective-permute-start(bf16[192,2688]{1,0:T(8,128)(2,1)S(1)} %copy-done.9), channel_id=1, source_target_pairs={{0,1},{1,0},{2,3},{3,2},{4,5},{5,4},{6,7},{7,6},{8,9},{9,8},{10,11... | collective-permute-start | bytes 3096584 | tf_op jit(solution)/shard_map/ppermute | solution.py:74
  86.5 286.9 %reduce-scatter.4.cloned.1.call-start = ((), (), s32[]{:S(2)}) async-start(), calls=%async_computation.8 | async-start | bytes 5898240 | tf_op jit(solution)/shard_map/reduce_scatter | solution.py:1164
  98.2 27.9 %collective-permute-start.20 = (bf16[192,1536]{1,0:T(8,128)(2,1)S(1)}, bf16[192,1536]{1,0:T(8,128)(2,1)}, u32[]{:S(2)}, u32[]{:S(2)}) collective-permute-start(bf16[192,1536]{1,0:T(8,128)(2,1)S(1)} %pad_maximum_fusion.2.refs_0_), channel_id=1, source_target_pairs={{0,1},{1,0},{2,3},{3,2},{4,5},{5,4},{6,7},{7,6},{8,9},{9,8},{10,11... | collective-permute-start | bytes 1769480 | tf_op jit(solution)/shard_map/ppermute | solution.py:74
  99.0 27.1 %collective-permute-start.19 = (bf16[192,1536]{1,0:T(8,128)(2,1)S(1)}, bf16[192,1536]{1,0:T(8,128)(2,1)S(1)}, u32[]{:S(2)}, u32[]{:S(2)}) collective-permute-start(bf16[192,1536]{1,0:T(8,128)(2,1)S(1)} %pad_maximum_fusion.2.refs_0_), channel_id=1, source_target_pairs={{0,4},{1,5},{2,6},{3,7},{4,0},{5,1},{6,2},{7,3},{8,12},{9,13},{10,... | collective-permute-start | bytes 1769480 | tf_op jit(solution)/shard_map/ppermute | solution.py:74
  99.7 26.4 %collective-permute-start.18 = (bf16[192,1536]{1,0:T(8,128)(2,1)S(1)}, bf16[192,1536]{1,0:T(8,128)(2,1)S(1)}, u32[]{:S(2)}, u32[]{:S(2)}) collective-permute-start(bf16[192,1536]{1,0:T(8,128)(2,1)S(1)} %pad_maximum_fusion.2.refs_0_), channel_id=1, source_target_pairs={{0,2},{1,3},{2,0},{3,1},{4,6},{5,7},{6,4},{7,5},{8,10},{9,11},{10,... | collective-permute-start | bytes 1769480 | tf_op jit(solution)/shard_map/ppermute | solution.py:74
  101.0 21.7 %collective-permute-start.22 = (bf16[128,1536]{1,0:T(8,128)(2,1)}, bf16[128,1536]{1,0:T(8,128)(2,1)S(1)}, u32[]{:S(2)}, u32[]{:S(2)}) collective-permute-start(bf16[128,1536]{1,0:T(8,128)(2,1)} %get-tuple-element.351), channel_id=1, source_target_pairs={{0,4},{1,5},{2,6},{3,7},{4,0},{5,1},{6,2},{7,3},{8,12},{9,13},{10,... | collective-permute-start | bytes 1179656 | tf_op jit(solution)/shard_map/ppermute | solution.py:74
  102.5 20.7 %collective-permute-start.21 = (bf16[128,1536]{1,0:T(8,128)(2,1)}, bf16[128,1536]{1,0:T(8,128)(2,1)S(1)}, u32[]{:S(2)}, u32[]{:S(2)}) collective-permute-start(bf16[128,1536]{1,0:T(8,128)(2,1)} %get-tuple-element.351), channel_id=1, source_target_pairs={{0,2},{1,3},{2,0},{3,1},{4,6},{5,7},{6,4},{7,5},{8,10},{9,11},{10,... | collective-permute-start | bytes 1179656 | tf_op jit(solution)/shard_map/ppermute | solution.py:74
  145.4 20.7 %collective-permute-start.32 = (bf16[256,1536]{1,0:T(8,128)(2,1)}, bf16[256,1536]{1,0:T(8,128)(2,1)}, u32[]{:S(2)}, u32[]{:S(2)}) collective-permute-start(bf16[256,1536]{1,0:T(8,128)(2,1)} %slice.100), channel_id=1, source_target_pairs={{0,4},{1,5},{2,6},{3,7},{4,0},{5,1},{6,2},{7,3},{8,12},{9,13},{10,... | collective-permute-start | bytes 2359304 | tf_op jit(solution)/shard_map/ppermute | solution.py:74
  146.2 20.8 %collective-permute-start.31 = (bf16[256,1536]{1,0:T(8,128)(2,1)}, bf16[256,1536]{1,0:T(8,128)(2,1)}, u32[]{:S(2)}, u32[]{:S(2)}) collective-permute-start(bf16[256,1536]{1,0:T(8,128)(2,1)} %slice.100), channel_id=1, source_target_pairs={{0,2},{1,3},{2,0},{3,1},{4,6},{5,7},{6,4},{7,5},{8,10},{9,11},{10,... | collective-permute-start | bytes 2359304 | tf_op jit(solution)/shard_map/ppermute | solution.py:74
  160.3 41.4 %collective-permute-start.39 = (bf16[512,1664]{1,0:T(8,128)(2,1)}, bf16[512,1664]{1,0:T(8,128)(2,1)S(1)}, u32[]{:S(2)}, u32[]{:S(2)}) collective-permute-start(bf16[512,1664]{1,0:T(8,128)(2,1)} %get-tuple-element.459.refs_1_.inner_ref), channel_id=1, source_target_pairs={{0,4},{1,5},{2,6},{3,7},{4,0},{5,1},{6,2},{7,3},{8,12},{9,13},{10,... | collective-permute-start | bytes 5111816 | tf_op jit(solution)/shard_map/ppermute | solution.py:74
  161.7 40.8 %collective-permute-start.38 = (bf16[512,1664]{1,0:T(8,128)(2,1)}, bf16[512,1664]{1,0:T(8,128)(2,1)S(1)}, u32[]{:S(2)}, u32[]{:S(2)}) collective-permute-start(bf16[512,1664]{1,0:T(8,128)(2,1)} %get-tuple-element.459.refs_1_.inner_ref), channel_id=1, source_target_pairs={{0,2},{1,3},{2,0},{3,1},{4,6},{5,7},{6,4},{7,5},{8,10},{9,11},{10,... | collective-permute-start | bytes 5111816 | tf_op jit(solution)/shard_map/ppermute | solution.py:74
  168.6 21.7 %collective-permute-start.40 = (bf16[256,1536]{1,0:T(8,128)(2,1)}, bf16[256,1536]{1,0:T(8,128)(2,1)}, u32[]{:S(2)}, u32[]{:S(2)}) collective-permute-start(bf16[256,1536]{1,0:T(8,128)(2,1)} %collective-permute-done.31.refs_7_), channel_id=1, source_target_pairs={{0,1},{1,0},{2,3},{3,2},{4,5},{5,4},{6,7},{7,6},{8,9},{9,8},{10,11... | collective-permute-start | bytes 2359304 | tf_op jit(solution)/shard_map/ppermute | solution.py:74
  169.0 21.2 %collective-permute-start.41 = (bf16[256,1536]{1,0:T(8,128)(2,1)}, bf16[256,1536]{1,0:T(8,128)(2,1)}, u32[]{:S(2)}, u32[]{:S(2)}) collective-permute-start(bf16[256,1536]{1,0:T(8,128)(2,1)} %collective-permute-done.32.refs_13_), channel_id=1, source_target_pairs={{0,1},{1,0},{2,3},{3,2},{4,5},{5,4},{6,7},{7,6},{8,9},{9,8},{10,11... | collective-permute-start | bytes 2359304 | tf_op jit(solution)/shard_map/ppermute | solution.py:74
  204.9 44.7 %collective-permute-start.43 = (bf16[256,1664]{1,0:T(8,128)(2,1)}, bf16[256,1664]{1,0:T(8,128)(2,1)}, u32[]{:S(2)}, u32[]{:S(2)}) collective-permute-start(bf16[256,1664]{1,0:T(8,128)(2,1)} %slice.109), channel_id=1, source_target_pairs={{0,2},{1,3},{2,0},{3,1},{4,6},{5,7},{6,4},{7,5},{8,10},{9,11},{10,... | collective-permute-start | bytes 2555912 | tf_op jit(solution)/shard_map/ppermute | solution.py:74
  206.4 43.2 %collective-permute-start.42 = (bf16[256,1664]{1,0:T(8,128)(2,1)}, bf16[256,1664]{1,0:T(8,128)(2,1)}, u32[]{:S(2)}, u32[]{:S(2)}) collective-permute-start(bf16[256,1664]{1,0:T(8,128)(2,1)} %slice.108), channel_id=1, source_target_pairs={{0,4},{1,5},{2,6},{3,7},{4,0},{5,1},{6,2},{7,3},{8,12},{9,13},{10,... | collective-permute-start | bytes 2555912 | tf_op jit(solution)/shard_map/ppermute | solution.py:74
  207.6 42.0 %collective-permute-start.46 = (bf16[256,1536]{1,0:T(8,128)(2,1)}, bf16[256,1536]{1,0:T(8,128)(2,1)}, u32[]{:S(2)}, u32[]{:S(2)}) collective-permute-start(bf16[256,1536]{1,0:T(8,128)(2,1)} %collective-permute-done.32.refs_13_), channel_id=1, source_target_pairs={{0,2},{1,3},{2,0},{3,1},{4,6},{5,7},{6,4},{7,5},{8,10},{9,11},{10,... | collective-permute-start | bytes 2359304 | tf_op jit(solution)/shard_map/ppermute | solution.py:74
  208.1 41.5 %collective-permute-start.44 = (bf16[128,1536]{1,0:T(8,128)(2,1)S(1)}, bf16[128,1536]{1,0:T(8,128)(2,1)S(1)}, u32[]{:S(2)}, u32[]{:S(2)}) collective-permute-start(bf16[128,1536]{1,0:T(8,128)(2,1)S(1)} %copy-done.27), channel_id=1, source_target_pairs={{0,4},{1,5},{2,6},{3,7},{4,0},{5,1},{6,2},{7,3},{8,12},{9,13},{10,... | collective-permute-start | bytes 1179656 | tf_op jit(solution)/shard_map/ppermute | solution.py:74
  210.4 39.1 %collective-permute-start.45 = (bf16[128,1536]{1,0:T(8,128)(2,1)}, bf16[128,1536]{1,0:T(8,128)(2,1)S(1)}, u32[]{:S(2)}, u32[]{:S(2)}) collective-permute-start(bf16[128,1536]{1,0:T(8,128)(2,1)} %collective-permute-done.25.refs_6_), channel_id=1, source_target_pairs={{0,4},{1,5},{2,6},{3,7},{4,0},{5,1},{6,2},{7,3},{8,12},{9,13},{10,... | collective-permute-start | bytes 1179656 | tf_op jit(solution)/shard_map/ppermute | solution.py:74
  280.7 240.4 %reduce-scatter.6.cloned.1.call-start = ((), (), s32[]{:S(2)}) async-start(), calls=%async_computation.9 | async-start | bytes 5898240 | tf_op jit(solution)/shard_map/reduce_scatter | solution.py:1164
  315.2 44.0 %collective-permute-start.56 = (bf16[256,1664]{1,0:T(8,128)(2,1)}, bf16[256,1664]{1,0:T(8,128)(2,1)S(1)}, u32[]{:S(2)}, u32[]{:S(2)}) collective-permute-start(bf16[256,1664]{1,0:T(8,128)(2,1)} %get-tuple-element.419), channel_id=1, source_target_pairs={{0,4},{1,5},{2,6},{3,7},{4,0},{5,1},{6,2},{7,3},{8,12},{9,13},{10,... | collective-permute-start | bytes 2555912 | tf_op jit(solution)/shard_map/ppermute | solution.py:74
  316.4 42.9 %collective-permute-start.57 = (bf16[256,1664]{1,0:T(8,128)(2,1)}, bf16[256,1664]{1,0:T(8,128)(2,1)S(1)}, u32[]{:S(2)}, u32[]{:S(2)}) collective-permute-start(bf16[256,1664]{1,0:T(8,128)(2,1)} %get-tuple-element.420), channel_id=1, source_target_pairs={{0,2},{1,3},{2,0},{3,1},{4,6},{5,7},{6,4},{7,5},{8,10},{9,11},{10,... | collective-permute-start | bytes 2555912 | tf_op jit(solution)/shard_map/ppermute | solution.py:74
  317.9 41.3 %collective-permute-start.58 = (bf16[256,1536]{1,0:T(8,128)(2,1)}, bf16[256,1536]{1,0:T(8,128)(2,1)S(1)}, u32[]{:S(2)}, u32[]{:S(2)}) collective-permute-start(bf16[256,1536]{1,0:T(8,128)(2,1)} %get-tuple-element.421), channel_id=1, source_target_pairs={{0,4},{1,5},{2,6},{3,7},{4,0},{5,1},{6,2},{7,3},{8,12},{9,13},{10,... | collective-permute-start | bytes 2359304 | tf_op jit(solution)/shard_map/ppermute | solution.py:74
  318.8 40.4 %collective-permute-start.59 = (bf16[256,1536]{1,0:T(8,128)(2,1)}, bf16[256,1536]{1,0:T(8,128)(2,1)S(1)}, u32[]{:S(2)}, u32[]{:S(2)}) collective-permute-start(bf16[256,1536]{1,0:T(8,128)(2,1)} %get-tuple-element.422), channel_id=1, source_target_pairs={{0,2},{1,3},{2,0},{3,1},{4,6},{5,7},{6,4},{7,5},{8,10},{9,11},{10,... | collective-permute-start | bytes 2359304 | tf_op jit(solution)/shard_map/ppermute | solution.py:74
  373.4 39.6 %collective-permute-start.62 = (bf16[512,1664]{1,0:T(8,128)(2,1)}, bf16[512,1664]{1,0:T(8,128)(2,1)}, u32[]{:S(2)}, u32[]{:S(2)}) collective-permute-start(bf16[512,1664]{1,0:T(8,128)(2,1)} %bitcast.77), channel_id=1, source_target_pairs={{0,2},{1,3},{2,0},{3,1},{4,6},{5,7},{6,4},{7,5},{8,10},{9,11},{10,... | collective-permute-start | bytes 5111816 | tf_op jit(solution)/shard_map/ppermute | solution.py:74
  375.0 39.3 %collective-permute-start.63 = (bf16[512,1664]{1,0:T(8,128)(2,1)}, bf16[512,1664]{1,0:T(8,128)(2,1)}, u32[]{:S(2)}, u32[]{:S(2)}) collective-permute-start(bf16[512,1664]{1,0:T(8,128)(2,1)} %bitcast.76), channel_id=1, source_target_pairs={{0,4},{1,5},{2,6},{3,7},{4,0},{5,1},{6,2},{7,3},{8,12},{9,13},{10,... | collective-permute-start | bytes 5111816 | tf_op jit(solution)/shard_map/ppermute | solution.py:74
  376.2 23.9 %collective-permute-start.64 = (bf16[512,1536]{1,0:T(8,128)(2,1)}, bf16[512,1536]{1,0:T(8,128)(2,1)S(1)}, u32[]{:S(2)}, u32[]{:S(2)}) collective-permute-start(bf16[512,1536]{1,0:T(8,128)(2,1)} %get-tuple-element.457), channel_id=1, source_target_pairs={{0,1},{1,0},{2,3},{3,2},{4,5},{5,4},{6,7},{7,6},{8,9},{9,8},{10,11... | collective-permute-start | bytes 4718600 | tf_op jit(solution)/shard_map/ppermute | solution.py:74
  376.2 24.0 %collective-permute-start.65 = (bf16[512,1536]{1,0:T(8,128)(2,1)}, bf16[512,1536]{1,0:T(8,128)(2,1)S(1)}, u32[]{:S(2)}, u32[]{:S(2)}) collective-permute-start(bf16[512,1536]{1,0:T(8,128)(2,1)} %get-tuple-element.458), channel_id=1, source_target_pairs={{0,1},{1,0},{2,3},{3,2},{4,5},{5,4},{6,7},{7,6},{8,9},{9,8},{10,11... | collective-permute-start | bytes 4718600 | tf_op jit(solution)/shard_map/ppermute | solution.py:74
  414.4 30.8 %collective-permute-start.69 = (bf16[512,1536]{1,0:T(8,128)(2,1)}, bf16[512,1536]{1,0:T(8,128)(2,1)S(1)}, u32[]{:S(2)}, u32[]{:S(2)}) collective-permute-start(bf16[512,1536]{1,0:T(8,128)(2,1)} %get-tuple-element.483), channel_id=1, source_target_pairs={{0,1},{1,0},{2,3},{3,2},{4,5},{5,4},{6,7},{7,6},{8,9},{9,8},{10,11... | collective-permute-start | bytes 4718600 | tf_op jit(solution)/shard_map/ppermute | solution.py:74
  414.9 30.3 %all-to-all-start.1 = ((bf16[8,144,512]{2,1,0:T(8,128)(2,1)}), bf16[8,144,512]{2,1,0:T(8,128)(2,1)S(1)}, u32[]{:S(2)}, u32[]{:S(2)}) async-start(bf16[8,144,512]{2,1,0:T(8,128)(2,1)} %bitcast.67), calls=%async_computation.2 | async-start | bytes 2359296 | tf_op jit(solution)/shard_map/all_to_all | solution.py:1231
  418.5 146.9 %reduce-scatter.8.cloned.1.call-start = ((), (), s32[]{:S(2)}) async-start(), calls=%async_computation.10 | async-start | bytes 798720 | tf_op jit(solution)/shard_map/reduce_scatter | solution.py:1284
  423.5 27.7 %collective-permute-start.67 = (bf16[256,1536]{1,0:T(8,128)(2,1)}, bf16[256,1536]{1,0:T(8,128)(2,1)S(1)}, u32[]{:S(2)}, u32[]{:S(2)}) collective-permute-start(bf16[256,1536]{1,0:T(8,128)(2,1)} %get-tuple-element.481), channel_id=1, source_target_pairs={{0,2},{1,3},{2,0},{3,1},{4,6},{5,7},{6,4},{7,5},{8,10},{9,11},{10,... | collective-permute-start | bytes 2359304 | tf_op jit(solution)/shard_map/ppermute | solution.py:74
  425.4 25.8 %collective-permute-start.68 = (bf16[256,1536]{1,0:T(8,128)(2,1)}, bf16[256,1536]{1,0:T(8,128)(2,1)}, u32[]{:S(2)}, u32[]{:S(2)}) collective-permute-start(bf16[256,1536]{1,0:T(8,128)(2,1)} %get-tuple-element.482), channel_id=1, source_target_pairs={{0,4},{1,5},{2,6},{3,7},{4,0},{5,1},{6,2},{7,3},{8,12},{9,13},{10,... | collective-permute-start | bytes 2359304 | tf_op jit(solution)/shard_map/ppermute | solution.py:74
  461.9 27.8 %collective-permute-start.71 = (bf16[256,1536]{1,0:T(8,128)(2,1)}, bf16[256,1536]{1,0:T(8,128)(2,1)S(1)}, u32[]{:S(2)}, u32[]{:S(2)}) collective-permute-start(bf16[256,1536]{1,0:T(8,128)(2,1)} %get-tuple-element.517), channel_id=1, source_target_pairs={{0,2},{1,3},{2,0},{3,1},{4,6},{5,7},{6,4},{7,5},{8,10},{9,11},{10,... | collective-permute-start | bytes 2359304 | tf_op jit(solution)/shard_map/ppermute | solution.py:74
  463.4 26.4 %collective-permute-start.72 = (bf16[256,1536]{1,0:T(8,128)(2,1)}, bf16[256,1536]{1,0:T(8,128)(2,1)S(1)}, u32[]{:S(2)}, u32[]{:S(2)}) collective-permute-start(bf16[256,1536]{1,0:T(8,128)(2,1)} %get-tuple-element.518), channel_id=1, source_target_pairs={{0,4},{1,5},{2,6},{3,7},{4,0},{5,1},{6,2},{7,3},{8,12},{9,13},{10,... | collective-permute-start | bytes 2359304 | tf_op jit(solution)/shard_map/ppermute | solution.py:74
  463.9 25.9 %collective-permute-start.73 = (bf16[96,1664]{1,0:T(8,128)(2,1)}, bf16[96,1664]{1,0:T(8,128)(2,1)S(1)}, u32[]{:S(2)}, u32[]{:S(2)}) collective-permute-start(bf16[96,1664]{1,0:T(8,128)(2,1)} %get-tuple-element.519), channel_id=1, source_target_pairs={{0,4},{1,5},{2,6},{3,7},{4,0},{5,1},{6,2},{7,3},{8,12},{9,13},{10,... | collective-permute-start | bytes 958472 | tf_op jit(solution)/shard_map/ppermute | solution.py:74
  465.4 24.4 %collective-permute-start.74 = (bf16[96,1664]{1,0:T(8,128)(2,1)}, bf16[96,1664]{1,0:T(8,128)(2,1)S(1)}, u32[]{:S(2)}, u32[]{:S(2)}) collective-permute-start(bf16[96,1664]{1,0:T(8,128)(2,1)} %get-tuple-element.520), channel_id=1, source_target_pairs={{0,2},{1,3},{2,0},{3,1},{4,6},{5,7},{6,4},{7,5},{8,10},{9,11},{10,... | collective-permute-start | bytes 958472 | tf_op jit(solution)/shard_map/ppermute | solution.py:74
  493.8 27.2 %collective-permute-start.75 = (bf16[192,1664]{1,0:T(8,128)(2,1)}, bf16[192,1664]{1,0:T(8,128)(2,1)S(1)}, u32[]{:S(2)}, u32[]{:S(2)}) collective-permute-start(bf16[192,1664]{1,0:T(8,128)(2,1)} %get-tuple-element.534), channel_id=1, source_target_pairs={{0,2},{1,3},{2,0},{3,1},{4,6},{5,7},{6,4},{7,5},{8,10},{9,11},{10,... | collective-permute-start | bytes 1916936 | tf_op jit(solution)/shard_map/ppermute | solution.py:74
  494.4 26.6 %collective-permute-start.76 = (bf16[192,1664]{1,0:T(8,128)(2,1)}, bf16[192,1664]{1,0:T(8,128)(2,1)S(1)}, u32[]{:S(2)}, u32[]{:S(2)}) collective-permute-start(bf16[192,1664]{1,0:T(8,128)(2,1)} %get-tuple-element.535), channel_id=1, source_target_pairs={{0,4},{1,5},{2,6},{3,7},{4,0},{5,1},{6,2},{7,3},{8,12},{9,13},{10,... | collective-permute-start | bytes 1916936 | tf_op jit(solution)/shard_map/ppermute | solution.py:74
  500.7 20.3 %collective-permute-start.78 = (bf16[96,1280]{1,0:T(8,128)(2,1)}, bf16[96,1280]{1,0:T(8,128)(2,1)S(1)}, u32[]{:S(2)}, u32[]{:S(2)}) collective-permute-start(bf16[96,1280]{1,0:T(8,128)(2,1)} %get-tuple-element.544), channel_id=1, source_target_pairs={{0,4},{1,5},{2,6},{3,7},{4,0},{5,1},{6,2},{7,3},{8,12},{9,13},{10,... | collective-permute-start | bytes 737288 | tf_op jit(solution)/shard_map/ppermute | solution.py:74
  501.3 19.8 %collective-permute-start.79 = (bf16[96,1280]{1,0:T(8,128)(2,1)}, bf16[96,1280]{1,0:T(8,128)(2,1)}, u32[]{:S(2)}, u32[]{:S(2)}) collective-permute-start(bf16[96,1280]{1,0:T(8,128)(2,1)} %get-tuple-element.545), channel_id=1, source_target_pairs={{0,2},{1,3},{2,0},{3,1},{4,6},{5,7},{6,4},{7,5},{8,10},{9,11},{10,... | collective-permute-start | bytes 737288 | tf_op jit(solution)/shard_map/ppermute | solution.py:74
  524.1 20.3 %collective-permute-start.81 = (bf16[192,1280]{1,0:T(8,128)(2,1)}, bf16[192,1280]{1,0:T(8,128)(2,1)}, u32[]{:S(2)}, u32[]{:S(2)}) collective-permute-start(bf16[192,1280]{1,0:T(8,128)(2,1)} %get-tuple-element.571), channel_id=1, source_target_pairs={{0,2},{1,3},{2,0},{3,1},{4,6},{5,7},{6,4},{7,5},{8,10},{9,11},{10,... | collective-permute-start | bytes 1474568 | tf_op jit(solution)/shard_map/ppermute | solution.py:74
  524.7 19.7 %collective-permute-start.82 = (bf16[192,1280]{1,0:T(8,128)(2,1)}, bf16[192,1280]{1,0:T(8,128)(2,1)}, u32[]{:S(2)}, u32[]{:S(2)}) collective-permute-start(bf16[192,1280]{1,0:T(8,128)(2,1)} %get-tuple-element.572), channel_id=1, source_target_pairs={{0,4},{1,5},{2,6},{3,7},{4,0},{5,1},{6,2},{7,3},{8,12},{9,13},{10,... | collective-permute-start | bytes 1474568 | tf_op jit(solution)/shard_map/ppermute | solution.py:74
  567.7 21.1 %all-to-all-start.2 = ((bf16[8,144,512]{2,1,0:T(8,128)(2,1)}), bf16[8,144,512]{2,1,0:T(8,128)(2,1)}, u32[]{:S(2)}, u32[]{:S(2)}) async-start(bf16[8,144,512]{2,1,0:T(8,128)(2,1)} %bitcast.66), calls=%async_computation.5 | async-start | bytes 2359296 | tf_op jit(solution)/shard_map/all_to_all | solution.py:1231
  (142 other events, 1052.1 us)
Sparse Core Ops, SparseCore 0:
  50.8 93.9 all-gather.2
  146.3 88.5 all-gather.4
  280.8 85.7 reduce-scatter.3
  414.4 84.8 reduce-scatter.5
  533.0 22.6 reduce-scatter.7

commit v6 on v5

--- a/solution.py
+++ b/solution.py
@@ -1069,6 +1069,7 @@
     per_expert = expert_rows.shape[1]
     expert_rows = expert_rows.reshape(GROUP, PAIR_E, per_expert, hidden).transpose(1, 0, 2, 3)
 
+    c_own, expert_rows = tie(core(cotangent), expert_rows)
     expert_rows = lax.all_to_all(expert_rows, "fsdp", 1, 1, tiled=True, axis_index_groups=inside)
 
     def over_all(block):
@@ -1088,7 +1089,6 @@
     cosine, sine_val = turn_tables(position)
     half = HK // 4
     c_parts = [cotangent[: rows // 4], cotangent[rows // 4 : rows // 2], cotangent[rows // 2 :]]
-    c_own = core(cotangent)
     near = lambda block: (swap(block, 2, n), swap(block, 4, n))
     cores = lambda *values: [core(value) for value in values]
     if split:
@@ -1099,7 +1099,7 @@
         cut = upper * own_rows
         blocks = ring_start(own_qkv, layers, n)
         column = joined_rows(ring_end(blocks, layers, n), ring)
-        column, expert_rows, w_out = tie(column, expert_rows, w_out)
+        column, w_out = tie(column, w_out)
 
         def far_ways(pair):
             ways = [swap(pair[0][:cut], 4, n)]
@@ -1110,8 +1110,8 @@
 
         near_qkv = near(column)
         wo_blocks = ring_start(w_out, layers, n)
-        near_qkv, wo_blocks, cosine, sine_val, c_own, c_parts = tie(
-            near_qkv, wo_blocks, cosine, sine_val, c_own, c_parts
+        near_qkv, wo_blocks, cosine, sine_val, expert_rows, c_parts = tie(
+            near_qkv, wo_blocks, cosine, sine_val, expert_rows, c_parts
         )
         far = far_ways(near_qkv)
         other = cores(column, *near_qkv)

time: 612 us -> 611 us (level)
    ppermute x79, waiting for transfers between devices: 85.6 us -> 95.5 us  [swap(): lax.ppermute(value, 'fsdp', [(i, i ^ bit) for i in range(device_count)])]
    unnamed x181 -> x183, local copies, waits for them, and re-layouts: 23.6 us -> 24.7 us
  transfers between devices with their start and end apart: 101 -> 101, of which waited for: 38 -> 37; matrix products, arithmetic and copies ran while one was open for 4% -> 5% of each run, Pallas kernels for 51% -> 52%
where the time goes in v6:
time: 611 us; the launch traced here: 606 us
  Pallas kernels  312 us (51%)
  waiting for transfers between devices  124 us (20%)
  starting transfers between devices  89.6 us (15%)
  local copies, waits for them, and re-layouts  39.7 us (6%)
  other arithmetic  24.8 us (4%)
  between operations  15.4 us (3%)
    pallas_call x6, Pallas kernels, experts_call(): pl.pallas_call(functools.partial(experts_kernel, [len(t) for t in tiles],...  167 us
    ppermute x79, waiting for transfers between devices, swap(): lax.ppermute(value, 'fsdp', [(i, i ^ bit) for i in range(device_count)])  95.5 us
    ppermute x79, starting transfers between devices, swap(): lax.ppermute(value, 'fsdp', [(i, i ^ bit) for i in range(device_count)])  52.9 us
    pallas_call x2, Pallas kernels, attend_backward(): pl.pallas_call(functools.partial(attend_back_kernel, 128, min(members, 2)...  36.4 us
    pallas_call x2, Pallas kernels, attend_forward(): pl.pallas_call(functools.partial(attend_kernel, 128, plan), grid=(steps,)...  30 us
    ppermute x14, waiting for transfers between devices, shift(): return lax.ppermute(value, 'fsdp', moved)  26.9 us
    unnamed x183, local copies, waits for them, and re-layouts  24.7 us
    ppermute x14, starting transfers between devices, shift(): return lax.ppermute(value, 'fsdp', moved)  23.5 us
  transfers between devices with their start and end apart: 101, of which 37 were waited for; matrix products, arithmetic and copies ran while one was open for 5% of the time, Pallas kernels for 52%

profile of v6, /device:TPU:0, one launch (start us, length us, event | category | flops | bytes accessed | tf_op | source)
XLA Modules:
  0.0 606.1 jit_solution(7254405179911217528)
XLA Ops:
  12.9 5.0 all-to-all-start
  18.5 4.3 collective-permute-start.2
  23.0 6.4 %collective-permute-done.2 = bf16[48,2688]{1,0:T(8,128)(2,1)S(1)} collective-permute-done((bf16[48,2688]{1,0:T(8,128)(2,1)S(1)}, bf16[48,2688]{1,0:T(8,128)(2,1)S(1)}, u32[]{:S(2)}, u32[]{:S(2)}) %collective-permute-start.2) | collective-permute-done | bytes 258080 | tf_op jit(solution)/shard_map/ppermute | solution.py:79
  29.4 4.3 collective-permute-start.3
  37.6 5.0 collective-permute-done.1
  52.3 3.0 collective-permute-done.7
  55.3 14.5 %collective-permute-done.5.refs_4_ = bf16[192,2688]{1,0:T(8,128)(2,1)S(1)} collective-permute-done((bf16[192,2688]{1,0:T(8,128)(2,1)S(1)}, bf16[192,2688]{1,0:T(8,128)(2,1)S(1)}, u32[]{:S(2)}, u32[]{:S(2)}) %collective-permute-start.5) | collective-permute-done | bytes 1032224 | tf_op jit(solution)/shard_map/ppermute | solution.py:74
  70.8 3.3 slice_bitcast_fusion
  81.1 3.9 collective-permute-start.15
  85.2 3.9 collective-permute-done.15
  89.1 4.1 collective-permute-done.14
  103.4 17.5 %shard_map.229 = (bf16[1536,2688]{1,0:T(8,128)(2,1)}, bf16[512,1536]{1,0:T(8,128)(2,1)}, bf16[1536,512]{1,0:T(8,128)(2,1)}, bf16[512,768]{1,0:T(8,128)(2,1)}, bf...) custom-call(s32[8,4]{1,0:T(8,128)} %get-tuple-element.715.table_ref, ...), custom_call_target="tpu_custom_call" | custom-call | flops 1000000 | bytes 100000 | tf_op jit(solution)/shard_map/pallas_call | solution.py:467
  126.6 12.5 %shard_map.230 = (bf16[512,768]{1,0:T(8,128)(2,1)}, bf16[512,256]{1,0:T(8,128)(2,1)}, bf16[512,256]{1,0:T(8,128)(2,1)}, bf16[512,768]{1,0:T(8,128)(2,1)}, f32[2,512,128]{2,1,0:T(8,128)}) custom-call(s32[8,4]{1,0:T(8,128)} %get-tuple-element.714.table_ref, bf16[512,1536]{1,0:T(8,128)(2,1)} %get-tuple-element.357.x_ref, ...), custom_call_target="tpu_custom_call" | custom-call | flops 1000000 | bytes 100000 | tf_op jit(solution)/shard_map/pallas_call | solution.py:467
  148.8 10.3 %shard_map.231 = (bf16[1536,1536]{1,0:T(8,128)(2,1)}, f32[512,1536]{1,0:T(8,128)}, bf16[512,1664]{1,0:T(8,128)(2,1)}, f32[512,128]{1,0:T(8,128)}) custom-call(s32[8,4]{1,0:T(8,128)} %get-tuple-element.715.table_ref, bf16[512,1536]{1,0:T(8,128)(2,1)} %x_ref.5, bf16[512,768]{1,0:T(8,128)(2,1)} %get-tuple-element.366.attn0_ref.attn0_src, ...), custom_call_target="tpu_custom_call" | custom-call | flops 1000000 | bytes 100000 | tf_op jit(solution)/shard_map/pallas_call | solution.py:528
  161.1 4.4 collective-permute-done.32.refs_13_
  168.6 21.0 %shard_map.232 = (bf16[512,1536]{1,0:T(8,128)(2,1)}, bf16[512,1664]{1,0:T(8,128)(2,1)}, bf16[512,1536]{1,0:T(8,128)(2,1)}, bf16[512,1664]{1,0:T(8,128)(2,1)}, f3...) custom-call(s32[1]{0:T(128)} %bitcast.10.refs_0_, ...), custom_call_target="tpu_custom_call" | custom-call | flops 1000000 | bytes 100000 | tf_op jit(solution)/shard_map/pallas_call | solution.py:1026
  189.6 11.4 %collective-permute-done.39.refs_3_ = bf16[512,1664]{1,0:T(8,128)(2,1)S(1)} collective-permute-done((bf16[512,1664]{1,0:T(8,128)(2,1)}, bf16[512,1664]{1,0:T(8,128)(2,1)S(1)}, u32[]{:S(2)}, u32[]{:S(2)}) %collective-permute-start.39) | collective-permute-done | bytes 1703968 | tf_op jit(solution)/shard_map/ppermute | solution.py:74
  210.7 38.3 %shard_map.233 = (bf16[512,1536]{1,0:T(8,128)(2,1)}, bf16[512,1664]{1,0:T(8,128)(2,1)}, bf16[512,1536]{1,0:T(8,128)(2,1)}, bf16[512,1664]{1,0:T(8,128)(2,1)}, bf...) custom-call(s32[1]{0:T(128)} %bitcast.10.refs_0_, ...), custom_call_target="tpu_custom_call" | custom-call | flops 1000000 | bytes 100000 | tf_op jit(solution)/shard_map/pallas_call | solution.py:1026
  250.2 2.4 collective-permute-done.51.refs_8_
  257.3 22.7 %shard_map.234 = (bf16[512,1536]{1,0:T(8,128)(2,1)}, bf16[512,1664]{1,0:T(8,128)(2,1)}, bf16[512,1536]{1,0:T(8,128)(2,1)}, bf16[512,1664]{1,0:T(8,128)(2,1)}, bf16[4,8,144,512]{3,2,1,0:T(8,128)(2,1)}) custom-call(s32[1]{0:T(128)} %bitcast.10.refs_0_, bf16[256,1664]{1,0:T(8,128)(2,1)} %collective-permute-done.42.refs_1_, ...), custom_call_target="tpu_custom_call" | custom-call | flops 1000000 | bytes 100000 | tf_op jit(solution)/shard_map/pallas_call | solution.py:1026
  280.2 21.7 %shard_map.235 = (bf16[512,1536]{1,0:T(8,128)(2,1)}, bf16[512,1664]{1,0:T(8,128)(2,1)}, bf16[512,1536]{1,0:T(8,128)(2,1)}, bf16[512,1664]{1,0:T(8,128)(2,1)}, f3...) custom-call(s32[1]{0:T(128)} %bitcast.10.refs_0_, bf16[256,1664]{1,0:T(8,128)(2,1)} %collective-permute-done.42.refs_1_, ...), custom_call_target="tpu_custom_call" | custom-call | flops 1000000 | bytes 100000 | tf_op jit(solution)/shard_map/pallas_call | solution.py:1026
  302.4 5.5 collective-permute-done.55
  309.7 5.0 shard_map.236
  318.7 40.0 %shard_map.237 = (bf16[512,1536]{1,0:T(8,128)(2,1)}, bf16[512,1664]{1,0:T(8,128)(2,1)}, bf16[512,1536]{1,0:T(8,128)(2,1)}, bf16[512,1664]{1,0:T(8,128)(2,1)}, bf...) custom-call(s32[1]{0:T(128)} %bitcast.10.refs_0_, ...), custom_call_target="tpu_custom_call" | custom-call | flops 1000000 | bytes 100000 | tf_op jit(solution)/shard_map/pallas_call | solution.py:1026
  360.2 3.3 collective-permute-done.60
  363.5 2.4 collective-permute-done.61
  367.1 5.8 shard_map.238
  375.8 23.4 %shard_map.239 = (bf16[512,1536]{1,0:T(8,128)(2,1)}, bf16[512,1664]{1,0:T(8,128)(2,1)}, bf16[512,1536]{1,0:T(8,128)(2,1)}, bf16[512,1664]{1,0:T(8,128)(2,1)}, bf16[4,8,144,512]{3,2,1,0:T(8,128)(2,1)}) custom-call(s32[1]{0:T(128)} %bitcast.10.refs_0_, bf16[512,1664]{1,0:T(8,128)(2,1)} %get-tuple-element.461.refs_1_.inner_ref, ...), custom_call_target="tpu_custom_call" | custom-call | flops 1000000 | bytes 100000 | tf_op jit(solution)/shard_map/pallas_call | solution.py:1026
  399.2 13.3 %collective-permute-done.62.near2_ref = bf16[512,1664]{1,0:T(8,128)(2,1)} collective-permute-done((bf16[512,1664]{1,0:T(8,128)(2,1)}, bf16[512,1664]{1,0:T(8,128)(2,1)}, u32[]{:S(2)}, u32[]{:S(2)}) %collective-permute-start.62) | collective-permute-done | bytes 1703968 | tf_op jit(solution)/shard_map/ppermute | solution.py:74
  414.3 3.6 all-to-all-start.1
  417.9 4.8 shard_map.240
  426.1 18.4 %shard_map.241 = (bf16[768,1664]{1,0:T(8,128)(2,1)}, bf16[768,1664]{1,0:T(8,128)(2,1)}, f32[512,1536]{1,0:T(8,128)}, bf16[512,768]{1,0:T(8,128)(2,1)}, bf16[512,768]{1,0:T(8,128)(2,1)}) custom-call(s32[8,4]{1,0:T(8,128)} %get-tuple-element.714.table_ref, bf16[512,1664]{1,0:T(8,128)(2,1)} %get-tuple-element.487.own0_ref, ...), custom_call_target="tpu_custom_call" | custom-call | flops 1000000 | bytes 100000 | tf_op jit(solution)/shard_map/pallas_call | solution.py:603
  444.5 6.1 %collective-permute-done.67 = bf16[256,1536]{1,0:T(8,128)(2,1)S(1)} collective-permute-done((bf16[256,1536]{1,0:T(8,128)(2,1)}, bf16[256,1536]{1,0:T(8,128)(2,1)S(1)}, u32[]{:S(2)}, u32[]{:S(2)}) %collective-permute-start.67) | collective-permute-done | bytes 786464 | tf_op jit(solution)/shard_map/ppermute | solution.py:74
  450.6 4.1 shard_map.243
  457.2 4.1 shard_map.242
  465.3 18.2 %shard_map.244 = (bf16[768,1280]{1,0:T(8,128)(2,1)}, bf16[768,1280]{1,0:T(8,128)(2,1)}, bf16[512,768]{1,0:T(8,128)(2,1)}, bf16[512,256]{1,0:T(8,128)(2,1)}, bf16[512,256]{1,0:T(8,128)(2,1)}) custom-call(s32[8,4]{1,0:T(8,128)} %get-tuple-element.714.table_ref, bf16[1536,512]{1,0:T(8,128)(2,1)} %get-tuple-element.523.turned_ref, ...), custom_call_target="tpu_custom_call" | custom-call | flops 1000000 | bytes 100000 | tf_op jit(solution)/shard_map/pallas_call | solution.py:714
  483.5 5.6 collective-permute-done.73.refs_2_
  490.6 2.7 shard_map.245
  496.6 3.6 shard_map.246
  502.3 18.2 %shard_map.247 = (bf16[768,1280]{1,0:T(8,128)(2,1)}, bf16[768,1280]{1,0:T(8,128)(2,1)}, bf16[512,768]{1,0:T(8,128)(2,1)}, bf16[512,256]{1,0:T(8,128)(2,1)}, bf16[512,256]{1,0:T(8,128)(2,1)}) custom-call(s32[8,4]{1,0:T(8,128)} %get-tuple-element.714.table_ref, bf16[1536,512]{1,0:T(8,128)(2,1)} %get-tuple-element.523.turned_ref, ...), custom_call_target="tpu_custom_call" | custom-call | flops 1000000 | bytes 100000 | tf_op jit(solution)/shard_map/pallas_call | solution.py:714
  525.6 3.6 shard_map.248
  532.4 11.6 %shard_map.250 = f32[512,1536]{1,0:T(8,128)} custom-call(bf16[512,1536]{1,0:T(8,128)(2,1)} %x_ref.5, f32[512,1536]{1,0:T(8,128)} %get-tuple-element.509.mgrad_ref, bf16[1536,2688]{1,0:T(8,128)(2,1)} %get-tuple-element.358.refs_0_.refs_1_.refs_2_.extras_ref.w_ref, bf16[512,768]{1,0:T(8,128)(2,1)} %get-tuple-element.577.refs_0_, ...), custom_call_target="tpu_custom_call" | custom-call | flops 1000000 | bytes 100000 | tf_op jit(solution)/shard_map/pallas_call | solution.py:775
  544.7 2.4 shard_map.251
  555.0 9.1 %collective-permute-done.85 = bf16[192,1280]{1,0:T(8,128)(2,1)} collective-permute-done((bf16[192,1280]{1,0:T(8,128)(2,1)S(1)}, bf16[192,1280]{1,0:T(8,128)(2,1)}, u32[]{:S(2)}, u32[]{:S(2)}) %collective-permute-start.85) | collective-permute-done | bytes 491552 | tf_op jit(solution)/shard_map/ppermute | solution.py:74
  566.7 4.2 all-to-all-start.2
  570.9 3.2 collective-permute-start.92
  577.6 4.3 fusion.2
  583.5 2.4 collective-permute-done.91
  (427 shorter events, 141.8 us)
Async XLA Ops:
  12.9 57.9 %all-to-all-start = ((bf16[2,8,144,512]{3,2,0,1:T(8,128)(2,1)}), bf16[2,8,144,512]{3,2,0,1:T(8,128)(2,1)}, u32[]{:S(2)}, u32[]{:S(2)}) async-start(bf16[2,8,144,512]{3,2,0,1:T(8,128)(2,1)} %bitcast.7), calls=%async_computation | async-start | bytes 4718592 | tf_op jit(solution)/shard_map/all_to_all | solution.py:1073
  18.0 150.7 %all-gather.3.cloned.1.call-start = ((), (), s32[]{:S(2)}) async-start(), calls=%async_computation.6 | async-start | bytes 5898240 | tf_op jit(solution)/shard_map/all_gather | solution.py:1076
  42.6 27.2 %collective-permute-start.5 = (bf16[192,2688]{1,0:T(8,128)(2,1)S(1)}, bf16[192,2688]{1,0:T(8,128)(2,1)S(1)}, u32[]{:S(2)}, u32[]{:S(2)}) collective-permute-start(bf16[192,2688]{1,0:T(8,128)(2,1)S(1)} %pad_maximum_fusion.1.refs_0_), channel_id=1, source_target_pairs={{0,4},{1,5},{2,6},{3,7},{4,0},{5,1},{6,2},{7,3},{8,12},{9,13},{10,... | collective-permute-start | bytes 3096584 | tf_op jit(solution)/shard_map/ppermute | solution.py:74
  44.6 26.2 %collective-permute-start.4 = (bf16[192,2688]{1,0:T(8,128)(2,1)S(1)}, bf16[192,2688]{1,0:T(8,128)(2,1)}, u32[]{:S(2)}, u32[]{:S(2)}) collective-permute-start(bf16[192,2688]{1,0:T(8,128)(2,1)S(1)} %pad_maximum_fusion.1.refs_0_), channel_id=1, source_target_pairs={{0,2},{1,3},{2,0},{3,1},{4,6},{5,7},{6,4},{7,5},{8,10},{9,11},{10,... | collective-permute-start | bytes 3096584 | tf_op jit(solution)/shard_map/ppermute | solution.py:74
  74.2 206.0 %all-gather.5.cloned.1.call-start = ((), (), s32[]{:S(2)}) async-start(), calls=%async_computation.7 | async-start | bytes 5898240 | tf_op jit(solution)/shard_map/all_gather | solution.py:1076
  85.0 288.0 %reduce-scatter.4.cloned.1.call-start = ((), (), s32[]{:S(2)}) async-start(), calls=%async_computation.8 | async-start | bytes 5898240 | tf_op jit(solution)/shard_map/reduce_scatter | solution.py:1164
  97.7 26.8 %collective-permute-start.20 = (bf16[192,1536]{1,0:T(8,128)(2,1)S(1)}, bf16[192,1536]{1,0:T(8,128)(2,1)}, u32[]{:S(2)}, u32[]{:S(2)}) collective-permute-start(bf16[192,1536]{1,0:T(8,128)(2,1)S(1)} %pad_maximum_fusion.2.refs_0_), channel_id=1, source_target_pairs={{0,1},{1,0},{2,3},{3,2},{4,5},{5,4},{6,7},{7,6},{8,9},{9,8},{10,11... | collective-permute-start | bytes 1769480 | tf_op jit(solution)/shard_map/ppermute | solution.py:74
  97.8 26.6 %collective-permute-start.19 = (bf16[192,1536]{1,0:T(8,128)(2,1)S(1)}, bf16[192,1536]{1,0:T(8,128)(2,1)S(1)}, u32[]{:S(2)}, u32[]{:S(2)}) collective-permute-start(bf16[192,1536]{1,0:T(8,128)(2,1)S(1)} %pad_maximum_fusion.2.refs_0_), channel_id=1, source_target_pairs={{0,4},{1,5},{2,6},{3,7},{4,0},{5,1},{6,2},{7,3},{8,12},{9,13},{10,... | collective-permute-start | bytes 1769480 | tf_op jit(solution)/shard_map/ppermute | solution.py:74
  98.7 25.8 %collective-permute-start.18 = (bf16[192,1536]{1,0:T(8,128)(2,1)S(1)}, bf16[192,1536]{1,0:T(8,128)(2,1)S(1)}, u32[]{:S(2)}, u32[]{:S(2)}) collective-permute-start(bf16[192,1536]{1,0:T(8,128)(2,1)S(1)} %pad_maximum_fusion.2.refs_0_), channel_id=1, source_target_pairs={{0,2},{1,3},{2,0},{3,1},{4,6},{5,7},{6,4},{7,5},{8,10},{9,11},{10,... | collective-permute-start | bytes 1769480 | tf_op jit(solution)/shard_map/ppermute | solution.py:74
  100.1 21.7 %collective-permute-start.22 = (bf16[128,1536]{1,0:T(8,128)(2,1)}, bf16[128,1536]{1,0:T(8,128)(2,1)S(1)}, u32[]{:S(2)}, u32[]{:S(2)}) collective-permute-start(bf16[128,1536]{1,0:T(8,128)(2,1)} %get-tuple-element.353), channel_id=1, source_target_pairs={{0,4},{1,5},{2,6},{3,7},{4,0},{5,1},{6,2},{7,3},{8,12},{9,13},{10,... | collective-permute-start | bytes 1179656 | tf_op jit(solution)/shard_map/ppermute | solution.py:74
  100.7 21.7 %collective-permute-start.21 = (bf16[128,1536]{1,0:T(8,128)(2,1)}, bf16[128,1536]{1,0:T(8,128)(2,1)S(1)}, u32[]{:S(2)}, u32[]{:S(2)}) collective-permute-start(bf16[128,1536]{1,0:T(8,128)(2,1)} %get-tuple-element.353), channel_id=1, source_target_pairs={{0,2},{1,3},{2,0},{3,1},{4,6},{5,7},{6,4},{7,5},{8,10},{9,11},{10,... | collective-permute-start | bytes 1179656 | tf_op jit(solution)/shard_map/ppermute | solution.py:74
  141.1 18.1 %collective-permute-start.35 = (bf16[128,1536]{1,0:T(8,128)(2,1)S(1)}, bf16[128,1536]{1,0:T(8,128)(2,1)}, u32[]{:S(2)}, u32[]{:S(2)}) collective-permute-start(bf16[128,1536]{1,0:T(8,128)(2,1)S(1)} %collective-permute-done.22.refs_11_), channel_id=1, source_target_pairs={{0,1},{1,0},{2,3},{3,2},{4,5},{5,4},{6,7},{7,6},{8,9},{9,8},{10,11... | collective-permute-start | bytes 1179656 | tf_op jit(solution)/shard_map/ppermute | solution.py:74
  144.8 20.7 %collective-permute-start.32 = (bf16[256,1536]{1,0:T(8,128)(2,1)}, bf16[256,1536]{1,0:T(8,128)(2,1)}, u32[]{:S(2)}, u32[]{:S(2)}) collective-permute-start(bf16[256,1536]{1,0:T(8,128)(2,1)} %slice.100), channel_id=1, source_target_pairs={{0,4},{1,5},{2,6},{3,7},{4,0},{5,1},{6,2},{7,3},{8,12},{9,13},{10,... | collective-permute-start | bytes 2359304 | tf_op jit(solution)/shard_map/ppermute | solution.py:74
  145.6 20.8 %collective-permute-start.31 = (bf16[256,1536]{1,0:T(8,128)(2,1)}, bf16[256,1536]{1,0:T(8,128)(2,1)}, u32[]{:S(2)}, u32[]{:S(2)}) collective-permute-start(bf16[256,1536]{1,0:T(8,128)(2,1)} %slice.100), channel_id=1, source_target_pairs={{0,2},{1,3},{2,0},{3,1},{4,6},{5,7},{6,4},{7,5},{8,10},{9,11},{10,... | collective-permute-start | bytes 2359304 | tf_op jit(solution)/shard_map/ppermute | solution.py:74
  159.2 41.8 %collective-permute-start.39 = (bf16[512,1664]{1,0:T(8,128)(2,1)}, bf16[512,1664]{1,0:T(8,128)(2,1)S(1)}, u32[]{:S(2)}, u32[]{:S(2)}) collective-permute-start(bf16[512,1664]{1,0:T(8,128)(2,1)} %get-tuple-element.461.refs_1_.inner_ref), channel_id=1, source_target_pairs={{0,4},{1,5},{2,6},{3,7},{4,0},{5,1},{6,2},{7,3},{8,12},{9,13},{10,... | collective-permute-start | bytes 5111816 | tf_op jit(solution)/shard_map/ppermute | solution.py:74
  160.0 41.8 %collective-permute-start.38 = (bf16[512,1664]{1,0:T(8,128)(2,1)}, bf16[512,1664]{1,0:T(8,128)(2,1)S(1)}, u32[]{:S(2)}, u32[]{:S(2)}) collective-permute-start(bf16[512,1664]{1,0:T(8,128)(2,1)} %get-tuple-element.461.refs_1_.inner_ref), channel_id=1, source_target_pairs={{0,2},{1,3},{2,0},{3,1},{4,6},{5,7},{6,4},{7,5},{8,10},{9,11},{10,... | collective-permute-start | bytes 5111816 | tf_op jit(solution)/shard_map/ppermute | solution.py:74
  167.9 21.7 %collective-permute-start.40 = (bf16[256,1536]{1,0:T(8,128)(2,1)}, bf16[256,1536]{1,0:T(8,128)(2,1)}, u32[]{:S(2)}, u32[]{:S(2)}) collective-permute-start(bf16[256,1536]{1,0:T(8,128)(2,1)} %collective-permute-done.31.refs_7_), channel_id=1, source_target_pairs={{0,1},{1,0},{2,3},{3,2},{4,5},{5,4},{6,7},{7,6},{8,9},{9,8},{10,11... | collective-permute-start | bytes 2359304 | tf_op jit(solution)/shard_map/ppermute | solution.py:74
  168.5 21.1 %collective-permute-start.41 = (bf16[256,1536]{1,0:T(8,128)(2,1)}, bf16[256,1536]{1,0:T(8,128)(2,1)}, u32[]{:S(2)}, u32[]{:S(2)}) collective-permute-start(bf16[256,1536]{1,0:T(8,128)(2,1)} %collective-permute-done.32.refs_13_), channel_id=1, source_target_pairs={{0,1},{1,0},{2,3},{3,2},{4,5},{5,4},{6,7},{7,6},{8,9},{9,8},{10,11... | collective-permute-start | bytes 2359304 | tf_op jit(solution)/shard_map/ppermute | solution.py:74
  204.2 44.8 %collective-permute-start.43 = (bf16[256,1664]{1,0:T(8,128)(2,1)}, bf16[256,1664]{1,0:T(8,128)(2,1)}, u32[]{:S(2)}, u32[]{:S(2)}) collective-permute-start(bf16[256,1664]{1,0:T(8,128)(2,1)} %slice.109), channel_id=1, source_target_pairs={{0,2},{1,3},{2,0},{3,1},{4,6},{5,7},{6,4},{7,5},{8,10},{9,11},{10,... | collective-permute-start | bytes 2555912 | tf_op jit(solution)/shard_map/ppermute | solution.py:74
  205.6 43.4 %collective-permute-start.42 = (bf16[256,1664]{1,0:T(8,128)(2,1)}, bf16[256,1664]{1,0:T(8,128)(2,1)}, u32[]{:S(2)}, u32[]{:S(2)}) collective-permute-start(bf16[256,1664]{1,0:T(8,128)(2,1)} %slice.108), channel_id=1, source_target_pairs={{0,4},{1,5},{2,6},{3,7},{4,0},{5,1},{6,2},{7,3},{8,12},{9,13},{10,... | collective-permute-start | bytes 2555912 | tf_op jit(solution)/shard_map/ppermute | solution.py:74
  206.5 42.5 %collective-permute-start.46 = (bf16[256,1536]{1,0:T(8,128)(2,1)}, bf16[256,1536]{1,0:T(8,128)(2,1)}, u32[]{:S(2)}, u32[]{:S(2)}) collective-permute-start(bf16[256,1536]{1,0:T(8,128)(2,1)} %collective-permute-done.32.refs_13_), channel_id=1, source_target_pairs={{0,2},{1,3},{2,0},{3,1},{4,6},{5,7},{6,4},{7,5},{8,10},{9,11},{10,... | collective-permute-start | bytes 2359304 | tf_op jit(solution)/shard_map/ppermute | solution.py:74
  207.4 41.6 %collective-permute-start.44 = (bf16[128,1536]{1,0:T(8,128)(2,1)S(1)}, bf16[128,1536]{1,0:T(8,128)(2,1)S(1)}, u32[]{:S(2)}, u32[]{:S(2)}) collective-permute-start(bf16[128,1536]{1,0:T(8,128)(2,1)S(1)} %copy-done.26), channel_id=1, source_target_pairs={{0,4},{1,5},{2,6},{3,7},{4,0},{5,1},{6,2},{7,3},{8,12},{9,13},{10,... | collective-permute-start | bytes 1179656 | tf_op jit(solution)/shard_map/ppermute | solution.py:74
  209.8 39.3 %collective-permute-start.45 = (bf16[128,1536]{1,0:T(8,128)(2,1)}, bf16[128,1536]{1,0:T(8,128)(2,1)S(1)}, u32[]{:S(2)}, u32[]{:S(2)}) collective-permute-start(bf16[128,1536]{1,0:T(8,128)(2,1)} %collective-permute-done.25.refs_6_), channel_id=1, source_target_pairs={{0,4},{1,5},{2,6},{3,7},{4,0},{5,1},{6,2},{7,3},{8,12},{9,13},{10,... | collective-permute-start | bytes 1179656 | tf_op jit(solution)/shard_map/ppermute | solution.py:74
  280.1 240.5 %reduce-scatter.6.cloned.1.call-start = ((), (), s32[]{:S(2)}) async-start(), calls=%async_computation.9 | async-start | bytes 5898240 | tf_op jit(solution)/shard_map/reduce_scatter | solution.py:1164
  314.7 44.1 %collective-permute-start.56 = (bf16[256,1664]{1,0:T(8,128)(2,1)}, bf16[256,1664]{1,0:T(8,128)(2,1)S(1)}, u32[]{:S(2)}, u32[]{:S(2)}) collective-permute-start(bf16[256,1664]{1,0:T(8,128)(2,1)} %get-tuple-element.421), channel_id=1, source_target_pairs={{0,4},{1,5},{2,6},{3,7},{4,0},{5,1},{6,2},{7,3},{8,12},{9,13},{10,... | collective-permute-start | bytes 2555912 | tf_op jit(solution)/shard_map/ppermute | solution.py:74
  315.7 43.0 %collective-permute-start.57 = (bf16[256,1664]{1,0:T(8,128)(2,1)}, bf16[256,1664]{1,0:T(8,128)(2,1)S(1)}, u32[]{:S(2)}, u32[]{:S(2)}) collective-permute-start(bf16[256,1664]{1,0:T(8,128)(2,1)} %get-tuple-element.422), channel_id=1, source_target_pairs={{0,2},{1,3},{2,0},{3,1},{4,6},{5,7},{6,4},{7,5},{8,10},{9,11},{10,... | collective-permute-start | bytes 2555912 | tf_op jit(solution)/shard_map/ppermute | solution.py:74
  317.0 41.8 %collective-permute-start.58 = (bf16[256,1536]{1,0:T(8,128)(2,1)}, bf16[256,1536]{1,0:T(8,128)(2,1)S(1)}, u32[]{:S(2)}, u32[]{:S(2)}) collective-permute-start(bf16[256,1536]{1,0:T(8,128)(2,1)} %get-tuple-element.423), channel_id=1, source_target_pairs={{0,4},{1,5},{2,6},{3,7},{4,0},{5,1},{6,2},{7,3},{8,12},{9,13},{10,... | collective-permute-start | bytes 2359304 | tf_op jit(solution)/shard_map/ppermute | solution.py:74
  318.1 40.7 %collective-permute-start.59 = (bf16[256,1536]{1,0:T(8,128)(2,1)}, bf16[256,1536]{1,0:T(8,128)(2,1)S(1)}, u32[]{:S(2)}, u32[]{:S(2)}) collective-permute-start(bf16[256,1536]{1,0:T(8,128)(2,1)} %get-tuple-element.424), channel_id=1, source_target_pairs={{0,2},{1,3},{2,0},{3,1},{4,6},{5,7},{6,4},{7,5},{8,10},{9,11},{10,... | collective-permute-start | bytes 2359304 | tf_op jit(solution)/shard_map/ppermute | solution.py:74
  373.0 39.6 %collective-permute-start.62 = (bf16[512,1664]{1,0:T(8,128)(2,1)}, bf16[512,1664]{1,0:T(8,128)(2,1)}, u32[]{:S(2)}, u32[]{:S(2)}) collective-permute-start(bf16[512,1664]{1,0:T(8,128)(2,1)} %bitcast.77), channel_id=1, source_target_pairs={{0,2},{1,3},{2,0},{3,1},{4,6},{5,7},{6,4},{7,5},{8,10},{9,11},{10,... | collective-permute-start | bytes 5111816 | tf_op jit(solution)/shard_map/ppermute | solution.py:74
  374.4 39.3 %collective-permute-start.63 = (bf16[512,1664]{1,0:T(8,128)(2,1)}, bf16[512,1664]{1,0:T(8,128)(2,1)}, u32[]{:S(2)}, u32[]{:S(2)}) collective-permute-start(bf16[512,1664]{1,0:T(8,128)(2,1)} %bitcast.76), channel_id=1, source_target_pairs={{0,4},{1,5},{2,6},{3,7},{4,0},{5,1},{6,2},{7,3},{8,12},{9,13},{10,... | collective-permute-start | bytes 5111816 | tf_op jit(solution)/shard_map/ppermute | solution.py:74
  375.2 23.9 %collective-permute-start.64 = (bf16[512,1536]{1,0:T(8,128)(2,1)}, bf16[512,1536]{1,0:T(8,128)(2,1)S(1)}, u32[]{:S(2)}, u32[]{:S(2)}) collective-permute-start(bf16[512,1536]{1,0:T(8,128)(2,1)} %get-tuple-element.459), channel_id=1, source_target_pairs={{0,1},{1,0},{2,3},{3,2},{4,5},{5,4},{6,7},{7,6},{8,9},{9,8},{10,11... | collective-permute-start | bytes 4718600 | tf_op jit(solution)/shard_map/ppermute | solution.py:74
  375.3 24.0 %collective-permute-start.65 = (bf16[512,1536]{1,0:T(8,128)(2,1)}, bf16[512,1536]{1,0:T(8,128)(2,1)S(1)}, u32[]{:S(2)}, u32[]{:S(2)}) collective-permute-start(bf16[512,1536]{1,0:T(8,128)(2,1)} %get-tuple-element.460), channel_id=1, source_target_pairs={{0,1},{1,0},{2,3},{3,2},{4,5},{5,4},{6,7},{7,6},{8,9},{9,8},{10,11... | collective-permute-start | bytes 4718600 | tf_op jit(solution)/shard_map/ppermute | solution.py:74
  413.8 30.7 %collective-permute-start.69 = (bf16[512,1536]{1,0:T(8,128)(2,1)}, bf16[512,1536]{1,0:T(8,128)(2,1)S(1)}, u32[]{:S(2)}, u32[]{:S(2)}) collective-permute-start(bf16[512,1536]{1,0:T(8,128)(2,1)} %get-tuple-element.485), channel_id=1, source_target_pairs={{0,1},{1,0},{2,3},{3,2},{4,5},{5,4},{6,7},{7,6},{8,9},{9,8},{10,11... | collective-permute-start | bytes 4718600 | tf_op jit(solution)/shard_map/ppermute | solution.py:74
  414.3 30.2 %all-to-all-start.1 = ((bf16[8,144,512]{2,1,0:T(8,128)(2,1)}), bf16[8,144,512]{2,1,0:T(8,128)(2,1)S(1)}, u32[]{:S(2)}, u32[]{:S(2)}) async-start(bf16[8,144,512]{2,1,0:T(8,128)(2,1)} %bitcast.67), calls=%async_computation.2 | async-start | bytes 2359296 | tf_op jit(solution)/shard_map/all_to_all | solution.py:1231
  417.8 146.5 %reduce-scatter.8.cloned.1.call-start = ((), (), s32[]{:S(2)}) async-start(), calls=%async_computation.10 | async-start | bytes 798720 | tf_op jit(solution)/shard_map/reduce_scatter | solution.py:1284
  422.7 27.9 %collective-permute-start.67 = (bf16[256,1536]{1,0:T(8,128)(2,1)}, bf16[256,1536]{1,0:T(8,128)(2,1)S(1)}, u32[]{:S(2)}, u32[]{:S(2)}) collective-permute-start(bf16[256,1536]{1,0:T(8,128)(2,1)} %get-tuple-element.483), channel_id=1, source_target_pairs={{0,2},{1,3},{2,0},{3,1},{4,6},{5,7},{6,4},{7,5},{8,10},{9,11},{10,... | collective-permute-start | bytes 2359304 | tf_op jit(solution)/shard_map/ppermute | solution.py:74
  424.6 26.0 %collective-permute-start.68 = (bf16[256,1536]{1,0:T(8,128)(2,1)}, bf16[256,1536]{1,0:T(8,128)(2,1)}, u32[]{:S(2)}, u32[]{:S(2)}) collective-permute-start(bf16[256,1536]{1,0:T(8,128)(2,1)} %get-tuple-element.484), channel_id=1, source_target_pairs={{0,4},{1,5},{2,6},{3,7},{4,0},{5,1},{6,2},{7,3},{8,12},{9,13},{10,... | collective-permute-start | bytes 2359304 | tf_op jit(solution)/shard_map/ppermute | solution.py:74
  461.3 27.8 %collective-permute-start.71 = (bf16[256,1536]{1,0:T(8,128)(2,1)}, bf16[256,1536]{1,0:T(8,128)(2,1)S(1)}, u32[]{:S(2)}, u32[]{:S(2)}) collective-permute-start(bf16[256,1536]{1,0:T(8,128)(2,1)} %get-tuple-element.519), channel_id=1, source_target_pairs={{0,2},{1,3},{2,0},{3,1},{4,6},{5,7},{6,4},{7,5},{8,10},{9,11},{10,... | collective-permute-start | bytes 2359304 | tf_op jit(solution)/shard_map/ppermute | solution.py:74
  462.8 26.4 %collective-permute-start.72 = (bf16[256,1536]{1,0:T(8,128)(2,1)}, bf16[256,1536]{1,0:T(8,128)(2,1)S(1)}, u32[]{:S(2)}, u32[]{:S(2)}) collective-permute-start(bf16[256,1536]{1,0:T(8,128)(2,1)} %get-tuple-element.520), channel_id=1, source_target_pairs={{0,4},{1,5},{2,6},{3,7},{4,0},{5,1},{6,2},{7,3},{8,12},{9,13},{10,... | collective-permute-start | bytes 2359304 | tf_op jit(solution)/shard_map/ppermute | solution.py:74
  463.4 25.7 %collective-permute-start.73 = (bf16[96,1664]{1,0:T(8,128)(2,1)}, bf16[96,1664]{1,0:T(8,128)(2,1)S(1)}, u32[]{:S(2)}, u32[]{:S(2)}) collective-permute-start(bf16[96,1664]{1,0:T(8,128)(2,1)} %get-tuple-element.521), channel_id=1, source_target_pairs={{0,4},{1,5},{2,6},{3,7},{4,0},{5,1},{6,2},{7,3},{8,12},{9,13},{10,... | collective-permute-start | bytes 958472 | tf_op jit(solution)/shard_map/ppermute | solution.py:74
  464.8 24.3 %collective-permute-start.74 = (bf16[96,1664]{1,0:T(8,128)(2,1)}, bf16[96,1664]{1,0:T(8,128)(2,1)S(1)}, u32[]{:S(2)}, u32[]{:S(2)}) collective-permute-start(bf16[96,1664]{1,0:T(8,128)(2,1)} %get-tuple-element.522), channel_id=1, source_target_pairs={{0,2},{1,3},{2,0},{3,1},{4,6},{5,7},{6,4},{7,5},{8,10},{9,11},{10,... | collective-permute-start | bytes 958472 | tf_op jit(solution)/shard_map/ppermute | solution.py:74
  493.2 27.3 %collective-permute-start.75 = (bf16[192,1664]{1,0:T(8,128)(2,1)}, bf16[192,1664]{1,0:T(8,128)(2,1)S(1)}, u32[]{:S(2)}, u32[]{:S(2)}) collective-permute-start(bf16[192,1664]{1,0:T(8,128)(2,1)} %get-tuple-element.536), channel_id=1, source_target_pairs={{0,2},{1,3},{2,0},{3,1},{4,6},{5,7},{6,4},{7,5},{8,10},{9,11},{10,... | collective-permute-start | bytes 1916936 | tf_op jit(solution)/shard_map/ppermute | solution.py:74
  493.8 26.8 %collective-permute-start.76 = (bf16[192,1664]{1,0:T(8,128)(2,1)}, bf16[192,1664]{1,0:T(8,128)(2,1)S(1)}, u32[]{:S(2)}, u32[]{:S(2)}) collective-permute-start(bf16[192,1664]{1,0:T(8,128)(2,1)} %get-tuple-element.537), channel_id=1, source_target_pairs={{0,4},{1,5},{2,6},{3,7},{4,0},{5,1},{6,2},{7,3},{8,12},{9,13},{10,... | collective-permute-start | bytes 1916936 | tf_op jit(solution)/shard_map/ppermute | solution.py:74
  500.2 20.4 %collective-permute-start.78 = (bf16[96,1280]{1,0:T(8,128)(2,1)}, bf16[96,1280]{1,0:T(8,128)(2,1)S(1)}, u32[]{:S(2)}, u32[]{:S(2)}) collective-permute-start(bf16[96,1280]{1,0:T(8,128)(2,1)} %get-tuple-element.546), channel_id=1, source_target_pairs={{0,4},{1,5},{2,6},{3,7},{4,0},{5,1},{6,2},{7,3},{8,12},{9,13},{10,... | collective-permute-start | bytes 737288 | tf_op jit(solution)/shard_map/ppermute | solution.py:74
  500.8 19.8 %collective-permute-start.79 = (bf16[96,1280]{1,0:T(8,128)(2,1)}, bf16[96,1280]{1,0:T(8,128)(2,1)}, u32[]{:S(2)}, u32[]{:S(2)}) collective-permute-start(bf16[96,1280]{1,0:T(8,128)(2,1)} %get-tuple-element.547), channel_id=1, source_target_pairs={{0,2},{1,3},{2,0},{3,1},{4,6},{5,7},{6,4},{7,5},{8,10},{9,11},{10,... | collective-permute-start | bytes 737288 | tf_op jit(solution)/shard_map/ppermute | solution.py:74
  523.6 20.4 %collective-permute-start.81 = (bf16[192,1280]{1,0:T(8,128)(2,1)}, bf16[192,1280]{1,0:T(8,128)(2,1)}, u32[]{:S(2)}, u32[]{:S(2)}) collective-permute-start(bf16[192,1280]{1,0:T(8,128)(2,1)} %get-tuple-element.573), channel_id=1, source_target_pairs={{0,2},{1,3},{2,0},{3,1},{4,6},{5,7},{6,4},{7,5},{8,10},{9,11},{10,... | collective-permute-start | bytes 1474568 | tf_op jit(solution)/shard_map/ppermute | solution.py:74
  524.2 19.8 %collective-permute-start.82 = (bf16[192,1280]{1,0:T(8,128)(2,1)}, bf16[192,1280]{1,0:T(8,128)(2,1)}, u32[]{:S(2)}, u32[]{:S(2)}) collective-permute-start(bf16[192,1280]{1,0:T(8,128)(2,1)} %get-tuple-element.574), channel_id=1, source_target_pairs={{0,4},{1,5},{2,6},{3,7},{4,0},{5,1},{6,2},{7,3},{8,12},{9,13},{10,... | collective-permute-start | bytes 1474568 | tf_op jit(solution)/shard_map/ppermute | solution.py:74
  566.7 21.1 %all-to-all-start.2 = ((bf16[8,144,512]{2,1,0:T(8,128)(2,1)}), bf16[8,144,512]{2,1,0:T(8,128)(2,1)}, u32[]{:S(2)}, u32[]{:S(2)}) async-start(bf16[8,144,512]{2,1,0:T(8,128)(2,1)} %bitcast.66), calls=%async_computation.5 | async-start | bytes 2359296 | tf_op jit(solution)/shard_map/all_to_all | solution.py:1231
  (143 other events, 1067.4 us)
Sparse Core Ops, SparseCore 0:
  74.3 90.7 all-gather.2
  166.7 88.7 all-gather.4
  280.2 84.1 reduce-scatter.3
  413.8 83.3 reduce-scatter.5
  532.5 20.9 reduce-scatter.7
